TPU v7x, 256 devices: a whole 4x4x8 slice. The times are simulated.
256 devices in a mesh: pb: 16 (over z, y_lo), ka: 16 (over y_hi, x, core).
Axes of the slice: x: 4, y: 4 (y_hi: 2, y_lo: 2; y = y_hi * 2 + y_lo), z: 8, core: 2. Of those that a mesh axis runs over, the one named last changes fastest.
Arguments:
- queries: bfloat16 [65536, 768], P(('pb', 'ka')), may hold values from -5 to 5
- key_heads: bfloat16 [65536, 128], P(('pb', 'ka')), may hold values from -5 to 5
- value_heads: bfloat16 [65536, 128], P(('pb', 'ka')), may hold values from -6 to 6
- grad_output: bfloat16 [65536, 768], P(('pb', 'ka')), may hold values from -6 to 6
- token_logprob: float32 [65536], P(('pb', 'ka')), may hold values from -8 to -0.05
- doc_ids: int32 [65536], P(('pb', 'ka')), may hold values from 0 to 63, as said below
- response: int32 [65536], P(('pb', 'ka')), may hold values from 0 to 1, as said below
Outputs:
- attention: bfloat16 [65536, 768], P(('pb', 'ka'))
- grad_queries: float32 [65536, 768], P(('pb', 'ka'))
- grad_keys: float32 [65536, 128], P(('pb', 'ka'))
- grad_values: float32 [65536, 128], P(('pb', 'ka'))
- margins: float32 [32], replicated
Inputs may be any that keep to these rules, and one draw needn't show every extreme that they name: `doc_ids`: never falling; documents 2p and 2p + 1 are the chosen and the rejected sequence of pair p and together fill positions p * 2048 to (p + 1) * 2048 - 1; every document starts at a multiple of 8 positions and has 8 positions or more; some document has exactly 2040 positions. Each document is 1 or more prompt positions followed by 1 or more response positions; both documents of a pair have prompts of equal length.
All inputs are finite; a program needn't handle non-finite values.
Results may differ from a plain program's by a relative error of at most 0.03.
Values may be sent and summed in bfloat16 or wider, within the bound.
No kernel may reach another device: no remote copies, remote signals or barrier semaphores. Data moves between devices by JAX's collectives and lax.ppermute only.
A program may use at most 64 MiB of HBM per device.

v0:
```python
import math

import jax
import jax.numpy as jnp
from jax import lax
from jax.sharding import PartitionSpec as P

HEAD_DIM = 128
GROUP_Q = 6
KV_GROUPS = 1
PAIR_SPAN = 2048


NEG = -1e30


def shifted(block, axis, distance):
    devices = range(lax.axis_size(axis))
    route = [(i - distance, i) for i in devices if i - distance in devices]
    return lax.ppermute(block, axis, route)


def split_heads(block):
    return block.reshape(block.shape[0], KV_GROUPS, GROUP_Q, HEAD_DIM)


def split_groups(block):
    return block.reshape(block.shape[0], KV_GROUPS, HEAD_DIM)


def mask_of(query_pos, query_doc, key_pos, key_doc):
    same_doc = query_doc[:, None] == key_doc[None, :]
    return same_doc & (key_pos[None, :] <= query_pos[:, None]) & (key_pos[None, :] >= 0)


def raw_scores(query_block, key_block, allowed):
    inv_root = 1.0 / math.sqrt(HEAD_DIM)
    scores = (
        jnp.einsum(
            "qghd,kgd->ghqk",
            split_heads(query_block),
            split_groups(key_block),
            preferred_element_type=jnp.float32,
        )
        * inv_root
    )
    return jnp.where(allowed, scores, NEG)


def tile_stats(query_block, key_block, allowed):
    stat_shape = (KV_GROUPS, GROUP_Q, query_block.shape[0])

    def active(unused):
        scores = raw_scores(query_block, key_block, allowed)
        row_max = jnp.max(scores, axis=-1)
        row_sum = jnp.sum(jnp.where(allowed, jnp.exp(scores - row_max[..., None]), 0.0), axis=-1)
        return (row_max, row_sum)

    def skipped(unused):
        return (jnp.full(stat_shape, NEG, jnp.float32), jnp.zeros(stat_shape, jnp.float32))

    return lax.cond(jnp.any(allowed), active, skipped, 0)


def merge_rows(first, second):
    row_max = jnp.maximum(first[0], second[0])
    return (
        row_max,
        first[1] * jnp.exp(first[0] - row_max) + second[1] * jnp.exp(second[0] - row_max),
    )


def tile_probs(query_block, key_block, allowed, log_total):
    scores = raw_scores(query_block, key_block, allowed)
    return jnp.where(allowed, jnp.exp(scores - log_total[..., None]), 0.0).astype(jnp.bfloat16)


def tile_output(query_block, key_block, value_block, allowed, log_total):

    def active(unused):
        prob_tile = tile_probs(query_block, key_block, allowed, log_total)
        summed = jnp.einsum(
            "ghqk,kgd->qghd",
            prob_tile,
            split_groups(value_block),
            preferred_element_type=jnp.float32,
        )
        return summed.reshape(query_block.shape)

    def skipped(unused):
        return jnp.zeros(query_block.shape, jnp.float32)

    return lax.cond(jnp.any(allowed), active, skipped, 0)


def tile_grads(query_block, key_block, value_block, grad_block, allowed, log_total, delta_heads):
    inv_root = 1.0 / math.sqrt(HEAD_DIM)

    def active(unused):
        prob_tile = tile_probs(query_block, key_block, allowed, log_total)
        grad_prob = jnp.einsum(
            "qghd,kgd->ghqk",
            split_heads(grad_block),
            split_groups(value_block),
            preferred_element_type=jnp.float32,
        )
        grad_score = (prob_tile.astype(jnp.float32) * (grad_prob - delta_heads[..., None])).astype(
            jnp.bfloat16
        )
        query_part = (
            jnp.einsum(
                "ghqk,kgd->qghd",
                grad_score,
                split_groups(key_block),
                preferred_element_type=jnp.float32,
            )
            * inv_root
        )
        key_part = (
            jnp.einsum(
                "ghqk,qghd->kgd",
                grad_score,
                split_heads(query_block),
                preferred_element_type=jnp.float32,
            )
            * inv_root
        )
        value_part = jnp.einsum(
            "ghqk,qghd->kgd", prob_tile, split_heads(grad_block), preferred_element_type=jnp.float32
        )
        return (
            query_part.reshape(query_block.shape),
            key_part.reshape(key_block.shape),
            value_part.reshape(key_block.shape),
        )

    def skipped(unused):
        return (
            jnp.zeros(query_block.shape, jnp.float32),
            jnp.zeros(key_block.shape, jnp.float32),
            jnp.zeros(key_block.shape, jnp.float32),
        )

    return lax.cond(jnp.any(allowed), active, skipped, 0)


def row_delta(grad_rows, output_rows):
    product = grad_rows.astype(jnp.float32) * output_rows.astype(jnp.float32)
    return jnp.sum(product.reshape(grad_rows.shape[0], KV_GROUPS * GROUP_Q, HEAD_DIM), axis=-1)


def to_heads(delta_rows):
    return delta_rows.T.reshape(KV_GROUPS, GROUP_Q, delta_rows.shape[0])


def per_device(queries, key_heads, value_heads, grad_output, token_logprob, doc_ids, response):
    count_pb = lax.axis_size("pb")
    count_ka = lax.axis_size("ka")
    local_rows = queries.shape[0]
    index = lax.axis_index("pb") * count_ka + lax.axis_index("ka")
    look_back = PAIR_SPAN // local_rows - 1
    window_len = look_back + 1
    own_pos = index * local_rows + jnp.arange(local_rows, dtype=jnp.int32)
    key_list, value_list, doc_list = ([], [], [])
    for distance in range(look_back, 0, -1):
        earlier = shifted((key_heads, value_heads, doc_ids), ("pb", "ka"), distance)
        key_list.append(earlier[0])
        value_list.append(earlier[1])
        doc_list.append(earlier[2])
    window_keys = jnp.concatenate(key_list + [key_heads], axis=0)
    window_values = jnp.concatenate(value_list + [value_heads], axis=0)
    window_docs = jnp.concatenate(doc_list + [doc_ids], axis=0)
    window_first = (index - look_back) * local_rows
    block_ids = jnp.arange(window_len, dtype=jnp.int32)

    def slice_keys(number):
        offset = number * local_rows
        key_part = lax.dynamic_slice_in_dim(window_keys, offset, local_rows, 0)
        value_part = lax.dynamic_slice_in_dim(window_values, offset, local_rows, 0)
        doc_part = lax.dynamic_slice_in_dim(window_docs, offset, local_rows, 0)
        pos_part = window_first + offset + jnp.arange(local_rows, dtype=jnp.int32)
        return (key_part, value_part, mask_of(own_pos, doc_ids, pos_part, doc_part))

    def stat_step(running, number):
        key_part, value_part, allowed = slice_keys(number)
        return (merge_rows(running, tile_stats(queries, key_part, allowed)), None)

    stat_shape = (KV_GROUPS, GROUP_Q, local_rows)
    stat_init = (jnp.full(stat_shape, NEG, jnp.float32), jnp.zeros(stat_shape, jnp.float32))
    (row_max, row_sum), unused = lax.scan(stat_step, stat_init, block_ids)
    log_total = row_max + jnp.log(row_sum)

    def out_step(running, number):
        key_part, value_part, allowed = slice_keys(number)
        return (running + tile_output(queries, key_part, value_part, allowed, log_total), None)

    summed, unused = lax.scan(out_step, jnp.zeros(queries.shape, jnp.float32), block_ids)
    attention = summed.astype(jnp.bfloat16)
    delta_heads = to_heads(row_delta(grad_output, attention))

    def grad_step(running, number):
        key_part, value_part, allowed = slice_keys(number)
        query_part, key_grad, value_grad = tile_grads(
            queries, key_part, value_part, grad_output, allowed, log_total, delta_heads
        )
        return (running + query_part, (key_grad, value_grad))

    grad_queries, (stacked_keys, stacked_values) = lax.scan(
        grad_step, jnp.zeros(queries.shape, jnp.float32), block_ids
    )
    key_terms = stacked_keys.reshape(window_len * local_rows, stacked_keys.shape[-1])
    value_terms = stacked_values.reshape(window_len * local_rows, stacked_values.shape[-1])
    grad_keys = key_terms[look_back * local_rows :]
    grad_values = value_terms[look_back * local_rows :]
    for distance in range(1, look_back + 1):
        begin = (look_back - distance) * local_rows
        returned = (
            shifted(
                key_terms[begin : begin + local_rows].astype(jnp.bfloat16), ("pb", "ka"), -distance
            ).astype(jnp.float32),
            shifted(
                value_terms[begin : begin + local_rows].astype(jnp.bfloat16),
                ("pb", "ka"),
                -distance,
            ).astype(jnp.float32),
        )
        grad_keys = grad_keys + returned[0]
        grad_values = grad_values + returned[1]
    documents = 2 * (local_rows * count_pb * count_ka // PAIR_SPAN)
    member = (doc_ids[:, None] == jnp.arange(documents, dtype=jnp.int32)[None, :]).astype(
        jnp.float32
    )
    live = response.astype(jnp.float32)
    doc_sum = jnp.sum(member * (token_logprob * live)[:, None], axis=0)
    doc_count = jnp.sum(member * live[:, None], axis=0)
    doc_sum, doc_count = lax.psum((doc_sum, doc_count), ("pb", "ka"))
    average = doc_sum / doc_count
    margins = average[0::2] - average[1::2]
    return (attention, grad_queries, grad_keys, grad_values, margins)


def solution(mesh):
    placed = (
        P(("pb", "ka"), None),
        P(("pb", "ka"), None),
        P(("pb", "ka"), None),
        P(("pb", "ka"), None),
        P(("pb", "ka")),
        P(("pb", "ka")),
        P(("pb", "ka")),
    )
    return jax.shard_map(
        per_device,
        mesh=mesh,
        in_specs=placed,
        out_specs=(
            P(("pb", "ka"), None),
            P(("pb", "ka"), None),
            P(("pb", "ka"), None),
            P(("pb", "ka"), None),
            P(),
        ),
        check_vma=False,
    )
```

profile of v0, /device:TPU:8, one launch (start us, length us, event | category | flops | bytes accessed | tf_op | source)
XLA Modules:
  0.0 381.5 jit_solution(1542776166243630926)
XLA Ops:
  0.7 4.2 %collective-permute-start = (s32[256]{0:T(256)}, s32[256]{0:T(256)S(1)}, u32[]{:S(2)}, u32[]{:S(2)}) collective-permute-start(s32[256]{0:T(256)} %param.24), channel_id=1, source_target_pairs={{0,7},{1,8},{2,9},{3,10},{4,11},{5,12},{6,13},{7,14},{8,15},{9,16}... | collective-permute-start | bytes 3080 | tf_op jit(solution)/shard_map/ppermute | solution.py:20
  4.9 4.5 %collective-permute-start.1 = (s32[256]{0:T(256)}, s32[256]{0:T(256)S(1)}, u32[]{:S(2)}, u32[]{:S(2)}) collective-permute-start(s32[256]{0:T(256)} %param.24), channel_id=1, source_target_pairs={{0,6},{1,7},{2,8},{3,9},{4,10},{5,11},{6,12},{7,13},{8,14},{9,15},... | collective-permute-start | bytes 3080 | tf_op jit(solution)/shard_map/ppermute | solution.py:20
  9.4 3.5 collective-permute-start.2
  12.8 4.7 %collective-permute-start.3 = (s32[256]{0:T(256)}, s32[256]{0:T(256)S(1)}, u32[]{:S(2)}, u32[]{:S(2)}) collective-permute-start(s32[256]{0:T(256)} %param.24), channel_id=1, source_target_pairs={{0,4},{1,5},{2,6},{3,7},{4,8},{5,9},{6,10},{7,11},{8,12},{9,13},{1... | collective-permute-start | bytes 3080 | tf_op jit(solution)/shard_map/ppermute | solution.py:20
  17.5 2.6 collective-permute-start.4
  24.5 4.0 %collective-permute-start.5 = (s32[256]{0:T(256)S(1)}, s32[256]{0:T(256)S(1)}, u32[]{:S(2)}, u32[]{:S(2)}) collective-permute-start(s32[256]{0:T(256)S(1)} %copy-done.2), channel_id=1, source_target_pairs={{0,2},{1,3},{2,4},{3,5},{4,6},{5,7},{6,8},{7,9},{8,10},{9,11},{10,... | collective-permute-start | bytes 3080 | tf_op jit(solution)/shard_map/ppermute | solution.py:20
  28.6 3.2 collective-permute-start.6
  31.8 3.8 collective-permute-start.7
  35.6 3.6 collective-permute-start.8
  39.2 3.9 %collective-permute-start.9 = (bf16[256,128]{1,0:T(8,128)(2,1)S(1)}, bf16[256,128]{1,0:T(8,128)(2,1)S(1)}, u32[]{:S(2)}, u32[]{:S(2)}) collective-permute-start(bf16[256,128]{1,0:T(8,128)(2,1)S(1)} %copy-done.3), channel_id=1, source_target_pairs={{0,5},{1,6},{2,7},{3,8},{4,9},{5,10},{6,11},{7,12},{8,13},{9,14},{... | collective-permute-start | bytes 196616 | tf_op jit(solution)/shard_map/ppermute | solution.py:20
  43.2 4.9 %collective-permute-start.10 = (bf16[256,128]{1,0:T(8,128)(2,1)S(1)}, bf16[256,128]{1,0:T(8,128)(2,1)S(1)}, u32[]{:S(2)}, u32[]{:S(2)}) collective-permute-start(bf16[256,128]{1,0:T(8,128)(2,1)S(1)} %copy-done.3), channel_id=1, source_target_pairs={{0,4},{1,5},{2,6},{3,7},{4,8},{5,9},{6,10},{7,11},{8,12},{9,13},{1... | collective-permute-start | bytes 196616 | tf_op jit(solution)/shard_map/ppermute | solution.py:20
  48.1 1.9 collective-permute-start.11
  50.1 3.9 %collective-permute-start.12 = (bf16[256,128]{1,0:T(8,128)(2,1)S(1)}, bf16[256,128]{1,0:T(8,128)(2,1)S(1)}, u32[]{:S(2)}, u32[]{:S(2)}) collective-permute-start(bf16[256,128]{1,0:T(8,128)(2,1)S(1)} %copy-done.3), channel_id=1, source_target_pairs={{0,2},{1,3},{2,4},{3,5},{4,6},{5,7},{6,8},{7,9},{8,10},{9,11},{10,... | collective-permute-start | bytes 196616 | tf_op jit(solution)/shard_map/ppermute | solution.py:20
  54.0 3.2 collective-permute-start.13
  57.2 6.2 %collective-permute-start.14 = (bf16[256,128]{1,0:T(8,128)(2,1)S(1)}, bf16[256,128]{1,0:T(8,128)(2,1)S(1)}, u32[]{:S(2)}, u32[]{:S(2)}) collective-permute-start(bf16[256,128]{1,0:T(8,128)(2,1)S(1)} %copy-done.4), channel_id=1, source_target_pairs={{0,7},{1,8},{2,9},{3,10},{4,11},{5,12},{6,13},{7,14},{8,15},{9,16}... | collective-permute-start | bytes 196616 | tf_op jit(solution)/shard_map/ppermute | solution.py:20
  63.5 1.9 collective-permute-start.15
  65.4 4.0 %collective-permute-start.16 = (bf16[256,128]{1,0:T(8,128)(2,1)S(1)}, bf16[256,128]{1,0:T(8,128)(2,1)S(1)}, u32[]{:S(2)}, u32[]{:S(2)}) collective-permute-start(bf16[256,128]{1,0:T(8,128)(2,1)S(1)} %copy-done.4), channel_id=1, source_target_pairs={{0,5},{1,6},{2,7},{3,8},{4,9},{5,10},{6,11},{7,12},{8,13},{9,14},{... | collective-permute-start | bytes 196616 | tf_op jit(solution)/shard_map/ppermute | solution.py:20
  69.4 4.7 %collective-permute-start.17 = (bf16[256,128]{1,0:T(8,128)(2,1)S(1)}, bf16[256,128]{1,0:T(8,128)(2,1)S(1)}, u32[]{:S(2)}, u32[]{:S(2)}) collective-permute-start(bf16[256,128]{1,0:T(8,128)(2,1)S(1)} %copy-done.4), channel_id=1, source_target_pairs={{0,4},{1,5},{2,6},{3,7},{4,8},{5,9},{6,10},{7,11},{8,12},{9,13},{1... | collective-permute-start | bytes 196616 | tf_op jit(solution)/shard_map/ppermute | solution.py:20
  74.1 1.9 collective-permute-start.18
  77.1 4.3 %collective-permute-start.19 = (bf16[256,128]{1,0:T(8,128)(2,1)S(1)}, bf16[256,128]{1,0:T(8,128)(2,1)S(1)}, u32[]{:S(2)}, u32[]{:S(2)}) collective-permute-start(bf16[256,128]{1,0:T(8,128)(2,1)S(1)} %copy-done.4), channel_id=1, source_target_pairs={{0,2},{1,3},{2,4},{3,5},{4,6},{5,7},{6,8},{7,9},{8,10},{9,11},{10,... | collective-permute-start | bytes 196616 | tf_op jit(solution)/shard_map/ppermute | solution.py:20
  82.1 1.9 collective-permute-start.20
  87.2 2.6 collective-permute-done.20
  91.1 35.4 %while.39 = (s32[]{:T(128)}, f32[1,6,256]{2,1,0:T(8,128)S(1)}, f32[1,6,256]{2,1,0:T(8,128)S(1)}, s32[256]{0:T(256)S(1)}, s32[8]{0:T(128)S(1)}, /*index=5*/s32[20...) while((s32[]{:T(128)}, f32[1,6,256]{2,1,0:T(8,128)S(1)}, ...), condition=%wide.region_6.7_spmd.clone, body=%wide.region_0.6_spmd.clone.sunk | while | flops 103360520 | bytes 3865891 | solution.py:190
  122.9 2.8 conditional.9
  123.0 1.8 fusion.66
  126.5 26.5 %while.40 = (s32[]{:T(128)}, f32[256,768]{0,1:T(8,128)S(1)}, s32[256]{0:T(256)S(1)}, s32[8]{0:T(128)S(1)}, s32[2048]{0:T(1024)S(1)}, /*index=5*/s32[]{:T(128)}, ...) while((s32[]{:T(128)}, f32[256,768]{0,1:T(8,128)S(1)}, ...), condition=%wide.region_11.12_spmd.clone, body=%wide.region_7.11_spmd.clone.sunk | while | flops 204014592 | bytes 3817267 | solution.py:197
  151.2 1.6 conditional.10
  151.3 1.6 fusion.14
  153.9 35.4 %while.41 = (s32[]{:T(128)}, f32[256,768]{0,1:T(8,128)S(1)}, f32[8,256,128]{2,1,0:T(8,128)}, f32[8,256,128]{2,1,0:T(8,128)}, s32[256]{0:T(256)S(1)}, /*index=5*/...) while((s32[]{:T(128)}, f32[256,768]{0,1:T(8,128)S(1)}, ...), condition=%wide.region_17.18_spmd.clone, body=%wide.region_13.17_spmd.clone.sunk | while | flops 507806720 | bytes 10576247 | solution.py:208
  183.8 4.5 %conditional.11 = (f32[256,768]{0,1:T(8,128)S(1)}, f32[1,256,128]{2,1,0:T(8,128)S(1)}, f32[1,256,128]{2,1,0:T(8,128)S(1)}) conditional(s32[]{:T(128)} %convert_element_type.210, () %tuple.158, (bf16[2048,128]{1,0:T(8,128)(2,1)}, s32[]{:T(128)}, pred[256,256]{0,1:T(8,128)(4,1)S(1)}, bf16[256,768]{0,1:T(8,128)(2,1)S(1)}, f32[1,6,256]{2,1,0:T(8,128)}, ...), branch_computations={%region_15.15_spmd, %region_16.16_spmd} | conditional | flops 507084800 | bytes 7618072 | solution.py:144
  183.9 1.4 fusion.36
  189.3 1.4 convert.18
  190.8 8.9 %collective-permute-start.27 = (bf16[256,128]{1,0:T(8,128)(2,1)S(1)}, bf16[256,128]{1,0:T(8,128)(2,1)S(1)}, u32[]{:S(2)}, u32[]{:S(2)}) collective-permute-start(bf16[256,128]{1,0:T(8,128)(2,1)S(1)} %get-tuple-element.679), channel_id=1, source_target_pairs={{7,0},{8,1},{9,2},{10,3},{11,4},{12,5},{13,6},{14,7},{15,8},{16,9}... | collective-permute-start | bytes 196616 | tf_op jit(solution)/shard_map/ppermute | solution.py:20
  199.7 13.5 %collective-permute-start.26 = (bf16[256,128]{1,0:T(8,128)(2,1)S(1)}, bf16[256,128]{1,0:T(8,128)(2,1)S(1)}, u32[]{:S(2)}, u32[]{:S(2)}) collective-permute-start(bf16[256,128]{1,0:T(8,128)(2,1)S(1)} %get-tuple-element.680), channel_id=1, source_target_pairs={{6,0},{7,1},{8,2},{9,3},{10,4},{11,5},{12,6},{13,7},{14,8},{15,9},... | collective-permute-start | bytes 196616 | tf_op jit(solution)/shard_map/ppermute | solution.py:20
  213.2 17.3 %collective-permute-start.25 = (bf16[256,128]{1,0:T(8,128)(2,1)S(1)}, bf16[256,128]{1,0:T(8,128)(2,1)S(1)}, u32[]{:S(2)}, u32[]{:S(2)}) collective-permute-start(bf16[256,128]{1,0:T(8,128)(2,1)S(1)} %get-tuple-element.681), channel_id=1, source_target_pairs={{5,0},{6,1},{7,2},{8,3},{9,4},{10,5},{11,6},{12,7},{13,8},{14,9},{... | collective-permute-start | bytes 196616 | tf_op jit(solution)/shard_map/ppermute | solution.py:20
  230.5 22.5 %collective-permute-start.24 = (bf16[256,128]{1,0:T(8,128)(2,1)S(1)}, bf16[256,128]{1,0:T(8,128)(2,1)S(1)}, u32[]{:S(2)}, u32[]{:S(2)}) collective-permute-start(bf16[256,128]{1,0:T(8,128)(2,1)S(1)} %get-tuple-element.682), channel_id=1, source_target_pairs={{4,0},{5,1},{6,2},{7,3},{8,4},{9,5},{10,6},{11,7},{12,8},{13,9},{1... | collective-permute-start | bytes 196616 | tf_op jit(solution)/shard_map/ppermute | solution.py:20
  253.0 1.9 collective-permute-start.23
  255.1 3.7 collective-permute-start.22
  258.9 1.9 collective-permute-start.21
  260.8 1.9 collective-permute-start.34
  262.7 1.9 collective-permute-start.33
  264.9 93.5 %all-reduce = (f32[64]{0:T(128)S(1)}, f32[64]{0:T(128)S(1)}) all-reduce(f32[64]{0:T(128)S(1)} %get-tuple-element.578, f32[64]{0:T(128)S(1)} %get-tuple-element.577), channel_id=1, replica_groups=mesh['pb'=16,'ka'=16] {'pb','ka'}, use_global_device_ids=true, to_apply=%region_19.20 | all-reduce | flops 128 | bytes 1024 | tf_op jit(solution)/shard_map/psum | solution.py:236
  361.2 2.2 collective-permute-start.32
  363.5 6.1 %collective-permute-start.31 = (bf16[256,128]{1,0:T(8,128)(2,1)S(1)}, bf16[256,128]{1,0:T(8,128)(2,1)S(1)}, u32[]{:S(2)}, u32[]{:S(2)}) collective-permute-start(bf16[256,128]{1,0:T(8,128)(2,1)S(1)} %get-tuple-element.675), channel_id=1, source_target_pairs={{4,0},{5,1},{6,2},{7,3},{8,4},{9,5},{10,6},{11,7},{12,8},{13,9},{1... | collective-permute-start | bytes 196616 | tf_op jit(solution)/shard_map/ppermute | solution.py:20
  369.6 3.6 collective-permute-start.30
  373.3 3.7 collective-permute-start.29
  377.0 1.9 collective-permute-start.28
  379.0 1.7 fusion.62
  (345 shorter events, 80.5 us)
Async XLA Ops:
  0.6 23.9 %copy-start.2 = (s32[256]{0:T(256)S(1)}, s32[256]{0:T(256)}, u32[]{:S(2)}) copy-start(s32[256]{0:T(256)} %param.24) | copy-start | bytes 3076
  0.6 31.2 %copy-start.3 = (bf16[256,128]{1,0:T(8,128)(2,1)S(1)}, bf16[256,128]{1,0:T(8,128)(2,1)}, u32[]{:S(2)}) copy-start(bf16[256,128]{1,0:T(8,128)(2,1)} %param.21) | copy-start | bytes 196612
  0.7 56.6 %copy-start.4 = (bf16[256,128]{1,0:T(8,128)(2,1)S(1)}, bf16[256,128]{1,0:T(8,128)(2,1)}, u32[]{:S(2)}) copy-start(bf16[256,128]{1,0:T(8,128)(2,1)} %param.20) | copy-start | bytes 196612
  0.7 23.8 %collective-permute-start = (s32[256]{0:T(256)}, s32[256]{0:T(256)S(1)}, u32[]{:S(2)}, u32[]{:S(2)}) collective-permute-start(s32[256]{0:T(256)} %param.24), channel_id=1, source_target_pairs={{0,7},{1,8},{2,9},{3,10},{4,11},{5,12},{6,13},{7,14},{8,15},{9,16}... | collective-permute-start | bytes 3080 | tf_op jit(solution)/shard_map/ppermute | solution.py:20
  4.9 23.6 %collective-permute-start.1 = (s32[256]{0:T(256)}, s32[256]{0:T(256)S(1)}, u32[]{:S(2)}, u32[]{:S(2)}) collective-permute-start(s32[256]{0:T(256)} %param.24), channel_id=1, source_target_pairs={{0,6},{1,7},{2,8},{3,9},{4,10},{5,11},{6,12},{7,13},{8,14},{9,15},... | collective-permute-start | bytes 3080 | tf_op jit(solution)/shard_map/ppermute | solution.py:20
  9.4 22.4 %collective-permute-start.2 = (s32[256]{0:T(256)}, s32[256]{0:T(256)S(1)}, u32[]{:S(2)}, u32[]{:S(2)}) collective-permute-start(s32[256]{0:T(256)} %param.24), channel_id=1, source_target_pairs={{0,5},{1,6},{2,7},{3,8},{4,9},{5,10},{6,11},{7,12},{8,13},{9,14},{... | collective-permute-start | bytes 3080 | tf_op jit(solution)/shard_map/ppermute | solution.py:20
  12.8 22.8 %collective-permute-start.3 = (s32[256]{0:T(256)}, s32[256]{0:T(256)S(1)}, u32[]{:S(2)}, u32[]{:S(2)}) collective-permute-start(s32[256]{0:T(256)} %param.24), channel_id=1, source_target_pairs={{0,4},{1,5},{2,6},{3,7},{4,8},{5,9},{6,10},{7,11},{8,12},{9,13},{1... | collective-permute-start | bytes 3080 | tf_op jit(solution)/shard_map/ppermute | solution.py:20
  17.5 21.7 %collective-permute-start.4 = (s32[256]{0:T(256)}, s32[256]{0:T(256)S(1)}, u32[]{:S(2)}, u32[]{:S(2)}) collective-permute-start(s32[256]{0:T(256)} %param.24), channel_id=1, source_target_pairs={{0,3},{1,4},{2,5},{3,6},{4,7},{5,8},{6,9},{7,10},{8,11},{9,12},{10... | collective-permute-start | bytes 3080 | tf_op jit(solution)/shard_map/ppermute | solution.py:20
  24.5 18.6 %collective-permute-start.5 = (s32[256]{0:T(256)S(1)}, s32[256]{0:T(256)S(1)}, u32[]{:S(2)}, u32[]{:S(2)}) collective-permute-start(s32[256]{0:T(256)S(1)} %copy-done.2), channel_id=1, source_target_pairs={{0,2},{1,3},{2,4},{3,5},{4,6},{5,7},{6,8},{7,9},{8,10},{9,11},{10,... | collective-permute-start | bytes 3080 | tf_op jit(solution)/shard_map/ppermute | solution.py:20
  28.6 19.5 %collective-permute-start.6 = (s32[256]{0:T(256)S(1)}, s32[256]{0:T(256)S(1)}, u32[]{:S(2)}, u32[]{:S(2)}) collective-permute-start(s32[256]{0:T(256)S(1)} %copy-done.2), channel_id=1, source_target_pairs={{0,1},{1,2},{2,3},{3,4},{4,5},{5,6},{6,7},{7,8},{8,9},{9,10},{10,1... | collective-permute-start | bytes 3080 | tf_op jit(solution)/shard_map/ppermute | solution.py:20
  31.8 18.2 %collective-permute-start.7 = (bf16[256,128]{1,0:T(8,128)(2,1)S(1)}, bf16[256,128]{1,0:T(8,128)(2,1)S(1)}, u32[]{:S(2)}, u32[]{:S(2)}) collective-permute-start(bf16[256,128]{1,0:T(8,128)(2,1)S(1)} %copy-done.3), channel_id=1, source_target_pairs={{0,7},{1,8},{2,9},{3,10},{4,11},{5,12},{6,13},{7,14},{8,15},{9,16}... | collective-permute-start | bytes 196616 | tf_op jit(solution)/shard_map/ppermute | solution.py:20
  35.6 18.3 %collective-permute-start.8 = (bf16[256,128]{1,0:T(8,128)(2,1)S(1)}, bf16[256,128]{1,0:T(8,128)(2,1)S(1)}, u32[]{:S(2)}, u32[]{:S(2)}) collective-permute-start(bf16[256,128]{1,0:T(8,128)(2,1)S(1)} %copy-done.3), channel_id=1, source_target_pairs={{0,6},{1,7},{2,8},{3,9},{4,10},{5,11},{6,12},{7,13},{8,14},{9,15},... | collective-permute-start | bytes 196616 | tf_op jit(solution)/shard_map/ppermute | solution.py:20
  39.2 18.0 %collective-permute-start.9 = (bf16[256,128]{1,0:T(8,128)(2,1)S(1)}, bf16[256,128]{1,0:T(8,128)(2,1)S(1)}, u32[]{:S(2)}, u32[]{:S(2)}) collective-permute-start(bf16[256,128]{1,0:T(8,128)(2,1)S(1)} %copy-done.3), channel_id=1, source_target_pairs={{0,5},{1,6},{2,7},{3,8},{4,9},{5,10},{6,11},{7,12},{8,13},{9,14},{... | collective-permute-start | bytes 196616 | tf_op jit(solution)/shard_map/ppermute | solution.py:20
  43.2 20.3 %collective-permute-start.10 = (bf16[256,128]{1,0:T(8,128)(2,1)S(1)}, bf16[256,128]{1,0:T(8,128)(2,1)S(1)}, u32[]{:S(2)}, u32[]{:S(2)}) collective-permute-start(bf16[256,128]{1,0:T(8,128)(2,1)S(1)} %copy-done.3), channel_id=1, source_target_pairs={{0,4},{1,5},{2,6},{3,7},{4,8},{5,9},{6,10},{7,11},{8,12},{9,13},{1... | collective-permute-start | bytes 196616 | tf_op jit(solution)/shard_map/ppermute | solution.py:20
  48.1 17.3 %collective-permute-start.11 = (bf16[256,128]{1,0:T(8,128)(2,1)S(1)}, bf16[256,128]{1,0:T(8,128)(2,1)S(1)}, u32[]{:S(2)}, u32[]{:S(2)}) collective-permute-start(bf16[256,128]{1,0:T(8,128)(2,1)S(1)} %copy-done.3), channel_id=1, source_target_pairs={{0,3},{1,4},{2,5},{3,6},{4,7},{5,8},{6,9},{7,10},{8,11},{9,12},{10... | collective-permute-start | bytes 196616 | tf_op jit(solution)/shard_map/ppermute | solution.py:20
  50.1 19.4 %collective-permute-start.12 = (bf16[256,128]{1,0:T(8,128)(2,1)S(1)}, bf16[256,128]{1,0:T(8,128)(2,1)S(1)}, u32[]{:S(2)}, u32[]{:S(2)}) collective-permute-start(bf16[256,128]{1,0:T(8,128)(2,1)S(1)} %copy-done.3), channel_id=1, source_target_pairs={{0,2},{1,3},{2,4},{3,5},{4,6},{5,7},{6,8},{7,9},{8,10},{9,11},{10,... | collective-permute-start | bytes 196616 | tf_op jit(solution)/shard_map/ppermute | solution.py:20
  54.0 20.2 %collective-permute-start.13 = (bf16[256,128]{1,0:T(8,128)(2,1)S(1)}, bf16[256,128]{1,0:T(8,128)(2,1)S(1)}, u32[]{:S(2)}, u32[]{:S(2)}) collective-permute-start(bf16[256,128]{1,0:T(8,128)(2,1)S(1)} %copy-done.3), channel_id=1, source_target_pairs={{0,1},{1,2},{2,3},{3,4},{4,5},{5,6},{6,7},{7,8},{8,9},{9,10},{10,1... | collective-permute-start | bytes 196616 | tf_op jit(solution)/shard_map/ppermute | solution.py:20
  57.2 19.9 %collective-permute-start.14 = (bf16[256,128]{1,0:T(8,128)(2,1)S(1)}, bf16[256,128]{1,0:T(8,128)(2,1)S(1)}, u32[]{:S(2)}, u32[]{:S(2)}) collective-permute-start(bf16[256,128]{1,0:T(8,128)(2,1)S(1)} %copy-done.4), channel_id=1, source_target_pairs={{0,7},{1,8},{2,9},{3,10},{4,11},{5,12},{6,13},{7,14},{8,15},{9,16}... | collective-permute-start | bytes 196616 | tf_op jit(solution)/shard_map/ppermute | solution.py:20
  63.5 18.6 %collective-permute-start.15 = (bf16[256,128]{1,0:T(8,128)(2,1)S(1)}, bf16[256,128]{1,0:T(8,128)(2,1)S(1)}, u32[]{:S(2)}, u32[]{:S(2)}) collective-permute-start(bf16[256,128]{1,0:T(8,128)(2,1)S(1)} %copy-done.4), channel_id=1, source_target_pairs={{0,6},{1,7},{2,8},{3,9},{4,10},{5,11},{6,12},{7,13},{8,14},{9,15},... | collective-permute-start | bytes 196616 | tf_op jit(solution)/shard_map/ppermute | solution.py:20
  65.4 19.2 %collective-permute-start.16 = (bf16[256,128]{1,0:T(8,128)(2,1)S(1)}, bf16[256,128]{1,0:T(8,128)(2,1)S(1)}, u32[]{:S(2)}, u32[]{:S(2)}) collective-permute-start(bf16[256,128]{1,0:T(8,128)(2,1)S(1)} %copy-done.4), channel_id=1, source_target_pairs={{0,5},{1,6},{2,7},{3,8},{4,9},{5,10},{6,11},{7,12},{8,13},{9,14},{... | collective-permute-start | bytes 196616 | tf_op jit(solution)/shard_map/ppermute | solution.py:20
  69.4 15.9 %collective-permute-start.17 = (bf16[256,128]{1,0:T(8,128)(2,1)S(1)}, bf16[256,128]{1,0:T(8,128)(2,1)S(1)}, u32[]{:S(2)}, u32[]{:S(2)}) collective-permute-start(bf16[256,128]{1,0:T(8,128)(2,1)S(1)} %copy-done.4), channel_id=1, source_target_pairs={{0,4},{1,5},{2,6},{3,7},{4,8},{5,9},{6,10},{7,11},{8,12},{9,13},{1... | collective-permute-start | bytes 196616 | tf_op jit(solution)/shard_map/ppermute | solution.py:20
  74.1 11.8 %collective-permute-start.18 = (bf16[256,128]{1,0:T(8,128)(2,1)S(1)}, bf16[256,128]{1,0:T(8,128)(2,1)S(1)}, u32[]{:S(2)}, u32[]{:S(2)}) collective-permute-start(bf16[256,128]{1,0:T(8,128)(2,1)S(1)} %copy-done.4), channel_id=1, source_target_pairs={{0,3},{1,4},{2,5},{3,6},{4,7},{5,8},{6,9},{7,10},{8,11},{9,12},{10... | collective-permute-start | bytes 196616 | tf_op jit(solution)/shard_map/ppermute | solution.py:20
  76.1 15.0 %copy-start = (bf16[2048,128]{1,0:T(8,128)(2,1)}, bf16[2048,128]{1,0:T(8,128)(2,1)S(1)}, u32[]{:S(2)}) copy-start(bf16[2048,128]{1,0:T(8,128)(2,1)S(1)} %constant_dynamic-update-slice_fusion.3) | copy-start | bytes 1572868
  77.1 9.4 %collective-permute-start.19 = (bf16[256,128]{1,0:T(8,128)(2,1)S(1)}, bf16[256,128]{1,0:T(8,128)(2,1)S(1)}, u32[]{:S(2)}, u32[]{:S(2)}) collective-permute-start(bf16[256,128]{1,0:T(8,128)(2,1)S(1)} %copy-done.4), channel_id=1, source_target_pairs={{0,2},{1,3},{2,4},{3,5},{4,6},{5,7},{6,8},{7,9},{8,10},{9,11},{10,... | collective-permute-start | bytes 196616 | tf_op jit(solution)/shard_map/ppermute | solution.py:20
  82.1 7.7 %collective-permute-start.20 = (bf16[256,128]{1,0:T(8,128)(2,1)S(1)}, bf16[256,128]{1,0:T(8,128)(2,1)S(1)}, u32[]{:S(2)}, u32[]{:S(2)}) collective-permute-start(bf16[256,128]{1,0:T(8,128)(2,1)S(1)} %copy-done.4), channel_id=1, source_target_pairs={{0,1},{1,2},{2,3},{3,4},{4,5},{5,6},{6,7},{7,8},{8,9},{9,10},{10,1... | collective-permute-start | bytes 196616 | tf_op jit(solution)/shard_map/ppermute | solution.py:20
  189.3 65.7 %copy-start.1 = (f32[8,256,128]{2,1,0:T(8,128)S(1)}, f32[8,256,128]{2,1,0:T(8,128)}, u32[]{:S(2)}) copy-start(f32[8,256,128]{2,1,0:T(8,128)} %get-tuple-element.347) | copy-start | bytes 3145732
  190.7 74.0 %copy-start.14 = (f32[256]{0:T(256)S(1)}, f32[256]{0:T(256)}, u32[]{:S(2)}) copy-start(f32[256]{0:T(256)} %convert_element_type.171) | copy-start | bytes 3076
  190.8 64.3 %collective-permute-start.27 = (bf16[256,128]{1,0:T(8,128)(2,1)S(1)}, bf16[256,128]{1,0:T(8,128)(2,1)S(1)}, u32[]{:S(2)}, u32[]{:S(2)}) collective-permute-start(bf16[256,128]{1,0:T(8,128)(2,1)S(1)} %get-tuple-element.679), channel_id=1, source_target_pairs={{7,0},{8,1},{9,2},{10,3},{11,4},{12,5},{13,6},{14,7},{15,8},{16,9}... | collective-permute-start | bytes 196616 | tf_op jit(solution)/shard_map/ppermute | solution.py:20
  199.7 59.2 %collective-permute-start.26 = (bf16[256,128]{1,0:T(8,128)(2,1)S(1)}, bf16[256,128]{1,0:T(8,128)(2,1)S(1)}, u32[]{:S(2)}, u32[]{:S(2)}) collective-permute-start(bf16[256,128]{1,0:T(8,128)(2,1)S(1)} %get-tuple-element.680), channel_id=1, source_target_pairs={{6,0},{7,1},{8,2},{9,3},{10,4},{11,5},{12,6},{13,7},{14,8},{15,9},... | collective-permute-start | bytes 196616 | tf_op jit(solution)/shard_map/ppermute | solution.py:20
  213.2 47.6 %collective-permute-start.25 = (bf16[256,128]{1,0:T(8,128)(2,1)S(1)}, bf16[256,128]{1,0:T(8,128)(2,1)S(1)}, u32[]{:S(2)}, u32[]{:S(2)}) collective-permute-start(bf16[256,128]{1,0:T(8,128)(2,1)S(1)} %get-tuple-element.681), channel_id=1, source_target_pairs={{5,0},{6,1},{7,2},{8,3},{9,4},{10,5},{11,6},{12,7},{13,8},{14,9},{... | collective-permute-start | bytes 196616 | tf_op jit(solution)/shard_map/ppermute | solution.py:20
  230.5 32.2 %collective-permute-start.24 = (bf16[256,128]{1,0:T(8,128)(2,1)S(1)}, bf16[256,128]{1,0:T(8,128)(2,1)S(1)}, u32[]{:S(2)}, u32[]{:S(2)}) collective-permute-start(bf16[256,128]{1,0:T(8,128)(2,1)S(1)} %get-tuple-element.682), channel_id=1, source_target_pairs={{4,0},{5,1},{6,2},{7,3},{8,4},{9,5},{10,6},{11,7},{12,8},{13,9},{1... | collective-permute-start | bytes 196616 | tf_op jit(solution)/shard_map/ppermute | solution.py:20
  253.0 108.2 %collective-permute-start.23 = (bf16[256,128]{1,0:T(8,128)(2,1)S(1)}, bf16[256,128]{1,0:T(8,128)(2,1)}, u32[]{:S(2)}, u32[]{:S(2)}) collective-permute-start(bf16[256,128]{1,0:T(8,128)(2,1)S(1)} %get-tuple-element.683), channel_id=1, source_target_pairs={{3,0},{4,1},{5,2},{6,3},{7,4},{8,5},{9,6},{10,7},{11,8},{12,9},{13... | collective-permute-start | bytes 196616 | tf_op jit(solution)/shard_map/ppermute | solution.py:20
  255.1 9.7 %copy-start.5 = (bf16[256,128]{1,0:T(8,128)(2,1)}, bf16[256,128]{1,0:T(8,128)(2,1)S(1)}, u32[]{:S(2)}) copy-start(bf16[256,128]{1,0:T(8,128)(2,1)S(1)} %collective-permute-done.27) | copy-start | bytes 196612
  255.1 108.3 %collective-permute-start.22 = (bf16[256,128]{1,0:T(8,128)(2,1)S(1)}, bf16[256,128]{1,0:T(8,128)(2,1)S(1)}, u32[]{:S(2)}, u32[]{:S(2)}) collective-permute-start(bf16[256,128]{1,0:T(8,128)(2,1)S(1)} %get-tuple-element.684), channel_id=1, source_target_pairs={{2,0},{3,1},{4,2},{5,3},{6,4},{7,5},{8,6},{9,7},{10,8},{11,9},{12,... | collective-permute-start | bytes 196616 | tf_op jit(solution)/shard_map/ppermute | solution.py:20
  258.8 6.0 %copy-start.7 = (bf16[256,128]{1,0:T(8,128)(2,1)}, bf16[256,128]{1,0:T(8,128)(2,1)S(1)}, u32[]{:S(2)}) copy-start(bf16[256,128]{1,0:T(8,128)(2,1)S(1)} %collective-permute-done.26) | copy-start | bytes 196612
  258.9 110.8 %collective-permute-start.21 = (bf16[256,128]{1,0:T(8,128)(2,1)S(1)}, bf16[256,128]{1,0:T(8,128)(2,1)S(1)}, u32[]{:S(2)}, u32[]{:S(2)}) collective-permute-start(bf16[256,128]{1,0:T(8,128)(2,1)S(1)} %get-tuple-element.678), channel_id=1, source_target_pairs={{1,0},{2,1},{3,2},{4,3},{5,4},{6,5},{7,6},{8,7},{9,8},{10,9},{11,1... | collective-permute-start | bytes 196616 | tf_op jit(solution)/shard_map/ppermute | solution.py:20
  260.8 4.0 %copy-start.9 = (bf16[256,128]{1,0:T(8,128)(2,1)}, bf16[256,128]{1,0:T(8,128)(2,1)S(1)}, u32[]{:S(2)}) copy-start(bf16[256,128]{1,0:T(8,128)(2,1)S(1)} %collective-permute-done.25) | copy-start | bytes 196612
  260.8 112.4 %collective-permute-start.34 = (bf16[256,128]{1,0:T(8,128)(2,1)S(1)}, bf16[256,128]{1,0:T(8,128)(2,1)S(1)}, u32[]{:S(2)}, u32[]{:S(2)}) collective-permute-start(bf16[256,128]{1,0:T(8,128)(2,1)S(1)} %get-tuple-element.672), channel_id=1, source_target_pairs={{7,0},{8,1},{9,2},{10,3},{11,4},{12,5},{13,6},{14,7},{15,8},{16,9}... | collective-permute-start | bytes 196616 | tf_op jit(solution)/shard_map/ppermute | solution.py:20
  262.7 114.3 %collective-permute-start.33 = (bf16[256,128]{1,0:T(8,128)(2,1)S(1)}, bf16[256,128]{1,0:T(8,128)(2,1)S(1)}, u32[]{:S(2)}, u32[]{:S(2)}) collective-permute-start(bf16[256,128]{1,0:T(8,128)(2,1)S(1)} %get-tuple-element.673), channel_id=1, source_target_pairs={{6,0},{7,1},{8,2},{9,3},{10,4},{11,5},{12,6},{13,7},{14,8},{15,9},... | collective-permute-start | bytes 196616 | tf_op jit(solution)/shard_map/ppermute | solution.py:20
  264.8 114.1 %copy-start.6 = (bf16[256,128]{1,0:T(8,128)(2,1)S(1)}, bf16[256,128]{1,0:T(8,128)(2,1)}, u32[]{:S(2)}) copy-start(bf16[256,128]{1,0:T(8,128)(2,1)} %copy-done.5) | copy-start | bytes 196612
  264.8 114.1 %copy-start.8 = (bf16[256,128]{1,0:T(8,128)(2,1)S(1)}, bf16[256,128]{1,0:T(8,128)(2,1)}, u32[]{:S(2)}) copy-start(bf16[256,128]{1,0:T(8,128)(2,1)} %copy-done.7) | copy-start | bytes 196612
  264.9 114.1 %copy-start.10 = (bf16[256,128]{1,0:T(8,128)(2,1)S(1)}, bf16[256,128]{1,0:T(8,128)(2,1)}, u32[]{:S(2)}) copy-start(bf16[256,128]{1,0:T(8,128)(2,1)} %copy-done.9) | copy-start | bytes 196612
  264.9 114.1 %copy-start.12 = (bf16[256,128]{1,0:T(8,128)(2,1)S(1)}, bf16[256,128]{1,0:T(8,128)(2,1)}, u32[]{:S(2)}) copy-start(bf16[256,128]{1,0:T(8,128)(2,1)} %copy-done.11) | copy-start | bytes 196612
  361.2 19.4 %collective-permute-start.32 = (bf16[256,128]{1,0:T(8,128)(2,1)S(1)}, bf16[256,128]{1,0:T(8,128)(2,1)S(1)}, u32[]{:S(2)}, u32[]{:S(2)}) collective-permute-start(bf16[256,128]{1,0:T(8,128)(2,1)S(1)} %get-tuple-element.674), channel_id=1, source_target_pairs={{5,0},{6,1},{7,2},{8,3},{9,4},{10,5},{11,6},{12,7},{13,8},{14,9},{... | collective-permute-start | bytes 196616 | tf_op jit(solution)/shard_map/ppermute | solution.py:20
  363.5 17.2 %collective-permute-start.31 = (bf16[256,128]{1,0:T(8,128)(2,1)S(1)}, bf16[256,128]{1,0:T(8,128)(2,1)S(1)}, u32[]{:S(2)}, u32[]{:S(2)}) collective-permute-start(bf16[256,128]{1,0:T(8,128)(2,1)S(1)} %get-tuple-element.675), channel_id=1, source_target_pairs={{4,0},{5,1},{6,2},{7,3},{8,4},{9,5},{10,6},{11,7},{12,8},{13,9},{1... | collective-permute-start | bytes 196616 | tf_op jit(solution)/shard_map/ppermute | solution.py:20
  369.6 11.0 %collective-permute-start.30 = (bf16[256,128]{1,0:T(8,128)(2,1)S(1)}, bf16[256,128]{1,0:T(8,128)(2,1)S(1)}, u32[]{:S(2)}, u32[]{:S(2)}) collective-permute-start(bf16[256,128]{1,0:T(8,128)(2,1)S(1)} %get-tuple-element.676), channel_id=1, source_target_pairs={{3,0},{4,1},{5,2},{6,3},{7,4},{8,5},{9,6},{10,7},{11,8},{12,9},{13... | collective-permute-start | bytes 196616 | tf_op jit(solution)/shard_map/ppermute | solution.py:20
  373.3 7.4 %collective-permute-start.29 = (bf16[256,128]{1,0:T(8,128)(2,1)S(1)}, bf16[256,128]{1,0:T(8,128)(2,1)S(1)}, u32[]{:S(2)}, u32[]{:S(2)}) collective-permute-start(bf16[256,128]{1,0:T(8,128)(2,1)S(1)} %get-tuple-element.677), channel_id=1, source_target_pairs={{2,0},{3,1},{4,2},{5,3},{6,4},{7,5},{8,6},{9,7},{10,8},{11,9},{12,... | collective-permute-start | bytes 196616 | tf_op jit(solution)/shard_map/ppermute | solution.py:20
  377.0 3.8 collective-permute-start.28
  (2 other events, 2.7 us)
where the time goes:
time: 389 us; the launch traced here: 382 us
  starting transfers between devices  168 us (43%)
  blocking collectives  93.5 us (24%)
  local copies, waits for them, and re-layouts  38.4 us (10%)
  other arithmetic  36.2 us (9%)
  loops' own time  33.2 us (9%)
  matrix products  7.89 us (2%)
    ppermute x35, starting transfers between devices, shifted(): return lax.ppermute(block, axis, route)  168 us
    psum x1, blocking collectives, per_device(): doc_sum, doc_count = lax.psum((doc_sum, doc_count), ('pb', 'ka'))  93.5 us
    dynamic_slice x24, local copies, waits for them, and re-layouts, per_device(): (row_max, row_sum), unused = lax.scan(stat_step, stat_init, block_ids)  14 us
    another operation x1, loops' own time, per_device(): lax.scan(out_step, jnp.zeros(queries.shape, jnp.float32), block_ids)  10.9 us
    another operation x1, loops' own time, per_device(): lax.scan(grad_step, jnp.zeros(queries.shape, jnp.float32), block_ids)  10.9 us
    another operation x1, loops' own time, per_device(): (row_max, row_sum), unused = lax.scan(stat_step, stat_init, block_ids)  10.8 us
    unnamed x56, local copies, waits for them, and re-layouts  10.7 us
  transfers between devices with their start and end apart: 35, of which 2 were waited for; matrix products, arithmetic and copies ran while one was open for 4% of the time, Pallas kernels for 0%

commit v1 on v0

v1 whole, which is shorter than its diff:
```python
import math

import jax
import jax.numpy as jnp
from jax import lax
from jax.experimental import pallas as pl
from jax.experimental.pallas import tpu as pltpu
from jax.sharding import PartitionSpec as P

HEAD_DIM = 128
HEADS = 6
PAIR_SPAN = 2048
ROWS = 256
BLOCKS = PAIR_SPAN // ROWS
NEG = -1e30
INV_ROOT = 1.0 / math.sqrt(HEAD_DIM)
SCALE2 = INV_ROOT * math.log2(math.e)

NT = (((1,), (1,)), ((), ()))
TN = (((0,), (0,)), ((), ()))


def dot(a, b, dims=(((1,), (0,)), ((), ()))):
    return lax.dot_general(a, b, dims, preferred_element_type=jnp.float32)


def attend_kernel(
    place, queries, grads, keys, values, attention, grad_queries, grad_kv,
    keys_t, values_t, scores, probs, grad_scores, acc_k, acc_v,
):
    first_row = place[0]
    cut = place[1]
    keys_t[...] = keys[...].T
    values_t[...] = values[...].T
    row = first_row + lax.broadcasted_iota(jnp.int32, (ROWS, ROWS), 0)
    lane = lax.broadcasted_iota(jnp.int32, (ROWS, ROWS), 1)
    start = jnp.where(row >= cut, cut, 0)
    for head in range(HEADS):
        cols = slice(head * HEAD_DIM, (head + 1) * HEAD_DIM)
        query = queries[:, cols]
        grad = grads[:, cols]
        top = None
        for block in range(BLOCKS):
            span = slice(block * ROWS, (block + 1) * ROWS)
            col = lane + block * ROWS
            score = dot(query, keys_t[:, span])
            score = jnp.where((col >= start) & (col <= row), score, NEG)
            scores[:, span] = score
            top = score if top is None else jnp.maximum(top, score)
        row_max = jnp.max(top, axis=1, keepdims=True) * SCALE2
        total = None
        for block in range(BLOCKS):
            span = slice(block * ROWS, (block + 1) * ROWS)
            prob = jnp.exp2(scores[:, span] * SCALE2 - row_max)
            probs[:, span] = prob.astype(jnp.bfloat16)
            total = prob if total is None else total + prob
        inv_total = 1.0 / jnp.sum(total, axis=1, keepdims=True)
        output = (dot(probs[...], values[...]) * inv_total).astype(jnp.bfloat16)
        attention[:, cols] = output
        grad_wide = grad.astype(jnp.float32)
        delta = jnp.sum(grad_wide * output.astype(jnp.float32), axis=1, keepdims=True) * inv_total
        grad_scaled = (grad_wide * inv_total).astype(jnp.bfloat16)
        for block in range(BLOCKS):
            span = slice(block * ROWS, (block + 1) * ROWS)
            grad_prob = dot(grad_scaled, values_t[:, span])
            grad_score = probs[:, span].astype(jnp.float32) * (grad_prob - delta)
            grad_scores[:, span] = grad_score.astype(jnp.bfloat16)
        grad_queries[:, cols] = dot(grad_scores[...], keys[...]) * INV_ROOT
        part_k = dot(grad_scores[...], query, TN)
        part_v = dot(probs[...], grad_scaled, TN)
        if head == 0:
            acc_k[...] = part_k
            acc_v[...] = part_v
        elif head < HEADS - 1:
            acc_k[...] += part_k
            acc_v[...] += part_v
        else:
            grad_kv[:, :HEAD_DIM] = ((acc_k[...] + part_k) * INV_ROOT).astype(jnp.bfloat16)
            grad_kv[:, HEAD_DIM:] = (acc_v[...] + part_v).astype(jnp.bfloat16)


def attend(place, queries, grads, keys, values):
    vmem = pl.BlockSpec(memory_space=pltpu.VMEM)
    width = HEADS * HEAD_DIM
    return pl.pallas_call(
        attend_kernel,
        out_shape=(
            jax.ShapeDtypeStruct((ROWS, width), jnp.bfloat16),
            jax.ShapeDtypeStruct((ROWS, width), jnp.float32),
            jax.ShapeDtypeStruct((PAIR_SPAN, 2 * HEAD_DIM), jnp.bfloat16),
        ),
        in_specs=[pl.BlockSpec(memory_space=pltpu.SMEM), vmem, vmem, vmem, vmem],
        out_specs=(vmem, vmem, vmem),
        scratch_shapes=[
            pltpu.VMEM((HEAD_DIM, PAIR_SPAN), jnp.bfloat16),
            pltpu.VMEM((HEAD_DIM, PAIR_SPAN), jnp.bfloat16),
            pltpu.VMEM((ROWS, PAIR_SPAN), jnp.float32),
            pltpu.VMEM((ROWS, PAIR_SPAN), jnp.bfloat16),
            pltpu.VMEM((ROWS, PAIR_SPAN), jnp.bfloat16),
            pltpu.VMEM((PAIR_SPAN, HEAD_DIM), jnp.float32),
            pltpu.VMEM((PAIR_SPAN, HEAD_DIM), jnp.float32),
        ],
        compiler_params=pltpu.CompilerParams(vmem_limit_bytes=48 * 1024 * 1024),
        cost_estimate=pl.CostEstimate(
            flops=12 * HEADS * ROWS * PAIR_SPAN * HEAD_DIM,
            bytes_accessed=4 * 1024 * 1024,
            transcendentals=HEADS * ROWS * PAIR_SPAN,
        ),
    )(place, queries, grads, keys, values)


def per_device(queries, key_heads, value_heads, grad_output, token_logprob, doc_ids, response):
    groups = [list(range(8)), list(range(8, 16))]
    rank = lax.axis_index("ka") % 8
    odd = (doc_ids & 1).astype(jnp.float32)
    live = response.astype(jnp.float32)
    mine = jnp.stack(
        [
            jnp.sum(token_logprob * live * (1.0 - odd)),
            jnp.sum(token_logprob * live * odd),
            jnp.sum(live * (1.0 - odd)),
            jnp.sum(live * odd),
        ]
    )
    kv = jnp.concatenate([key_heads, value_heads], axis=1)
    kv = lax.all_gather(kv, "ka", axis_index_groups=groups, tiled=True)
    docs = lax.all_gather(doc_ids, "ka", axis_index_groups=groups, tiled=True)
    cut = jnp.sum(1 - (docs & 1)).astype(jnp.int32)
    place = jnp.stack([(rank * ROWS).astype(jnp.int32), cut])
    stats = lax.all_gather(mine, ("pb", "ka"))
    attention, grad_queries, grad_kv = attend(
        place, queries, grad_output, kv[:, :HEAD_DIM], kv[:, HEAD_DIM:]
    )
    grad_kv = lax.psum_scatter(
        grad_kv, "ka", scatter_dimension=0, axis_index_groups=groups, tiled=True
    ).astype(jnp.float32)
    sums = jnp.sum(stats.reshape(-1, 8, 4), axis=1)
    average = sums[:, :2] / sums[:, 2:]
    margins = average[:, 0] - average[:, 1]
    return (attention, grad_queries, grad_kv[:, :HEAD_DIM], grad_kv[:, HEAD_DIM:], margins)


def solution(mesh):
    rows = P(("pb", "ka"), None)
    line = P(("pb", "ka"))
    return jax.shard_map(
        per_device,
        mesh=mesh,
        in_specs=(rows, rows, rows, rows, line, line, line),
        out_specs=(rows, rows, rows, rows, P()),
        check_vma=False,
    )
```

time: 389 us -> 147 us (0.38); the launches traced: 382 us -> 145 us
  starting transfers between devices: 168 us -> 0.08 us
  local copies, waits for them, and re-layouts: 38.4 us -> 4.34 us
  loops' own time: 33.2 us -> 0 us
  other arithmetic: 36.2 us -> 7.14 us
  Pallas kernels: 0 us -> 15.1 us
  waiting for transfers between devices: 2.81 us -> 17.8 us
  between operations: 1.58 us -> 14.1 us
  matrix products: 7.89 us -> 0 us
  blocking collectives: 93.5 us -> 86.5 us
    ppermute x35 -> x0, starting transfers between devices: 168 us -> none  [shifted(): return lax.ppermute(block, axis, route)]
    psum x1 -> x0, blocking collectives: 93.5 us -> none  [per_device(): doc_sum, doc_count = lax.psum((doc_sum, doc_count), ('pb', 'ka'))]
    unnamed x0 -> x1, blocking collectives: none -> 75.9 us
    another operation x27 -> x0, loops' own time: 33.2 us -> none  [the longest x1 10.9 us: per_device(): lax.scan(out_step, jnp.zeros(queries.shape, jnp.float32), block_ids)]
    reduce_or x24 -> x0, other arithmetic: 19.4 us -> none  [the longest x8 6.45 us: tile_grads(): return lax.cond(jnp.any(allowed), active, skipped, 0)]
    all_gather x0 -> x1, waiting for transfers between devices: none -> 17.8 us  [per_device(): kv = lax.all_gather(kv, 'ka', axis_index_groups=groups, tiled=True)]
    dynamic_slice x48 -> x0, local copies, waits for them, and re-layouts: 15.9 us -> none  [the longest x24 14 us: per_device(): (row_max, row_sum), unused = lax.scan(stat_step, stat_init, block_ids)]
    pallas_call x0 -> x1, Pallas kernels: none -> 15.1 us  [attend(): pl.pallas_call(attend_kernel, out_shape=(jax.ShapeDtypeStruct((ROWS, widt...]
  transfers between devices with their start and end apart: 35 -> 2, of which waited for: 2 -> 1; matrix products, arithmetic and copies ran while one was open for 4% -> 4% of each run, Pallas kernels for 0% -> 0%
where the time goes in v1:
time: 147 us; the launch traced here: 145 us
  blocking collectives  86.5 us (59%)
  waiting for transfers between devices  17.8 us (12%)
  Pallas kernels  15.1 us (10%)
  between operations  14.1 us (10%)
  other arithmetic  7.14 us (5%)
  local copies, waits for them, and re-layouts  4.34 us (3%)
    unnamed x1, blocking collectives  75.9 us
    all_gather x1, waiting for transfers between devices, per_device(): kv = lax.all_gather(kv, 'ka', axis_index_groups=groups, tiled=True)  17.8 us
    pallas_call x1, Pallas kernels, attend(): pl.pallas_call(attend_kernel, out_shape=(jax.ShapeDtypeStruct((ROWS, widt...  15.1 us
    all_gather x1, blocking collectives, per_device(): docs = lax.all_gather(doc_ids, 'ka', axis_index_groups=groups, tiled=True)  10.5 us
  transfers between devices with their start and end apart: 2, of which 1 were waited for; matrix products, arithmetic and copies ran while one was open for 4% of the time, Pallas kernels for 0%

profile of v1, /device:TPU:8, one launch (start us, length us, event | category | flops | bytes accessed | tf_op | source)
XLA Modules:
  0.0 145.1 jit_solution(2103782623065022992)
XLA Ops:
  7.2 0.0 all-gather.4.cloned.1.call-start
  7.2 1.5 %pad_maximum_fusion = bf16[256,256]{1,0:T(8,128)(2,1)} fusion(bf16[256,128]{1,0:T(8,128)(2,1)} %param.9, bf16[256,128]{1,0:T(8,128)(2,1)} %param.8), kind=kLoop, calls=%fused_computation | loop fusion | flops 262144 | bytes 262144 | tf_op jit(solution)/shard_map/concatenate | solution.py:125
  8.8 0.0 all-gather.4.cloned.1.call-update
  8.8 0.0 reduce-scatter.2.cloned.1.call-start
  8.8 0.0 copy-start.2
  8.9 0.7 copy-done.2
  9.5 10.5 %all-gather.1 = s32[8,1,256]{2,1,0:T(1,128)S(1)} all-gather(s32[1,1,256]{2,1,0:T(1,128)S(1)} %bitcast.7), channel_id=1, replica_groups={{0,1,2,3,4,5,6,7},{8,9,10,11,12,13,14,15},{16,17,18,19,20,21,22,23},{24..., dimensions={0}, use_global_device_ids=true | all-gather | bytes 9216 | tf_op jit(solution)/shard_map/all_gather | solution.py:127
  20.1 0.6 subtract_reduce_fusion
  20.7 0.7 pad_add_fusion.place
  21.4 0.0 copy-start
  21.4 0.0 copy-start.1
  21.4 17.8 %all-gather.4.cloned.1.call-done = bf16[2048,256]{1,0:T(8,128)(2,1)} async-done(((bf16[256,256]{1,0:T(8,128)(2,1)}), bf16[2048,256]{1,0:T(8,128)(2,1)}) %all-gather.4.cloned.1.call-update) | async-done | bytes 1048592 | tf_op jit(solution)/shard_map/all_gather | solution.py:126
  39.2 1.3 fusion.1
  40.5 0.0 copy-done
  40.5 0.0 copy-done.1
  40.5 15.1 %shard_map.110 = (bf16[256,768]{1,0:T(8,128)(2,1)}, f32[256,768]{1,0:T(8,128)}, bf16[2048,256]{1,0:T(8,128)(2,1)}) custom-call(s32[2]{0:T(128)S(1)} %pad_add_fusion.place, bf16[256,768]{1,0:T(8,128)(2,1)S(1)} %copy-done, bf16[256,768]{1,0:T(8,128)(2,1)S(1)} %copy-done.1, bf16[2048,128]{1,0:T(8,128)(2,1)S(1)} %get-tuple-element.16.keys, ...), custom_call_target="tpu_custom_call" | custom-call | flops 4831838208 | bytes 4194304 | tf_op jit(solution)/shard_map/pallas_call | solution.py:85
  55.6 0.0 copy-start.4
  55.6 0.0 reduce-scatter.2.cloned.1.call-update
  55.7 0.0 copy-start.3
  55.7 0.6 copy-done.4
  56.3 0.0 copy-done.3
  56.4 0.7 multiply_reduce_fusion.3
  57.0 2.7 %maximum_dynamic-update-slice_fusion = f32[1024]{0:T(1024)S(1)} fusion(f32[1024]{0:T(1024)S(1)} %broadcast.9, u32[]{:T(128)S(6)} %multiply.1, f32[1]{0:T(128)} %bitcast.6, f32[1]{0:T(128)} %bitcast.5, f32[1]{0:T(128)} %bitcast.4, f32[1]{0:T(128)} %bitcast.3), kind=kLoop, calls=%fused_computation.12 | loop fusion | flops 12 | bytes 532
  59.8 75.9 %all-reduce = f32[1024]{0:T(1024)S(1)} all-reduce(f32[1024]{0:T(1024)S(1)} %maximum_dynamic-update-slice_fusion), channel_id=2, replica_groups=mesh['pb'=16,'ka'=16] {'pb','ka'}, use_global_device_ids=true, to_apply=%add | all-reduce | flops 1024 | bytes 8192
  135.7 0.1 reshape.14
  135.9 0.1 slice_divide_fusion
  136.0 0.7 fusion
  136.7 0.0 reduce-scatter.2.cloned.1.call-done
  136.7 1.6 %fusion.2 = (f32[256,128]{1,0:T(8,128)}, f32[256,128]{1,0:T(8,128)}) fusion(bf16[256,256]{1,0:T(8,128)(2,1)} %reduce-scatter.2.cloned.1.call-done), kind=kLoop, calls=%fused_computation.15 | loop fusion | bytes 524288 | tf_op jit(solution)/shard_map/slice | solution.py:140
  (2 shorter events, 0.0 us)
Async XLA Ops:
  7.2 32.1 %all-gather.4.cloned.1.call-start = ((), (), s32[]{:S(2)}) async-start(), calls=%async_computation.1 | async-start | bytes 1179648 | tf_op jit(solution)/shard_map/all_gather | solution.py:126
  8.8 127.9 %reduce-scatter.2.cloned.1.call-start = ((), (), s32[]{:S(2)}) async-start(), calls=%async_computation.2 | async-start | bytes 1179648 | tf_op jit(solution)/shard_map/reduce_scatter | solution.py:134
  8.8 0.7 copy-start.2
  21.4 19.1 %copy-start = (bf16[256,768]{1,0:T(8,128)(2,1)S(1)}, bf16[256,768]{1,0:T(8,128)(2,1)}, u32[]{:S(2)}) copy-start(bf16[256,768]{1,0:T(8,128)(2,1)} %queries.1) | copy-start | bytes 1179652
  21.4 19.1 %copy-start.1 = (bf16[256,768]{1,0:T(8,128)(2,1)S(1)}, bf16[256,768]{1,0:T(8,128)(2,1)}, u32[]{:S(2)}) copy-start(bf16[256,768]{1,0:T(8,128)(2,1)} %grads.1) | copy-start | bytes 1179652
  55.6 0.7 copy-start.4
  55.7 0.7 copy-start.3
Sparse Core Ops, SparseCore 0:
  10.4 28.7 all-gather.3
  55.8 34.3 reduce-scatter.1

commit v2 on v1

--- a/solution.py
+++ b/solution.py
@@ -12,26 +12,89 @@
 PAIR_SPAN = 2048
 ROWS = 256
 BLOCKS = PAIR_SPAN // ROWS
+PACKED = 2 * ROWS + 16
 NEG = -1e30
 INV_ROOT = 1.0 / math.sqrt(HEAD_DIM)
 SCALE2 = INV_ROOT * math.log2(math.e)
 
-NT = (((1,), (1,)), ((), ()))
 TN = (((0,), (0,)), ((), ()))
+VMEM = pl.BlockSpec(memory_space=pltpu.VMEM)
+MIB = 1024 * 1024
 
 
 def dot(a, b, dims=(((1,), (0,)), ((), ()))):
     return lax.dot_general(a, b, dims, preferred_element_type=jnp.float32)
 
 
+def pack_kernel(keys, values, logprob, docs, response, packed, sums):
+    odd = (docs[...] & 1).astype(jnp.float32)
+    even = 1.0 - odd
+    live = response[...].astype(jnp.float32)
+    scored = logprob[...] * live
+    lane = lax.broadcasted_iota(jnp.int32, (1, 128), 1)
+    terms = (scored * even, scored * odd, live * even, live * odd)
+    line = jnp.zeros((1, 128), jnp.float32)
+    for place, term in enumerate(terms):
+        line = jnp.where(lane == place, jnp.sum(term, keepdims=True), line)
+    sums[...] = jnp.broadcast_to(line[None], sums.shape)
+    count = jnp.broadcast_to(jnp.sum(even, keepdims=True), (16, 128)).astype(jnp.bfloat16)
+    for copy in range(BLOCKS):
+        packed[copy, :ROWS, :] = keys[...]
+        packed[copy, ROWS : 2 * ROWS, :] = values[...]
+        packed[copy, 2 * ROWS :, :] = count
+
+
+def pack(keys, values, logprob, docs, response, copies):
+    wide = (ROWS // 128, 128)
+    return pl.pallas_call(
+        pack_kernel,
+        out_shape=(
+            jax.ShapeDtypeStruct((BLOCKS, PACKED, HEAD_DIM), jnp.bfloat16),
+            jax.ShapeDtypeStruct((copies, 8, 128), jnp.float32),
+        ),
+        in_specs=[VMEM] * 5,
+        out_specs=(VMEM, VMEM),
+        cost_estimate=pl.CostEstimate(flops=10000, bytes_accessed=2 * MIB, transcendentals=0),
+    )(keys, values, logprob.reshape(wide), docs.reshape(wide), response.reshape(wide))
+
+
+def margin_kernel(sums, margins):
+    lane = lax.broadcasted_iota(jnp.int32, (1, 128), 1)
+    line = jnp.zeros((1, 128), jnp.float32)
+    for pair in range(2):
+        total = jnp.sum(sums[pair * BLOCKS : (pair + 1) * BLOCKS, 0, :], axis=0, keepdims=True)
+        each = [jnp.sum(jnp.where(lane == at, total, 0.0), keepdims=True) for at in range(4)]
+        line = jnp.where(lane == pair, each[0] / each[2] - each[1] / each[3], line)
+    margins[...] = jnp.broadcast_to(line[None], margins.shape)
+
+
+def pair_margins(sums, copies):
+    return pl.pallas_call(
+        margin_kernel,
+        out_shape=jax.ShapeDtypeStruct((copies, 8, 128), jnp.float32),
+        in_specs=[VMEM],
+        out_specs=VMEM,
+        cost_estimate=pl.CostEstimate(flops=10000, bytes_accessed=65536, transcendentals=0),
+    )(sums)
+
+
 def attend_kernel(
-    place, queries, grads, keys, values, attention, grad_queries, grad_kv,
-    keys_t, values_t, scores, probs, grad_scores, acc_k, acc_v,
+    queries, grads, packed, attention, grad_queries, grad_kv,
+    keys, values, keys_t, values_t, scores, probs, grad_scores, acc_k, acc_v,
 ):
-    first_row = place[0]
-    cut = place[1]
-    keys_t[...] = keys[...].T
-    values_t[...] = values[...].T
+    first_row = lax.rem(lax.axis_index("ka"), BLOCKS) * ROWS
+    count = packed[0, 2 * ROWS : 2 * ROWS + 16, :].astype(jnp.float32)
+    for block in range(BLOCKS):
+        span = slice(block * ROWS, (block + 1) * ROWS)
+        key = packed[block, :ROWS, :]
+        value = packed[block, ROWS : 2 * ROWS, :]
+        keys[span, :] = key
+        values[span, :] = value
+        keys_t[:, span] = key.T
+        values_t[:, span] = value.T
+        if block:
+            count += packed[block, 2 * ROWS : 2 * ROWS + 16, :].astype(jnp.float32)
+    cut = count[:1, :1].astype(jnp.int32)
     row = first_row + lax.broadcasted_iota(jnp.int32, (ROWS, ROWS), 0)
     lane = lax.broadcasted_iota(jnp.int32, (ROWS, ROWS), 1)
     start = jnp.where(row >= cut, cut, 0)
@@ -79,8 +142,7 @@
             grad_kv[:, HEAD_DIM:] = (acc_v[...] + part_v).astype(jnp.bfloat16)
 
 
-def attend(place, queries, grads, keys, values):
-    vmem = pl.BlockSpec(memory_space=pltpu.VMEM)
+def attend(queries, grads, packed):
     width = HEADS * HEAD_DIM
     return pl.pallas_call(
         attend_kernel,
@@ -89,9 +151,11 @@
             jax.ShapeDtypeStruct((ROWS, width), jnp.float32),
             jax.ShapeDtypeStruct((PAIR_SPAN, 2 * HEAD_DIM), jnp.bfloat16),
         ),
-        in_specs=[pl.BlockSpec(memory_space=pltpu.SMEM), vmem, vmem, vmem, vmem],
-        out_specs=(vmem, vmem, vmem),
+        in_specs=[VMEM] * 3,
+        out_specs=(VMEM,) * 3,
         scratch_shapes=[
+            pltpu.VMEM((PAIR_SPAN, HEAD_DIM), jnp.bfloat16),
+            pltpu.VMEM((PAIR_SPAN, HEAD_DIM), jnp.bfloat16),
             pltpu.VMEM((HEAD_DIM, PAIR_SPAN), jnp.bfloat16),
             pltpu.VMEM((HEAD_DIM, PAIR_SPAN), jnp.bfloat16),
             pltpu.VMEM((ROWS, PAIR_SPAN), jnp.float32),
@@ -100,44 +164,45 @@
             pltpu.VMEM((PAIR_SPAN, HEAD_DIM), jnp.float32),
             pltpu.VMEM((PAIR_SPAN, HEAD_DIM), jnp.float32),
         ],
-        compiler_params=pltpu.CompilerParams(vmem_limit_bytes=48 * 1024 * 1024),
+        compiler_params=pltpu.CompilerParams(vmem_limit_bytes=32 * MIB),
         cost_estimate=pl.CostEstimate(
             flops=12 * HEADS * ROWS * PAIR_SPAN * HEAD_DIM,
-            bytes_accessed=4 * 1024 * 1024,
+            bytes_accessed=4 * MIB,
             transcendentals=HEADS * ROWS * PAIR_SPAN,
         ),
-    )(place, queries, grads, keys, values)
+    )(queries, grads, packed)
+
+
+def collect_kernel(parts, grad_keys, grad_values):
+    total = parts[0].astype(jnp.float32)
+    for block in range(1, BLOCKS):
+        total += parts[block].astype(jnp.float32)
+    grad_keys[...] = total[:, :HEAD_DIM]
+    grad_values[...] = total[:, HEAD_DIM:]
+
+
+def collect(parts):
+    shape = jax.ShapeDtypeStruct((ROWS, HEAD_DIM), jnp.float32)
+    return pl.pallas_call(
+        collect_kernel,
+        out_shape=(shape, shape),
+        in_specs=[VMEM],
+        out_specs=(VMEM, VMEM),
+        cost_estimate=pl.CostEstimate(flops=MIB, bytes_accessed=2 * MIB, transcendentals=0),
+    )(parts)
 
 
 def per_device(queries, key_heads, value_heads, grad_output, token_logprob, doc_ids, response):
     groups = [list(range(8)), list(range(8, 16))]
-    rank = lax.axis_index("ka") % 8
-    odd = (doc_ids & 1).astype(jnp.float32)
-    live = response.astype(jnp.float32)
-    mine = jnp.stack(
-        [
-            jnp.sum(token_logprob * live * (1.0 - odd)),
-            jnp.sum(token_logprob * live * odd),
-            jnp.sum(live * (1.0 - odd)),
-            jnp.sum(live * odd),
-        ]
-    )
-    kv = jnp.concatenate([key_heads, value_heads], axis=1)
-    kv = lax.all_gather(kv, "ka", axis_index_groups=groups, tiled=True)
-    docs = lax.all_gather(doc_ids, "ka", axis_index_groups=groups, tiled=True)
-    cut = jnp.sum(1 - (docs & 1)).astype(jnp.int32)
-    place = jnp.stack([(rank * ROWS).astype(jnp.int32), cut])
-    stats = lax.all_gather(mine, ("pb", "ka"))
-    attention, grad_queries, grad_kv = attend(
-        place, queries, grad_output, kv[:, :HEAD_DIM], kv[:, HEAD_DIM:]
-    )
-    grad_kv = lax.psum_scatter(
-        grad_kv, "ka", scatter_dimension=0, axis_index_groups=groups, tiled=True
-    ).astype(jnp.float32)
-    sums = jnp.sum(stats.reshape(-1, 8, 4), axis=1)
-    average = sums[:, :2] / sums[:, 2:]
-    margins = average[:, 0] - average[:, 1]
-    return (attention, grad_queries, grad_kv[:, :HEAD_DIM], grad_kv[:, HEAD_DIM:], margins)
+    packed, sums = pack(key_heads, value_heads, token_logprob, doc_ids, response, 16)
+    packed = lax.all_to_all(packed, "ka", 0, 0, axis_index_groups=groups, tiled=True)
+    sums = lax.all_to_all(sums, "ka", 0, 0, tiled=True)
+    margins = lax.all_to_all(pair_margins(sums, 16), "pb", 0, 0, tiled=True)
+    attention, grad_queries, grad_kv = attend(queries, grad_output, packed)
+    parts = grad_kv.reshape(BLOCKS, ROWS, 2 * HEAD_DIM)
+    parts = lax.all_to_all(parts, "ka", 0, 0, axis_index_groups=groups, tiled=True)
+    grad_keys, grad_values = collect(parts)
+    return (attention, grad_queries, grad_keys, grad_values, margins[:, 0, :2].reshape(-1))
 
 
 def solution(mesh):

time: 147 us -> 84.2 us (0.57)
  blocking collectives: 86.5 us -> 13.9 us
  starting transfers between devices: 0.08 us -> 17.2 us
  between operations: 14.1 us -> 0.67 us
  waiting for transfers between devices: 17.8 us -> 29.9 us
  other arithmetic: 7.14 us -> 0 us
  Pallas kernels: 15.1 us -> 20.2 us
  local copies, waits for them, and re-layouts: 4.34 us -> 1.6 us
    unnamed x1 -> x0, blocking collectives: 75.9 us -> none
    all_to_all x0 -> x3, waiting for transfers between devices: none -> 29.9 us  [the longest x1 15.3 us: per_device(): lax.all_to_all(parts, 'ka', 0, 0, axis_index_groups=groups, tiled=True)]
    all_gather x1 -> x0, waiting for transfers between devices: 17.8 us -> none  [per_device(): kv = lax.all_gather(kv, 'ka', axis_index_groups=groups, tiled=True)]
    all_to_all x0 -> x3, starting transfers between devices: none -> 17.2 us  [the longest x1 9.94 us: per_device(): margins = lax.all_to_all(pair_margins(sums, 16), 'pb', 0, 0, tiled=True)]
    all_to_all x0 -> x1, blocking collectives: none -> 13.9 us  [per_device(): sums = lax.all_to_all(sums, 'ka', 0, 0, tiled=True)]
    all_gather x1 -> x0, blocking collectives: 10.5 us -> none  [per_device(): docs = lax.all_gather(doc_ids, 'ka', axis_index_groups=groups, tiled=True)]
    pallas_call x0 -> x3, Pallas kernels: none -> 5.7 us  [the longest x1 2.07 us: pack(): pl.pallas_call(pack_kernel, out_shape=(jax.ShapeDtypeStruct((BLOCKS, PACK...]
    slice x2 -> x1, local copies, waits for them, and re-layouts: 2.86 us -> 0.03 us  [per_device(): margins[:, 0, :2].reshape(-1)]
  transfers between devices with their start and end apart: 2 -> 3, of which waited for: 1 -> 2; matrix products, arithmetic and copies ran while one was open for 4% -> 1% of each run, Pallas kernels for 0% -> 19%
where the time goes in v2:
time: 84.2 us; the launch traced here: 83.4 us
  waiting for transfers between devices  29.9 us (36%)
  Pallas kernels  20.2 us (24%)
  starting transfers between devices  17.2 us (20%)
  blocking collectives  13.9 us (17%)
  local copies, waits for them, and re-layouts  1.6 us (2%)
    all_to_all x1, waiting for transfers between devices, per_device(): lax.all_to_all(parts, 'ka', 0, 0, axis_index_groups=groups, tiled=True)  15.3 us
    all_to_all x1, waiting for transfers between devices, per_device(): lax.all_to_all(packed, 'ka', 0, 0, axis_index_groups=groups, tiled=True)  14.6 us
    pallas_call x1, Pallas kernels, attend(): pl.pallas_call(attend_kernel, out_shape=(jax.ShapeDtypeStruct((ROWS, widt...  14.5 us
    all_to_all x1, blocking collectives, per_device(): sums = lax.all_to_all(sums, 'ka', 0, 0, tiled=True)  13.9 us
    all_to_all x1, starting transfers between devices, per_device(): margins = lax.all_to_all(pair_margins(sums, 16), 'pb', 0, 0, tiled=True)  9.94 us
    all_to_all x1, starting transfers between devices, per_device(): lax.all_to_all(packed, 'ka', 0, 0, axis_index_groups=groups, tiled=True)  3.69 us
    all_to_all x1, starting transfers between devices, per_device(): lax.all_to_all(parts, 'ka', 0, 0, axis_index_groups=groups, tiled=True)  3.56 us
    pallas_call x1, Pallas kernels, pack(): pl.pallas_call(pack_kernel, out_shape=(jax.ShapeDtypeStruct((BLOCKS, PACK...  2.07 us
  transfers between devices with their start and end apart: 3, of which 2 were waited for; matrix products, arithmetic and copies ran while one was open for 1% of the time, Pallas kernels for 19%

profile of v2, /device:TPU:8, one launch (start us, length us, event | category | flops | bytes accessed | tf_op | source)
XLA Modules:
  0.0 83.4 jit_solution(9242549336931025113)
XLA Ops:
  0.6 2.1 %shard_map.110 = (bf16[8,528,128]{2,1,0:T(8,128)(2,1)}, f32[16,8,128]{2,1,0:T(8,128)}) custom-call(bf16[256,128]{1,0:T(8,128)(2,1)} %keys.1, bf16[256,128]{1,0:T(8,128)(2,1)} %values.1, f32[2,128]{1,0:T(2,128)} %bitcast.4, s32[2,128]{1,0:T(2,128)} %bitcast.5, s32[2,128]{1,0:T(2,128)} %bitcast.6), custom_call_target="tpu_custom_call" | custom-call | flops 10000 | bytes 2097152 | tf_op jit(solution)/shard_map/pallas_call | solution.py:49
  2.7 13.9 %all_to_all.20.sums = f32[16,8,128]{2,1,0:T(8,128)} all-to-all(f32[16,8,128]{2,1,0:T(8,128)} %get-tuple-element.18), channel_id=1, replica_groups=mesh['pb'=16,'ka'=16] {'ka'}, dimensions={0} | all-to-all | bytes 131072 | tf_op jit(solution)/shard_map/all_to_all | solution.py:199
  16.6 0.0 copy-start
  16.6 0.0 copy-start.1
  16.6 3.7 %all-to-all-start = ((bf16[8,528,128]{2,1,0:T(8,128)(2,1)}), bf16[8,528,128]{2,1,0:T(8,128)(2,1)S(1)}, u32[]{:S(2)}, u32[]{:S(2)}) async-start(bf16[8,528,128]{2,1,0:T(8,128)(2,1)} %get-tuple-element.12), calls=%async_computation | async-start | bytes 2162688 | tf_op jit(solution)/shard_map/all_to_all | solution.py:198
  20.3 1.6 %shard_map.113 = f32[16,8,128]{2,1,0:T(8,128)} custom-call(f32[16,8,128]{2,1,0:T(8,128)} %all_to_all.20.sums), custom_call_target="tpu_custom_call" | custom-call | flops 10000 | bytes 65536 | tf_op jit(solution)/shard_map/pallas_call | solution.py:72
  21.9 14.6 %all-to-all-done.packed = bf16[8,528,128]{2,1,0:T(8,128)(2,1)S(1)} async-done(((bf16[8,528,128]{2,1,0:T(8,128)(2,1)}), bf16[8,528,128]{2,1,0:T(8,128)(2,1)S(1)}, u32[]{:S(2)}, u32[]{:S(2)}) %all-to-all-start) | async-done | bytes 1081376 | tf_op jit(solution)/shard_map/all_to_all | solution.py:198
  36.5 9.9 %all-to-all-start.3 = ((f32[16,8,128]{2,1,0:T(8,128)}), f32[16,8,128]{2,1,0:T(8,128)S(1)}, u32[]{:S(2)}, u32[]{:S(2)}) async-start(f32[16,8,128]{2,1,0:T(8,128)} %shard_map.113), calls=%async_computation.3 | async-start | bytes 131072 | tf_op jit(solution)/shard_map/all_to_all | solution.py:200
  46.4 0.0 copy-done
  46.5 0.0 copy-done.1
  46.5 14.5 %shard_map.111 = (bf16[256,768]{1,0:T(8,128)(2,1)}, f32[256,768]{1,0:T(8,128)}, bf16[2048,256]{1,0:T(8,128)(2,1)}) custom-call(bf16[256,768]{1,0:T(8,128)(2,1)S(1)} %copy-done, bf16[256,768]{1,0:T(8,128)(2,1)S(1)} %copy-done.1, bf16[8,528,128]{2,1,0:T(8,128)(2,1)S(1)} %all-to-all-done.packed), custom_call_target="tpu_custom_call" | custom-call | flops 4831838208 | bytes 4194304 | tf_op jit(solution)/shard_map/pallas_call | solution.py:147
  61.0 0.0 all-to-all-done.3
  61.0 3.6 %all-to-all-start.1 = ((bf16[8,256,256]{2,1,0:T(8,128)(2,1)}), bf16[8,256,256]{2,1,0:T(8,128)(2,1)S(1)}, u32[]{:S(2)}, u32[]{:S(2)}) async-start(bf16[8,256,256]{2,1,0:T(8,128)(2,1)} %bitcast.3), calls=%async_computation.1 | async-start | bytes 2097152 | tf_op jit(solution)/shard_map/all_to_all | solution.py:203
  64.6 0.6 reshape_squeeze.3
  65.2 15.3 %all-to-all-done.1.parts = bf16[8,256,256]{2,1,0:T(8,128)(2,1)S(1)} async-done(((bf16[8,256,256]{2,1,0:T(8,128)(2,1)}), bf16[8,256,256]{2,1,0:T(8,128)(2,1)S(1)}, u32[]{:S(2)}, u32[]{:S(2)}) %all-to-all-start.1) | async-done | bytes 1048608 | tf_op jit(solution)/shard_map/all_to_all | solution.py:203
  80.4 0.0 copy-start.2
  80.4 1.0 %copy-done.2 = bf16[8,256,256]{2,1,0:T(8,128)(2,1)} copy-done((bf16[8,256,256]{2,1,0:T(8,128)(2,1)}, bf16[8,256,256]{2,1,0:T(8,128)(2,1)S(1)}, u32[]{:S(2)}) %copy-start.2) | copy-done | bytes 1048600
  81.4 2.0 %shard_map.112 = (f32[256,128]{1,0:T(8,128)}, f32[256,128]{1,0:T(8,128)}) custom-call(bf16[8,256,256]{2,1,0:T(8,128)(2,1)} %copy-done.2), custom_call_target="tpu_custom_call" | custom-call | flops 1048576 | bytes 2097152 | tf_op jit(solution)/shard_map/pallas_call | solution.py:186
  (1 shorter events, 0.0 us)
Async XLA Ops:
  16.6 29.9 %copy-start = (bf16[256,768]{1,0:T(8,128)(2,1)S(1)}, bf16[256,768]{1,0:T(8,128)(2,1)}, u32[]{:S(2)}) copy-start(bf16[256,768]{1,0:T(8,128)(2,1)} %queries.1) | copy-start | bytes 1179652
  16.6 29.9 %copy-start.1 = (bf16[256,768]{1,0:T(8,128)(2,1)S(1)}, bf16[256,768]{1,0:T(8,128)(2,1)}, u32[]{:S(2)}) copy-start(bf16[256,768]{1,0:T(8,128)(2,1)} %grads.1) | copy-start | bytes 1179652
  16.6 19.9 %all-to-all-start = ((bf16[8,528,128]{2,1,0:T(8,128)(2,1)}), bf16[8,528,128]{2,1,0:T(8,128)(2,1)S(1)}, u32[]{:S(2)}, u32[]{:S(2)}) async-start(bf16[8,528,128]{2,1,0:T(8,128)(2,1)} %get-tuple-element.12), calls=%async_computation | async-start | bytes 2162688 | tf_op jit(solution)/shard_map/all_to_all | solution.py:198
  36.5 24.5 %all-to-all-start.3 = ((f32[16,8,128]{2,1,0:T(8,128)}), f32[16,8,128]{2,1,0:T(8,128)S(1)}, u32[]{:S(2)}, u32[]{:S(2)}) async-start(f32[16,8,128]{2,1,0:T(8,128)} %shard_map.113), calls=%async_computation.3 | async-start | bytes 131072 | tf_op jit(solution)/shard_map/all_to_all | solution.py:200
  61.0 19.4 %all-to-all-start.1 = ((bf16[8,256,256]{2,1,0:T(8,128)(2,1)}), bf16[8,256,256]{2,1,0:T(8,128)(2,1)S(1)}, u32[]{:S(2)}, u32[]{:S(2)}) async-start(bf16[8,256,256]{2,1,0:T(8,128)(2,1)} %bitcast.3), calls=%async_computation.1 | async-start | bytes 2097152 | tf_op jit(solution)/shard_map/all_to_all | solution.py:203
  80.4 1.0 %copy-start.2 = (bf16[8,256,256]{2,1,0:T(8,128)(2,1)}, bf16[8,256,256]{2,1,0:T(8,128)(2,1)S(1)}, u32[]{:S(2)}) copy-start(bf16[8,256,256]{2,1,0:T(8,128)(2,1)S(1)} %all-to-all-done.1.parts) | copy-start | bytes 3145732

commit v3 on v2

--- a/solution.py
+++ b/solution.py
@@ -13,6 +13,7 @@
 ROWS = 256
 BLOCKS = PAIR_SPAN // ROWS
 PACKED = 2 * ROWS + 16
+CHIPS = 4
 NEG = -1e30
 INV_ROOT = 1.0 / math.sqrt(HEAD_DIM)
 SCALE2 = INV_ROOT * math.log2(math.e)
@@ -36,21 +37,21 @@
     line = jnp.zeros((1, 128), jnp.float32)
     for place, term in enumerate(terms):
         line = jnp.where(lane == place, jnp.sum(term, keepdims=True), line)
-    sums[...] = jnp.broadcast_to(line[None], sums.shape)
+    sums[...] = jnp.broadcast_to(line, sums.shape)
     count = jnp.broadcast_to(jnp.sum(even, keepdims=True), (16, 128)).astype(jnp.bfloat16)
-    for copy in range(BLOCKS):
+    for copy in range(CHIPS):
         packed[copy, :ROWS, :] = keys[...]
         packed[copy, ROWS : 2 * ROWS, :] = values[...]
         packed[copy, 2 * ROWS :, :] = count
 
 
-def pack(keys, values, logprob, docs, response, copies):
+def pack(keys, values, logprob, docs, response):
     wide = (ROWS // 128, 128)
     return pl.pallas_call(
         pack_kernel,
         out_shape=(
-            jax.ShapeDtypeStruct((BLOCKS, PACKED, HEAD_DIM), jnp.bfloat16),
-            jax.ShapeDtypeStruct((copies, 8, 128), jnp.float32),
+            jax.ShapeDtypeStruct((CHIPS, PACKED, HEAD_DIM), jnp.bfloat16),
+            jax.ShapeDtypeStruct((8, 128), jnp.float32),
         ),
         in_specs=[VMEM] * 5,
         out_specs=(VMEM, VMEM),
@@ -65,13 +66,13 @@
         total = jnp.sum(sums[pair * BLOCKS : (pair + 1) * BLOCKS, 0, :], axis=0, keepdims=True)
         each = [jnp.sum(jnp.where(lane == at, total, 0.0), keepdims=True) for at in range(4)]
         line = jnp.where(lane == pair, each[0] / each[2] - each[1] / each[3], line)
-    margins[...] = jnp.broadcast_to(line[None], margins.shape)
-
-
-def pair_margins(sums, copies):
+    margins[...] = jnp.broadcast_to(line, margins.shape)
+
+
+def pair_margins(sums):
     return pl.pallas_call(
         margin_kernel,
-        out_shape=jax.ShapeDtypeStruct((copies, 8, 128), jnp.float32),
+        out_shape=jax.ShapeDtypeStruct((8, 128), jnp.float32),
         in_specs=[VMEM],
         out_specs=VMEM,
         cost_estimate=pl.CostEstimate(flops=10000, bytes_accessed=65536, transcendentals=0),
@@ -79,21 +80,26 @@
 
 
 def attend_kernel(
-    queries, grads, packed, attention, grad_queries, grad_kv,
+    queries, grads, same_core, other_core, attention, grad_queries, same_grads, other_grads,
     keys, values, keys_t, values_t, scores, probs, grad_scores, acc_k, acc_v,
 ):
-    first_row = lax.rem(lax.axis_index("ka"), BLOCKS) * ROWS
-    count = packed[0, 2 * ROWS : 2 * ROWS + 16, :].astype(jnp.float32)
-    for block in range(BLOCKS):
+    place = lax.axis_index("ka")
+    core = lax.rem(place, 2)
+    first_row = lax.rem(place, BLOCKS) * ROWS
+    sources = [(ref, chip) for ref in (same_core, other_core) for chip in range(CHIPS)]
+    firsts = [2 * chip * ROWS + core * ROWS for chip in range(CHIPS)]
+    firsts += [2 * chip * ROWS + (1 - core) * ROWS for chip in range(CHIPS)]
+    count = None
+    for block, (ref, chip) in enumerate(sources):
         span = slice(block * ROWS, (block + 1) * ROWS)
-        key = packed[block, :ROWS, :]
-        value = packed[block, ROWS : 2 * ROWS, :]
+        key = ref[chip, :ROWS, :]
+        value = ref[chip, ROWS : 2 * ROWS, :]
         keys[span, :] = key
         values[span, :] = value
         keys_t[:, span] = key.T
         values_t[:, span] = value.T
-        if block:
-            count += packed[block, 2 * ROWS : 2 * ROWS + 16, :].astype(jnp.float32)
+        term = ref[chip, 2 * ROWS : 2 * ROWS + 16, :].astype(jnp.float32)
+        count = term if count is None else count + term
     cut = count[:1, :1].astype(jnp.int32)
     row = first_row + lax.broadcasted_iota(jnp.int32, (ROWS, ROWS), 0)
     lane = lax.broadcasted_iota(jnp.int32, (ROWS, ROWS), 1)
@@ -105,7 +111,7 @@
         top = None
         for block in range(BLOCKS):
             span = slice(block * ROWS, (block + 1) * ROWS)
-            col = lane + block * ROWS
+            col = lane + firsts[block]
             score = dot(query, keys_t[:, span])
             score = jnp.where((col >= start) & (col <= row), score, NEG)
             scores[:, span] = score
@@ -138,21 +144,27 @@
             acc_k[...] += part_k
             acc_v[...] += part_v
         else:
-            grad_kv[:, :HEAD_DIM] = ((acc_k[...] + part_k) * INV_ROOT).astype(jnp.bfloat16)
-            grad_kv[:, HEAD_DIM:] = (acc_v[...] + part_v).astype(jnp.bfloat16)
-
-
-def attend(queries, grads, packed):
+            for block in range(BLOCKS):
+                span = slice(block * ROWS, (block + 1) * ROWS)
+                ref = same_grads if block < CHIPS else other_grads
+                chip = block % CHIPS
+                grad_key = (acc_k[span, :] + part_k[span, :]) * INV_ROOT
+                ref[chip, :, :HEAD_DIM] = grad_key.astype(jnp.bfloat16)
+                ref[chip, :, HEAD_DIM:] = (acc_v[span, :] + part_v[span, :]).astype(jnp.bfloat16)
+
+
+def attend(queries, grads, same_core, other_core):
     width = HEADS * HEAD_DIM
     return pl.pallas_call(
         attend_kernel,
         out_shape=(
             jax.ShapeDtypeStruct((ROWS, width), jnp.bfloat16),
             jax.ShapeDtypeStruct((ROWS, width), jnp.float32),
-            jax.ShapeDtypeStruct((PAIR_SPAN, 2 * HEAD_DIM), jnp.bfloat16),
+            jax.ShapeDtypeStruct((CHIPS, ROWS, 2 * HEAD_DIM), jnp.bfloat16),
+            jax.ShapeDtypeStruct((CHIPS, ROWS, 2 * HEAD_DIM), jnp.bfloat16),
         ),
-        in_specs=[VMEM] * 3,
-        out_specs=(VMEM,) * 3,
+        in_specs=[VMEM] * 4,
+        out_specs=(VMEM,) * 4,
         scratch_shapes=[
             pltpu.VMEM((PAIR_SPAN, HEAD_DIM), jnp.bfloat16),
             pltpu.VMEM((PAIR_SPAN, HEAD_DIM), jnp.bfloat16),
@@ -170,12 +182,12 @@
             bytes_accessed=4 * MIB,
             transcendentals=HEADS * ROWS * PAIR_SPAN,
         ),
-    )(queries, grads, packed)
+    )(queries, grads, same_core, other_core)
 
 
 def collect_kernel(parts, grad_keys, grad_values):
     total = parts[0].astype(jnp.float32)
-    for block in range(1, BLOCKS):
+    for block in range(1, CHIPS):
         total += parts[block].astype(jnp.float32)
     grad_keys[...] = total[:, :HEAD_DIM]
     grad_values[...] = total[:, HEAD_DIM:]
@@ -193,14 +205,18 @@
 
 
 def per_device(queries, key_heads, value_heads, grad_output, token_logprob, doc_ids, response):
-    groups = [list(range(8)), list(range(8, 16))]
-    packed, sums = pack(key_heads, value_heads, token_logprob, doc_ids, response, 16)
-    packed = lax.all_to_all(packed, "ka", 0, 0, axis_index_groups=groups, tiled=True)
-    sums = lax.all_to_all(sums, "ka", 0, 0, tiled=True)
-    margins = lax.all_to_all(pair_margins(sums, 16), "pb", 0, 0, tiled=True)
-    attention, grad_queries, grad_kv = attend(queries, grad_output, packed)
-    parts = grad_kv.reshape(BLOCKS, ROWS, 2 * HEAD_DIM)
-    parts = lax.all_to_all(parts, "ka", 0, 0, axis_index_groups=groups, tiled=True)
+    rings = [[half * 8 + 2 * chip + core for chip in range(CHIPS)] for half in (0, 1) for core in (0, 1)]
+    swap = [(place, place ^ 1) for place in range(16)]
+    packed, sums = pack(key_heads, value_heads, token_logprob, doc_ids, response)
+    same_core = lax.all_to_all(packed, "ka", 0, 0, axis_index_groups=rings, tiled=True)
+    sums = lax.all_gather(sums, "ka")
+    margins = lax.all_gather(pair_margins(sums), "pb")
+    other_core = lax.ppermute(same_core, "ka", swap)
+    attention, grad_queries, same_grads, other_grads = attend(
+        queries, grad_output, same_core, other_core
+    )
+    same_grads = same_grads + lax.ppermute(other_grads, "ka", swap)
+    parts = lax.all_to_all(same_grads, "ka", 0, 0, axis_index_groups=rings, tiled=True)
     grad_keys, grad_values = collect(parts)
     return (attention, grad_queries, grad_keys, grad_values, margins[:, 0, :2].reshape(-1))
 

time: 84.2 us -> 106 us (1.26); the launches traced: 83.4 us -> 104 us
  blocking collectives: 13.9 us -> 74.1 us
  waiting for transfers between devices: 29.9 us -> 3.69 us
  starting transfers between devices: 17.2 us -> 3.76 us
    all_gather x0 -> x2, blocking collectives: none -> 60 us  [the longest x1 34.2 us: per_device(): margins = lax.all_gather(pair_margins(sums), 'pb')]
    all_to_all x3 -> x1, waiting for transfers between devices: 29.9 us -> 0.01 us  [per_device(): lax.all_to_all(same_grads, 'ka', 0, 0, axis_index_groups=rings, tiled=True)]
    all_to_all x3 -> x1, starting transfers between devices: 17.2 us -> 3.6 us  [per_device(): lax.all_to_all(same_grads, 'ka', 0, 0, axis_index_groups=rings, tiled=True)]
    ppermute x0 -> x2, waiting for transfers between devices: none -> 3.69 us  [the longest x1 1.93 us: per_device(): other_core = lax.ppermute(same_core, 'ka', swap)]
  transfers between devices with their start and end apart: 3 -> 3, of which waited for: 2 -> 2; matrix products, arithmetic and copies ran while one was open for 1% -> 1% of each run, Pallas kernels for 19% -> 2%
where the time goes in v3:
time: 106 us; the launch traced here: 104 us
  blocking collectives  74.1 us (70%)
  Pallas kernels  19.2 us (18%)
  starting transfers between devices  3.76 us (4%)
  waiting for transfers between devices  3.69 us (3%)
  local copies, waits for them, and re-layouts  1.41 us (1%)
    all_gather x1, blocking collectives, per_device(): margins = lax.all_gather(pair_margins(sums), 'pb')  34.2 us
    all_gather x1, blocking collectives, per_device(): sums = lax.all_gather(sums, 'ka')  25.8 us
    all_to_all x1, blocking collectives, per_device(): lax.all_to_all(packed, 'ka', 0, 0, axis_index_groups=rings, tiled=True)  14.1 us
    pallas_call x1, Pallas kernels, attend(): pl.pallas_call(attend_kernel, out_shape=(jax.ShapeDtypeStruct((ROWS, widt...  14 us
    all_to_all x1, starting transfers between devices, per_device(): lax.all_to_all(same_grads, 'ka', 0, 0, axis_index_groups=rings, tiled=True)  3.6 us
  transfers between devices with their start and end apart: 3, of which 2 were waited for; matrix products, arithmetic and copies ran while one was open for 1% of the time, Pallas kernels for 2%

profile of v3, /device:TPU:8, one launch (start us, length us, event | category | flops | bytes accessed | tf_op | source)
XLA Modules:
  0.0 103.7 jit_solution(8775573340201742818)
XLA Ops:
  0.6 1.8 %shard_map.110 = (bf16[4,528,128]{2,1,0:T(8,128)(2,1)}, f32[8,128]{1,0:T(8,128)}) custom-call(bf16[256,128]{1,0:T(8,128)(2,1)} %keys.1, bf16[256,128]{1,0:T(8,128)(2,1)} %values.1, f32[2,128]{1,0:T(2,128)} %bitcast.11, s32[2,128]{1,0:T(2,128)} %bitcast.12, s32[2,128]{1,0:T(2,128)} %bitcast.13), custom_call_target="tpu_custom_call" | custom-call | flops 10000 | bytes 2097152 | tf_op jit(solution)/shard_map/pallas_call | solution.py:50
  2.5 0.0 copy-start
  2.5 0.0 copy-start.1
  2.5 14.1 %all_to_all.10.same_core = bf16[4,528,128]{2,1,0:T(8,128)(2,1)S(1)} all-to-all(bf16[4,528,128]{2,1,0:T(8,128)(2,1)} %get-tuple-element.13), channel_id=1, replica_groups={{0,2,4,6},{1,3,5,7},{8,10,12,14},{9,11,13,15},{16,18,20,22},{17,19,21,2..., dimensions={0} | all-to-all | bytes 1081344 | tf_op jit(solution)/shard_map/all_to_all | solution.py:211
  16.5 0.0 collective-permute-start
  16.5 1.9 %collective-permute-done.other_core = bf16[4,528,128]{2,1,0:T(8,128)(2,1)S(1)} collective-permute-done((bf16[4,528,128]{2,1,0:T(8,128)(2,1)S(1)}, bf16[4,528,128]{2,1,0:T(8,128)(2,1)S(1)}, u32[]{:S(2)}, u32[]{:S(2)}) %collective-permute-start) | collective-permute-done | bytes 540704 | tf_op jit(solution)/shard_map/ppermute | solution.py:214
  18.5 0.0 copy-done
  18.5 0.0 copy-done.1
  18.5 14.0 %shard_map.111 = (bf16[256,768]{1,0:T(8,128)(2,1)}, f32[256,768]{1,0:T(8,128)}, bf16[4,256,256]{2,1,0:T(8,128)(2,1)S(1)}, bf16[4,256,256]{2,1,0:T(8,128)(2,1)S(1)}) custom-call(bf16[256,768]{1,0:T(8,128)(2,1)S(1)} %copy-done, bf16[256,768]{1,0:T(8,128)(2,1)S(1)} %copy-done.1, bf16[4,528,128]{2,1,0:T(8,128)(2,1)S(1)} %all_to_all.10.same_core, ...), custom_call_target="tpu_custom_call" | custom-call | flops 4831838208 | bytes 4194304 | tf_op jit(solution)/shard_map/pallas_call | solution.py:158
  32.5 0.2 collective-permute-start.1
  32.7 1.8 %collective-permute-done.1 = bf16[4,256,256]{2,1,0:T(8,128)(2,1)S(1)} collective-permute-done((bf16[4,256,256]{2,1,0:T(8,128)(2,1)S(1)}, bf16[4,256,256]{2,1,0:T(8,128)(2,1)S(1)}, u32[]{:S(2)}, u32[]{:S(2)}) %collective-permute-start.1) | collective-permute-done | bytes 524320 | tf_op jit(solution)/shard_map/ppermute | solution.py:218
  34.4 0.9 add.3
  35.3 0.0 copy-start.3
  35.3 3.6 %all-to-all-start.1 = ((bf16[4,256,256]{2,1,0:T(8,128)(2,1)}), bf16[4,256,256]{2,1,0:T(8,128)(2,1)S(1)}, u32[]{:S(2)}, u32[]{:S(2)}) async-start(bf16[4,256,256]{2,1,0:T(8,128)(2,1)} %add.3), calls=%async_computation.1 | async-start | bytes 1048576 | tf_op jit(solution)/shard_map/all_to_all | solution.py:219
  38.9 0.0 copy-done.3
  39.0 25.8 %all-gather = f32[128,128]{1,0:T(8,128)} all-gather(f32[8,128]{1,0:T(8,128)S(1)} %copy-done.3), channel_id=2, replica_groups=mesh['pb'=16,'ka'=16] {'ka'}, dimensions={0}, use_global_device_ids=true | all-gather | bytes 69632 | tf_op jit(solution)/shard_map/all_gather | solution.py:212
  64.7 1.6 %shard_map.113 = f32[8,128]{1,0:T(8,128)} custom-call(f32[16,8,128]{2,1,0:T(8,128)} %bitcast.8), custom_call_target="tpu_custom_call" | custom-call | flops 10000 | bytes 65536 | tf_op jit(solution)/shard_map/pallas_call | solution.py:73
  66.3 34.2 %all-gather.1 = f32[128,128]{1,0:T(8,128)S(1)} all-gather(f32[8,128]{1,0:T(8,128)} %shard_map.113), channel_id=3, replica_groups=mesh['pb'=16,'ka'=16] {'pb'}, dimensions={0}, use_global_device_ids=true | all-gather | bytes 69632 | tf_op jit(solution)/shard_map/all_gather | solution.py:213
  100.5 0.6 reshape_squeeze.3
  101.1 0.0 all-to-all-done.1.parts
  101.1 0.0 copy-start.2
  101.1 0.8 copy-done.2
  101.9 1.8 %shard_map.112 = (f32[256,128]{1,0:T(8,128)}, f32[256,128]{1,0:T(8,128)}) custom-call(bf16[4,256,256]{2,1,0:T(8,128)(2,1)} %copy-done.2), custom_call_target="tpu_custom_call" | custom-call | flops 1048576 | bytes 2097152 | tf_op jit(solution)/shard_map/pallas_call | solution.py:198
  (1 shorter events, 0.0 us)
Async XLA Ops:
  2.5 16.0 %copy-start = (bf16[256,768]{1,0:T(8,128)(2,1)S(1)}, bf16[256,768]{1,0:T(8,128)(2,1)}, u32[]{:S(2)}) copy-start(bf16[256,768]{1,0:T(8,128)(2,1)} %queries.1) | copy-start | bytes 1179652
  2.5 16.0 %copy-start.1 = (bf16[256,768]{1,0:T(8,128)(2,1)S(1)}, bf16[256,768]{1,0:T(8,128)(2,1)}, u32[]{:S(2)}) copy-start(bf16[256,768]{1,0:T(8,128)(2,1)} %grads.1) | copy-start | bytes 1179652
  16.5 1.9 %collective-permute-start = (bf16[4,528,128]{2,1,0:T(8,128)(2,1)S(1)}, bf16[4,528,128]{2,1,0:T(8,128)(2,1)S(1)}, u32[]{:S(2)}, u32[]{:S(2)}) collective-permute-start(bf16[4,528,128]{2,1,0:T(8,128)(2,1)S(1)} %all_to_all.10.same_core), channel_id=1, source_target_pairs={{0,1},{1,0},{2,3},{3,2},{4,5},{5,4},{6,7},{7,6},{8,9},{9,8},{10,11... | collective-permute-start | bytes 1622024 | tf_op jit(solution)/shard_map/ppermute | solution.py:214
  32.5 1.9 %collective-permute-start.1 = (bf16[4,256,256]{2,1,0:T(8,128)(2,1)S(1)}, bf16[4,256,256]{2,1,0:T(8,128)(2,1)S(1)}, u32[]{:S(2)}, u32[]{:S(2)}) collective-permute-start(bf16[4,256,256]{2,1,0:T(8,128)(2,1)S(1)} %get-tuple-element.17), channel_id=1, source_target_pairs={{0,1},{1,0},{2,3},{3,2},{4,5},{5,4},{6,7},{7,6},{8,9},{9,8},{10,11... | collective-permute-start | bytes 1572872 | tf_op jit(solution)/shard_map/ppermute | solution.py:218
  35.3 3.6 %copy-start.3 = (f32[8,128]{1,0:T(8,128)S(1)}, f32[8,128]{1,0:T(8,128)}, u32[]{:S(2)}) copy-start(f32[8,128]{1,0:T(8,128)} %get-tuple-element.20) | copy-start | bytes 12292
  35.3 65.8 %all-to-all-start.1 = ((bf16[4,256,256]{2,1,0:T(8,128)(2,1)}), bf16[4,256,256]{2,1,0:T(8,128)(2,1)S(1)}, u32[]{:S(2)}, u32[]{:S(2)}) async-start(bf16[4,256,256]{2,1,0:T(8,128)(2,1)} %add.3), calls=%async_computation.1 | async-start | bytes 1048576 | tf_op jit(solution)/shard_map/all_to_all | solution.py:219
  101.1 0.8 copy-start.2

commit v4 on v3

v4 whole, which is shorter than its diff:
```python
import math

import jax
import jax.numpy as jnp
from jax import lax
from jax.experimental import pallas as pl
from jax.experimental.pallas import tpu as pltpu
from jax.sharding import PartitionSpec as P

HEAD_DIM = 128
HEADS = 6
PAIR_SPAN = 2048
ROWS = 256
BLOCKS = PAIR_SPAN // ROWS
CHIPS = 4
PAIRS = 32
PACKED = 2 * ROWS + 16
NEG = -1e30
INV_ROOT = 1.0 / math.sqrt(HEAD_DIM)
SCALE2 = INV_ROOT * math.log2(math.e)

VMEM = pl.BlockSpec(memory_space=pltpu.VMEM)
MIB = 1024 * 1024


def dot(a, b):
    return jnp.dot(a, b, preferred_element_type=jnp.float32)


def pack_kernel(keys, values, logprob, docs, response, packed, sums):
    pair = lax.axis_index("pb") * 2 + lax.axis_index("ka") // BLOCKS
    odd = (docs[...] & 1).astype(jnp.float32)
    even = 1.0 - odd
    live = response[...].astype(jnp.float32)
    scored = logprob[...] * live
    row = lax.broadcasted_iota(jnp.int32, (8, 128), 0)
    lane = lax.broadcasted_iota(jnp.int32, (8, 128), 1)
    table = jnp.zeros((8, 128), jnp.float32)
    for place, term in enumerate((scored * even, scored * odd, live * even, live * odd)):
        here = (row == place) & (lane == pair)
        table = jnp.where(here, jnp.sum(term, keepdims=True), table)
    sums[...] = table
    packed[:ROWS, :] = keys[...]
    packed[ROWS : 2 * ROWS, :] = values[...]
    count = jnp.broadcast_to(jnp.sum(even, keepdims=True), (16, 128))
    packed[2 * ROWS :, :] = count.astype(jnp.bfloat16)


def pack(keys, values, logprob, docs, response):
    wide = (ROWS // 128, 128)
    return pl.pallas_call(
        pack_kernel,
        out_shape=(
            jax.ShapeDtypeStruct((PACKED, HEAD_DIM), jnp.bfloat16),
            jax.ShapeDtypeStruct((8, 128), jnp.float32),
        ),
        in_specs=[VMEM] * 5,
        out_specs=(VMEM, VMEM),
        cost_estimate=pl.CostEstimate(flops=10000, bytes_accessed=MIB // 2, transcendentals=0),
    )(keys, values, logprob.reshape(wide), docs.reshape(wide), response.reshape(wide))


def attend_kernel(
    queries, grads, own, near, far, opposite, own_s, near_s, far_s, opposite_s,
    attention, grad_queries, same_grads, other_grads,
    keys, values, keys_t, values_t, bias, scores, probs, grad_scores, acc_k, acc_v,
):
    place = lax.axis_index("ka")
    core = lax.rem(place, 2)
    chip = lax.rem(place // 2, CHIPS)
    step = 1 - 2 * core
    chips = [chip, chip - step, chip + step, chip + 2, chip, chip + step, chip - step, chip + 2]
    first_row = lax.rem(place, BLOCKS) * ROWS
    count = None
    for block, ref in enumerate((own, near, far, opposite, own_s, near_s, far_s, opposite_s)):
        span = slice(block * ROWS, (block + 1) * ROWS)
        key = ref[:ROWS, :]
        value = ref[ROWS : 2 * ROWS, :]
        keys[span, :] = key
        values[span, :] = value
        keys_t[:, span] = key.T
        values_t[:, span] = value.T
        term = ref[2 * ROWS :, :].astype(jnp.float32)
        count = term if count is None else count + term
    cut = count[:1, :1].astype(jnp.int32)
    row = first_row + lax.broadcasted_iota(jnp.int32, (ROWS, ROWS), 0)
    lane = lax.broadcasted_iota(jnp.int32, (ROWS, ROWS), 1)
    start = jnp.where(row >= cut, cut, 0)
    for block in range(BLOCKS):
        span = slice(block * ROWS, (block + 1) * ROWS)
        side = core if block < CHIPS else 1 - core
        col = lane + (lax.rem(chips[block] + CHIPS, CHIPS) * 2 + side) * ROWS
        bias[:, span] = jnp.where((col >= start) & (col <= row), 0.0, NEG)
    for head in range(HEADS):
        cols = slice(head * HEAD_DIM, (head + 1) * HEAD_DIM)
        score_ref, prob_ref, grad_ref = (ref.at[head % 2] for ref in (scores, probs, grad_scores))
        query = queries[:, cols]
        grad = grads[:, cols]
        top = None
        for block in range(BLOCKS):
            span = slice(block * ROWS, (block + 1) * ROWS)
            score = dot(query, keys_t[:, span]) + bias[:, span]
            score_ref[:, span] = score
            top = score if top is None else jnp.maximum(top, score)
        row_max = jnp.max(top, axis=1, keepdims=True) * SCALE2
        total = None
        for block in range(BLOCKS):
            span = slice(block * ROWS, (block + 1) * ROWS)
            prob = jnp.exp2(score_ref[:, span] * SCALE2 - row_max)
            prob_ref[:, span] = prob.astype(jnp.bfloat16)
            total = prob if total is None else total + prob
        inv_total = 1.0 / jnp.sum(total, axis=1, keepdims=True)
        output = (dot(prob_ref[...], values[...]) * inv_total).astype(jnp.bfloat16)
        attention[:, cols] = output
        grad_wide = grad.astype(jnp.float32)
        delta = jnp.sum(grad_wide * output.astype(jnp.float32), axis=1, keepdims=True) * inv_total
        grad_scaled = (grad_wide * inv_total).astype(jnp.bfloat16)
        for block in range(BLOCKS):
            span = slice(block * ROWS, (block + 1) * ROWS)
            grad_prob = dot(grad_scaled, values_t[:, span])
            grad_score = prob_ref[:, span].astype(jnp.float32) * (grad_prob - delta)
            grad_ref[:, span] = grad_score.astype(jnp.bfloat16)
        grad_queries[:, cols] = dot(grad_ref[...], keys[...]) * INV_ROOT
        query_t = query.T
        grad_t = grad_scaled.T
        for block in range(BLOCKS):
            span = slice(block * ROWS, (block + 1) * ROWS)
            part_k = dot(query_t, grad_ref[:, span])
            part_v = dot(grad_t, prob_ref[:, span])
            if head:
                part_k += acc_k[:, span]
                part_v += acc_v[:, span]
            if head < HEADS - 1:
                acc_k[:, span] = part_k
                acc_v[:, span] = part_v
            else:
                out = same_grads if block < CHIPS else other_grads
                out[block % CHIPS, :, :HEAD_DIM] = (part_k * INV_ROOT).astype(jnp.bfloat16).T
                out[block % CHIPS, :, HEAD_DIM:] = part_v.astype(jnp.bfloat16).T


def attend(queries, grads, blocks):
    width = HEADS * HEAD_DIM
    part = jax.ShapeDtypeStruct((CHIPS, ROWS, 2 * HEAD_DIM), jnp.bfloat16)
    return pl.pallas_call(
        attend_kernel,
        out_shape=(
            jax.ShapeDtypeStruct((ROWS, width), jnp.bfloat16),
            jax.ShapeDtypeStruct((ROWS, width), jnp.float32),
            part,
            part,
        ),
        in_specs=[VMEM] * (2 + BLOCKS),
        out_specs=(VMEM,) * 4,
        scratch_shapes=[
            pltpu.VMEM((PAIR_SPAN, HEAD_DIM), jnp.bfloat16),
            pltpu.VMEM((PAIR_SPAN, HEAD_DIM), jnp.bfloat16),
            pltpu.VMEM((HEAD_DIM, PAIR_SPAN), jnp.bfloat16),
            pltpu.VMEM((HEAD_DIM, PAIR_SPAN), jnp.bfloat16),
            pltpu.VMEM((ROWS, PAIR_SPAN), jnp.float32),
            pltpu.VMEM((2, ROWS, PAIR_SPAN), jnp.float32),
            pltpu.VMEM((2, ROWS, PAIR_SPAN), jnp.bfloat16),
            pltpu.VMEM((2, ROWS, PAIR_SPAN), jnp.bfloat16),
            pltpu.VMEM((HEAD_DIM, PAIR_SPAN), jnp.float32),
            pltpu.VMEM((HEAD_DIM, PAIR_SPAN), jnp.float32),
        ],
        compiler_params=pltpu.CompilerParams(vmem_limit_bytes=32 * MIB),
        cost_estimate=pl.CostEstimate(
            flops=12 * HEADS * ROWS * PAIR_SPAN * HEAD_DIM,
            bytes_accessed=4 * MIB,
            transcendentals=HEADS * ROWS * PAIR_SPAN,
        ),
    )(queries, grads, *blocks)


def collect_kernel(own, near, far, grad_keys, grad_values):
    total = own[...].astype(jnp.float32) + near[...].astype(jnp.float32)
    total += far[...].astype(jnp.float32)
    grad_keys[...] = total[:, :HEAD_DIM]
    grad_values[...] = total[:, HEAD_DIM:]


def collect(own, near, far):
    shape = jax.ShapeDtypeStruct((ROWS, HEAD_DIM), jnp.float32)
    return pl.pallas_call(
        collect_kernel,
        out_shape=(shape, shape),
        in_specs=[VMEM] * 3,
        out_specs=(VMEM, VMEM),
        cost_estimate=pl.CostEstimate(flops=MIB, bytes_accessed=MIB, transcendentals=0),
    )(own, near, far)


def at(half, chip, core):
    return half * 8 + (chip % CHIPS) * 2 + core


def per_device(queries, key_heads, value_heads, grad_output, token_logprob, doc_ids, response):
    spots = [(half, chip, core) for half in (0, 1) for chip in range(CHIPS) for core in (0, 1)]
    ahead = [(at(h, x, k), at(h, x + 1 - 2 * k, k)) for h, x, k in spots]
    back = [(there, here) for here, there in ahead]
    swap = [(place, place ^ 1) for place in range(16)]

    own, sums = pack(key_heads, value_heads, token_logprob, doc_ids, response)
    near = lax.ppermute(own, "ka", ahead)
    far = lax.ppermute(own, "ka", back)
    own_s = lax.ppermute(own, "ka", swap)
    opposite = lax.ppermute(near, "ka", ahead)
    near_s = lax.ppermute(near, "ka", swap)
    far_s = lax.ppermute(far, "ka", swap)
    opposite_s = lax.ppermute(opposite, "ka", swap)

    for bit in (1, 2, 4, 8):
        sums = sums + lax.ppermute(sums, "pb", [(place, place ^ bit) for place in range(16)])
    queries, sums = lax.optimization_barrier((queries, sums))

    blocks = (own, near, far, opposite, own_s, near_s, far_s, opposite_s)
    attention, grad_queries, same_grads, other_grads = attend(queries, grad_output, blocks)
    other_grads, sums = lax.optimization_barrier((other_grads, sums))
    for bit in (8, 1, 2, 6):
        sums = sums + lax.ppermute(sums, "ka", [(place, place ^ bit) for place in range(16)])
    margins = (sums[0] / sums[2] - sums[1] / sums[3])[:PAIRS]
    same_grads = same_grads + lax.ppermute(other_grads, "ka", swap)
    far_part = lax.ppermute(same_grads[2], "ka", ahead)
    passed = lax.ppermute(same_grads[3], "ka", back)
    near_part = lax.ppermute(same_grads[1] + passed, "ka", back)
    grad_keys, grad_values = collect(same_grads[0], near_part, far_part)
    return (attention, grad_queries, grad_keys, grad_values, margins)


def solution(mesh):
    rows = P(("pb", "ka"), None)
    line = P(("pb", "ka"))
    return jax.shard_map(
        per_device,
        mesh=mesh,
        in_specs=(rows, rows, rows, rows, line, line, line),
        out_specs=(rows, rows, rows, rows, P()),
        check_vma=False,
    )
```

time: 106 us -> 82.4 us (0.78)
  the two profiles are of different devices: /device:TPU:8 before, /device:TPU:6 now
where the time goes in v4:
time: 82.4 us; the launch traced here: 82.1 us
  waiting for transfers between devices  33.7 us (41%)
  starting transfers between devices  26.3 us (32%)
  Pallas kernels  15.8 us (19%)
  local copies, waits for them, and re-layouts  4.72 us (6%)
  other arithmetic  0.86 us (1%)
    pallas_call x1, Pallas kernels, attend(): pl.pallas_call(attend_kernel, out_shape=(jax.ShapeDtypeStruct((ROWS, widt...  12.4 us
    ppermute x4, waiting for transfers between devices, per_device(): lax.ppermute(sums, 'pb', [(place, place ^ bit) for place in range(16)])  10.3 us
    ppermute x4, starting transfers between devices, per_device(): lax.ppermute(sums, 'pb', [(place, place ^ bit) for place in range(16)])  9.29 us
    ppermute x4, waiting for transfers between devices, per_device(): lax.ppermute(sums, 'ka', [(place, place ^ bit) for place in range(16)])  7.7 us
    ppermute x4, starting transfers between devices, per_device(): lax.ppermute(sums, 'ka', [(place, place ^ bit) for place in range(16)])  7.34 us
    ppermute x1, waiting for transfers between devices, per_device(): near_part = lax.ppermute(same_grads[1] + passed, 'ka', back)  5.65 us
    ppermute x1, waiting for transfers between devices, per_device(): passed = lax.ppermute(same_grads[3], 'ka', back)  4.12 us
    ppermute x1, waiting for transfers between devices, per_device(): near = lax.ppermute(own, 'ka', ahead)  3.9 us
  transfers between devices with their start and end apart: 19, of which 12 were waited for; matrix products, arithmetic and copies ran while one was open for 2% of the time, Pallas kernels for 0%

profile of v4, /device:TPU:6, one launch (start us, length us, event | category | flops | bytes accessed | tf_op | source)
XLA Modules:
  0.0 82.1 jit_solution(3336795002137079298)
XLA Ops:
  0.6 1.7 %shard_map.110 = (bf16[528,128]{1,0:T(8,128)(2,1)}, f32[8,128]{1,0:T(8,128)}) custom-call(bf16[256,128]{1,0:T(8,128)(2,1)} %keys.1, bf16[256,128]{1,0:T(8,128)(2,1)} %values.1, f32[2,128]{1,0:T(2,128)} %bitcast.15, s32[2,128]{1,0:T(2,128)} %bitcast.16, s32[2,128]{1,0:T(2,128)} %bitcast.17), custom_call_target="tpu_custom_call" | custom-call | flops 10000 | bytes 524288 | tf_op jit(solution)/shard_map/pallas_call | solution.py:51
  2.3 2.2 %collective-permute-start.4 = (bf16[528,128]{1,0:T(8,128)(2,1)}, bf16[528,128]{1,0:T(8,128)(2,1)S(1)}, u32[]{:S(2)}, u32[]{:S(2)}) collective-permute-start(bf16[528,128]{1,0:T(8,128)(2,1)} %get-tuple-element.19.own), channel_id=1, source_target_pairs={{0,2},{1,7},{2,4},{3,1},{4,6},{5,3},{6,0},{7,5},{8,10},{9,15},{10,... | collective-permute-start | bytes 405512 | tf_op jit(solution)/shard_map/ppermute | solution.py:205
  4.5 0.0 collective-permute-start.5
  4.5 3.9 %collective-permute-done.4.near = bf16[528,128]{1,0:T(8,128)(2,1)S(1)} collective-permute-done((bf16[528,128]{1,0:T(8,128)(2,1)}, bf16[528,128]{1,0:T(8,128)(2,1)S(1)}, u32[]{:S(2)}, u32[]{:S(2)}) %collective-permute-start.4) | collective-permute-done | bytes 135200 | tf_op jit(solution)/shard_map/ppermute | solution.py:205
  8.4 3.6 %collective-permute-start.6 = (bf16[528,128]{1,0:T(8,128)(2,1)S(1)}, bf16[528,128]{1,0:T(8,128)(2,1)S(1)}, u32[]{:S(2)}, u32[]{:S(2)}) collective-permute-start(bf16[528,128]{1,0:T(8,128)(2,1)S(1)} %collective-permute-done.4.near), channel_id=1, source_target_pairs={{0,2},{1,7},{2,4},{3,1},{4,6},{5,3},{6,0},{7,5},{8,10},{9,15},{10,... | collective-permute-start | bytes 405512 | tf_op jit(solution)/shard_map/ppermute | solution.py:208
  12.0 0.0 collective-permute-start.7
  12.0 0.5 collective-permute-start.8
  12.5 0.0 collective-permute-done.5.far
  12.5 0.0 collective-permute-start.9
  12.5 2.0 %collective-permute-done.6.opposite = bf16[528,128]{1,0:T(8,128)(2,1)S(1)} collective-permute-done((bf16[528,128]{1,0:T(8,128)(2,1)S(1)}, bf16[528,128]{1,0:T(8,128)(2,1)S(1)}, u32[]{:S(2)}, u32[]{:S(2)}) %collective-permute-start.6) | collective-permute-done | bytes 135200 | tf_op jit(solution)/shard_map/ppermute | solution.py:208
  14.6 0.0 collective-permute-start.10
  14.6 0.4 collective-permute-start
  15.0 3.4 %collective-permute-done = f32[8,128]{1,0:T(8,128)S(1)} collective-permute-done((f32[8,128]{1,0:T(8,128)}, f32[8,128]{1,0:T(8,128)S(1)}, u32[]{:S(2)}, u32[]{:S(2)}) %collective-permute-start) | collective-permute-done | bytes 4128 | tf_op jit(solution)/shard_map/ppermute | solution.py:214
  18.4 0.7 add.30
  19.1 0.8 collective-permute-start.1
  19.8 2.9 %collective-permute-done.1 = f32[8,128]{1,0:T(8,128)S(1)} collective-permute-done((f32[8,128]{1,0:T(8,128)S(1)}, f32[8,128]{1,0:T(8,128)S(1)}, u32[]{:S(2)}, u32[]{:S(2)}) %collective-permute-start.1) | collective-permute-done | bytes 4128 | tf_op jit(solution)/shard_map/ppermute | solution.py:214
  22.7 2.1 %collective-permute-start.2 = (f32[8,128]{1,0:T(8,128)S(1)}, f32[8,128]{1,0:T(8,128)S(1)}, u32[]{:S(2)}, u32[]{:S(2)}) collective-permute-start(f32[8,128]{1,0:T(8,128)S(1)} %add.31), channel_id=1, source_target_pairs={{0,64},{16,80},{32,96},{48,112},{64,0},{80,16},{96,32},{112,48},{1... | collective-permute-start | bytes 12296 | tf_op jit(solution)/shard_map/ppermute | solution.py:214
  24.8 2.4 %collective-permute-done.2 = f32[8,128]{1,0:T(8,128)S(1)} collective-permute-done((f32[8,128]{1,0:T(8,128)S(1)}, f32[8,128]{1,0:T(8,128)S(1)}, u32[]{:S(2)}, u32[]{:S(2)}) %collective-permute-start.2) | collective-permute-done | bytes 4128 | tf_op jit(solution)/shard_map/ppermute | solution.py:214
  27.2 6.0 %collective-permute-start.3 = (f32[8,128]{1,0:T(8,128)S(1)}, f32[8,128]{1,0:T(8,128)S(1)}, u32[]{:S(2)}, u32[]{:S(2)}) collective-permute-start(f32[8,128]{1,0:T(8,128)S(1)} %add.32), channel_id=1, source_target_pairs={{0,128},{16,144},{32,160},{48,176},{64,192},{80,208},{96,224},{112... | collective-permute-start | bytes 12296 | tf_op jit(solution)/shard_map/ppermute | solution.py:214
  33.2 1.6 %collective-permute-done.3 = f32[8,128]{1,0:T(8,128)S(1)} collective-permute-done((f32[8,128]{1,0:T(8,128)S(1)}, f32[8,128]{1,0:T(8,128)S(1)}, u32[]{:S(2)}, u32[]{:S(2)}) %collective-permute-start.3) | collective-permute-done | bytes 4128 | tf_op jit(solution)/shard_map/ppermute | solution.py:214
  34.8 0.0 collective-permute-done.7.own_s
  34.8 0.0 collective-permute-done.9.far_s
  34.8 0.0 collective-permute-done.8.near_s
  34.8 0.0 collective-permute-done.10.opposite_s
  34.8 0.0 copy-start
  34.9 1.0 %copy-done = bf16[256,768]{1,0:T(8,128)(2,1)S(1)} copy-done((bf16[256,768]{1,0:T(8,128)(2,1)S(1)}, bf16[256,768]{1,0:T(8,128)(2,1)}, u32[]{:S(2)}) %copy-start) | copy-done | bytes 393240
  35.9 1.0 %copy-done.1 = bf16[256,768]{1,0:T(8,128)(2,1)S(1)} copy-done((bf16[256,768]{1,0:T(8,128)(2,1)S(1)}, bf16[256,768]{1,0:T(8,128)(2,1)}, u32[]{:S(2)}) %copy-start.1) | copy-done | bytes 393240
  36.8 0.9 %copy-done.2 = bf16[528,128]{1,0:T(8,128)(2,1)S(1)} copy-done((bf16[528,128]{1,0:T(8,128)(2,1)S(1)}, bf16[528,128]{1,0:T(8,128)(2,1)}, u32[]{:S(2)}) %copy-start.2) | copy-done | bytes 135192
  37.8 12.4 %shard_map.111 = (bf16[256,768]{1,0:T(8,128)(2,1)}, f32[256,768]{1,0:T(8,128)}, bf16[4,256,256]{2,1,0:T(8,128)(2,1)S(1)}, bf16[4,256,256]{2,1,0:T(8,128)(2,1)S(1)}) custom-call(bf16[256,768]{1,0:T(8,128)(2,1)S(1)} %copy-done, bf16[256,768]{1,0:T(8,128)(2,1)S(1)} %copy-done.1, bf16[528,128]{1,0:T(8,128)(2,1)S(1)} %copy-done.2, ...), custom_call_target="tpu_custom_call" | custom-call | flops 4831838208 | bytes 4194304 | tf_op jit(solution)/shard_map/pallas_call | solution.py:145
  50.1 0.0 collective-permute-start.11
  50.1 3.2 %collective-permute-start.15 = (f32[8,128]{1,0:T(8,128)S(1)}, f32[8,128]{1,0:T(8,128)S(1)}, u32[]{:S(2)}, u32[]{:S(2)}) collective-permute-start(f32[8,128]{1,0:T(8,128)S(1)} %add.33), channel_id=1, source_target_pairs={{0,8},{1,9},{2,10},{3,11},{4,12},{5,13},{6,14},{7,15},{8,0},{9,1},... | collective-permute-start | bytes 12296 | tf_op jit(solution)/shard_map/ppermute | solution.py:221
  53.3 1.9 %collective-permute-done.15 = f32[8,128]{1,0:T(8,128)S(1)} collective-permute-done((f32[8,128]{1,0:T(8,128)S(1)}, f32[8,128]{1,0:T(8,128)S(1)}, u32[]{:S(2)}, u32[]{:S(2)}) %collective-permute-start.15) | collective-permute-done | bytes 4128 | tf_op jit(solution)/shard_map/ppermute | solution.py:221
  55.2 0.0 collective-permute-start.16
  55.2 1.2 %collective-permute-done.16 = f32[8,128]{1,0:T(8,128)S(1)} collective-permute-done((f32[8,128]{1,0:T(8,128)S(1)}, f32[8,128]{1,0:T(8,128)S(1)}, u32[]{:S(2)}, u32[]{:S(2)}) %collective-permute-start.16) | collective-permute-done | bytes 4128 | tf_op jit(solution)/shard_map/ppermute | solution.py:221
  56.4 0.6 collective-permute-start.17
  57.0 3.1 %collective-permute-done.17 = f32[8,128]{1,0:T(8,128)S(1)} collective-permute-done((f32[8,128]{1,0:T(8,128)S(1)}, f32[8,128]{1,0:T(8,128)S(1)}, u32[]{:S(2)}, u32[]{:S(2)}) %collective-permute-start.17) | collective-permute-done | bytes 4128 | tf_op jit(solution)/shard_map/ppermute | solution.py:221
  60.0 3.6 %collective-permute-start.18 = (f32[8,128]{1,0:T(8,128)S(1)}, f32[8,128]{1,0:T(8,128)S(1)}, u32[]{:S(2)}, u32[]{:S(2)}) collective-permute-start(f32[8,128]{1,0:T(8,128)S(1)} %add.38), channel_id=1, source_target_pairs={{0,6},{1,7},{2,4},{3,5},{4,2},{5,3},{6,0},{7,1},{8,14},{9,15},{10,... | collective-permute-start | bytes 12296 | tf_op jit(solution)/shard_map/ppermute | solution.py:221
  63.6 1.6 %collective-permute-done.18 = f32[8,128]{1,0:T(8,128)S(1)} collective-permute-done((f32[8,128]{1,0:T(8,128)S(1)}, f32[8,128]{1,0:T(8,128)S(1)}, u32[]{:S(2)}, u32[]{:S(2)}) %collective-permute-start.18) | collective-permute-done | bytes 4128 | tf_op jit(solution)/shard_map/ppermute | solution.py:221
  65.2 0.1 add.34
  65.3 0.7 slice_bitcast_fusion
  66.0 3.3 %collective-permute-start.14 = (bf16[256,256]{1,0:T(8,128)(2,1)S(1)}, bf16[256,256]{1,0:T(8,128)(2,1)S(1)}, u32[]{:S(2)}, u32[]{:S(2)}) collective-permute-start(bf16[256,256]{1,0:T(8,128)(2,1)S(1)} %get-tuple-element.29), channel_id=1, source_target_pairs={{0,2},{1,7},{2,4},{3,1},{4,6},{5,3},{6,0},{7,5},{8,10},{9,15},{10,... | collective-permute-start | bytes 393224 | tf_op jit(solution)/shard_map/ppermute | solution.py:224
  69.3 4.1 %collective-permute-done.12 = bf16[256,256]{1,0:T(8,128)(2,1)S(1)} collective-permute-done((bf16[256,256]{1,0:T(8,128)(2,1)S(1)}, bf16[256,256]{1,0:T(8,128)(2,1)S(1)}, u32[]{:S(2)}, u32[]{:S(2)}) %collective-permute-start.12) | collective-permute-done | bytes 131104 | tf_op jit(solution)/shard_map/ppermute | solution.py:225
  73.5 0.1 collective-permute-start.13
  73.6 0.5 slice_bitcast_fusion.4
  74.1 0.0 collective-permute-done.14.far
  74.1 5.6 %collective-permute-done.13.near = bf16[256,256]{1,0:T(8,128)(2,1)S(1)} collective-permute-done((bf16[256,256]{1,0:T(8,128)(2,1)S(1)}, bf16[256,256]{1,0:T(8,128)(2,1)S(1)}, u32[]{:S(2)}, u32[]{:S(2)}) %collective-permute-start.13) | collective-permute-done | bytes 131104 | tf_op jit(solution)/shard_map/ppermute | solution.py:226
  79.7 0.6 copy-done.4
  80.4 1.8 %shard_map.112 = (f32[256,128]{1,0:T(8,128)}, f32[256,128]{1,0:T(8,128)}) custom-call(bf16[256,256]{1,0:T(8,128)(2,1)} %get-tuple-element.31.own, bf16[256,256]{1,0:T(8,128)(2,1)} %copy-done.4, bf16[256,256]{1,0:T(8,128)(2,1)} %copy-done.3), custom_call_target="tpu_custom_call" | custom-call | flops 1048576 | bytes 1048576 | tf_op jit(solution)/shard_map/pallas_call | solution.py:185
  (16 shorter events, 0.1 us)
Async XLA Ops:
  2.3 6.1 %collective-permute-start.4 = (bf16[528,128]{1,0:T(8,128)(2,1)}, bf16[528,128]{1,0:T(8,128)(2,1)S(1)}, u32[]{:S(2)}, u32[]{:S(2)}) collective-permute-start(bf16[528,128]{1,0:T(8,128)(2,1)} %get-tuple-element.19.own), channel_id=1, source_target_pairs={{0,2},{1,7},{2,4},{3,1},{4,6},{5,3},{6,0},{7,5},{8,10},{9,15},{10,... | collective-permute-start | bytes 405512 | tf_op jit(solution)/shard_map/ppermute | solution.py:205
  4.5 8.0 %collective-permute-start.5 = (bf16[528,128]{1,0:T(8,128)(2,1)}, bf16[528,128]{1,0:T(8,128)(2,1)S(1)}, u32[]{:S(2)}, u32[]{:S(2)}) collective-permute-start(bf16[528,128]{1,0:T(8,128)(2,1)} %get-tuple-element.19.own), channel_id=1, source_target_pairs={{2,0},{7,1},{4,2},{1,3},{6,4},{3,5},{0,6},{5,7},{10,8},{15,9},{12,... | collective-permute-start | bytes 405512 | tf_op jit(solution)/shard_map/ppermute | solution.py:206
  8.4 6.1 %collective-permute-start.6 = (bf16[528,128]{1,0:T(8,128)(2,1)S(1)}, bf16[528,128]{1,0:T(8,128)(2,1)S(1)}, u32[]{:S(2)}, u32[]{:S(2)}) collective-permute-start(bf16[528,128]{1,0:T(8,128)(2,1)S(1)} %collective-permute-done.4.near), channel_id=1, source_target_pairs={{0,2},{1,7},{2,4},{3,1},{4,6},{5,3},{6,0},{7,5},{8,10},{9,15},{10,... | collective-permute-start | bytes 405512 | tf_op jit(solution)/shard_map/ppermute | solution.py:208
  12.0 22.8 %collective-permute-start.7 = (bf16[528,128]{1,0:T(8,128)(2,1)}, bf16[528,128]{1,0:T(8,128)(2,1)S(1)}, u32[]{:S(2)}, u32[]{:S(2)}) collective-permute-start(bf16[528,128]{1,0:T(8,128)(2,1)} %get-tuple-element.19.own), channel_id=1, source_target_pairs={{0,1},{1,0},{2,3},{3,2},{4,5},{5,4},{6,7},{7,6},{8,9},{9,8},{10,11... | collective-permute-start | bytes 405512 | tf_op jit(solution)/shard_map/ppermute | solution.py:207
  12.0 22.8 %collective-permute-start.8 = (bf16[528,128]{1,0:T(8,128)(2,1)S(1)}, bf16[528,128]{1,0:T(8,128)(2,1)S(1)}, u32[]{:S(2)}, u32[]{:S(2)}) collective-permute-start(bf16[528,128]{1,0:T(8,128)(2,1)S(1)} %collective-permute-done.4.near), channel_id=1, source_target_pairs={{0,1},{1,0},{2,3},{3,2},{4,5},{5,4},{6,7},{7,6},{8,9},{9,8},{10,11... | collective-permute-start | bytes 405512 | tf_op jit(solution)/shard_map/ppermute | solution.py:209
  12.5 22.3 %collective-permute-start.9 = (bf16[528,128]{1,0:T(8,128)(2,1)S(1)}, bf16[528,128]{1,0:T(8,128)(2,1)S(1)}, u32[]{:S(2)}, u32[]{:S(2)}) collective-permute-start(bf16[528,128]{1,0:T(8,128)(2,1)S(1)} %collective-permute-done.5.far), channel_id=1, source_target_pairs={{0,1},{1,0},{2,3},{3,2},{4,5},{5,4},{6,7},{7,6},{8,9},{9,8},{10,11... | collective-permute-start | bytes 405512 | tf_op jit(solution)/shard_map/ppermute | solution.py:210
  14.6 20.3 %collective-permute-start.10 = (bf16[528,128]{1,0:T(8,128)(2,1)S(1)}, bf16[528,128]{1,0:T(8,128)(2,1)S(1)}, u32[]{:S(2)}, u32[]{:S(2)}) collective-permute-start(bf16[528,128]{1,0:T(8,128)(2,1)S(1)} %collective-permute-done.6.opposite), channel_id=1, source_target_pairs={{0,1},{1,0},{2,3},{3,2},{4,5},{5,4},{6,7},{7,6},{8,9},{9,8},{10,11... | collective-permute-start | bytes 405512 | tf_op jit(solution)/shard_map/ppermute | solution.py:211
  14.6 3.8 %collective-permute-start = (f32[8,128]{1,0:T(8,128)}, f32[8,128]{1,0:T(8,128)S(1)}, u32[]{:S(2)}, u32[]{:S(2)}) collective-permute-start(f32[8,128]{1,0:T(8,128)} %get-tuple-element.17), channel_id=1, source_target_pairs={{0,16},{16,0},{32,48},{48,32},{64,80},{80,64},{96,112},{112,96},{1... | collective-permute-start | bytes 12296 | tf_op jit(solution)/shard_map/ppermute | solution.py:214
  19.1 3.6 %collective-permute-start.1 = (f32[8,128]{1,0:T(8,128)S(1)}, f32[8,128]{1,0:T(8,128)S(1)}, u32[]{:S(2)}, u32[]{:S(2)}) collective-permute-start(f32[8,128]{1,0:T(8,128)S(1)} %add.30), channel_id=1, source_target_pairs={{0,32},{16,48},{32,0},{48,16},{64,96},{80,112},{96,64},{112,80},{1... | collective-permute-start | bytes 12296 | tf_op jit(solution)/shard_map/ppermute | solution.py:214
  22.7 4.5 %collective-permute-start.2 = (f32[8,128]{1,0:T(8,128)S(1)}, f32[8,128]{1,0:T(8,128)S(1)}, u32[]{:S(2)}, u32[]{:S(2)}) collective-permute-start(f32[8,128]{1,0:T(8,128)S(1)} %add.31), channel_id=1, source_target_pairs={{0,64},{16,80},{32,96},{48,112},{64,0},{80,16},{96,32},{112,48},{1... | collective-permute-start | bytes 12296 | tf_op jit(solution)/shard_map/ppermute | solution.py:214
  27.2 7.6 %collective-permute-start.3 = (f32[8,128]{1,0:T(8,128)S(1)}, f32[8,128]{1,0:T(8,128)S(1)}, u32[]{:S(2)}, u32[]{:S(2)}) collective-permute-start(f32[8,128]{1,0:T(8,128)S(1)} %add.32), channel_id=1, source_target_pairs={{0,128},{16,144},{32,160},{48,176},{64,192},{80,208},{96,224},{112... | collective-permute-start | bytes 12296 | tf_op jit(solution)/shard_map/ppermute | solution.py:214
  34.8 1.0 %copy-start = (bf16[256,768]{1,0:T(8,128)(2,1)S(1)}, bf16[256,768]{1,0:T(8,128)(2,1)}, u32[]{:S(2)}) copy-start(bf16[256,768]{1,0:T(8,128)(2,1)} %queries) | copy-start | bytes 1179652
  35.8 1.0 %copy-start.1 = (bf16[256,768]{1,0:T(8,128)(2,1)S(1)}, bf16[256,768]{1,0:T(8,128)(2,1)}, u32[]{:S(2)}) copy-start(bf16[256,768]{1,0:T(8,128)(2,1)} %grads.1) | copy-start | bytes 1179652
  36.8 0.9 %copy-start.2 = (bf16[528,128]{1,0:T(8,128)(2,1)S(1)}, bf16[528,128]{1,0:T(8,128)(2,1)}, u32[]{:S(2)}) copy-start(bf16[528,128]{1,0:T(8,128)(2,1)} %get-tuple-element.19.own) | copy-start | bytes 405508
  50.1 15.1 %collective-permute-start.11 = (bf16[4,256,256]{2,1,0:T(8,128)(2,1)S(1)}, bf16[4,256,256]{2,1,0:T(8,128)(2,1)S(1)}, u32[]{:S(2)}, u32[]{:S(2)}) collective-permute-start(bf16[4,256,256]{2,1,0:T(8,128)(2,1)S(1)} %get-tuple-element.25), channel_id=1, source_target_pairs={{0,1},{1,0},{2,3},{3,2},{4,5},{5,4},{6,7},{7,6},{8,9},{9,8},{10,11... | collective-permute-start | bytes 1572872 | tf_op jit(solution)/shard_map/ppermute | solution.py:223
  50.1 5.1 %collective-permute-start.15 = (f32[8,128]{1,0:T(8,128)S(1)}, f32[8,128]{1,0:T(8,128)S(1)}, u32[]{:S(2)}, u32[]{:S(2)}) collective-permute-start(f32[8,128]{1,0:T(8,128)S(1)} %add.33), channel_id=1, source_target_pairs={{0,8},{1,9},{2,10},{3,11},{4,12},{5,13},{6,14},{7,15},{8,0},{9,1},... | collective-permute-start | bytes 12296 | tf_op jit(solution)/shard_map/ppermute | solution.py:221
  55.2 1.2 %collective-permute-start.16 = (f32[8,128]{1,0:T(8,128)S(1)}, f32[8,128]{1,0:T(8,128)S(1)}, u32[]{:S(2)}, u32[]{:S(2)}) collective-permute-start(f32[8,128]{1,0:T(8,128)S(1)} %add.36), channel_id=1, source_target_pairs={{0,1},{1,0},{2,3},{3,2},{4,5},{5,4},{6,7},{7,6},{8,9},{9,8},{10,11... | collective-permute-start | bytes 12296 | tf_op jit(solution)/shard_map/ppermute | solution.py:221
  56.4 3.6 %collective-permute-start.17 = (f32[8,128]{1,0:T(8,128)S(1)}, f32[8,128]{1,0:T(8,128)S(1)}, u32[]{:S(2)}, u32[]{:S(2)}) collective-permute-start(f32[8,128]{1,0:T(8,128)S(1)} %add.37), channel_id=1, source_target_pairs={{0,2},{1,3},{2,0},{3,1},{4,6},{5,7},{6,4},{7,5},{8,10},{9,11},{10,... | collective-permute-start | bytes 12296 | tf_op jit(solution)/shard_map/ppermute | solution.py:221
  60.0 5.2 %collective-permute-start.18 = (f32[8,128]{1,0:T(8,128)S(1)}, f32[8,128]{1,0:T(8,128)S(1)}, u32[]{:S(2)}, u32[]{:S(2)}) collective-permute-start(f32[8,128]{1,0:T(8,128)S(1)} %add.38), channel_id=1, source_target_pairs={{0,6},{1,7},{2,4},{3,5},{4,2},{5,3},{6,0},{7,1},{8,14},{9,15},{10,... | collective-permute-start | bytes 12296 | tf_op jit(solution)/shard_map/ppermute | solution.py:221
  66.0 7.4 %collective-permute-start.12 = (bf16[256,256]{1,0:T(8,128)(2,1)S(1)}, bf16[256,256]{1,0:T(8,128)(2,1)S(1)}, u32[]{:S(2)}, u32[]{:S(2)}) collective-permute-start(bf16[256,256]{1,0:T(8,128)(2,1)S(1)} %get-tuple-element.30), channel_id=1, source_target_pairs={{2,0},{7,1},{4,2},{1,3},{6,4},{3,5},{0,6},{5,7},{10,8},{15,9},{12,... | collective-permute-start | bytes 393224 | tf_op jit(solution)/shard_map/ppermute | solution.py:225
  66.0 8.1 %collective-permute-start.14 = (bf16[256,256]{1,0:T(8,128)(2,1)S(1)}, bf16[256,256]{1,0:T(8,128)(2,1)S(1)}, u32[]{:S(2)}, u32[]{:S(2)}) collective-permute-start(bf16[256,256]{1,0:T(8,128)(2,1)S(1)} %get-tuple-element.29), channel_id=1, source_target_pairs={{0,2},{1,7},{2,4},{3,1},{4,6},{5,3},{6,0},{7,5},{8,10},{9,15},{10,... | collective-permute-start | bytes 393224 | tf_op jit(solution)/shard_map/ppermute | solution.py:224
  73.5 6.3 %collective-permute-start.13 = (bf16[256,256]{1,0:T(8,128)(2,1)S(1)}, bf16[256,256]{1,0:T(8,128)(2,1)S(1)}, u32[]{:S(2)}, u32[]{:S(2)}) collective-permute-start(bf16[256,256]{1,0:T(8,128)(2,1)S(1)} %fusion), channel_id=1, source_target_pairs={{2,0},{7,1},{4,2},{1,3},{6,4},{3,5},{0,6},{5,7},{10,8},{15,9},{12,... | collective-permute-start | bytes 393224 | tf_op jit(solution)/shard_map/ppermute | solution.py:226
  74.1 5.7 %copy-start.3 = (bf16[256,256]{1,0:T(8,128)(2,1)}, bf16[256,256]{1,0:T(8,128)(2,1)S(1)}, u32[]{:S(2)}) copy-start(bf16[256,256]{1,0:T(8,128)(2,1)S(1)} %collective-permute-done.14.far) | copy-start | bytes 393220
  79.7 0.6 copy-start.4

commit v5 on v4

v5 whole, which is shorter than its diff:
```python
import math

import jax
import jax.numpy as jnp
from jax import lax
from jax.experimental import pallas as pl
from jax.experimental.pallas import tpu as pltpu
from jax.sharding import PartitionSpec as P

HEAD_DIM = 128
HEADS = 6
PAIR_SPAN = 2048
ROWS = 256
BLOCKS = PAIR_SPAN // ROWS
CHIPS = 4
PAIRS = 32
PACKED = 2 * ROWS + 16
NEG = -1e30
INV_ROOT = 1.0 / math.sqrt(HEAD_DIM)
SCALE2 = INV_ROOT * math.log2(math.e)

VMEM = pl.BlockSpec(memory_space=pltpu.VMEM)
MIB = 1024 * 1024


def dot(a, b):
    return jnp.dot(a, b, preferred_element_type=jnp.float32)


def split(value):
    high = value.astype(jnp.bfloat16).astype(jnp.float32)
    middle = (value - high).astype(jnp.bfloat16).astype(jnp.float32)
    return high, middle, value - high - middle


def pack_kernel(keys, values, logprob, docs, response, packed):
    odd = (docs[...] & 1).astype(jnp.float32)
    even = 1.0 - odd
    live = response[...].astype(jnp.float32)
    scored = logprob[...] * live
    first, second, first_live, second_live, count = (
        jnp.sum(term, keepdims=True)
        for term in (scored * even, scored * odd, live * even, live * odd, even)
    )
    terms = (*split(first), *split(second), first_live, second_live, count)
    lane = lax.broadcasted_iota(jnp.int32, (16, HEAD_DIM), 1)
    table = jnp.zeros((16, HEAD_DIM), jnp.float32)
    for place, term in enumerate(terms):
        table = jnp.where(lane == place, term, table)
    packed[:ROWS, :] = keys[...]
    packed[ROWS : 2 * ROWS, :] = values[...]
    packed[2 * ROWS :, :] = table.astype(jnp.bfloat16)


def pack(keys, values, logprob, docs, response):
    wide = (ROWS // 128, 128)
    return pl.pallas_call(
        pack_kernel,
        out_shape=jax.ShapeDtypeStruct((PACKED, HEAD_DIM), jnp.bfloat16),
        in_specs=[VMEM] * 5,
        out_specs=VMEM,
        cost_estimate=pl.CostEstimate(flops=10000, bytes_accessed=MIB // 2, transcendentals=0),
    )(keys, values, logprob.reshape(wide), docs.reshape(wide), response.reshape(wide))


def spans():
    return [(block, slice(block * ROWS, (block + 1) * ROWS)) for block in range(BLOCKS)]


def attend_kernel(
    queries, grads, own, near, far, opposite, own_s, near_s, far_s, opposite_s,
    attention, grad_queries, own_part, near_part, far_part, opposite_part, swap_parts,
    opposite_s_part, margin,
    keys, values, keys_t, values_t, bias, scores, probs, grad_scores, acc_k, acc_v,
):
    place = lax.axis_index("ka")
    core = lax.rem(place, 2)
    chip = lax.rem(place // 2, CHIPS)
    step = 1 - 2 * core
    chips = [chip, chip - step, chip + step, chip + 2, chip, chip + step, chip - step, chip + 2]
    first_row = lax.rem(place, BLOCKS) * ROWS
    blocks = (own, near, far, opposite, own_s, near_s, far_s, opposite_s)
    parts = (
        own_part, near_part, far_part, opposite_part,
        swap_parts.at[0], swap_parts.at[1], swap_parts.at[2], opposite_s_part,
    )
    totals = None
    for block, span in spans():
        key = blocks[block][:ROWS, :]
        value = blocks[block][ROWS : 2 * ROWS, :]
        keys[span, :] = key
        values[span, :] = value
        keys_t[:, span] = key.T
        values_t[:, span] = value.T
        term = blocks[block][2 * ROWS :, :].astype(jnp.float32)
        totals = term if totals is None else totals + term
    totals = totals[:8, :]
    wide = lax.broadcasted_iota(jnp.int32, (8, HEAD_DIM), 1)

    def total_of(low, high):
        chosen = jnp.where((wide >= low) & (wide < high), totals, 0.0)
        return jnp.sum(chosen, axis=1, keepdims=True)

    pair = lax.axis_index("pb") * 2 + place // BLOCKS
    value = total_of(0, 3) / total_of(6, 7) - total_of(3, 6) / total_of(7, 8)
    margin[...] = jnp.where(wide == pair, value, 0.0)
    cut = total_of(8, 9)[:1, :1].astype(jnp.int32)
    row = first_row + lax.broadcasted_iota(jnp.int32, (ROWS, ROWS), 0)
    lane = lax.broadcasted_iota(jnp.int32, (ROWS, ROWS), 1)
    start = jnp.where(row >= cut, cut, 0)
    for block, span in spans():
        side = core if block < CHIPS else 1 - core
        col = lane + (lax.rem(chips[block] + CHIPS, CHIPS) * 2 + side) * ROWS
        bias[:, span] = jnp.where((col >= start) & (col <= row), 0.0, NEG)

    columns = [slice(head * HEAD_DIM, (head + 1) * HEAD_DIM) for head in range(HEADS)]

    def score_step(head, span, top):
        score = dot(queries[:, columns[head]], keys_t[:, span]) + bias[:, span]
        scores[head % 2, :, span] = score
        return score if top is None else jnp.maximum(top, score)

    def prob_step(head, span, row_max, total):
        prob = jnp.exp2(scores[head % 2, :, span] * SCALE2 - row_max)
        probs[head % 2, :, span] = prob.astype(jnp.bfloat16)
        return prob if total is None else total + prob

    def max_of(top):
        return jnp.max(top, axis=1, keepdims=True) * SCALE2

    top = total = None
    for block, span in spans():
        top = score_step(0, span, top)
    row_max = max_of(top)
    for block, span in spans():
        total = prob_step(0, span, row_max, total)
    for head in range(HEADS):
        slot = head % 2
        query = queries[:, columns[head]]
        inv_total = 1.0 / jnp.sum(total, axis=1, keepdims=True)
        output = (dot(probs[slot], values[...]) * inv_total).astype(jnp.bfloat16)
        attention[:, columns[head]] = output
        grad_wide = grads[:, columns[head]].astype(jnp.float32)
        delta = jnp.sum(grad_wide * output.astype(jnp.float32), axis=1, keepdims=True) * inv_total
        grad_scaled = (grad_wide * inv_total).astype(jnp.bfloat16)
        top = total = None
        for block, span in spans():
            grad_prob = dot(grad_scaled, values_t[:, span])
            if head < HEADS - 1:
                top = score_step(head + 1, span, top)
            grad_score = probs[slot, :, span].astype(jnp.float32) * (grad_prob - delta)
            grad_scores[slot, :, span] = grad_score.astype(jnp.bfloat16)
        if head < HEADS - 1:
            row_max = max_of(top)
        query_t = query.T
        grad_t = grad_scaled.T
        for block, span in spans():
            part_k = dot(query_t, grad_scores[slot, :, span])
            part_v = dot(grad_t, probs[slot, :, span])
            if head < HEADS - 1:
                total = prob_step(head + 1, span, row_max, total)
            if head:
                part_k += acc_k[:, span]
                part_v += acc_v[:, span]
            if head < HEADS - 1:
                acc_k[:, span] = part_k
                acc_v[:, span] = part_v
            else:
                parts[block][:, :HEAD_DIM] = (part_k * INV_ROOT).astype(jnp.bfloat16).T
                parts[block][:, HEAD_DIM:] = part_v.astype(jnp.bfloat16).T
        grad_queries[:, columns[head]] = dot(grad_scores[slot], keys[...]) * INV_ROOT


def attend(queries, grads, blocks):
    width = HEADS * HEAD_DIM
    part = jax.ShapeDtypeStruct((ROWS, 2 * HEAD_DIM), jnp.bfloat16)
    return pl.pallas_call(
        attend_kernel,
        out_shape=(
            jax.ShapeDtypeStruct((ROWS, width), jnp.bfloat16),
            jax.ShapeDtypeStruct((ROWS, width), jnp.float32),
            part,
            part,
            part,
            part,
            jax.ShapeDtypeStruct((3, ROWS, 2 * HEAD_DIM), jnp.bfloat16),
            part,
            jax.ShapeDtypeStruct((8, HEAD_DIM), jnp.float32),
        ),
        in_specs=[VMEM] * (2 + BLOCKS),
        out_specs=(VMEM,) * 9,
        scratch_shapes=[
            pltpu.VMEM((PAIR_SPAN, HEAD_DIM), jnp.bfloat16),
            pltpu.VMEM((PAIR_SPAN, HEAD_DIM), jnp.bfloat16),
            pltpu.VMEM((HEAD_DIM, PAIR_SPAN), jnp.bfloat16),
            pltpu.VMEM((HEAD_DIM, PAIR_SPAN), jnp.bfloat16),
            pltpu.VMEM((ROWS, PAIR_SPAN), jnp.float32),
            pltpu.VMEM((2, ROWS, PAIR_SPAN), jnp.float32),
            pltpu.VMEM((2, ROWS, PAIR_SPAN), jnp.bfloat16),
            pltpu.VMEM((2, ROWS, PAIR_SPAN), jnp.bfloat16),
            pltpu.VMEM((HEAD_DIM, PAIR_SPAN), jnp.float32),
            pltpu.VMEM((HEAD_DIM, PAIR_SPAN), jnp.float32),
        ],
        compiler_params=pltpu.CompilerParams(vmem_limit_bytes=32 * MIB),
        cost_estimate=pl.CostEstimate(
            flops=12 * HEADS * ROWS * PAIR_SPAN * HEAD_DIM,
            bytes_accessed=4 * MIB,
            transcendentals=HEADS * ROWS * PAIR_SPAN,
        ),
    )(queries, grads, *blocks)


def collect_kernel(own, swapped, near, far, grad_keys, grad_values):
    total = own[...].astype(jnp.float32) + swapped[0].astype(jnp.float32)
    total += near[...].astype(jnp.float32) + far[...].astype(jnp.float32)
    grad_keys[...] = total[:, :HEAD_DIM]
    grad_values[...] = total[:, HEAD_DIM:]


def collect(own, swapped, near, far):
    shape = jax.ShapeDtypeStruct((ROWS, HEAD_DIM), jnp.float32)
    return pl.pallas_call(
        collect_kernel,
        out_shape=(shape, shape),
        in_specs=[VMEM] * 4,
        out_specs=(VMEM, VMEM),
        cost_estimate=pl.CostEstimate(flops=MIB, bytes_accessed=MIB, transcendentals=0),
    )(own, swapped, near, far)


def at(half, chip, core):
    return half * 8 + (chip % CHIPS) * 2 + core


def per_device(queries, key_heads, value_heads, grad_output, token_logprob, doc_ids, response):
    spots = [(half, chip, core) for half in (0, 1) for chip in range(CHIPS) for core in (0, 1)]
    ahead = [(at(h, x, k), at(h, x + 1 - 2 * k, k)) for h, x, k in spots]
    cross = [(at(h, x, k), at(h, x + 1 - 2 * k, 1 - k)) for h, x, k in spots]
    back = [(there, here) for here, there in ahead]
    cross_back = [(there, here) for here, there in cross]
    swap = [(place, place ^ 1) for place in range(16)]

    def send(block, route):
        return lax.ppermute(block, "ka", route)

    own = pack(key_heads, value_heads, token_logprob, doc_ids, response)
    near = send(own, ahead)
    far = send(own, back)
    own_s = send(own, swap)
    opposite = send(near, ahead)
    opposite_s = send(near, cross)
    near_s = send(near, swap)
    far_s = send(far, swap)

    blocks = (own, near, far, opposite, own_s, near_s, far_s, opposite_s)
    attention, grad_queries, own_p, near_p, far_p, opposite_p, swap_p, opposite_s_p, margin = (
        attend(queries, grad_output, blocks)
    )
    passed = send(opposite_p, back)
    passed_s = send(opposite_s_p, cross_back)
    swapped = send(swap_p, swap)
    whole = range(256)
    margin = sum(
        (lax.ppermute(margin, ("pb", "ka"), [(p, p ^ bits) for p in whole]) for bits in (8, 16, 24)),
        margin,
    )
    wide = jnp.float32
    near_sum = (near_p.astype(wide) + swapped[1] + passed + passed_s).astype(jnp.bfloat16)
    far_sum = far_p + swapped[2]
    near_part = send(near_sum, back)
    far_part = send(far_sum, ahead)
    margin = sum(
        (lax.ppermute(margin, "pb", [(p, p ^ bits) for p in range(16)]) for bits in range(2, 16, 2)),
        margin,
    )
    grad_keys, grad_values = collect(own_p, swapped, near_part, far_part)
    return (attention, grad_queries, grad_keys, grad_values, margin[0, :PAIRS])


def solution(mesh):
    rows = P(("pb", "ka"), None)
    line = P(("pb", "ka"))
    return jax.shard_map(
        per_device,
        mesh=mesh,
        in_specs=(rows, rows, rows, rows, line, line, line),
        out_specs=(rows, rows, rows, rows, P()),
        check_vma=False,
    )
```

time: 82.4 us -> 74.4 us (0.903)
  the two profiles are of different devices: /device:TPU:6 before, /device:TPU:8 now
where the time goes in v5:
time: 74.4 us; the launch traced here: 74.1 us
  starting transfers between devices  28.2 us (38%)
  waiting for transfers between devices  25.1 us (34%)
  Pallas kernels  15.9 us (21%)
  local copies, waits for them, and re-layouts  4.06 us (5%)
    ppermute x12, waiting for transfers between devices, send(): return lax.ppermute(block, 'ka', route)  18.2 us
    ppermute x7, starting transfers between devices, per_device(): lax.ppermute(margin, 'pb', [(p, p ^ bits) for p in range(16)])  16.6 us
    pallas_call x1, Pallas kernels, attend(): pl.pallas_call(attend_kernel, out_shape=(jax.ShapeDtypeStruct((ROWS, widt...  12.3 us
    ppermute x12, starting transfers between devices, send(): return lax.ppermute(block, 'ka', route)  8.13 us
    ppermute x3, waiting for transfers between devices, per_device(): lax.ppermute(margin, ('pb', 'ka'), [(p, p ^ bits) for p in whole])  5.08 us
    unnamed x14, local copies, waits for them, and re-layouts  3.55 us
    ppermute x3, starting transfers between devices, per_device(): lax.ppermute(margin, ('pb', 'ka'), [(p, p ^ bits) for p in whole])  3.49 us
    pallas_call x1, Pallas kernels, collect(): pl.pallas_call(collect_kernel, out_shape=(shape, shape), in_specs=[VMEM]...  1.86 us
  transfers between devices with their start and end apart: 22, of which 11 were waited for; matrix products, arithmetic and copies ran while one was open for 1% of the time, Pallas kernels for 0%

profile of v5, /device:TPU:8, one launch (start us, length us, event | category | flops | bytes accessed | tf_op | source)
XLA Modules:
  0.0 74.1 jit_solution(2738711283946557341)
XLA Ops:
  0.6 1.7 %shard_map.110.own = bf16[528,128]{1,0:T(8,128)(2,1)} custom-call(bf16[256,128]{1,0:T(8,128)(2,1)} %keys.1, bf16[256,128]{1,0:T(8,128)(2,1)} %values.1, f32[2,128]{1,0:T(2,128)} %bitcast.14, s32[2,128]{1,0:T(2,128)} %bitcast.15, s32[2,128]{1,0:T(2,128)} %bitcast.16), custom_call_target="tpu_custom_call" | custom-call | flops 10000 | bytes 524288 | tf_op jit(solution)/shard_map/pallas_call | solution.py:57
  2.3 2.8 %collective-permute-start.1 = (bf16[528,128]{1,0:T(8,128)(2,1)}, bf16[528,128]{1,0:T(8,128)(2,1)S(1)}, u32[]{:S(2)}, u32[]{:S(2)}) collective-permute-start(bf16[528,128]{1,0:T(8,128)(2,1)} %shard_map.110.own), channel_id=1, source_target_pairs={{2,0},{7,1},{4,2},{1,3},{6,4},{3,5},{0,6},{5,7},{10,8},{15,9},{12,... | collective-permute-start | bytes 405512 | tf_op jit(solution)/shard_map/ppermute | solution.py:244
  5.1 0.0 collective-permute-start
  5.1 0.0 collective-permute-start.3
  5.1 3.8 %collective-permute-done.1.far = bf16[528,128]{1,0:T(8,128)(2,1)S(1)} collective-permute-done((bf16[528,128]{1,0:T(8,128)(2,1)}, bf16[528,128]{1,0:T(8,128)(2,1)S(1)}, u32[]{:S(2)}, u32[]{:S(2)}) %collective-permute-start.1) | collective-permute-done | bytes 135200 | tf_op jit(solution)/shard_map/ppermute | solution.py:244
  8.9 0.0 collective-permute-start.5
  8.9 2.6 %collective-permute-done.near = bf16[528,128]{1,0:T(8,128)(2,1)S(1)} collective-permute-done((bf16[528,128]{1,0:T(8,128)(2,1)}, bf16[528,128]{1,0:T(8,128)(2,1)S(1)}, u32[]{:S(2)}, u32[]{:S(2)}) %collective-permute-start) | collective-permute-done | bytes 135200 | tf_op jit(solution)/shard_map/ppermute | solution.py:244
  11.5 0.0 collective-permute-start.6
  11.5 0.6 collective-permute-start.4
  12.1 1.5 %collective-permute-start.2 = (bf16[528,128]{1,0:T(8,128)(2,1)S(1)}, bf16[528,128]{1,0:T(8,128)(2,1)S(1)}, u32[]{:S(2)}, u32[]{:S(2)}) collective-permute-start(bf16[528,128]{1,0:T(8,128)(2,1)S(1)} %collective-permute-done.near), channel_id=1, source_target_pairs={{0,2},{1,7},{2,4},{3,1},{4,6},{5,3},{6,0},{7,5},{8,10},{9,15},{10,... | collective-permute-start | bytes 405512 | tf_op jit(solution)/shard_map/ppermute | solution.py:244
  13.6 0.0 collective-permute-done.3.own_s
  13.7 2.3 %collective-permute-done.6.opposite_s = bf16[528,128]{1,0:T(8,128)(2,1)S(1)} collective-permute-done((bf16[528,128]{1,0:T(8,128)(2,1)S(1)}, bf16[528,128]{1,0:T(8,128)(2,1)S(1)}, u32[]{:S(2)}, u32[]{:S(2)}) %collective-permute-start.6) | collective-permute-done | bytes 135200 | tf_op jit(solution)/shard_map/ppermute | solution.py:244
  15.9 0.0 collective-permute-done.4.near_s
  15.9 2.4 %collective-permute-done.2.opposite = bf16[528,128]{1,0:T(8,128)(2,1)S(1)} collective-permute-done((bf16[528,128]{1,0:T(8,128)(2,1)S(1)}, bf16[528,128]{1,0:T(8,128)(2,1)S(1)}, u32[]{:S(2)}, u32[]{:S(2)}) %collective-permute-start.2) | collective-permute-done | bytes 135200 | tf_op jit(solution)/shard_map/ppermute | solution.py:244
  18.4 0.9 %copy-done = bf16[528,128]{1,0:T(8,128)(2,1)S(1)} copy-done((bf16[528,128]{1,0:T(8,128)(2,1)S(1)}, bf16[528,128]{1,0:T(8,128)(2,1)}, u32[]{:S(2)}) %copy-start) | copy-done | bytes 135192
  19.3 1.0 %copy-done.2 = bf16[256,768]{1,0:T(8,128)(2,1)S(1)} copy-done((bf16[256,768]{1,0:T(8,128)(2,1)S(1)}, bf16[256,768]{1,0:T(8,128)(2,1)}, u32[]{:S(2)}) %copy-start.2) | copy-done | bytes 393240
  20.3 1.0 %copy-done.3 = bf16[256,768]{1,0:T(8,128)(2,1)S(1)} copy-done((bf16[256,768]{1,0:T(8,128)(2,1)S(1)}, bf16[256,768]{1,0:T(8,128)(2,1)}, u32[]{:S(2)}) %copy-start.3) | copy-done | bytes 393240
  21.3 12.3 %shard_map.111 = (bf16[256,768]{1,0:T(8,128)(2,1)}, f32[256,768]{1,0:T(8,128)}, bf16[256,256]{1,0:T(8,128)(2,1)S(1)}, bf16[256,256]{1,0:T(8,128)(2,1)S(1)}, bf16...) custom-call(bf16[256,768]{1,0:T(8,128)(2,1)S(1)} %copy-done.2, ...), custom_call_target="tpu_custom_call" | custom-call | flops 4831838208 | bytes 4194304 | tf_op jit(solution)/shard_map/pallas_call | solution.py:177
  33.6 1.6 %collective-permute-start.14 = (f32[8,128]{1,0:T(8,128)S(1)}, f32[8,128]{1,0:T(8,128)S(1)}, u32[]{:S(2)}, u32[]{:S(2)}) collective-permute-start(f32[8,128]{1,0:T(8,128)S(1)} %get-tuple-element.26), channel_id=1, source_target_pairs={{0,24},{1,25},{2,26},{3,27},{4,28},{5,29},{6,30},{7,31},{8,16},{9,... | collective-permute-start | bytes 12296 | tf_op jit(solution)/shard_map/ppermute | solution.py:264
  35.2 1.9 %collective-permute-start.13 = (f32[8,128]{1,0:T(8,128)S(1)}, f32[8,128]{1,0:T(8,128)S(1)}, u32[]{:S(2)}, u32[]{:S(2)}) collective-permute-start(f32[8,128]{1,0:T(8,128)S(1)} %get-tuple-element.26), channel_id=1, source_target_pairs={{0,16},{1,17},{2,18},{3,19},{4,20},{5,21},{6,22},{7,23},{8,24},{9,... | collective-permute-start | bytes 12296 | tf_op jit(solution)/shard_map/ppermute | solution.py:264
  37.1 0.0 collective-permute-start.12
  37.1 0.1 collective-permute-done.14
  37.2 1.6 %collective-permute-done.13 = f32[8,128]{1,0:T(8,128)S(1)} collective-permute-done((f32[8,128]{1,0:T(8,128)S(1)}, f32[8,128]{1,0:T(8,128)S(1)}, u32[]{:S(2)}, u32[]{:S(2)}) %collective-permute-start.13) | collective-permute-done | bytes 4128 | tf_op jit(solution)/shard_map/ppermute | solution.py:264
  38.8 3.4 %collective-permute-done.12 = f32[8,128]{1,0:T(8,128)S(1)} collective-permute-done((f32[8,128]{1,0:T(8,128)S(1)}, f32[8,128]{1,0:T(8,128)S(1)}, u32[]{:S(2)}, u32[]{:S(2)}) %collective-permute-start.12) | collective-permute-done | bytes 4128 | tf_op jit(solution)/shard_map/ppermute | solution.py:264
  42.2 5.9 %collective-permute-start.21 = (f32[8,128]{1,0:T(8,128)S(1)}, f32[8,128]{1,0:T(8,128)S(1)}, u32[]{:S(2)}, u32[]{:S(2)}) collective-permute-start(f32[8,128]{1,0:T(8,128)S(1)} %add_add_fusion.1), channel_id=1, source_target_pairs={{0,224},{16,240},{32,192},{48,208},{64,160},{80,176},{96,128},{112... | collective-permute-start | bytes 12296 | tf_op jit(solution)/shard_map/ppermute | solution.py:273
  48.0 0.5 collective-permute-start.20
  48.6 4.0 %collective-permute-start.19 = (f32[8,128]{1,0:T(8,128)S(1)}, f32[8,128]{1,0:T(8,128)S(1)}, u32[]{:S(2)}, u32[]{:S(2)}) collective-permute-start(f32[8,128]{1,0:T(8,128)S(1)} %add_add_fusion.1), channel_id=1, source_target_pairs={{0,160},{16,176},{32,128},{48,144},{64,224},{80,240},{96,192},{112... | collective-permute-start | bytes 12296 | tf_op jit(solution)/shard_map/ppermute | solution.py:273
  52.6 1.8 %collective-permute-start.18 = (f32[8,128]{1,0:T(8,128)S(1)}, f32[8,128]{1,0:T(8,128)S(1)}, u32[]{:S(2)}, u32[]{:S(2)}) collective-permute-start(f32[8,128]{1,0:T(8,128)S(1)} %add_add_fusion.1), channel_id=1, source_target_pairs={{0,128},{16,144},{32,160},{48,176},{64,192},{80,208},{96,224},{112... | collective-permute-start | bytes 12296 | tf_op jit(solution)/shard_map/ppermute | solution.py:273
  54.4 0.0 collective-permute-done.21
  54.4 1.9 %collective-permute-start.17 = (f32[8,128]{1,0:T(8,128)S(1)}, f32[8,128]{1,0:T(8,128)S(1)}, u32[]{:S(2)}, u32[]{:S(2)}) collective-permute-start(f32[8,128]{1,0:T(8,128)S(1)} %add_add_fusion.1), channel_id=1, source_target_pairs={{0,96},{16,112},{32,64},{48,80},{64,32},{80,48},{96,0},{112,16},{1... | collective-permute-start | bytes 12296 | tf_op jit(solution)/shard_map/ppermute | solution.py:273
  56.3 0.0 collective-permute-done.20
  56.3 0.2 collective-permute-start.16
  56.5 2.3 %collective-permute-start.15 = (f32[8,128]{1,0:T(8,128)S(1)}, f32[8,128]{1,0:T(8,128)S(1)}, u32[]{:S(2)}, u32[]{:S(2)}) collective-permute-start(f32[8,128]{1,0:T(8,128)S(1)} %add_add_fusion.1), channel_id=1, source_target_pairs={{0,32},{16,48},{32,0},{48,16},{64,96},{80,112},{96,64},{112,80},{1... | collective-permute-start | bytes 12296 | tf_op jit(solution)/shard_map/ppermute | solution.py:273
  58.8 1.4 %collective-permute-done.18 = f32[8,128]{1,0:T(8,128)S(1)} collective-permute-done((f32[8,128]{1,0:T(8,128)S(1)}, f32[8,128]{1,0:T(8,128)S(1)}, u32[]{:S(2)}, u32[]{:S(2)}) %collective-permute-start.18) | collective-permute-done | bytes 4128 | tf_op jit(solution)/shard_map/ppermute | solution.py:273
  60.2 0.2 collective-permute-start.8
  60.4 0.5 collective-permute-done.16
  60.8 0.0 collective-permute-done.15
  60.9 0.0 collective-permute-done.7.swapped
  60.9 1.5 %collective-permute-start.11 = (bf16[256,256]{1,0:T(8,128)(2,1)S(1)}, bf16[256,256]{1,0:T(8,128)(2,1)S(1)}, u32[]{:S(2)}, u32[]{:S(2)}) collective-permute-start(bf16[256,256]{1,0:T(8,128)(2,1)S(1)} %fusion.3), channel_id=1, source_target_pairs={{0,2},{1,7},{2,4},{3,1},{4,6},{5,3},{6,0},{7,5},{8,10},{9,15},{10,... | collective-permute-start | bytes 393224 | tf_op jit(solution)/shard_map/ppermute | solution.py:244
  62.4 4.1 %collective-permute-done.8 = bf16[256,256]{1,0:T(8,128)(2,1)S(1)} collective-permute-done((bf16[256,256]{1,0:T(8,128)(2,1)S(1)}, bf16[256,256]{1,0:T(8,128)(2,1)S(1)}, u32[]{:S(2)}, u32[]{:S(2)}) %collective-permute-start.8) | collective-permute-done | bytes 131104 | tf_op jit(solution)/shard_map/ppermute | solution.py:244
  66.5 0.0 collective-permute-done.9
  66.5 0.1 fusion.2
  66.5 1.6 %collective-permute-start.10 = (bf16[256,256]{1,0:T(8,128)(2,1)S(1)}, bf16[256,256]{1,0:T(8,128)(2,1)S(1)}, u32[]{:S(2)}, u32[]{:S(2)}) collective-permute-start(bf16[256,256]{1,0:T(8,128)(2,1)S(1)} %fusion.2), channel_id=1, source_target_pairs={{2,0},{7,1},{4,2},{1,3},{6,4},{3,5},{0,6},{5,7},{10,8},{15,9},{12,... | collective-permute-start | bytes 393224 | tf_op jit(solution)/shard_map/ppermute | solution.py:244
  68.1 0.5 slice_bitcast_fusion.2
  68.6 0.0 collective-permute-done.11.far
  68.6 3.0 %collective-permute-done.10.near = bf16[256,256]{1,0:T(8,128)(2,1)S(1)} collective-permute-done((bf16[256,256]{1,0:T(8,128)(2,1)S(1)}, bf16[256,256]{1,0:T(8,128)(2,1)S(1)}, u32[]{:S(2)}, u32[]{:S(2)}) %collective-permute-start.10) | collective-permute-done | bytes 131104 | tf_op jit(solution)/shard_map/ppermute | solution.py:244
  71.6 0.6 copy-done.6
  72.2 1.9 %shard_map.112 = (f32[256,128]{1,0:T(8,128)}, f32[256,128]{1,0:T(8,128)}) custom-call(bf16[256,256]{1,0:T(8,128)(2,1)} %copy-done.1, bf16[3,256,256]{2,1,0:T(8,128)(2,1)} %copy-done.4, bf16[256,256]{1,0:T(8,128)(2,1)} %copy-done.6, bf16[256,256]{1,0:T(8,128)(2,1)} %copy-done.5), custom_call_target="tpu_custom_call" | custom-call | flops 1048576 | bytes 1048576 | tf_op jit(solution)/shard_map/pallas_call | solution.py:222
  (18 shorter events, 0.1 us)
Async XLA Ops:
  2.3 6.6 %collective-permute-start.1 = (bf16[528,128]{1,0:T(8,128)(2,1)}, bf16[528,128]{1,0:T(8,128)(2,1)S(1)}, u32[]{:S(2)}, u32[]{:S(2)}) collective-permute-start(bf16[528,128]{1,0:T(8,128)(2,1)} %shard_map.110.own), channel_id=1, source_target_pairs={{2,0},{7,1},{4,2},{1,3},{6,4},{3,5},{0,6},{5,7},{10,8},{15,9},{12,... | collective-permute-start | bytes 405512 | tf_op jit(solution)/shard_map/ppermute | solution.py:244
  5.1 6.4 %collective-permute-start = (bf16[528,128]{1,0:T(8,128)(2,1)}, bf16[528,128]{1,0:T(8,128)(2,1)S(1)}, u32[]{:S(2)}, u32[]{:S(2)}) collective-permute-start(bf16[528,128]{1,0:T(8,128)(2,1)} %shard_map.110.own), channel_id=1, source_target_pairs={{0,2},{1,7},{2,4},{3,1},{4,6},{5,3},{6,0},{7,5},{8,10},{9,15},{10,... | collective-permute-start | bytes 405512 | tf_op jit(solution)/shard_map/ppermute | solution.py:244
  5.1 8.6 %collective-permute-start.3 = (bf16[528,128]{1,0:T(8,128)(2,1)}, bf16[528,128]{1,0:T(8,128)(2,1)S(1)}, u32[]{:S(2)}, u32[]{:S(2)}) collective-permute-start(bf16[528,128]{1,0:T(8,128)(2,1)} %shard_map.110.own), channel_id=1, source_target_pairs={{0,1},{1,0},{2,3},{3,2},{4,5},{5,4},{6,7},{7,6},{8,9},{9,8},{10,11... | collective-permute-start | bytes 405512 | tf_op jit(solution)/shard_map/ppermute | solution.py:244
  8.9 4.7 %collective-permute-start.5 = (bf16[528,128]{1,0:T(8,128)(2,1)S(1)}, bf16[528,128]{1,0:T(8,128)(2,1)S(1)}, u32[]{:S(2)}, u32[]{:S(2)}) collective-permute-start(bf16[528,128]{1,0:T(8,128)(2,1)S(1)} %collective-permute-done.1.far), channel_id=1, source_target_pairs={{0,1},{1,0},{2,3},{3,2},{4,5},{5,4},{6,7},{7,6},{8,9},{9,8},{10,11... | collective-permute-start | bytes 405512 | tf_op jit(solution)/shard_map/ppermute | solution.py:244
  11.5 4.4 %collective-permute-start.6 = (bf16[528,128]{1,0:T(8,128)(2,1)S(1)}, bf16[528,128]{1,0:T(8,128)(2,1)S(1)}, u32[]{:S(2)}, u32[]{:S(2)}) collective-permute-start(bf16[528,128]{1,0:T(8,128)(2,1)S(1)} %collective-permute-done.near), channel_id=1, source_target_pairs={{0,3},{1,6},{2,5},{3,0},{4,7},{5,2},{6,1},{7,4},{8,11},{9,14},{10,... | collective-permute-start | bytes 405512 | tf_op jit(solution)/shard_map/ppermute | solution.py:244
  11.5 4.4 %collective-permute-start.4 = (bf16[528,128]{1,0:T(8,128)(2,1)S(1)}, bf16[528,128]{1,0:T(8,128)(2,1)S(1)}, u32[]{:S(2)}, u32[]{:S(2)}) collective-permute-start(bf16[528,128]{1,0:T(8,128)(2,1)S(1)} %collective-permute-done.near), channel_id=1, source_target_pairs={{0,1},{1,0},{2,3},{3,2},{4,5},{5,4},{6,7},{7,6},{8,9},{9,8},{10,11... | collective-permute-start | bytes 405512 | tf_op jit(solution)/shard_map/ppermute | solution.py:244
  12.1 6.2 %collective-permute-start.2 = (bf16[528,128]{1,0:T(8,128)(2,1)S(1)}, bf16[528,128]{1,0:T(8,128)(2,1)S(1)}, u32[]{:S(2)}, u32[]{:S(2)}) collective-permute-start(bf16[528,128]{1,0:T(8,128)(2,1)S(1)} %collective-permute-done.near), channel_id=1, source_target_pairs={{0,2},{1,7},{2,4},{3,1},{4,6},{5,3},{6,0},{7,5},{8,10},{9,15},{10,... | collective-permute-start | bytes 405512 | tf_op jit(solution)/shard_map/ppermute | solution.py:244
  18.4 0.9 %copy-start = (bf16[528,128]{1,0:T(8,128)(2,1)S(1)}, bf16[528,128]{1,0:T(8,128)(2,1)}, u32[]{:S(2)}) copy-start(bf16[528,128]{1,0:T(8,128)(2,1)} %shard_map.110.own) | copy-start | bytes 405508
  19.3 1.0 %copy-start.2 = (bf16[256,768]{1,0:T(8,128)(2,1)S(1)}, bf16[256,768]{1,0:T(8,128)(2,1)}, u32[]{:S(2)}) copy-start(bf16[256,768]{1,0:T(8,128)(2,1)} %queries.1) | copy-start | bytes 1179652
  20.3 1.0 %copy-start.3 = (bf16[256,768]{1,0:T(8,128)(2,1)S(1)}, bf16[256,768]{1,0:T(8,128)(2,1)}, u32[]{:S(2)}) copy-start(bf16[256,768]{1,0:T(8,128)(2,1)} %grads.1) | copy-start | bytes 1179652
  33.6 27.3 %copy-start.1 = (bf16[256,256]{1,0:T(8,128)(2,1)}, bf16[256,256]{1,0:T(8,128)(2,1)S(1)}, u32[]{:S(2)}) copy-start(bf16[256,256]{1,0:T(8,128)(2,1)S(1)} %get-tuple-element.18.own) | copy-start | bytes 393220
  33.6 3.6 %collective-permute-start.14 = (f32[8,128]{1,0:T(8,128)S(1)}, f32[8,128]{1,0:T(8,128)S(1)}, u32[]{:S(2)}, u32[]{:S(2)}) collective-permute-start(f32[8,128]{1,0:T(8,128)S(1)} %get-tuple-element.26), channel_id=1, source_target_pairs={{0,24},{1,25},{2,26},{3,27},{4,28},{5,29},{6,30},{7,31},{8,16},{9,... | collective-permute-start | bytes 12296 | tf_op jit(solution)/shard_map/ppermute | solution.py:264
  35.2 3.6 %collective-permute-start.13 = (f32[8,128]{1,0:T(8,128)S(1)}, f32[8,128]{1,0:T(8,128)S(1)}, u32[]{:S(2)}, u32[]{:S(2)}) collective-permute-start(f32[8,128]{1,0:T(8,128)S(1)} %get-tuple-element.26), channel_id=1, source_target_pairs={{0,16},{1,17},{2,18},{3,19},{4,20},{5,21},{6,22},{7,23},{8,24},{9,... | collective-permute-start | bytes 12296 | tf_op jit(solution)/shard_map/ppermute | solution.py:264
  37.1 5.1 %collective-permute-start.12 = (f32[8,128]{1,0:T(8,128)S(1)}, f32[8,128]{1,0:T(8,128)S(1)}, u32[]{:S(2)}, u32[]{:S(2)}) collective-permute-start(f32[8,128]{1,0:T(8,128)S(1)} %get-tuple-element.26), channel_id=1, source_target_pairs={{0,8},{1,9},{2,10},{3,11},{4,12},{5,13},{6,14},{7,15},{8,0},{9,1},... | collective-permute-start | bytes 12296 | tf_op jit(solution)/shard_map/ppermute | solution.py:264
  37.1 23.8 %collective-permute-start.7 = (bf16[3,256,256]{2,1,0:T(8,128)(2,1)S(1)}, bf16[3,256,256]{2,1,0:T(8,128)(2,1)S(1)}, u32[]{:S(2)}, u32[]{:S(2)}) collective-permute-start(bf16[3,256,256]{2,1,0:T(8,128)(2,1)S(1)} %get-tuple-element.19), channel_id=1, source_target_pairs={{0,1},{1,0},{2,3},{3,2},{4,5},{5,4},{6,7},{7,6},{8,9},{9,8},{10,11... | collective-permute-start | bytes 1179656 | tf_op jit(solution)/shard_map/ppermute | solution.py:244
  42.2 12.2 %collective-permute-start.21 = (f32[8,128]{1,0:T(8,128)S(1)}, f32[8,128]{1,0:T(8,128)S(1)}, u32[]{:S(2)}, u32[]{:S(2)}) collective-permute-start(f32[8,128]{1,0:T(8,128)S(1)} %add_add_fusion.1), channel_id=1, source_target_pairs={{0,224},{16,240},{32,192},{48,208},{64,160},{80,176},{96,128},{112... | collective-permute-start | bytes 12296 | tf_op jit(solution)/shard_map/ppermute | solution.py:273
  48.0 8.3 %collective-permute-start.20 = (f32[8,128]{1,0:T(8,128)S(1)}, f32[8,128]{1,0:T(8,128)S(1)}, u32[]{:S(2)}, u32[]{:S(2)}) collective-permute-start(f32[8,128]{1,0:T(8,128)S(1)} %add_add_fusion.1), channel_id=1, source_target_pairs={{0,192},{16,208},{32,224},{48,240},{64,128},{80,144},{96,160},{112... | collective-permute-start | bytes 12296 | tf_op jit(solution)/shard_map/ppermute | solution.py:273
  48.6 8.0 %collective-permute-start.19 = (f32[8,128]{1,0:T(8,128)S(1)}, f32[8,128]{1,0:T(8,128)S(1)}, u32[]{:S(2)}, u32[]{:S(2)}) collective-permute-start(f32[8,128]{1,0:T(8,128)S(1)} %add_add_fusion.1), channel_id=1, source_target_pairs={{0,160},{16,176},{32,128},{48,144},{64,224},{80,240},{96,192},{112... | collective-permute-start | bytes 12296 | tf_op jit(solution)/shard_map/ppermute | solution.py:273
  52.6 7.6 %collective-permute-start.18 = (f32[8,128]{1,0:T(8,128)S(1)}, f32[8,128]{1,0:T(8,128)S(1)}, u32[]{:S(2)}, u32[]{:S(2)}) collective-permute-start(f32[8,128]{1,0:T(8,128)S(1)} %add_add_fusion.1), channel_id=1, source_target_pairs={{0,128},{16,144},{32,160},{48,176},{64,192},{80,208},{96,224},{112... | collective-permute-start | bytes 12296 | tf_op jit(solution)/shard_map/ppermute | solution.py:273
  54.4 5.9 %collective-permute-start.17 = (f32[8,128]{1,0:T(8,128)S(1)}, f32[8,128]{1,0:T(8,128)S(1)}, u32[]{:S(2)}, u32[]{:S(2)}) collective-permute-start(f32[8,128]{1,0:T(8,128)S(1)} %add_add_fusion.1), channel_id=1, source_target_pairs={{0,96},{16,112},{32,64},{48,80},{64,32},{80,48},{96,0},{112,16},{1... | collective-permute-start | bytes 12296 | tf_op jit(solution)/shard_map/ppermute | solution.py:273
  56.3 4.5 %collective-permute-start.16 = (f32[8,128]{1,0:T(8,128)S(1)}, f32[8,128]{1,0:T(8,128)S(1)}, u32[]{:S(2)}, u32[]{:S(2)}) collective-permute-start(f32[8,128]{1,0:T(8,128)S(1)} %add_add_fusion.1), channel_id=1, source_target_pairs={{0,64},{16,80},{32,96},{48,112},{64,0},{80,16},{96,32},{112,48},{1... | collective-permute-start | bytes 12296 | tf_op jit(solution)/shard_map/ppermute | solution.py:273
  56.5 4.3 %collective-permute-start.15 = (f32[8,128]{1,0:T(8,128)S(1)}, f32[8,128]{1,0:T(8,128)S(1)}, u32[]{:S(2)}, u32[]{:S(2)}) collective-permute-start(f32[8,128]{1,0:T(8,128)S(1)} %add_add_fusion.1), channel_id=1, source_target_pairs={{0,32},{16,48},{32,0},{48,16},{64,96},{80,112},{96,64},{112,80},{1... | collective-permute-start | bytes 12296 | tf_op jit(solution)/shard_map/ppermute | solution.py:273
  60.2 6.3 %collective-permute-start.8 = (bf16[256,256]{1,0:T(8,128)(2,1)S(1)}, bf16[256,256]{1,0:T(8,128)(2,1)S(1)}, u32[]{:S(2)}, u32[]{:S(2)}) collective-permute-start(bf16[256,256]{1,0:T(8,128)(2,1)S(1)} %get-tuple-element.21), channel_id=1, source_target_pairs={{2,0},{7,1},{4,2},{1,3},{6,4},{3,5},{0,6},{5,7},{10,8},{15,9},{12,... | collective-permute-start | bytes 393224 | tf_op jit(solution)/shard_map/ppermute | solution.py:244
  60.4 6.1 %collective-permute-start.9 = (bf16[256,256]{1,0:T(8,128)(2,1)S(1)}, bf16[256,256]{1,0:T(8,128)(2,1)S(1)}, u32[]{:S(2)}, u32[]{:S(2)}) collective-permute-start(bf16[256,256]{1,0:T(8,128)(2,1)S(1)} %get-tuple-element.22), channel_id=1, source_target_pairs={{3,0},{6,1},{5,2},{0,3},{7,4},{2,5},{1,6},{4,7},{11,8},{14,9},{13,... | collective-permute-start | bytes 393224 | tf_op jit(solution)/shard_map/ppermute | solution.py:244
  60.9 5.7 %copy-start.4 = (bf16[3,256,256]{2,1,0:T(8,128)(2,1)}, bf16[3,256,256]{2,1,0:T(8,128)(2,1)S(1)}, u32[]{:S(2)}) copy-start(bf16[3,256,256]{2,1,0:T(8,128)(2,1)S(1)} %collective-permute-done.7.swapped) | copy-start | bytes 1179652
  60.9 7.7 %collective-permute-start.11 = (bf16[256,256]{1,0:T(8,128)(2,1)S(1)}, bf16[256,256]{1,0:T(8,128)(2,1)S(1)}, u32[]{:S(2)}, u32[]{:S(2)}) collective-permute-start(bf16[256,256]{1,0:T(8,128)(2,1)S(1)} %fusion.3), channel_id=1, source_target_pairs={{0,2},{1,7},{2,4},{3,1},{4,6},{5,3},{6,0},{7,5},{8,10},{9,15},{10,... | collective-permute-start | bytes 393224 | tf_op jit(solution)/shard_map/ppermute | solution.py:244
  66.5 5.0 %collective-permute-start.10 = (bf16[256,256]{1,0:T(8,128)(2,1)S(1)}, bf16[256,256]{1,0:T(8,128)(2,1)S(1)}, u32[]{:S(2)}, u32[]{:S(2)}) collective-permute-start(bf16[256,256]{1,0:T(8,128)(2,1)S(1)} %fusion.2), channel_id=1, source_target_pairs={{2,0},{7,1},{4,2},{1,3},{6,4},{3,5},{0,6},{5,7},{10,8},{15,9},{12,... | collective-permute-start | bytes 393224 | tf_op jit(solution)/shard_map/ppermute | solution.py:244
  68.6 3.0 %copy-start.5 = (bf16[256,256]{1,0:T(8,128)(2,1)}, bf16[256,256]{1,0:T(8,128)(2,1)S(1)}, u32[]{:S(2)}) copy-start(bf16[256,256]{1,0:T(8,128)(2,1)S(1)} %collective-permute-done.11.far) | copy-start | bytes 393220
  71.6 0.6 copy-start.6

commit v6 on v5

--- a/solution.py
+++ b/solution.py
@@ -20,6 +20,7 @@
 SCALE2 = INV_ROOT * math.log2(math.e)
 
 VMEM = pl.BlockSpec(memory_space=pltpu.VMEM)
+HBM = pl.BlockSpec(memory_space=pltpu.HBM)
 MIB = 1024 * 1024
 
 
@@ -68,11 +69,19 @@
 
 
 def attend_kernel(
-    queries, grads, own, near, far, opposite, own_s, near_s, far_s, opposite_s,
+    queries_hbm, grads_hbm, own_hbm, near, far, opposite, own_s, near_s, far_s, opposite_s,
     attention, grad_queries, own_part, near_part, far_part, opposite_part, swap_parts,
-    opposite_s_part, margin,
-    keys, values, keys_t, values_t, bias, scores, probs, grad_scores, acc_k, acc_v,
+    opposite_s_part,
+    queries, grads, own, arrived, keys, values, keys_t, values_t, bias, scores, probs, grad_scores, acc_k, acc_v,
 ):
+    fetches = [
+        pltpu.make_async_copy(source, target, arrived.at[number])
+        for number, (source, target) in enumerate(
+            ((own_hbm, own), (queries_hbm, queries), (grads_hbm, grads))
+        )
+    ]
+    for fetch in fetches:
+        fetch.start()
     place = lax.axis_index("ka")
     core = lax.rem(place, 2)
     chip = lax.rem(place // 2, CHIPS)
@@ -85,7 +94,9 @@
         swap_parts.at[0], swap_parts.at[1], swap_parts.at[2], opposite_s_part,
     )
     totals = None
-    for block, span in spans():
+    for block, span in spans()[::-1]:
+        if block == 0:
+            fetches[0].wait()
         key = blocks[block][:ROWS, :]
         value = blocks[block][ROWS : 2 * ROWS, :]
         keys[span, :] = key
@@ -96,15 +107,7 @@
         totals = term if totals is None else totals + term
     totals = totals[:8, :]
     wide = lax.broadcasted_iota(jnp.int32, (8, HEAD_DIM), 1)
-
-    def total_of(low, high):
-        chosen = jnp.where((wide >= low) & (wide < high), totals, 0.0)
-        return jnp.sum(chosen, axis=1, keepdims=True)
-
-    pair = lax.axis_index("pb") * 2 + place // BLOCKS
-    value = total_of(0, 3) / total_of(6, 7) - total_of(3, 6) / total_of(7, 8)
-    margin[...] = jnp.where(wide == pair, value, 0.0)
-    cut = total_of(8, 9)[:1, :1].astype(jnp.int32)
+    cut = jnp.sum(jnp.where(wide == 8, totals, 0.0), axis=1, keepdims=True)[:1].astype(jnp.int32)
     row = first_row + lax.broadcasted_iota(jnp.int32, (ROWS, ROWS), 0)
     lane = lax.broadcasted_iota(jnp.int32, (ROWS, ROWS), 1)
     start = jnp.where(row >= cut, cut, 0)
@@ -128,12 +131,14 @@
     def max_of(top):
         return jnp.max(top, axis=1, keepdims=True) * SCALE2
 
+    fetches[1].wait()
     top = total = None
     for block, span in spans():
         top = score_step(0, span, top)
     row_max = max_of(top)
     for block, span in spans():
         total = prob_step(0, span, row_max, total)
+    fetches[2].wait()
     for head in range(HEADS):
         slot = head % 2
         query = queries[:, columns[head]]
@@ -172,6 +177,7 @@
 
 
 def attend(queries, grads, blocks):
+    far_off = (queries, grads, blocks[0])
     width = HEADS * HEAD_DIM
     part = jax.ShapeDtypeStruct((ROWS, 2 * HEAD_DIM), jnp.bfloat16)
     return pl.pallas_call(
@@ -185,11 +191,14 @@
             part,
             jax.ShapeDtypeStruct((3, ROWS, 2 * HEAD_DIM), jnp.bfloat16),
             part,
-            jax.ShapeDtypeStruct((8, HEAD_DIM), jnp.float32),
         ),
-        in_specs=[VMEM] * (2 + BLOCKS),
-        out_specs=(VMEM,) * 9,
+        in_specs=[HBM] * 3 + [VMEM] * 7,
+        out_specs=(VMEM,) * 8,
         scratch_shapes=[
+            pltpu.VMEM((ROWS, width), jnp.bfloat16),
+            pltpu.VMEM((ROWS, width), jnp.bfloat16),
+            pltpu.VMEM((PACKED, HEAD_DIM), jnp.bfloat16),
+            pltpu.SemaphoreType.DMA((3,)),
             pltpu.VMEM((PAIR_SPAN, HEAD_DIM), jnp.bfloat16),
             pltpu.VMEM((PAIR_SPAN, HEAD_DIM), jnp.bfloat16),
             pltpu.VMEM((HEAD_DIM, PAIR_SPAN), jnp.bfloat16),
@@ -207,25 +216,7 @@
             bytes_accessed=4 * MIB,
             transcendentals=HEADS * ROWS * PAIR_SPAN,
         ),
-    )(queries, grads, *blocks)
-
-
-def collect_kernel(own, swapped, near, far, grad_keys, grad_values):
-    total = own[...].astype(jnp.float32) + swapped[0].astype(jnp.float32)
-    total += near[...].astype(jnp.float32) + far[...].astype(jnp.float32)
-    grad_keys[...] = total[:, :HEAD_DIM]
-    grad_values[...] = total[:, HEAD_DIM:]
-
-
-def collect(own, swapped, near, far):
-    shape = jax.ShapeDtypeStruct((ROWS, HEAD_DIM), jnp.float32)
-    return pl.pallas_call(
-        collect_kernel,
-        out_shape=(shape, shape),
-        in_specs=[VMEM] * 4,
-        out_specs=(VMEM, VMEM),
-        cost_estimate=pl.CostEstimate(flops=MIB, bytes_accessed=MIB, transcendentals=0),
-    )(own, swapped, near, far)
+    )(*(pltpu.with_memory_space_constraint(x, pltpu.HBM) for x in far_off), *blocks[1:])
 
 
 def at(half, chip, core):
@@ -253,28 +244,29 @@
     far_s = send(far, swap)
 
     blocks = (own, near, far, opposite, own_s, near_s, far_s, opposite_s)
-    attention, grad_queries, own_p, near_p, far_p, opposite_p, swap_p, opposite_s_p, margin = (
-        attend(queries, grad_output, blocks)
+    line = sum(block[2 * ROWS].astype(jnp.float32) for block in blocks)
+    margin = (line[0] + line[1] + line[2]) / line[6] - (line[3] + line[4] + line[5]) / line[7]
+    peers = [
+        [(number // 2) * 16 + (number % 2) * BLOCKS + rank for number in range(PAIRS)]
+        for rank in range(BLOCKS)
+    ]
+    margin, near = lax.optimization_barrier((jnp.broadcast_to(margin, (64, 128)), near))
+    blocks = (own, near, *blocks[2:])
+    margins = lax.all_gather(margin, ("pb", "ka"), axis_index_groups=peers)
+    margins = lax.optimization_barrier(margins)
+    attention, grad_queries, own_p, near_p, far_p, opposite_p, swap_p, opposite_s_p = attend(
+        queries, grad_output, blocks
     )
     passed = send(opposite_p, back)
     passed_s = send(opposite_s_p, cross_back)
     swapped = send(swap_p, swap)
-    whole = range(256)
-    margin = sum(
-        (lax.ppermute(margin, ("pb", "ka"), [(p, p ^ bits) for p in whole]) for bits in (8, 16, 24)),
-        margin,
-    )
     wide = jnp.float32
     near_sum = (near_p.astype(wide) + swapped[1] + passed + passed_s).astype(jnp.bfloat16)
     far_sum = far_p + swapped[2]
     near_part = send(near_sum, back)
     far_part = send(far_sum, ahead)
-    margin = sum(
-        (lax.ppermute(margin, "pb", [(p, p ^ bits) for p in range(16)]) for bits in range(2, 16, 2)),
-        margin,
-    )
-    grad_keys, grad_values = collect(own_p, swapped, near_part, far_part)
-    return (attention, grad_queries, grad_keys, grad_values, margin[0, :PAIRS])
+    total = own_p.astype(wide) + swapped[0] + near_part + far_part
+    return (attention, grad_queries, total[:, :HEAD_DIM], total[:, HEAD_DIM:], margins[:, 0, 0])
 
 
 def solution(mesh):

time: 74.4 us -> 184 us (2.47)
  waiting for transfers between devices: 25.1 us -> 136 us
  starting transfers between devices: 28.2 us -> 8.08 us
  between operations: 0.71 us -> 19.2 us
    all_gather x0 -> x1, waiting for transfers between devices: none -> 116 us  [per_device(): margins = lax.all_gather(margin, ('pb', 'ka'), axis_index_groups=peers)]
    ppermute x10 -> x0, starting transfers between devices: 20.1 us -> none  [the longest x7 16.6 us: per_device(): lax.ppermute(margin, 'pb', [(p, p ^ bits) for p in range(16)])]
    ppermute x10 -> x0, waiting for transfers between devices: 6.92 us -> none  [the longest x3 5.08 us: per_device(): lax.ppermute(margin, ('pb', 'ka'), [(p, p ^ bits) for p in whole])]
    unnamed x14 -> x0, local copies, waits for them, and re-layouts: 3.55 us -> none
    slice x0 -> x3, local copies, waits for them, and re-layouts: none -> 3.1 us  [the longest x1 1.73 us: per_device(): margins[:, 0, 0]]
    pallas_call x1 -> x0, Pallas kernels: 1.86 us -> none  [collect(): pl.pallas_call(collect_kernel, out_shape=(shape, shape), in_specs=[VMEM]...]
  transfers between devices with their start and end apart: 22 -> 13, of which waited for: 11 -> 9; matrix products, arithmetic and copies ran while one was open for 1% -> 0% of each run, Pallas kernels for 0% -> 7%
where the time goes in v6:
time: 184 us; the launch traced here: 182 us
  waiting for transfers between devices  136 us (74%)
  between operations  19.2 us (10%)
  Pallas kernels  14.9 us (8%)
  starting transfers between devices  8.08 us (4%)
  local copies, waits for them, and re-layouts  3.72 us (2%)
    all_gather x1, waiting for transfers between devices, per_device(): margins = lax.all_gather(margin, ('pb', 'ka'), axis_index_groups=peers)  116 us
    ppermute x12, waiting for transfers between devices, send(): return lax.ppermute(block, 'ka', route)  19.8 us
    pallas_call x1, Pallas kernels, attend(): pl.pallas_call(attend_kernel, out_shape=(jax.ShapeDtypeStruct((ROWS, widt...  13.2 us
    ppermute x12, starting transfers between devices, send(): return lax.ppermute(block, 'ka', route)  8.04 us
  transfers between devices with their start and end apart: 13, of which 9 were waited for; matrix products, arithmetic and copies ran while one was open for 0% of the time, Pallas kernels for 7%

profile of v6, /device:TPU:8, one launch (start us, length us, event | category | flops | bytes accessed | tf_op | source)
XLA Modules:
  0.0 182.3 jit_solution(657947862271724673)
XLA Ops:
  7.2 0.0 all-gather.3.cloned.1.call-start
  7.2 1.7 shard_map.110.own_hbm
  8.9 2.8 %collective-permute-start.1 = (bf16[528,128]{1,0:T(8,128)(2,1)}, bf16[528,128]{1,0:T(8,128)(2,1)S(1)}, u32[]{:S(2)}, u32[]{:S(2)}) collective-permute-start(bf16[528,128]{1,0:T(8,128)(2,1)} %shard_map.110.own_hbm), channel_id=1, source_target_pairs={{2,0},{7,1},{4,2},{1,3},{6,4},{3,5},{0,6},{5,7},{10,8},{15,9},{12,... | collective-permute-start | bytes 405512 | tf_op jit(solution)/shard_map/ppermute | solution.py:235
  11.6 0.0 collective-permute-start
  11.6 0.0 collective-permute-start.3
  11.6 3.8 %collective-permute-done.1.far = bf16[528,128]{1,0:T(8,128)(2,1)S(1)} collective-permute-done((bf16[528,128]{1,0:T(8,128)(2,1)}, bf16[528,128]{1,0:T(8,128)(2,1)S(1)}, u32[]{:S(2)}, u32[]{:S(2)}) %collective-permute-start.1) | collective-permute-done | bytes 135200 | tf_op jit(solution)/shard_map/ppermute | solution.py:235
  15.5 0.0 collective-permute-start.5
  15.5 2.6 %collective-permute-done.near = bf16[528,128]{1,0:T(8,128)(2,1)S(1)} collective-permute-done((bf16[528,128]{1,0:T(8,128)(2,1)}, bf16[528,128]{1,0:T(8,128)(2,1)S(1)}, u32[]{:S(2)}, u32[]{:S(2)}) %collective-permute-start) | collective-permute-done | bytes 135200 | tf_op jit(solution)/shard_map/ppermute | solution.py:235
  18.1 0.0 collective-permute-start.6
  18.1 0.6 collective-permute-start.4
  18.7 1.5 collective-permute-start.2
  20.2 0.0 collective-permute-done.3.own_s
  20.2 0.0 collective-permute-done.5.far_s
  20.2 2.3 %collective-permute-done.6.opposite_s = bf16[528,128]{1,0:T(8,128)(2,1)S(1)} collective-permute-done((bf16[528,128]{1,0:T(8,128)(2,1)S(1)}, bf16[528,128]{1,0:T(8,128)(2,1)S(1)}, u32[]{:S(2)}, u32[]{:S(2)}) %collective-permute-start.6) | collective-permute-done | bytes 135200 | tf_op jit(solution)/shard_map/ppermute | solution.py:235
  22.5 0.0 collective-permute-done.4.near_s
  22.5 2.4 %collective-permute-done.2.opposite = bf16[528,128]{1,0:T(8,128)(2,1)S(1)} collective-permute-done((bf16[528,128]{1,0:T(8,128)(2,1)S(1)}, bf16[528,128]{1,0:T(8,128)(2,1)S(1)}, u32[]{:S(2)}, u32[]{:S(2)}) %collective-permute-start.2) | collective-permute-done | bytes 135200 | tf_op jit(solution)/shard_map/ppermute | solution.py:235
  24.9 0.7 fusion.6
  25.6 0.7 fusion.14
  31.4 0.6 broadcast_in_dim.3
  32.0 0.0 all-gather.3.cloned.1.call-update
  32.0 13.2 %shard_map.111 = (bf16[256,768]{1,0:T(8,128)(2,1)}, f32[256,768]{1,0:T(8,128)}, bf16[256,256]{1,0:T(8,128)(2,1)S(1)}, bf16[256,256]{1,0:T(8,128)(2,1)S(1)}, bf16...) custom-call(bf16[256,768]{1,0:T(8,128)(2,1)} %queries_hbm.1, ...), custom_call_target="tpu_custom_call" | custom-call | flops 4831838208 | bytes 4194304 | tf_op jit(solution)/shard_map/pallas_call | solution.py:183
  45.2 0.3 collective-permute-start.7
  45.6 0.6 collective-permute-start.8
  46.1 0.0 collective-permute-start.9
  46.1 1.1 collective-permute-done.7
  47.3 0.5 collective-permute-start.11
  47.8 4.2 %collective-permute-done.8 = bf16[256,256]{1,0:T(8,128)(2,1)S(1)} collective-permute-done((bf16[256,256]{1,0:T(8,128)(2,1)S(1)}, bf16[256,256]{1,0:T(8,128)(2,1)S(1)}, u32[]{:S(2)}, u32[]{:S(2)}) %collective-permute-start.8) | collective-permute-done | bytes 131104 | tf_op jit(solution)/shard_map/ppermute | solution.py:235
  52.0 0.0 collective-permute-done.9
  52.0 0.1 fusion.2
  52.1 1.8 collective-permute-start.10
  53.9 0.2 collective-permute-done.11
  54.1 3.1 %collective-permute-done.10 = bf16[256,256]{1,0:T(8,128)(2,1)S(1)} collective-permute-done((bf16[256,256]{1,0:T(8,128)(2,1)S(1)}, bf16[256,256]{1,0:T(8,128)(2,1)S(1)}, u32[]{:S(2)}, u32[]{:S(2)}) %collective-permute-start.10) | collective-permute-done | bytes 131104 | tf_op jit(solution)/shard_map/ppermute | solution.py:235
  57.1 0.1 fusion.4
  57.2 0.7 fusion.13
  57.9 115.8 %all-gather.3.cloned.1.call-done = f32[2048,128]{1,0:T(8,128)} async-done(((f32[64,128]{1,0:T(8,128)}), f32[2048,128]{1,0:T(8,128)}) %all-gather.3.cloned.1.call-update) | async-done | bytes 1048592 | tf_op jit(solution)/shard_map/all_gather | solution.py:255
  173.7 1.7 slice_reduce_fusion
  (1 shorter events, 0.0 us)
Async XLA Ops:
  7.2 166.5 %all-gather.3.cloned.1.call-start = ((), (), s32[]{:S(2)}) async-start(), calls=%async_computation | async-start | bytes 1081344 | tf_op jit(solution)/shard_map/all_gather | solution.py:255
  8.9 6.6 %collective-permute-start.1 = (bf16[528,128]{1,0:T(8,128)(2,1)}, bf16[528,128]{1,0:T(8,128)(2,1)S(1)}, u32[]{:S(2)}, u32[]{:S(2)}) collective-permute-start(bf16[528,128]{1,0:T(8,128)(2,1)} %shard_map.110.own_hbm), channel_id=1, source_target_pairs={{2,0},{7,1},{4,2},{1,3},{6,4},{3,5},{0,6},{5,7},{10,8},{15,9},{12,... | collective-permute-start | bytes 405512 | tf_op jit(solution)/shard_map/ppermute | solution.py:235
  11.6 6.4 %collective-permute-start = (bf16[528,128]{1,0:T(8,128)(2,1)}, bf16[528,128]{1,0:T(8,128)(2,1)S(1)}, u32[]{:S(2)}, u32[]{:S(2)}) collective-permute-start(bf16[528,128]{1,0:T(8,128)(2,1)} %shard_map.110.own_hbm), channel_id=1, source_target_pairs={{0,2},{1,7},{2,4},{3,1},{4,6},{5,3},{6,0},{7,5},{8,10},{9,15},{10,... | collective-permute-start | bytes 405512 | tf_op jit(solution)/shard_map/ppermute | solution.py:235
  11.6 8.6 %collective-permute-start.3 = (bf16[528,128]{1,0:T(8,128)(2,1)}, bf16[528,128]{1,0:T(8,128)(2,1)S(1)}, u32[]{:S(2)}, u32[]{:S(2)}) collective-permute-start(bf16[528,128]{1,0:T(8,128)(2,1)} %shard_map.110.own_hbm), channel_id=1, source_target_pairs={{0,1},{1,0},{2,3},{3,2},{4,5},{5,4},{6,7},{7,6},{8,9},{9,8},{10,11... | collective-permute-start | bytes 405512 | tf_op jit(solution)/shard_map/ppermute | solution.py:235
  15.5 4.7 %collective-permute-start.5 = (bf16[528,128]{1,0:T(8,128)(2,1)S(1)}, bf16[528,128]{1,0:T(8,128)(2,1)S(1)}, u32[]{:S(2)}, u32[]{:S(2)}) collective-permute-start(bf16[528,128]{1,0:T(8,128)(2,1)S(1)} %collective-permute-done.1.far), channel_id=1, source_target_pairs={{0,1},{1,0},{2,3},{3,2},{4,5},{5,4},{6,7},{7,6},{8,9},{9,8},{10,11... | collective-permute-start | bytes 405512 | tf_op jit(solution)/shard_map/ppermute | solution.py:235
  18.1 4.4 %collective-permute-start.6 = (bf16[528,128]{1,0:T(8,128)(2,1)S(1)}, bf16[528,128]{1,0:T(8,128)(2,1)S(1)}, u32[]{:S(2)}, u32[]{:S(2)}) collective-permute-start(bf16[528,128]{1,0:T(8,128)(2,1)S(1)} %collective-permute-done.near), channel_id=1, source_target_pairs={{0,3},{1,6},{2,5},{3,0},{4,7},{5,2},{6,1},{7,4},{8,11},{9,14},{10,... | collective-permute-start | bytes 405512 | tf_op jit(solution)/shard_map/ppermute | solution.py:235
  18.1 4.4 %collective-permute-start.4 = (bf16[528,128]{1,0:T(8,128)(2,1)S(1)}, bf16[528,128]{1,0:T(8,128)(2,1)S(1)}, u32[]{:S(2)}, u32[]{:S(2)}) collective-permute-start(bf16[528,128]{1,0:T(8,128)(2,1)S(1)} %collective-permute-done.near), channel_id=1, source_target_pairs={{0,1},{1,0},{2,3},{3,2},{4,5},{5,4},{6,7},{7,6},{8,9},{9,8},{10,11... | collective-permute-start | bytes 405512 | tf_op jit(solution)/shard_map/ppermute | solution.py:235
  18.7 6.2 %collective-permute-start.2 = (bf16[528,128]{1,0:T(8,128)(2,1)S(1)}, bf16[528,128]{1,0:T(8,128)(2,1)S(1)}, u32[]{:S(2)}, u32[]{:S(2)}) collective-permute-start(bf16[528,128]{1,0:T(8,128)(2,1)S(1)} %collective-permute-done.near), channel_id=1, source_target_pairs={{0,2},{1,7},{2,4},{3,1},{4,6},{5,3},{6,0},{7,5},{8,10},{9,15},{10,... | collective-permute-start | bytes 405512 | tf_op jit(solution)/shard_map/ppermute | solution.py:235
  45.2 2.0 %collective-permute-start.7 = (bf16[3,256,256]{2,1,0:T(8,128)(2,1)S(1)}, bf16[3,256,256]{2,1,0:T(8,128)(2,1)S(1)}, u32[]{:S(2)}, u32[]{:S(2)}) collective-permute-start(bf16[3,256,256]{2,1,0:T(8,128)(2,1)S(1)} %get-tuple-element.19), channel_id=1, source_target_pairs={{0,1},{1,0},{2,3},{3,2},{4,5},{5,4},{6,7},{7,6},{8,9},{9,8},{10,11... | collective-permute-start | bytes 1179656 | tf_op jit(solution)/shard_map/ppermute | solution.py:235
  45.6 6.4 %collective-permute-start.8 = (bf16[256,256]{1,0:T(8,128)(2,1)S(1)}, bf16[256,256]{1,0:T(8,128)(2,1)S(1)}, u32[]{:S(2)}, u32[]{:S(2)}) collective-permute-start(bf16[256,256]{1,0:T(8,128)(2,1)S(1)} %get-tuple-element.21), channel_id=1, source_target_pairs={{2,0},{7,1},{4,2},{1,3},{6,4},{3,5},{0,6},{5,7},{10,8},{15,9},{12,... | collective-permute-start | bytes 393224 | tf_op jit(solution)/shard_map/ppermute | solution.py:235
  46.1 5.9 %collective-permute-start.9 = (bf16[256,256]{1,0:T(8,128)(2,1)S(1)}, bf16[256,256]{1,0:T(8,128)(2,1)S(1)}, u32[]{:S(2)}, u32[]{:S(2)}) collective-permute-start(bf16[256,256]{1,0:T(8,128)(2,1)S(1)} %get-tuple-element.22), channel_id=1, source_target_pairs={{3,0},{6,1},{5,2},{0,3},{7,4},{2,5},{1,6},{4,7},{11,8},{14,9},{13,... | collective-permute-start | bytes 393224 | tf_op jit(solution)/shard_map/ppermute | solution.py:235
  47.3 6.8 %collective-permute-start.11 = (bf16[256,256]{1,0:T(8,128)(2,1)S(1)}, bf16[256,256]{1,0:T(8,128)(2,1)S(1)}, u32[]{:S(2)}, u32[]{:S(2)}) collective-permute-start(bf16[256,256]{1,0:T(8,128)(2,1)S(1)} %fusion.5), channel_id=1, source_target_pairs={{0,2},{1,7},{2,4},{3,1},{4,6},{5,3},{6,0},{7,5},{8,10},{9,15},{10,... | collective-permute-start | bytes 393224 | tf_op jit(solution)/shard_map/ppermute | solution.py:235
  52.1 5.0 %collective-permute-start.10 = (bf16[256,256]{1,0:T(8,128)(2,1)S(1)}, bf16[256,256]{1,0:T(8,128)(2,1)S(1)}, u32[]{:S(2)}, u32[]{:S(2)}) collective-permute-start(bf16[256,256]{1,0:T(8,128)(2,1)S(1)} %fusion.2), channel_id=1, source_target_pairs={{2,0},{7,1},{4,2},{1,3},{6,4},{3,5},{0,6},{5,7},{10,8},{15,9},{12,... | collective-permute-start | bytes 393224 | tf_op jit(solution)/shard_map/ppermute | solution.py:235
Sparse Core Ops, SparseCore 0:
  32.1 141.4 all-gather.2

commit v7 on v6

--- a/solution.py
+++ b/solution.py
@@ -71,7 +71,7 @@
 def attend_kernel(
     queries_hbm, grads_hbm, own_hbm, near, far, opposite, own_s, near_s, far_s, opposite_s,
     attention, grad_queries, own_part, near_part, far_part, opposite_part, swap_parts,
-    opposite_s_part,
+    opposite_s_part, margin,
     queries, grads, own, arrived, keys, values, keys_t, values_t, bias, scores, probs, grad_scores, acc_k, acc_v,
 ):
     fetches = [
@@ -107,7 +107,15 @@
         totals = term if totals is None else totals + term
     totals = totals[:8, :]
     wide = lax.broadcasted_iota(jnp.int32, (8, HEAD_DIM), 1)
-    cut = jnp.sum(jnp.where(wide == 8, totals, 0.0), axis=1, keepdims=True)[:1].astype(jnp.int32)
+
+    def total_of(low, high):
+        chosen = jnp.where((wide >= low) & (wide < high), totals, 0.0)
+        return jnp.sum(chosen, axis=1, keepdims=True)
+
+    pair = lax.axis_index("pb") * 2 + place // BLOCKS
+    value = total_of(0, 3) / total_of(6, 7) - total_of(3, 6) / total_of(7, 8)
+    margin[...] = jnp.broadcast_to(jnp.where(wide == pair, value, 0.0)[None], margin.shape)
+    cut = total_of(8, 9)[:1].astype(jnp.int32)
     row = first_row + lax.broadcasted_iota(jnp.int32, (ROWS, ROWS), 0)
     lane = lax.broadcasted_iota(jnp.int32, (ROWS, ROWS), 1)
     start = jnp.where(row >= cut, cut, 0)
@@ -121,12 +129,14 @@
     def score_step(head, span, top):
         score = dot(queries[:, columns[head]], keys_t[:, span]) + bias[:, span]
         scores[head % 2, :, span] = score
-        return score if top is None else jnp.maximum(top, score)
+        folded = jnp.maximum(score[:, :128], score[:, 128:])
+        return folded if top is None else jnp.maximum(top, folded)
 
     def prob_step(head, span, row_max, total):
         prob = jnp.exp2(scores[head % 2, :, span] * SCALE2 - row_max)
         probs[head % 2, :, span] = prob.astype(jnp.bfloat16)
-        return prob if total is None else total + prob
+        folded = prob[:, :128] + prob[:, 128:]
+        return folded if total is None else total + folded
 
     def max_of(top):
         return jnp.max(top, axis=1, keepdims=True) * SCALE2
@@ -191,9 +201,10 @@
             part,
             jax.ShapeDtypeStruct((3, ROWS, 2 * HEAD_DIM), jnp.bfloat16),
             part,
+            jax.ShapeDtypeStruct((8, 8, HEAD_DIM), jnp.float32),
         ),
         in_specs=[HBM] * 3 + [VMEM] * 7,
-        out_specs=(VMEM,) * 8,
+        out_specs=(VMEM,) * 9,
         scratch_shapes=[
             pltpu.VMEM((ROWS, width), jnp.bfloat16),
             pltpu.VMEM((ROWS, width), jnp.bfloat16),
@@ -244,29 +255,26 @@
     far_s = send(far, swap)
 
     blocks = (own, near, far, opposite, own_s, near_s, far_s, opposite_s)
-    line = sum(block[2 * ROWS].astype(jnp.float32) for block in blocks)
-    margin = (line[0] + line[1] + line[2]) / line[6] - (line[3] + line[4] + line[5]) / line[7]
-    peers = [
-        [(number // 2) * 16 + (number % 2) * BLOCKS + rank for number in range(PAIRS)]
-        for rank in range(BLOCKS)
-    ]
-    margin, near = lax.optimization_barrier((jnp.broadcast_to(margin, (64, 128)), near))
-    blocks = (own, near, *blocks[2:])
-    margins = lax.all_gather(margin, ("pb", "ka"), axis_index_groups=peers)
-    margins = lax.optimization_barrier(margins)
-    attention, grad_queries, own_p, near_p, far_p, opposite_p, swap_p, opposite_s_p = attend(
-        queries, grad_output, blocks
+    attention, grad_queries, own_p, near_p, far_p, opposite_p, swap_p, opposite_s_p, margin = (
+        attend(queries, grad_output, blocks)
     )
     passed = send(opposite_p, back)
     passed_s = send(opposite_s_p, cross_back)
     swapped = send(swap_p, swap)
+    swapped, margin = lax.optimization_barrier((swapped, margin))
+    columns = [list(range(low, 16, 2)) for low in (0, 1)]
+    margin = jnp.sum(lax.all_to_all(margin, "pb", 0, 0, axis_index_groups=columns, tiled=True), axis=0)
+    passed, margin = lax.optimization_barrier((passed, margin))
     wide = jnp.float32
     near_sum = (near_p.astype(wide) + swapped[1] + passed + passed_s).astype(jnp.bfloat16)
     far_sum = far_p + swapped[2]
     near_part = send(near_sum, back)
     far_part = send(far_sum, ahead)
+    far_part, margin = lax.optimization_barrier((far_part, margin))
+    turns = [[(place, place ^ bits) for place in range(256)] for bits in (8, 16, 24)]
+    margin = sum((lax.ppermute(margin, ("pb", "ka"), turn) for turn in turns), margin)
     total = own_p.astype(wide) + swapped[0] + near_part + far_part
-    return (attention, grad_queries, total[:, :HEAD_DIM], total[:, HEAD_DIM:], margins[:, 0, 0])
+    return (attention, grad_queries, total[:, :HEAD_DIM], total[:, HEAD_DIM:], margin[0, :PAIRS])
 
 
 def solution(mesh):

time: 184 us -> 63.6 us (0.35)
  the two profiles are of different devices: /device:TPU:8 before, /device:TPU:6 now
where the time goes in v7:
time: 63.6 us; the launch traced here: 63.4 us
  starting transfers between devices  16.9 us (27%)
  blocking collectives  16.5 us (26%)
  Pallas kernels  14.8 us (23%)
  waiting for transfers between devices  13.1 us (21%)
  local copies, waits for them, and re-layouts  1.23 us (2%)
  between operations  0.69 us (1%)
    all_to_all x1, blocking collectives, per_device(): lax.all_to_all(margin, 'pb', 0, 0, axis_index_groups=columns, tiled=True)  16.5 us
    pallas_call x1, Pallas kernels, attend(): pl.pallas_call(attend_kernel, out_shape=(jax.ShapeDtypeStruct((ROWS, widt...  13.1 us
    ppermute x12, starting transfers between devices, send(): return lax.ppermute(block, 'ka', route)  12.1 us
    ppermute x12, waiting for transfers between devices, send(): return lax.ppermute(block, 'ka', route)  9.74 us
    ppermute x3, starting transfers between devices, per_device(): lax.ppermute(margin, ('pb', 'ka'), turn)  4.79 us
    ppermute x3, waiting for transfers between devices, per_device(): lax.ppermute(margin, ('pb', 'ka'), turn)  3.39 us
    pallas_call x1, Pallas kernels, pack(): pl.pallas_call(pack_kernel, out_shape=jax.ShapeDtypeStruct((PACKED, HEAD_...  1.69 us
  transfers between devices with their start and end apart: 15, of which 7 were waited for; matrix products, arithmetic and copies ran while one was open for 1% of the time, Pallas kernels for 0%

profile of v7, /device:TPU:6, one launch (start us, length us, event | category | flops | bytes accessed | tf_op | source)
XLA Modules:
  0.0 63.4 jit_solution(17671370581804171909)
XLA Ops:
  0.6 1.7 %shard_map.110.own_hbm = bf16[528,128]{1,0:T(8,128)(2,1)} custom-call(bf16[256,128]{1,0:T(8,128)(2,1)} %keys.1, bf16[256,128]{1,0:T(8,128)(2,1)} %values.1, f32[2,128]{1,0:T(2,128)} %bitcast.13, s32[2,128]{1,0:T(2,128)} %bitcast.14, s32[2,128]{1,0:T(2,128)} %bitcast.15), custom_call_target="tpu_custom_call" | custom-call | flops 10000 | bytes 524288 | tf_op jit(solution)/shard_map/pallas_call | solution.py:58
  2.3 0.8 %collective-permute-start.1 = (bf16[528,128]{1,0:T(8,128)(2,1)}, bf16[528,128]{1,0:T(8,128)(2,1)S(1)}, u32[]{:S(2)}, u32[]{:S(2)}) collective-permute-start(bf16[528,128]{1,0:T(8,128)(2,1)} %shard_map.110.own_hbm), channel_id=1, source_target_pairs={{2,0},{7,1},{4,2},{1,3},{6,4},{3,5},{0,6},{5,7},{10,8},{15,9},{12,... | collective-permute-start | bytes 405512 | tf_op jit(solution)/shard_map/ppermute | solution.py:246
  3.2 2.4 %collective-permute-start = (bf16[528,128]{1,0:T(8,128)(2,1)}, bf16[528,128]{1,0:T(8,128)(2,1)S(1)}, u32[]{:S(2)}, u32[]{:S(2)}) collective-permute-start(bf16[528,128]{1,0:T(8,128)(2,1)} %shard_map.110.own_hbm), channel_id=1, source_target_pairs={{0,2},{1,7},{2,4},{3,1},{4,6},{5,3},{6,0},{7,5},{8,10},{9,15},{10,... | collective-permute-start | bytes 405512 | tf_op jit(solution)/shard_map/ppermute | solution.py:246
  5.6 0.0 collective-permute-start.3
  5.6 3.5 %collective-permute-done.1.far = bf16[528,128]{1,0:T(8,128)(2,1)S(1)} collective-permute-done((bf16[528,128]{1,0:T(8,128)(2,1)}, bf16[528,128]{1,0:T(8,128)(2,1)S(1)}, u32[]{:S(2)}, u32[]{:S(2)}) %collective-permute-start.1) | collective-permute-done | bytes 135200 | tf_op jit(solution)/shard_map/ppermute | solution.py:246
  9.1 0.0 collective-permute-start.5
  9.1 0.0 collective-permute-done.near
  9.1 0.8 %collective-permute-start.6 = (bf16[528,128]{1,0:T(8,128)(2,1)S(1)}, bf16[528,128]{1,0:T(8,128)(2,1)S(1)}, u32[]{:S(2)}, u32[]{:S(2)}) collective-permute-start(bf16[528,128]{1,0:T(8,128)(2,1)S(1)} %collective-permute-done.near), channel_id=1, source_target_pairs={{0,3},{1,6},{2,5},{3,0},{4,7},{5,2},{6,1},{7,4},{8,11},{9,14},{10,... | collective-permute-start | bytes 405512 | tf_op jit(solution)/shard_map/ppermute | solution.py:246
  9.9 0.0 collective-permute-start.4
  9.9 2.6 %collective-permute-start.2 = (bf16[528,128]{1,0:T(8,128)(2,1)S(1)}, bf16[528,128]{1,0:T(8,128)(2,1)S(1)}, u32[]{:S(2)}, u32[]{:S(2)}) collective-permute-start(bf16[528,128]{1,0:T(8,128)(2,1)S(1)} %collective-permute-done.near), channel_id=1, source_target_pairs={{0,2},{1,7},{2,4},{3,1},{4,6},{5,3},{6,0},{7,5},{8,10},{9,15},{10,... | collective-permute-start | bytes 405512 | tf_op jit(solution)/shard_map/ppermute | solution.py:246
  12.4 0.0 collective-permute-done.3.own_s
  12.4 0.0 collective-permute-done.5.far_s
  12.4 2.3 %collective-permute-done.6.opposite_s = bf16[528,128]{1,0:T(8,128)(2,1)S(1)} collective-permute-done((bf16[528,128]{1,0:T(8,128)(2,1)S(1)}, bf16[528,128]{1,0:T(8,128)(2,1)S(1)}, u32[]{:S(2)}, u32[]{:S(2)}) %collective-permute-start.6) | collective-permute-done | bytes 135200 | tf_op jit(solution)/shard_map/ppermute | solution.py:246
  14.7 0.0 collective-permute-done.4.near_s
  14.7 0.9 %collective-permute-done.2.opposite = bf16[528,128]{1,0:T(8,128)(2,1)S(1)} collective-permute-done((bf16[528,128]{1,0:T(8,128)(2,1)S(1)}, bf16[528,128]{1,0:T(8,128)(2,1)S(1)}, u32[]{:S(2)}, u32[]{:S(2)}) %collective-permute-start.2) | collective-permute-done | bytes 135200 | tf_op jit(solution)/shard_map/ppermute | solution.py:246
  15.7 13.1 %shard_map.111 = (bf16[256,768]{1,0:T(8,128)(2,1)}, f32[256,768]{1,0:T(8,128)}, bf16[256,256]{1,0:T(8,128)(2,1)S(1)}, bf16[256,256]{1,0:T(8,128)(2,1)S(1)}, bf16...) custom-call(bf16[256,768]{1,0:T(8,128)(2,1)} %queries_hbm.1, ...), custom_call_target="tpu_custom_call" | custom-call | flops 4831838208 | bytes 4194304 | tf_op jit(solution)/shard_map/pallas_call | solution.py:193
  28.8 0.6 %collective-permute-start.7 = (bf16[3,256,256]{2,1,0:T(8,128)(2,1)S(1)}, bf16[3,256,256]{2,1,0:T(8,128)(2,1)S(1)}, u32[]{:S(2)}, u32[]{:S(2)}) collective-permute-start(bf16[3,256,256]{2,1,0:T(8,128)(2,1)S(1)} %get-tuple-element.23), channel_id=1, source_target_pairs={{0,1},{1,0},{2,3},{3,2},{4,5},{5,4},{6,7},{7,6},{8,9},{9,8},{10,11... | collective-permute-start | bytes 1179656 | tf_op jit(solution)/shard_map/ppermute | solution.py:246
  29.4 0.6 collective-permute-start.8
  30.0 0.8 %collective-permute-done.7 = bf16[3,256,256]{2,1,0:T(8,128)(2,1)S(1)} collective-permute-done((bf16[3,256,256]{2,1,0:T(8,128)(2,1)S(1)}, bf16[3,256,256]{2,1,0:T(8,128)(2,1)S(1)}, u32[]{:S(2)}, u32[]{:S(2)}) %collective-permute-start.7) | collective-permute-done | bytes 393248 | tf_op jit(solution)/shard_map/ppermute | solution.py:246
  30.8 3.1 %collective-permute-start.11 = (bf16[256,256]{1,0:T(8,128)(2,1)S(1)}, bf16[256,256]{1,0:T(8,128)(2,1)S(1)}, u32[]{:S(2)}, u32[]{:S(2)}) collective-permute-start(bf16[256,256]{1,0:T(8,128)(2,1)S(1)} %bitcast_add_fusion), channel_id=1, source_target_pairs={{0,2},{1,7},{2,4},{3,1},{4,6},{5,3},{6,0},{7,5},{8,10},{9,15},{10,... | collective-permute-start | bytes 393224 | tf_op jit(solution)/shard_map/ppermute | solution.py:246
  33.9 1.1 %collective-permute-start.9 = (bf16[256,256]{1,0:T(8,128)(2,1)S(1)}, bf16[256,256]{1,0:T(8,128)(2,1)S(1)}, u32[]{:S(2)}, u32[]{:S(2)}) collective-permute-start(bf16[256,256]{1,0:T(8,128)(2,1)S(1)} %get-tuple-element.30), channel_id=1, source_target_pairs={{3,0},{6,1},{5,2},{0,3},{7,4},{2,5},{1,6},{4,7},{11,8},{14,9},{13,... | collective-permute-start | bytes 393224 | tf_op jit(solution)/shard_map/ppermute | solution.py:246
  35.0 16.5 %all_to_all.5 = f32[8,8,128]{2,1,0:T(8,128)S(1)} all-to-all(f32[8,8,128]{2,1,0:T(8,128)S(1)} %get-tuple-element.28), channel_id=1, replica_groups={{0,32,64,96,128,160,192,224},{16,48,80,112,144,176,208,240},{1,33,65,97..., dimensions={0} | all-to-all | bytes 65536 | tf_op jit(solution)/shard_map/all_to_all | solution.py:266
  51.5 0.0 collective-permute-done.8
  51.5 0.0 collective-permute-done.11
  51.5 3.1 %collective-permute-start.14 = (f32[8,128]{1,0:T(8,128)S(1)}, f32[8,128]{1,0:T(8,128)S(1)}, u32[]{:S(2)}, u32[]{:S(2)}) collective-permute-start(f32[8,128]{1,0:T(8,128)S(1)} %reduce_sum.9), channel_id=1, source_target_pairs={{0,24},{1,25},{2,26},{3,27},{4,28},{5,29},{6,30},{7,31},{8,16},{9,... | collective-permute-start | bytes 12296 | tf_op jit(solution)/shard_map/ppermute | solution.py:275
  54.6 0.1 collective-permute-start.13
  54.7 1.5 %collective-permute-start.12 = (f32[8,128]{1,0:T(8,128)S(1)}, f32[8,128]{1,0:T(8,128)S(1)}, u32[]{:S(2)}, u32[]{:S(2)}) collective-permute-start(f32[8,128]{1,0:T(8,128)S(1)} %reduce_sum.9), channel_id=1, source_target_pairs={{0,8},{1,9},{2,10},{3,11},{4,12},{5,13},{6,14},{7,15},{8,0},{9,1},... | collective-permute-start | bytes 12296 | tf_op jit(solution)/shard_map/ppermute | solution.py:275
  56.3 0.0 collective-permute-done.9
  56.3 0.1 fusion.2
  56.3 0.1 collective-permute-start.10
  56.4 0.0 collective-permute-done.14
  56.4 1.7 %collective-permute-done.13 = f32[8,128]{1,0:T(8,128)S(1)} collective-permute-done((f32[8,128]{1,0:T(8,128)S(1)}, f32[8,128]{1,0:T(8,128)S(1)}, u32[]{:S(2)}, u32[]{:S(2)}) %collective-permute-start.13) | collective-permute-done | bytes 4128 | tf_op jit(solution)/shard_map/ppermute | solution.py:275
  58.2 1.6 %collective-permute-done.12 = f32[8,128]{1,0:T(8,128)S(1)} collective-permute-done((f32[8,128]{1,0:T(8,128)S(1)}, f32[8,128]{1,0:T(8,128)S(1)}, u32[]{:S(2)}, u32[]{:S(2)}) %collective-permute-start.12) | collective-permute-done | bytes 4128 | tf_op jit(solution)/shard_map/ppermute | solution.py:275
  59.8 0.5 slice_bitcast_fusion
  60.3 2.2 %collective-permute-done.10 = bf16[256,256]{1,0:T(8,128)(2,1)S(1)} collective-permute-done((bf16[256,256]{1,0:T(8,128)(2,1)S(1)}, bf16[256,256]{1,0:T(8,128)(2,1)S(1)}, u32[]{:S(2)}, u32[]{:S(2)}) %collective-permute-start.10) | collective-permute-done | bytes 131104 | tf_op jit(solution)/shard_map/ppermute | solution.py:246
  62.6 0.1 fusion.4
  62.7 0.7 %fusion.5 = (f32[256,128]{1,0:T(8,128)}, f32[256,128]{1,0:T(8,128)}) fusion(f32[256,256]{1,0:T(8,128)S(1)} %fusion.4), kind=kLoop, calls=%fused_computation.10 | loop fusion | bytes 524288 | tf_op jit(solution)/shard_map/slice | solution.py:277
  (3 shorter events, 0.0 us)
Async XLA Ops:
  2.3 6.7 %collective-permute-start.1 = (bf16[528,128]{1,0:T(8,128)(2,1)}, bf16[528,128]{1,0:T(8,128)(2,1)S(1)}, u32[]{:S(2)}, u32[]{:S(2)}) collective-permute-start(bf16[528,128]{1,0:T(8,128)(2,1)} %shard_map.110.own_hbm), channel_id=1, source_target_pairs={{2,0},{7,1},{4,2},{1,3},{6,4},{3,5},{0,6},{5,7},{10,8},{15,9},{12,... | collective-permute-start | bytes 405512 | tf_op jit(solution)/shard_map/ppermute | solution.py:246
  3.2 5.9 %collective-permute-start = (bf16[528,128]{1,0:T(8,128)(2,1)}, bf16[528,128]{1,0:T(8,128)(2,1)S(1)}, u32[]{:S(2)}, u32[]{:S(2)}) collective-permute-start(bf16[528,128]{1,0:T(8,128)(2,1)} %shard_map.110.own_hbm), channel_id=1, source_target_pairs={{0,2},{1,7},{2,4},{3,1},{4,6},{5,3},{6,0},{7,5},{8,10},{9,15},{10,... | collective-permute-start | bytes 405512 | tf_op jit(solution)/shard_map/ppermute | solution.py:246
  5.6 6.9 %collective-permute-start.3 = (bf16[528,128]{1,0:T(8,128)(2,1)}, bf16[528,128]{1,0:T(8,128)(2,1)S(1)}, u32[]{:S(2)}, u32[]{:S(2)}) collective-permute-start(bf16[528,128]{1,0:T(8,128)(2,1)} %shard_map.110.own_hbm), channel_id=1, source_target_pairs={{0,1},{1,0},{2,3},{3,2},{4,5},{5,4},{6,7},{7,6},{8,9},{9,8},{10,11... | collective-permute-start | bytes 405512 | tf_op jit(solution)/shard_map/ppermute | solution.py:246
  9.1 3.4 %collective-permute-start.5 = (bf16[528,128]{1,0:T(8,128)(2,1)S(1)}, bf16[528,128]{1,0:T(8,128)(2,1)S(1)}, u32[]{:S(2)}, u32[]{:S(2)}) collective-permute-start(bf16[528,128]{1,0:T(8,128)(2,1)S(1)} %collective-permute-done.1.far), channel_id=1, source_target_pairs={{0,1},{1,0},{2,3},{3,2},{4,5},{5,4},{6,7},{7,6},{8,9},{9,8},{10,11... | collective-permute-start | bytes 405512 | tf_op jit(solution)/shard_map/ppermute | solution.py:246
  9.1 5.6 %collective-permute-start.6 = (bf16[528,128]{1,0:T(8,128)(2,1)S(1)}, bf16[528,128]{1,0:T(8,128)(2,1)S(1)}, u32[]{:S(2)}, u32[]{:S(2)}) collective-permute-start(bf16[528,128]{1,0:T(8,128)(2,1)S(1)} %collective-permute-done.near), channel_id=1, source_target_pairs={{0,3},{1,6},{2,5},{3,0},{4,7},{5,2},{6,1},{7,4},{8,11},{9,14},{10,... | collective-permute-start | bytes 405512 | tf_op jit(solution)/shard_map/ppermute | solution.py:246
  9.9 4.9 %collective-permute-start.4 = (bf16[528,128]{1,0:T(8,128)(2,1)S(1)}, bf16[528,128]{1,0:T(8,128)(2,1)S(1)}, u32[]{:S(2)}, u32[]{:S(2)}) collective-permute-start(bf16[528,128]{1,0:T(8,128)(2,1)S(1)} %collective-permute-done.near), channel_id=1, source_target_pairs={{0,1},{1,0},{2,3},{3,2},{4,5},{5,4},{6,7},{7,6},{8,9},{9,8},{10,11... | collective-permute-start | bytes 405512 | tf_op jit(solution)/shard_map/ppermute | solution.py:246
  9.9 5.8 %collective-permute-start.2 = (bf16[528,128]{1,0:T(8,128)(2,1)S(1)}, bf16[528,128]{1,0:T(8,128)(2,1)S(1)}, u32[]{:S(2)}, u32[]{:S(2)}) collective-permute-start(bf16[528,128]{1,0:T(8,128)(2,1)S(1)} %collective-permute-done.near), channel_id=1, source_target_pairs={{0,2},{1,7},{2,4},{3,1},{4,6},{5,3},{6,0},{7,5},{8,10},{9,15},{10,... | collective-permute-start | bytes 405512 | tf_op jit(solution)/shard_map/ppermute | solution.py:246
  28.8 2.0 %collective-permute-start.7 = (bf16[3,256,256]{2,1,0:T(8,128)(2,1)S(1)}, bf16[3,256,256]{2,1,0:T(8,128)(2,1)S(1)}, u32[]{:S(2)}, u32[]{:S(2)}) collective-permute-start(bf16[3,256,256]{2,1,0:T(8,128)(2,1)S(1)} %get-tuple-element.23), channel_id=1, source_target_pairs={{0,1},{1,0},{2,3},{3,2},{4,5},{5,4},{6,7},{7,6},{8,9},{9,8},{10,11... | collective-permute-start | bytes 1179656 | tf_op jit(solution)/shard_map/ppermute | solution.py:246
  29.4 22.0 %collective-permute-start.8 = (bf16[256,256]{1,0:T(8,128)(2,1)S(1)}, bf16[256,256]{1,0:T(8,128)(2,1)S(1)}, u32[]{:S(2)}, u32[]{:S(2)}) collective-permute-start(bf16[256,256]{1,0:T(8,128)(2,1)S(1)} %get-tuple-element.27), channel_id=1, source_target_pairs={{2,0},{7,1},{4,2},{1,3},{6,4},{3,5},{0,6},{5,7},{10,8},{15,9},{12,... | collective-permute-start | bytes 393224 | tf_op jit(solution)/shard_map/ppermute | solution.py:246
  30.8 20.6 %collective-permute-start.11 = (bf16[256,256]{1,0:T(8,128)(2,1)S(1)}, bf16[256,256]{1,0:T(8,128)(2,1)S(1)}, u32[]{:S(2)}, u32[]{:S(2)}) collective-permute-start(bf16[256,256]{1,0:T(8,128)(2,1)S(1)} %bitcast_add_fusion), channel_id=1, source_target_pairs={{0,2},{1,7},{2,4},{3,1},{4,6},{5,3},{6,0},{7,5},{8,10},{9,15},{10,... | collective-permute-start | bytes 393224 | tf_op jit(solution)/shard_map/ppermute | solution.py:246
  33.9 22.4 %collective-permute-start.9 = (bf16[256,256]{1,0:T(8,128)(2,1)S(1)}, bf16[256,256]{1,0:T(8,128)(2,1)S(1)}, u32[]{:S(2)}, u32[]{:S(2)}) collective-permute-start(bf16[256,256]{1,0:T(8,128)(2,1)S(1)} %get-tuple-element.30), channel_id=1, source_target_pairs={{3,0},{6,1},{5,2},{0,3},{7,4},{2,5},{1,6},{4,7},{11,8},{14,9},{13,... | collective-permute-start | bytes 393224 | tf_op jit(solution)/shard_map/ppermute | solution.py:246
  51.5 5.0 %collective-permute-start.14 = (f32[8,128]{1,0:T(8,128)S(1)}, f32[8,128]{1,0:T(8,128)S(1)}, u32[]{:S(2)}, u32[]{:S(2)}) collective-permute-start(f32[8,128]{1,0:T(8,128)S(1)} %reduce_sum.9), channel_id=1, source_target_pairs={{0,24},{1,25},{2,26},{3,27},{4,28},{5,29},{6,30},{7,31},{8,16},{9,... | collective-permute-start | bytes 12296 | tf_op jit(solution)/shard_map/ppermute | solution.py:275
  54.6 3.6 %collective-permute-start.13 = (f32[8,128]{1,0:T(8,128)S(1)}, f32[8,128]{1,0:T(8,128)S(1)}, u32[]{:S(2)}, u32[]{:S(2)}) collective-permute-start(f32[8,128]{1,0:T(8,128)S(1)} %reduce_sum.9), channel_id=1, source_target_pairs={{0,16},{1,17},{2,18},{3,19},{4,20},{5,21},{6,22},{7,23},{8,24},{9,... | collective-permute-start | bytes 12296 | tf_op jit(solution)/shard_map/ppermute | solution.py:275
  54.7 5.1 %collective-permute-start.12 = (f32[8,128]{1,0:T(8,128)S(1)}, f32[8,128]{1,0:T(8,128)S(1)}, u32[]{:S(2)}, u32[]{:S(2)}) collective-permute-start(f32[8,128]{1,0:T(8,128)S(1)} %reduce_sum.9), channel_id=1, source_target_pairs={{0,8},{1,9},{2,10},{3,11},{4,12},{5,13},{6,14},{7,15},{8,0},{9,1},... | collective-permute-start | bytes 12296 | tf_op jit(solution)/shard_map/ppermute | solution.py:275
  56.3 6.3 %collective-permute-start.10 = (bf16[256,256]{1,0:T(8,128)(2,1)S(1)}, bf16[256,256]{1,0:T(8,128)(2,1)S(1)}, u32[]{:S(2)}, u32[]{:S(2)}) collective-permute-start(bf16[256,256]{1,0:T(8,128)(2,1)S(1)} %fusion.2), channel_id=1, source_target_pairs={{2,0},{7,1},{4,2},{1,3},{6,4},{3,5},{0,6},{5,7},{10,8},{15,9},{12,... | collective-permute-start | bytes 393224 | tf_op jit(solution)/shard_map/ppermute | solution.py:246

commit v8 on v7

--- a/solution.py
+++ b/solution.py
@@ -57,7 +57,7 @@
     wide = (ROWS // 128, 128)
     return pl.pallas_call(
         pack_kernel,
-        out_shape=jax.ShapeDtypeStruct((PACKED, HEAD_DIM), jnp.bfloat16),
+        out_shape=pltpu.VMEM((PACKED, HEAD_DIM), jnp.bfloat16),
         in_specs=[VMEM] * 5,
         out_specs=VMEM,
         cost_estimate=pl.CostEstimate(flops=10000, bytes_accessed=MIB // 2, transcendentals=0),
@@ -69,15 +69,15 @@
 
 
 def attend_kernel(
-    queries_hbm, grads_hbm, own_hbm, near, far, opposite, own_s, near_s, far_s, opposite_s,
-    attention, grad_queries, own_part, near_part, far_part, opposite_part, swap_parts,
+    queries_hbm, grads_hbm, own, near, far, opposite, own_s, near_s, far_s, opposite_s,
+    attention_hbm, grad_queries_hbm, own_part, near_part, far_part, opposite_part, swap_parts,
     opposite_s_part, margin,
-    queries, grads, own, arrived, keys, values, keys_t, values_t, bias, scores, probs, grad_scores, acc_k, acc_v,
+    queries, grads, attention, grad_queries, arrived, left, keys, values, keys_t, values_t, bias, scores, probs, grad_scores, acc_k, acc_v,
 ):
     fetches = [
         pltpu.make_async_copy(source, target, arrived.at[number])
         for number, (source, target) in enumerate(
-            ((own_hbm, own), (queries_hbm, queries), (grads_hbm, grads))
+            ((queries_hbm, queries), (grads_hbm, grads))
         )
     ]
     for fetch in fetches:
@@ -94,9 +94,7 @@
         swap_parts.at[0], swap_parts.at[1], swap_parts.at[2], opposite_s_part,
     )
     totals = None
-    for block, span in spans()[::-1]:
-        if block == 0:
-            fetches[0].wait()
+    for block, span in spans():
         key = blocks[block][:ROWS, :]
         value = blocks[block][ROWS : 2 * ROWS, :]
         keys[span, :] = key
@@ -141,14 +139,15 @@
     def max_of(top):
         return jnp.max(top, axis=1, keepdims=True) * SCALE2
 
-    fetches[1].wait()
+    fetches[0].wait()
     top = total = None
     for block, span in spans():
         top = score_step(0, span, top)
     row_max = max_of(top)
     for block, span in spans():
         total = prob_step(0, span, row_max, total)
-    fetches[2].wait()
+    fetches[1].wait()
+    writes = []
     for head in range(HEADS):
         slot = head % 2
         query = queries[:, columns[head]]
@@ -167,6 +166,15 @@
             grad_scores[slot, :, span] = grad_score.astype(jnp.bfloat16)
         if head < HEADS - 1:
             row_max = max_of(top)
+        grad_queries[:, columns[head]] = dot(grad_scores[slot], keys[...]) * INV_ROOT
+        for kind, (source, target) in enumerate(
+            ((attention, attention_hbm), (grad_queries, grad_queries_hbm))
+        ):
+            write = pltpu.make_async_copy(
+                source.at[:, columns[head]], target.at[:, columns[head]], left.at[2 * head + kind]
+            )
+            write.start()
+            writes.append(write)
         query_t = query.T
         grad_t = grad_scaled.T
         for block, span in spans():
@@ -183,11 +191,11 @@
             else:
                 parts[block][:, :HEAD_DIM] = (part_k * INV_ROOT).astype(jnp.bfloat16).T
                 parts[block][:, HEAD_DIM:] = part_v.astype(jnp.bfloat16).T
-        grad_queries[:, columns[head]] = dot(grad_scores[slot], keys[...]) * INV_ROOT
+    for write in writes:
+        write.wait()
 
 
 def attend(queries, grads, blocks):
-    far_off = (queries, grads, blocks[0])
     width = HEADS * HEAD_DIM
     part = jax.ShapeDtypeStruct((ROWS, 2 * HEAD_DIM), jnp.bfloat16)
     return pl.pallas_call(
@@ -203,13 +211,15 @@
             part,
             jax.ShapeDtypeStruct((8, 8, HEAD_DIM), jnp.float32),
         ),
-        in_specs=[HBM] * 3 + [VMEM] * 7,
-        out_specs=(VMEM,) * 9,
+        in_specs=[HBM] * 2 + [VMEM] * BLOCKS,
+        out_specs=(HBM,) * 2 + (VMEM,) * 7,
         scratch_shapes=[
             pltpu.VMEM((ROWS, width), jnp.bfloat16),
             pltpu.VMEM((ROWS, width), jnp.bfloat16),
-            pltpu.VMEM((PACKED, HEAD_DIM), jnp.bfloat16),
-            pltpu.SemaphoreType.DMA((3,)),
+            pltpu.VMEM((ROWS, width), jnp.bfloat16),
+            pltpu.VMEM((ROWS, width), jnp.float32),
+            pltpu.SemaphoreType.DMA((2,)),
+            pltpu.SemaphoreType.DMA((2 * HEADS,)),
             pltpu.VMEM((PAIR_SPAN, HEAD_DIM), jnp.bfloat16),
             pltpu.VMEM((PAIR_SPAN, HEAD_DIM), jnp.bfloat16),
             pltpu.VMEM((HEAD_DIM, PAIR_SPAN), jnp.bfloat16),
@@ -227,7 +237,7 @@
             bytes_accessed=4 * MIB,
             transcendentals=HEADS * ROWS * PAIR_SPAN,
         ),
-    )(*(pltpu.with_memory_space_constraint(x, pltpu.HBM) for x in far_off), *blocks[1:])
+    )(*(pltpu.with_memory_space_constraint(x, pltpu.HBM) for x in (queries, grads)), *blocks)
 
 
 def at(half, chip, core):
@@ -270,7 +280,7 @@
     far_sum = far_p + swapped[2]
     near_part = send(near_sum, back)
     far_part = send(far_sum, ahead)
-    far_part, margin = lax.optimization_barrier((far_part, margin))
+    _, far_part, margin = lax.optimization_barrier((near_sum, far_part, margin))
     turns = [[(place, place ^ bits) for place in range(256)] for bits in (8, 16, 24)]
     margin = sum((lax.ppermute(margin, ("pb", "ka"), turn) for turn in turns), margin)
     total = own_p.astype(wide) + swapped[0] + near_part + far_part

time: 63.6 us -> 60.6 us (0.953)
  the two profiles are of different devices: /device:TPU:6 before, /device:TPU:8 now
where the time goes in v8:
time: 60.6 us; the launch traced here: 59.7 us
  waiting for transfers between devices  23 us (38%)
  starting transfers between devices  20 us (33%)
  Pallas kernels  14.6 us (24%)
  local copies, waits for them, and re-layouts  1.23 us (2%)
  between operations  0.7 us (1%)
    pallas_call x1, Pallas kernels, attend(): pl.pallas_call(attend_kernel, out_shape=(jax.ShapeDtypeStruct((ROWS, widt...  13.5 us
    ppermute x12, waiting for transfers between devices, send(): return lax.ppermute(block, 'ka', route)  12.1 us
    all_to_all x1, starting transfers between devices, per_device(): lax.all_to_all(margin, 'pb', 0, 0, axis_index_groups=columns, tiled=True)  8.46 us
    ppermute x12, starting transfers between devices, send(): return lax.ppermute(block, 'ka', route)  8.01 us
    all_to_all x1, waiting for transfers between devices, per_device(): lax.all_to_all(margin, 'pb', 0, 0, axis_index_groups=columns, tiled=True)  7.53 us
    ppermute x3, starting transfers between devices, per_device(): lax.ppermute(margin, ('pb', 'ka'), turn)  3.57 us
    ppermute x3, waiting for transfers between devices, per_device(): lax.ppermute(margin, ('pb', 'ka'), turn)  3.42 us
  transfers between devices with their start and end apart: 16, of which 7 were waited for; matrix products, arithmetic and copies ran while one was open for 1% of the time, Pallas kernels for 0%

profile of v8, /device:TPU:8, one launch (start us, length us, event | category | flops | bytes accessed | tf_op | source)
XLA Modules:
  0.0 59.7 jit_solution(5606686667625592589)
XLA Ops:
  0.6 1.0 %shard_map.110.own = bf16[528,128]{1,0:T(8,128)(2,1)S(1)} custom-call(bf16[256,128]{1,0:T(8,128)(2,1)} %keys.1, bf16[256,128]{1,0:T(8,128)(2,1)} %values.1, f32[2,128]{1,0:T(2,128)} %bitcast.13, s32[2,128]{1,0:T(2,128)} %bitcast.14, s32[2,128]{1,0:T(2,128)} %bitcast.15), custom_call_target="tpu_custom_call" | custom-call | flops 10000 | bytes 524288 | tf_op jit(solution)/shard_map/pallas_call | solution.py:58
  1.7 2.8 %collective-permute-start.1 = (bf16[528,128]{1,0:T(8,128)(2,1)S(1)}, bf16[528,128]{1,0:T(8,128)(2,1)S(1)}, u32[]{:S(2)}, u32[]{:S(2)}) collective-permute-start(bf16[528,128]{1,0:T(8,128)(2,1)S(1)} %shard_map.110.own), channel_id=1, source_target_pairs={{2,0},{7,1},{4,2},{1,3},{6,4},{3,5},{0,6},{5,7},{10,8},{15,9},{12,... | collective-permute-start | bytes 405512 | tf_op jit(solution)/shard_map/ppermute | solution.py:256
  4.5 0.0 collective-permute-start
  4.5 0.0 collective-permute-start.3
  4.5 3.6 %collective-permute-done.1.far = bf16[528,128]{1,0:T(8,128)(2,1)S(1)} collective-permute-done((bf16[528,128]{1,0:T(8,128)(2,1)S(1)}, bf16[528,128]{1,0:T(8,128)(2,1)S(1)}, u32[]{:S(2)}, u32[]{:S(2)}) %collective-permute-start.1) | collective-permute-done | bytes 135200 | tf_op jit(solution)/shard_map/ppermute | solution.py:256
  8.1 0.0 collective-permute-start.5
  8.1 2.6 %collective-permute-done.near = bf16[528,128]{1,0:T(8,128)(2,1)S(1)} collective-permute-done((bf16[528,128]{1,0:T(8,128)(2,1)S(1)}, bf16[528,128]{1,0:T(8,128)(2,1)S(1)}, u32[]{:S(2)}, u32[]{:S(2)}) %collective-permute-start) | collective-permute-done | bytes 135200 | tf_op jit(solution)/shard_map/ppermute | solution.py:256
  10.7 0.0 collective-permute-start.6
  10.7 0.6 %collective-permute-start.4 = (bf16[528,128]{1,0:T(8,128)(2,1)S(1)}, bf16[528,128]{1,0:T(8,128)(2,1)S(1)}, u32[]{:S(2)}, u32[]{:S(2)}) collective-permute-start(bf16[528,128]{1,0:T(8,128)(2,1)S(1)} %collective-permute-done.near), channel_id=1, source_target_pairs={{0,1},{1,0},{2,3},{3,2},{4,5},{5,4},{6,7},{7,6},{8,9},{9,8},{10,11... | collective-permute-start | bytes 405512 | tf_op jit(solution)/shard_map/ppermute | solution.py:256
  11.4 1.5 %collective-permute-start.2 = (bf16[528,128]{1,0:T(8,128)(2,1)S(1)}, bf16[528,128]{1,0:T(8,128)(2,1)S(1)}, u32[]{:S(2)}, u32[]{:S(2)}) collective-permute-start(bf16[528,128]{1,0:T(8,128)(2,1)S(1)} %collective-permute-done.near), channel_id=1, source_target_pairs={{0,2},{1,7},{2,4},{3,1},{4,6},{5,3},{6,0},{7,5},{8,10},{9,15},{10,... | collective-permute-start | bytes 405512 | tf_op jit(solution)/shard_map/ppermute | solution.py:256
  12.9 0.0 collective-permute-done.3.own_s
  12.9 0.0 collective-permute-done.5.far_s
  12.9 2.3 %collective-permute-done.6.opposite_s = bf16[528,128]{1,0:T(8,128)(2,1)S(1)} collective-permute-done((bf16[528,128]{1,0:T(8,128)(2,1)S(1)}, bf16[528,128]{1,0:T(8,128)(2,1)S(1)}, u32[]{:S(2)}, u32[]{:S(2)}) %collective-permute-start.6) | collective-permute-done | bytes 135200 | tf_op jit(solution)/shard_map/ppermute | solution.py:256
  15.2 0.0 collective-permute-done.4.near_s
  15.2 2.4 %collective-permute-done.2.opposite = bf16[528,128]{1,0:T(8,128)(2,1)S(1)} collective-permute-done((bf16[528,128]{1,0:T(8,128)(2,1)S(1)}, bf16[528,128]{1,0:T(8,128)(2,1)S(1)}, u32[]{:S(2)}, u32[]{:S(2)}) %collective-permute-start.2) | collective-permute-done | bytes 135200 | tf_op jit(solution)/shard_map/ppermute | solution.py:256
  17.6 13.5 %shard_map.111 = (bf16[256,768]{1,0:T(8,128)(2,1)}, f32[256,768]{1,0:T(8,128)}, bf16[256,256]{1,0:T(8,128)(2,1)S(1)}, bf16[256,256]{1,0:T(8,128)(2,1)S(1)}, bf16...) custom-call(bf16[256,768]{1,0:T(8,128)(2,1)} %queries_hbm.1, ...), custom_call_target="tpu_custom_call" | custom-call | flops 4831838208 | bytes 4194304 | tf_op jit(solution)/shard_map/pallas_call | solution.py:201
  31.1 0.3 collective-permute-start.7
  31.4 0.6 collective-permute-start.8
  32.0 0.0 collective-permute-start.9
  32.0 1.1 %collective-permute-done.7 = bf16[3,256,256]{2,1,0:T(8,128)(2,1)S(1)} collective-permute-done((bf16[3,256,256]{2,1,0:T(8,128)(2,1)S(1)}, bf16[3,256,256]{2,1,0:T(8,128)(2,1)S(1)}, u32[]{:S(2)}, u32[]{:S(2)}) %collective-permute-start.7) | collective-permute-done | bytes 393248 | tf_op jit(solution)/shard_map/ppermute | solution.py:256
  33.2 8.5 %all-to-all-start = ((f32[8,8,128]{2,1,0:T(8,128)}), f32[8,8,128]{2,1,0:T(8,128)S(1)}, u32[]{:S(2)}, u32[]{:S(2)}) async-start(f32[8,8,128]{2,1,0:T(8,128)} %get-tuple-element.28), calls=%async_computation | async-start | bytes 65536 | tf_op jit(solution)/shard_map/all_to_all | solution.py:276
  41.6 0.5 collective-permute-start.11
  42.1 7.5 %all-to-all-done = f32[8,8,128]{2,1,0:T(8,128)S(1)} async-done(((f32[8,8,128]{2,1,0:T(8,128)}), f32[8,8,128]{2,1,0:T(8,128)S(1)}, u32[]{:S(2)}, u32[]{:S(2)}) %all-to-all-start) | async-done | bytes 32800 | tf_op jit(solution)/shard_map/all_to_all | solution.py:276
  49.7 0.0 collective-permute-done.8
  49.7 0.0 collective-permute-done.9
  49.7 0.1 fusion.2
  49.7 0.0 collective-permute-done.11
  49.8 1.7 %collective-permute-start.14 = (f32[8,128]{1,0:T(8,128)S(1)}, f32[8,128]{1,0:T(8,128)S(1)}, u32[]{:S(2)}, u32[]{:S(2)}) collective-permute-start(f32[8,128]{1,0:T(8,128)S(1)} %reduce_sum.9), channel_id=1, source_target_pairs={{0,24},{1,25},{2,26},{3,27},{4,28},{5,29},{6,30},{7,31},{8,16},{9,... | collective-permute-start | bytes 12296 | tf_op jit(solution)/shard_map/ppermute | solution.py:285
  51.4 1.9 %collective-permute-start.13 = (f32[8,128]{1,0:T(8,128)S(1)}, f32[8,128]{1,0:T(8,128)S(1)}, u32[]{:S(2)}, u32[]{:S(2)}) collective-permute-start(f32[8,128]{1,0:T(8,128)S(1)} %reduce_sum.9), channel_id=1, source_target_pairs={{0,16},{1,17},{2,18},{3,19},{4,20},{5,21},{6,22},{7,23},{8,24},{9,... | collective-permute-start | bytes 12296 | tf_op jit(solution)/shard_map/ppermute | solution.py:285
  53.3 0.0 collective-permute-start.12
  53.3 1.7 %collective-permute-start.10 = (bf16[256,256]{1,0:T(8,128)(2,1)S(1)}, bf16[256,256]{1,0:T(8,128)(2,1)S(1)}, u32[]{:S(2)}, u32[]{:S(2)}) collective-permute-start(bf16[256,256]{1,0:T(8,128)(2,1)S(1)} %fusion.2), channel_id=1, source_target_pairs={{2,0},{7,1},{4,2},{1,3},{6,4},{3,5},{0,6},{5,7},{10,8},{15,9},{12,... | collective-permute-start | bytes 393224 | tf_op jit(solution)/shard_map/ppermute | solution.py:256
  55.0 0.0 collective-permute-done.14
  55.0 0.0 collective-permute-done.13
  55.0 3.4 %collective-permute-done.12 = f32[8,128]{1,0:T(8,128)S(1)} collective-permute-done((f32[8,128]{1,0:T(8,128)S(1)}, f32[8,128]{1,0:T(8,128)S(1)}, u32[]{:S(2)}, u32[]{:S(2)}) %collective-permute-start.12) | collective-permute-done | bytes 4128 | tf_op jit(solution)/shard_map/ppermute | solution.py:285
  58.4 0.5 slice_bitcast_fusion
  58.9 0.0 collective-permute-done.10
  58.9 0.1 fusion.4
  59.0 0.7 %fusion.5 = (f32[256,128]{1,0:T(8,128)}, f32[256,128]{1,0:T(8,128)}) fusion(f32[256,256]{1,0:T(8,128)S(1)} %fusion.4), kind=kLoop, calls=%fused_computation.10 | loop fusion | bytes 524288 | tf_op jit(solution)/shard_map/slice | solution.py:287
  (3 shorter events, 0.0 us)
Async XLA Ops:
  1.7 6.5 %collective-permute-start.1 = (bf16[528,128]{1,0:T(8,128)(2,1)S(1)}, bf16[528,128]{1,0:T(8,128)(2,1)S(1)}, u32[]{:S(2)}, u32[]{:S(2)}) collective-permute-start(bf16[528,128]{1,0:T(8,128)(2,1)S(1)} %shard_map.110.own), channel_id=1, source_target_pairs={{2,0},{7,1},{4,2},{1,3},{6,4},{3,5},{0,6},{5,7},{10,8},{15,9},{12,... | collective-permute-start | bytes 405512 | tf_op jit(solution)/shard_map/ppermute | solution.py:256
  4.5 6.2 %collective-permute-start = (bf16[528,128]{1,0:T(8,128)(2,1)S(1)}, bf16[528,128]{1,0:T(8,128)(2,1)S(1)}, u32[]{:S(2)}, u32[]{:S(2)}) collective-permute-start(bf16[528,128]{1,0:T(8,128)(2,1)S(1)} %shard_map.110.own), channel_id=1, source_target_pairs={{0,2},{1,7},{2,4},{3,1},{4,6},{5,3},{6,0},{7,5},{8,10},{9,15},{10,... | collective-permute-start | bytes 405512 | tf_op jit(solution)/shard_map/ppermute | solution.py:256
  4.5 8.4 %collective-permute-start.3 = (bf16[528,128]{1,0:T(8,128)(2,1)S(1)}, bf16[528,128]{1,0:T(8,128)(2,1)S(1)}, u32[]{:S(2)}, u32[]{:S(2)}) collective-permute-start(bf16[528,128]{1,0:T(8,128)(2,1)S(1)} %shard_map.110.own), channel_id=1, source_target_pairs={{0,1},{1,0},{2,3},{3,2},{4,5},{5,4},{6,7},{7,6},{8,9},{9,8},{10,11... | collective-permute-start | bytes 405512 | tf_op jit(solution)/shard_map/ppermute | solution.py:256
  8.1 4.7 %collective-permute-start.5 = (bf16[528,128]{1,0:T(8,128)(2,1)S(1)}, bf16[528,128]{1,0:T(8,128)(2,1)S(1)}, u32[]{:S(2)}, u32[]{:S(2)}) collective-permute-start(bf16[528,128]{1,0:T(8,128)(2,1)S(1)} %collective-permute-done.1.far), channel_id=1, source_target_pairs={{0,1},{1,0},{2,3},{3,2},{4,5},{5,4},{6,7},{7,6},{8,9},{9,8},{10,11... | collective-permute-start | bytes 405512 | tf_op jit(solution)/shard_map/ppermute | solution.py:256
  10.7 4.4 %collective-permute-start.6 = (bf16[528,128]{1,0:T(8,128)(2,1)S(1)}, bf16[528,128]{1,0:T(8,128)(2,1)S(1)}, u32[]{:S(2)}, u32[]{:S(2)}) collective-permute-start(bf16[528,128]{1,0:T(8,128)(2,1)S(1)} %collective-permute-done.near), channel_id=1, source_target_pairs={{0,3},{1,6},{2,5},{3,0},{4,7},{5,2},{6,1},{7,4},{8,11},{9,14},{10,... | collective-permute-start | bytes 405512 | tf_op jit(solution)/shard_map/ppermute | solution.py:256
  10.7 4.4 %collective-permute-start.4 = (bf16[528,128]{1,0:T(8,128)(2,1)S(1)}, bf16[528,128]{1,0:T(8,128)(2,1)S(1)}, u32[]{:S(2)}, u32[]{:S(2)}) collective-permute-start(bf16[528,128]{1,0:T(8,128)(2,1)S(1)} %collective-permute-done.near), channel_id=1, source_target_pairs={{0,1},{1,0},{2,3},{3,2},{4,5},{5,4},{6,7},{7,6},{8,9},{9,8},{10,11... | collective-permute-start | bytes 405512 | tf_op jit(solution)/shard_map/ppermute | solution.py:256
  11.4 6.2 %collective-permute-start.2 = (bf16[528,128]{1,0:T(8,128)(2,1)S(1)}, bf16[528,128]{1,0:T(8,128)(2,1)S(1)}, u32[]{:S(2)}, u32[]{:S(2)}) collective-permute-start(bf16[528,128]{1,0:T(8,128)(2,1)S(1)} %collective-permute-done.near), channel_id=1, source_target_pairs={{0,2},{1,7},{2,4},{3,1},{4,6},{5,3},{6,0},{7,5},{8,10},{9,15},{10,... | collective-permute-start | bytes 405512 | tf_op jit(solution)/shard_map/ppermute | solution.py:256
  31.1 2.0 %collective-permute-start.7 = (bf16[3,256,256]{2,1,0:T(8,128)(2,1)S(1)}, bf16[3,256,256]{2,1,0:T(8,128)(2,1)S(1)}, u32[]{:S(2)}, u32[]{:S(2)}) collective-permute-start(bf16[3,256,256]{2,1,0:T(8,128)(2,1)S(1)} %get-tuple-element.23), channel_id=1, source_target_pairs={{0,1},{1,0},{2,3},{3,2},{4,5},{5,4},{6,7},{7,6},{8,9},{9,8},{10,11... | collective-permute-start | bytes 1179656 | tf_op jit(solution)/shard_map/ppermute | solution.py:256
  31.4 18.2 %collective-permute-start.8 = (bf16[256,256]{1,0:T(8,128)(2,1)S(1)}, bf16[256,256]{1,0:T(8,128)(2,1)S(1)}, u32[]{:S(2)}, u32[]{:S(2)}) collective-permute-start(bf16[256,256]{1,0:T(8,128)(2,1)S(1)} %get-tuple-element.27), channel_id=1, source_target_pairs={{2,0},{7,1},{4,2},{1,3},{6,4},{3,5},{0,6},{5,7},{10,8},{15,9},{12,... | collective-permute-start | bytes 393224 | tf_op jit(solution)/shard_map/ppermute | solution.py:256
  32.0 17.7 %collective-permute-start.9 = (bf16[256,256]{1,0:T(8,128)(2,1)S(1)}, bf16[256,256]{1,0:T(8,128)(2,1)S(1)}, u32[]{:S(2)}, u32[]{:S(2)}) collective-permute-start(bf16[256,256]{1,0:T(8,128)(2,1)S(1)} %get-tuple-element.30), channel_id=1, source_target_pairs={{3,0},{6,1},{5,2},{0,3},{7,4},{2,5},{1,6},{4,7},{11,8},{14,9},{13,... | collective-permute-start | bytes 393224 | tf_op jit(solution)/shard_map/ppermute | solution.py:256
  33.2 16.5 %all-to-all-start = ((f32[8,8,128]{2,1,0:T(8,128)}), f32[8,8,128]{2,1,0:T(8,128)S(1)}, u32[]{:S(2)}, u32[]{:S(2)}) async-start(f32[8,8,128]{2,1,0:T(8,128)} %get-tuple-element.28), calls=%async_computation | async-start | bytes 65536 | tf_op jit(solution)/shard_map/all_to_all | solution.py:276
  41.6 8.1 %collective-permute-start.11 = (bf16[256,256]{1,0:T(8,128)(2,1)S(1)}, bf16[256,256]{1,0:T(8,128)(2,1)S(1)}, u32[]{:S(2)}, u32[]{:S(2)}) collective-permute-start(bf16[256,256]{1,0:T(8,128)(2,1)S(1)} %bitcast_add_fusion), channel_id=1, source_target_pairs={{0,2},{1,7},{2,4},{3,1},{4,6},{5,3},{6,0},{7,5},{8,10},{9,15},{10,... | collective-permute-start | bytes 393224 | tf_op jit(solution)/shard_map/ppermute | solution.py:256
  49.8 5.2 %collective-permute-start.14 = (f32[8,128]{1,0:T(8,128)S(1)}, f32[8,128]{1,0:T(8,128)S(1)}, u32[]{:S(2)}, u32[]{:S(2)}) collective-permute-start(f32[8,128]{1,0:T(8,128)S(1)} %reduce_sum.9), channel_id=1, source_target_pairs={{0,24},{1,25},{2,26},{3,27},{4,28},{5,29},{6,30},{7,31},{8,16},{9,... | collective-permute-start | bytes 12296 | tf_op jit(solution)/shard_map/ppermute | solution.py:285
  51.4 3.6 %collective-permute-start.13 = (f32[8,128]{1,0:T(8,128)S(1)}, f32[8,128]{1,0:T(8,128)S(1)}, u32[]{:S(2)}, u32[]{:S(2)}) collective-permute-start(f32[8,128]{1,0:T(8,128)S(1)} %reduce_sum.9), channel_id=1, source_target_pairs={{0,16},{1,17},{2,18},{3,19},{4,20},{5,21},{6,22},{7,23},{8,24},{9,... | collective-permute-start | bytes 12296 | tf_op jit(solution)/shard_map/ppermute | solution.py:285
  53.3 5.1 %collective-permute-start.12 = (f32[8,128]{1,0:T(8,128)S(1)}, f32[8,128]{1,0:T(8,128)S(1)}, u32[]{:S(2)}, u32[]{:S(2)}) collective-permute-start(f32[8,128]{1,0:T(8,128)S(1)} %reduce_sum.9), channel_id=1, source_target_pairs={{0,8},{1,9},{2,10},{3,11},{4,12},{5,13},{6,14},{7,15},{8,0},{9,1},... | collective-permute-start | bytes 12296 | tf_op jit(solution)/shard_map/ppermute | solution.py:285
  53.3 5.6 %collective-permute-start.10 = (bf16[256,256]{1,0:T(8,128)(2,1)S(1)}, bf16[256,256]{1,0:T(8,128)(2,1)S(1)}, u32[]{:S(2)}, u32[]{:S(2)}) collective-permute-start(bf16[256,256]{1,0:T(8,128)(2,1)S(1)} %fusion.2), channel_id=1, source_target_pairs={{2,0},{7,1},{4,2},{1,3},{6,4},{3,5},{0,6},{5,7},{10,8},{15,9},{12,... | collective-permute-start | bytes 393224 | tf_op jit(solution)/shard_map/ppermute | solution.py:256

commit v9 on v6

--- a/solution.py
+++ b/solution.py
@@ -15,6 +15,8 @@
 CHIPS = 4
 PAIRS = 32
 PACKED = 2 * ROWS + 16
+EXTRA = 16
+LIMBS = tuple(2.0 ** (6 - 5 * place) for place in range(6))
 NEG = -1e30
 INV_ROOT = 1.0 / math.sqrt(HEAD_DIM)
 SCALE2 = INV_ROOT * math.log2(math.e)
@@ -28,40 +30,50 @@
     return jnp.dot(a, b, preferred_element_type=jnp.float32)
 
 
-def split(value):
-    high = value.astype(jnp.bfloat16).astype(jnp.float32)
-    middle = (value - high).astype(jnp.bfloat16).astype(jnp.float32)
-    return high, middle, value - high - middle
-
-
-def pack_kernel(keys, values, logprob, docs, response, packed):
+def pack_kernel(
+    keys, values, logprob, docs, response, queries_hbm, grads_hbm,
+    packed, sums, queries, grads, arrived,
+):
+    fetches = [
+        pltpu.make_async_copy(source, target, arrived.at[number])
+        for number, (source, target) in enumerate(((queries_hbm, queries), (grads_hbm, grads)))
+    ]
+    for fetch in fetches:
+        fetch.start()
+    pair = lax.axis_index("pb") * 2 + lax.axis_index("ka") // BLOCKS
     odd = (docs[...] & 1).astype(jnp.float32)
     even = 1.0 - odd
     live = response[...].astype(jnp.float32)
     scored = logprob[...] * live
-    first, second, first_live, second_live, count = (
-        jnp.sum(term, keepdims=True)
-        for term in (scored * even, scored * odd, live * even, live * odd, even)
-    )
-    terms = (*split(first), *split(second), first_live, second_live, count)
-    lane = lax.broadcasted_iota(jnp.int32, (16, HEAD_DIM), 1)
-    table = jnp.zeros((16, HEAD_DIM), jnp.float32)
-    for place, term in enumerate(terms):
-        table = jnp.where(lane == place, term, table)
+    lane = lax.broadcasted_iota(jnp.int32, (8, HEAD_DIM), 1)
+    table = jnp.zeros((8, HEAD_DIM), jnp.float32)
+    for kind, term in enumerate((scored * even, scored * odd, live * even, live * odd)):
+        table = jnp.where(lane == kind * PAIRS + pair, jnp.sum(term, keepdims=True), table)
+    sums[...] = table
     packed[:ROWS, :] = keys[...]
     packed[ROWS : 2 * ROWS, :] = values[...]
-    packed[2 * ROWS :, :] = table.astype(jnp.bfloat16)
-
-
-def pack(keys, values, logprob, docs, response):
+    count = jnp.broadcast_to(jnp.sum(even, keepdims=True), (16, HEAD_DIM))
+    packed[2 * ROWS :, :] = count.astype(jnp.bfloat16)
+    for fetch in fetches:
+        fetch.wait()
+
+
+def pack(keys, values, logprob, docs, response, queries, grads):
     wide = (ROWS // 128, 128)
+    far_off = (pltpu.with_memory_space_constraint(x, pltpu.HBM) for x in (queries, grads))
     return pl.pallas_call(
         pack_kernel,
-        out_shape=jax.ShapeDtypeStruct((PACKED, HEAD_DIM), jnp.bfloat16),
-        in_specs=[VMEM] * 5,
-        out_specs=VMEM,
-        cost_estimate=pl.CostEstimate(flops=10000, bytes_accessed=MIB // 2, transcendentals=0),
-    )(keys, values, logprob.reshape(wide), docs.reshape(wide), response.reshape(wide))
+        out_shape=(
+            pltpu.VMEM((PACKED, HEAD_DIM), jnp.bfloat16),
+            pltpu.VMEM((8, HEAD_DIM), jnp.float32),
+            pltpu.VMEM(queries.shape, jnp.bfloat16),
+            pltpu.VMEM(grads.shape, jnp.bfloat16),
+        ),
+        in_specs=[VMEM] * 5 + [HBM] * 2,
+        out_specs=(VMEM,) * 4,
+        scratch_shapes=[pltpu.SemaphoreType.DMA((2,))],
+        cost_estimate=pl.CostEstimate(flops=10000, bytes_accessed=2 * MIB, transcendentals=0),
+    )(keys, values, logprob.reshape(wide), docs.reshape(wide), response.reshape(wide), *far_off)
 
 
 def spans():
@@ -69,19 +81,11 @@
 
 
 def attend_kernel(
-    queries_hbm, grads_hbm, own_hbm, near, far, opposite, own_s, near_s, far_s, opposite_s,
+    queries, grads, table, own, near, far, opposite, own_s, near_s, far_s, opposite_s,
     attention, grad_queries, own_part, near_part, far_part, opposite_part, swap_parts,
     opposite_s_part,
-    queries, grads, own, arrived, keys, values, keys_t, values_t, bias, scores, probs, grad_scores, acc_k, acc_v,
+    keys, values, keys_t, values_t, bias, scores, probs, grad_scores, acc_k, acc_v,
 ):
-    fetches = [
-        pltpu.make_async_copy(source, target, arrived.at[number])
-        for number, (source, target) in enumerate(
-            ((own_hbm, own), (queries_hbm, queries), (grads_hbm, grads))
-        )
-    ]
-    for fetch in fetches:
-        fetch.start()
     place = lax.axis_index("ka")
     core = lax.rem(place, 2)
     chip = lax.rem(place // 2, CHIPS)
@@ -93,10 +97,8 @@
         own_part, near_part, far_part, opposite_part,
         swap_parts.at[0], swap_parts.at[1], swap_parts.at[2], opposite_s_part,
     )
-    totals = None
-    for block, span in spans()[::-1]:
-        if block == 0:
-            fetches[0].wait()
+    count = None
+    for block, span in spans():
         key = blocks[block][:ROWS, :]
         value = blocks[block][ROWS : 2 * ROWS, :]
         keys[span, :] = key
@@ -104,10 +106,19 @@
         keys_t[:, span] = key.T
         values_t[:, span] = value.T
         term = blocks[block][2 * ROWS :, :].astype(jnp.float32)
-        totals = term if totals is None else totals + term
-    totals = totals[:8, :]
-    wide = lax.broadcasted_iota(jnp.int32, (8, HEAD_DIM), 1)
-    cut = jnp.sum(jnp.where(wide == 8, totals, 0.0), axis=1, keepdims=True)[:1].astype(jnp.int32)
+        count = term if count is None else count + term
+    cut = count[:1, :1].astype(jnp.int32)
+    rest = jnp.abs(table[:1, :])
+    place_row = lax.broadcasted_iota(jnp.int32, (EXTRA, HEAD_DIM), 0)
+    limbs = jnp.zeros((EXTRA, HEAD_DIM), jnp.float32)
+    for number, scale in enumerate(LIMBS):
+        limb = jnp.floor(rest * (1.0 / scale))
+        rest = rest - limb * scale
+        limbs = jnp.where(place_row == number, limb, limbs)
+    limbs = limbs.astype(jnp.bfloat16)
+    for part in parts:
+        part[ROWS:, :HEAD_DIM] = limbs
+        part[ROWS:, HEAD_DIM:] = limbs
     row = first_row + lax.broadcasted_iota(jnp.int32, (ROWS, ROWS), 0)
     lane = lax.broadcasted_iota(jnp.int32, (ROWS, ROWS), 1)
     start = jnp.where(row >= cut, cut, 0)
@@ -121,24 +132,24 @@
     def score_step(head, span, top):
         score = dot(queries[:, columns[head]], keys_t[:, span]) + bias[:, span]
         scores[head % 2, :, span] = score
-        return score if top is None else jnp.maximum(top, score)
+        folded = jnp.maximum(score[:, :128], score[:, 128:])
+        return folded if top is None else jnp.maximum(top, folded)
 
     def prob_step(head, span, row_max, total):
         prob = jnp.exp2(scores[head % 2, :, span] * SCALE2 - row_max)
         probs[head % 2, :, span] = prob.astype(jnp.bfloat16)
-        return prob if total is None else total + prob
+        folded = prob[:, :128] + prob[:, 128:]
+        return folded if total is None else total + folded
 
     def max_of(top):
         return jnp.max(top, axis=1, keepdims=True) * SCALE2
 
-    fetches[1].wait()
     top = total = None
     for block, span in spans():
         top = score_step(0, span, top)
     row_max = max_of(top)
     for block, span in spans():
         total = prob_step(0, span, row_max, total)
-    fetches[2].wait()
     for head in range(HEADS):
         slot = head % 2
         query = queries[:, columns[head]]
@@ -171,15 +182,14 @@
                 acc_k[:, span] = part_k
                 acc_v[:, span] = part_v
             else:
-                parts[block][:, :HEAD_DIM] = (part_k * INV_ROOT).astype(jnp.bfloat16).T
-                parts[block][:, HEAD_DIM:] = part_v.astype(jnp.bfloat16).T
+                parts[block][:ROWS, :HEAD_DIM] = (part_k * INV_ROOT).astype(jnp.bfloat16).T
+                parts[block][:ROWS, HEAD_DIM:] = part_v.astype(jnp.bfloat16).T
         grad_queries[:, columns[head]] = dot(grad_scores[slot], keys[...]) * INV_ROOT
 
 
-def attend(queries, grads, blocks):
-    far_off = (queries, grads, blocks[0])
+def attend(queries, grads, table, blocks):
     width = HEADS * HEAD_DIM
-    part = jax.ShapeDtypeStruct((ROWS, 2 * HEAD_DIM), jnp.bfloat16)
+    part = jax.ShapeDtypeStruct((ROWS + EXTRA, 2 * HEAD_DIM), jnp.bfloat16)
     return pl.pallas_call(
         attend_kernel,
         out_shape=(
@@ -189,16 +199,12 @@
             part,
             part,
             part,
-            jax.ShapeDtypeStruct((3, ROWS, 2 * HEAD_DIM), jnp.bfloat16),
+            jax.ShapeDtypeStruct((3, ROWS + EXTRA, 2 * HEAD_DIM), jnp.bfloat16),
             part,
         ),
-        in_specs=[HBM] * 3 + [VMEM] * 7,
+        in_specs=[VMEM] * (3 + BLOCKS),
         out_specs=(VMEM,) * 8,
         scratch_shapes=[
-            pltpu.VMEM((ROWS, width), jnp.bfloat16),
-            pltpu.VMEM((ROWS, width), jnp.bfloat16),
-            pltpu.VMEM((PACKED, HEAD_DIM), jnp.bfloat16),
-            pltpu.SemaphoreType.DMA((3,)),
             pltpu.VMEM((PAIR_SPAN, HEAD_DIM), jnp.bfloat16),
             pltpu.VMEM((PAIR_SPAN, HEAD_DIM), jnp.bfloat16),
             pltpu.VMEM((HEAD_DIM, PAIR_SPAN), jnp.bfloat16),
@@ -216,7 +222,7 @@
             bytes_accessed=4 * MIB,
             transcendentals=HEADS * ROWS * PAIR_SPAN,
         ),
-    )(*(pltpu.with_memory_space_constraint(x, pltpu.HBM) for x in far_off), *blocks[1:])
+    )(queries, grads, table, *blocks)
 
 
 def at(half, chip, core):
@@ -234,28 +240,30 @@
     def send(block, route):
         return lax.ppermute(block, "ka", route)
 
-    own = pack(key_heads, value_heads, token_logprob, doc_ids, response)
+    def exchange(table, axis, masks):
+        extent = range(lax.axis_size(axis))
+        routes = [[(place, place ^ mask) for place in extent] for mask in masks]
+        return sum((lax.ppermute(table, axis, route) for route in routes), table)
+
+    own, table, queries, grad_output = pack(
+        key_heads, value_heads, token_logprob, doc_ids, response, queries, grad_output
+    )
     near = send(own, ahead)
     far = send(own, back)
     own_s = send(own, swap)
+    own_s, table = lax.optimization_barrier((own_s, table))
+    table = exchange(table, "pb", (4, 8, 12))
+    table = exchange(table, "ka", (8,))
     opposite = send(near, ahead)
     opposite_s = send(near, cross)
     near_s = send(near, swap)
     far_s = send(far, swap)
+    near_s, table = lax.optimization_barrier((near_s, table))
+    table = exchange(table, "pb", (1, 2, 3))
 
     blocks = (own, near, far, opposite, own_s, near_s, far_s, opposite_s)
-    line = sum(block[2 * ROWS].astype(jnp.float32) for block in blocks)
-    margin = (line[0] + line[1] + line[2]) / line[6] - (line[3] + line[4] + line[5]) / line[7]
-    peers = [
-        [(number // 2) * 16 + (number % 2) * BLOCKS + rank for number in range(PAIRS)]
-        for rank in range(BLOCKS)
-    ]
-    margin, near = lax.optimization_barrier((jnp.broadcast_to(margin, (64, 128)), near))
-    blocks = (own, near, *blocks[2:])
-    margins = lax.all_gather(margin, ("pb", "ka"), axis_index_groups=peers)
-    margins = lax.optimization_barrier(margins)
     attention, grad_queries, own_p, near_p, far_p, opposite_p, swap_p, opposite_s_p = attend(
-        queries, grad_output, blocks
+        queries, grad_output, table, blocks
     )
     passed = send(opposite_p, back)
     passed_s = send(opposite_s_p, cross_back)
@@ -266,7 +274,11 @@
     near_part = send(near_sum, back)
     far_part = send(far_sum, ahead)
     total = own_p.astype(wide) + swapped[0] + near_part + far_part
-    return (attention, grad_queries, total[:, :HEAD_DIM], total[:, HEAD_DIM:], margins[:, 0, 0])
+    grad_keys, grad_values = total[:ROWS, :HEAD_DIM], total[:ROWS, HEAD_DIM:]
+    sums = sum(total[ROWS + number, :HEAD_DIM] * scale for number, scale in enumerate(LIMBS))
+    sums = sums.reshape(4, PAIRS)
+    margins = sums[1] / sums[3] - sums[0] / sums[2]
+    return (attention, grad_queries, grad_keys, grad_values, margins)
 
 
 def solution(mesh):

time: 184 us -> 61.5 us (0.33)
  waiting for transfers between devices: 136 us -> 15.4 us
  starting transfers between devices: 8.08 us -> 28.5 us
  between operations: 19.2 us -> 0.69 us
  local copies, waits for them, and re-layouts: 3.72 us -> 0.72 us
    all_gather x1 -> x0, waiting for transfers between devices: 116 us -> none  [per_device(): margins = lax.all_gather(margin, ('pb', 'ka'), axis_index_groups=peers)]
    ppermute x0 -> x7, starting transfers between devices: none -> 14.5 us  [exchange(): return sum((lax.ppermute(table, axis, route) for route in routes), table)]
    ppermute x12, waiting for transfers between devices: 19.8 us -> 9.99 us  [send(): return lax.ppermute(block, 'ka', route)]
    ppermute x12, starting transfers between devices: 8.04 us -> 14 us  [send(): return lax.ppermute(block, 'ka', route)]
    ppermute x0 -> x7, waiting for transfers between devices: none -> 5.44 us  [exchange(): return sum((lax.ppermute(table, axis, route) for route in routes), table)]
    slice x3 -> x1, local copies, waits for them, and re-layouts: 3.1 us -> 0.72 us  [per_device(): grad_keys, grad_values = (total[:ROWS, :HEAD_DIM], total[:ROWS, HEAD_DIM:])]
  transfers between devices with their start and end apart: 13 -> 19, of which waited for: 9 -> 8; matrix products, arithmetic and copies ran while one was open for 0% -> 0% of each run, Pallas kernels for 7% -> 0%
where the time goes in v9:
time: 61.5 us; the launch traced here: 60.4 us
  starting transfers between devices  28.5 us (46%)
  waiting for transfers between devices  15.4 us (25%)
  Pallas kernels  14.3 us (23%)
  other arithmetic  0.78 us (1%)
  local copies, waits for them, and re-layouts  0.72 us (1%)
  between operations  0.69 us (1%)
    ppermute x7, starting transfers between devices, exchange(): return sum((lax.ppermute(table, axis, route) for route in routes), table)  14.5 us
    ppermute x12, starting transfers between devices, send(): return lax.ppermute(block, 'ka', route)  14 us
    pallas_call x1, Pallas kernels, attend(): pl.pallas_call(attend_kernel, out_shape=(jax.ShapeDtypeStruct((ROWS, widt...  12.3 us
    ppermute x12, waiting for transfers between devices, send(): return lax.ppermute(block, 'ka', route)  9.99 us
    ppermute x7, waiting for transfers between devices, exchange(): return sum((lax.ppermute(table, axis, route) for route in routes), table)  5.44 us
    pallas_call x1, Pallas kernels, pack(): pl.pallas_call(pack_kernel, out_shape=(pltpu.VMEM((PACKED, HEAD_DIM), jnp...  2.02 us
  transfers between devices with their start and end apart: 19, of which 8 were waited for; matrix products, arithmetic and copies ran while one was open for 0% of the time, Pallas kernels for 0%

profile of v9, /device:TPU:8, one launch (start us, length us, event | category | flops | bytes accessed | tf_op | source)
XLA Modules:
  0.0 60.4 jit_solution(4291902319996506798)
XLA Ops:
  0.6 2.0 %shard_map.110 = (bf16[528,128]{1,0:T(8,128)(2,1)S(1)}, f32[8,128]{1,0:T(8,128)S(1)}, bf16[256,768]{1,0:T(8,128)(2,1)S(1)}, bf16[256,768]{1,0:T(8,128)(2,1)S(1)}) custom-call(bf16[256,128]{1,0:T(8,128)(2,1)} %keys.1, bf16[256,128]{1,0:T(8,128)(2,1)} %values.1, f32[2,128]{1,0:T(2,128)} %bitcast.19, s32[2,128]{1,0:T(2,128)} %bitcast.20, s32[2,128]{1,0:T(2,128)} %bitcast.21, ...), custom_call_target="tpu_custom_call" | custom-call | flops 10000 | bytes 2097152 | tf_op jit(solution)/shard_map/pallas_call | solution.py:64
  2.7 0.1 collective-permute-start.2
  2.8 1.6 %collective-permute-start = (bf16[528,128]{1,0:T(8,128)(2,1)S(1)}, bf16[528,128]{1,0:T(8,128)(2,1)S(1)}, u32[]{:S(2)}, u32[]{:S(2)}) collective-permute-start(bf16[528,128]{1,0:T(8,128)(2,1)S(1)} %get-tuple-element.23.own), channel_id=1, source_target_pairs={{0,2},{1,7},{2,4},{3,1},{4,6},{5,3},{6,0},{7,5},{8,10},{9,15},{10,... | collective-permute-start | bytes 405512 | tf_op jit(solution)/shard_map/ppermute | solution.py:241
  4.3 0.0 collective-permute-done.2.own_s
  4.3 6.3 %collective-permute-start.5 = (f32[8,128]{1,0:T(8,128)S(1)}, f32[8,128]{1,0:T(8,128)S(1)}, u32[]{:S(2)}, u32[]{:S(2)}) collective-permute-start(f32[8,128]{1,0:T(8,128)S(1)} %get-tuple-element.25), channel_id=1, source_target_pairs={{0,192},{16,208},{32,224},{48,240},{64,128},{80,144},{96,160},{112... | collective-permute-start | bytes 12296 | tf_op jit(solution)/shard_map/ppermute | solution.py:246
  10.6 0.9 %collective-permute-start.4 = (f32[8,128]{1,0:T(8,128)S(1)}, f32[8,128]{1,0:T(8,128)S(1)}, u32[]{:S(2)}, u32[]{:S(2)}) collective-permute-start(f32[8,128]{1,0:T(8,128)S(1)} %get-tuple-element.25), channel_id=1, source_target_pairs={{0,128},{16,144},{32,160},{48,176},{64,192},{80,208},{96,224},{112... | collective-permute-start | bytes 12296 | tf_op jit(solution)/shard_map/ppermute | solution.py:246
  11.5 1.5 %collective-permute-start.3 = (f32[8,128]{1,0:T(8,128)S(1)}, f32[8,128]{1,0:T(8,128)S(1)}, u32[]{:S(2)}, u32[]{:S(2)}) collective-permute-start(f32[8,128]{1,0:T(8,128)S(1)} %get-tuple-element.25), channel_id=1, source_target_pairs={{0,64},{16,80},{32,96},{48,112},{64,0},{80,16},{96,32},{112,48},{1... | collective-permute-start | bytes 12296 | tf_op jit(solution)/shard_map/ppermute | solution.py:246
  13.0 2.5 %collective-permute-start.10 = (bf16[528,128]{1,0:T(8,128)(2,1)S(1)}, bf16[528,128]{1,0:T(8,128)(2,1)S(1)}, u32[]{:S(2)}, u32[]{:S(2)}) collective-permute-start(bf16[528,128]{1,0:T(8,128)(2,1)S(1)} %get-tuple-element.23.own), channel_id=1, source_target_pairs={{2,0},{7,1},{4,2},{1,3},{6,4},{3,5},{0,6},{5,7},{10,8},{15,9},{12,... | collective-permute-start | bytes 405512 | tf_op jit(solution)/shard_map/ppermute | solution.py:241
  15.5 0.0 collective-permute-done.near
  15.5 0.0 collective-permute-start.1
  15.5 0.0 collective-permute-done.5
  15.5 2.6 %collective-permute-done.4 = f32[8,128]{1,0:T(8,128)S(1)} collective-permute-done((f32[8,128]{1,0:T(8,128)S(1)}, f32[8,128]{1,0:T(8,128)S(1)}, u32[]{:S(2)}, u32[]{:S(2)}) %collective-permute-start.4) | collective-permute-done | bytes 4128 | tf_op jit(solution)/shard_map/ppermute | solution.py:246
  18.2 0.0 collective-permute-done.3
  18.2 2.4 %collective-permute-start.6 = (f32[8,128]{1,0:T(8,128)S(1)}, f32[8,128]{1,0:T(8,128)S(1)}, u32[]{:S(2)}, u32[]{:S(2)}) collective-permute-start(f32[8,128]{1,0:T(8,128)S(1)} %add_add_fusion.1), channel_id=1, source_target_pairs={{0,8},{1,9},{2,10},{3,11},{4,12},{5,13},{6,14},{7,15},{8,0},{9,1},... | collective-permute-start | bytes 12296 | tf_op jit(solution)/shard_map/ppermute | solution.py:246
  20.5 2.8 %collective-permute-done.6 = f32[8,128]{1,0:T(8,128)S(1)} collective-permute-done((f32[8,128]{1,0:T(8,128)S(1)}, f32[8,128]{1,0:T(8,128)S(1)}, u32[]{:S(2)}, u32[]{:S(2)}) %collective-permute-start.6) | collective-permute-done | bytes 4128 | tf_op jit(solution)/shard_map/ppermute | solution.py:246
  23.4 0.0 collective-permute-done.1.near_s
  23.4 0.9 %collective-permute-start.9 = (f32[8,128]{1,0:T(8,128)S(1)}, f32[8,128]{1,0:T(8,128)S(1)}, u32[]{:S(2)}, u32[]{:S(2)}) collective-permute-start(f32[8,128]{1,0:T(8,128)S(1)} %add.65), channel_id=1, source_target_pairs={{0,48},{16,32},{32,16},{48,0},{64,112},{80,96},{96,80},{112,64},{1... | collective-permute-start | bytes 12296 | tf_op jit(solution)/shard_map/ppermute | solution.py:246
  24.3 1.0 %collective-permute-start.8 = (f32[8,128]{1,0:T(8,128)S(1)}, f32[8,128]{1,0:T(8,128)S(1)}, u32[]{:S(2)}, u32[]{:S(2)}) collective-permute-start(f32[8,128]{1,0:T(8,128)S(1)} %add.65), channel_id=1, source_target_pairs={{0,32},{16,48},{32,0},{48,16},{64,96},{80,112},{96,64},{112,80},{1... | collective-permute-start | bytes 12296 | tf_op jit(solution)/shard_map/ppermute | solution.py:246
  25.3 1.6 %collective-permute-start.7 = (f32[8,128]{1,0:T(8,128)S(1)}, f32[8,128]{1,0:T(8,128)S(1)}, u32[]{:S(2)}, u32[]{:S(2)}) collective-permute-start(f32[8,128]{1,0:T(8,128)S(1)} %add.65), channel_id=1, source_target_pairs={{0,16},{16,0},{32,48},{48,32},{64,80},{80,64},{96,112},{112,96},{1... | collective-permute-start | bytes 12296 | tf_op jit(solution)/shard_map/ppermute | solution.py:246
  26.9 0.0 collective-permute-start.13
  26.9 0.0 collective-permute-done.10.far
  26.9 1.5 %collective-permute-start.11 = (bf16[528,128]{1,0:T(8,128)(2,1)S(1)}, bf16[528,128]{1,0:T(8,128)(2,1)S(1)}, u32[]{:S(2)}, u32[]{:S(2)}) collective-permute-start(bf16[528,128]{1,0:T(8,128)(2,1)S(1)} %collective-permute-done.near), channel_id=1, source_target_pairs={{0,2},{1,7},{2,4},{3,1},{4,6},{5,3},{6,0},{7,5},{8,10},{9,15},{10,... | collective-permute-start | bytes 405512 | tf_op jit(solution)/shard_map/ppermute | solution.py:241
  28.4 0.0 collective-permute-done.9
  28.4 1.7 %collective-permute-start.12 = (bf16[528,128]{1,0:T(8,128)(2,1)S(1)}, bf16[528,128]{1,0:T(8,128)(2,1)S(1)}, u32[]{:S(2)}, u32[]{:S(2)}) collective-permute-start(bf16[528,128]{1,0:T(8,128)(2,1)S(1)} %collective-permute-done.10.far), channel_id=1, source_target_pairs={{0,1},{1,0},{2,3},{3,2},{4,5},{5,4},{6,7},{7,6},{8,9},{9,8},{10,11... | collective-permute-start | bytes 405512 | tf_op jit(solution)/shard_map/ppermute | solution.py:241
  30.1 0.0 collective-permute-done.8
  30.1 0.0 collective-permute-done.7
  30.1 1.0 %collective-permute-done.12.far_s = bf16[528,128]{1,0:T(8,128)(2,1)S(1)} collective-permute-done((bf16[528,128]{1,0:T(8,128)(2,1)S(1)}, bf16[528,128]{1,0:T(8,128)(2,1)S(1)}, u32[]{:S(2)}, u32[]{:S(2)}) %collective-permute-start.12) | collective-permute-done | bytes 135200 | tf_op jit(solution)/shard_map/ppermute | solution.py:241
  31.1 0.2 collective-permute-done.13.opposite_s
  31.3 2.5 %collective-permute-done.11.opposite = bf16[528,128]{1,0:T(8,128)(2,1)S(1)} collective-permute-done((bf16[528,128]{1,0:T(8,128)(2,1)S(1)}, bf16[528,128]{1,0:T(8,128)(2,1)S(1)}, u32[]{:S(2)}, u32[]{:S(2)}) %collective-permute-start.11) | collective-permute-done | bytes 135200 | tf_op jit(solution)/shard_map/ppermute | solution.py:241
  33.8 12.3 %shard_map.111 = (bf16[256,768]{1,0:T(8,128)(2,1)}, f32[256,768]{1,0:T(8,128)}, bf16[272,256]{1,0:T(8,128)(2,1)S(1)}, bf16[272,256]{1,0:T(8,128)(2,1)S(1)}, bf16...) custom-call(bf16[256,768]{1,0:T(8,128)(2,1)S(1)} %get-tuple-element., ...), custom_call_target="tpu_custom_call" | custom-call | flops 4831838208 | bytes 4194304 | tf_op jit(solution)/shard_map/pallas_call | solution.py:193
  46.1 0.0 collective-permute-start.14
  46.1 2.5 %collective-permute-start.15 = (bf16[272,256]{1,0:T(8,128)(2,1)S(1)}, bf16[272,256]{1,0:T(8,128)(2,1)S(1)}, u32[]{:S(2)}, u32[]{:S(2)}) collective-permute-start(bf16[272,256]{1,0:T(8,128)(2,1)S(1)} %get-tuple-element.34), channel_id=1, source_target_pairs={{2,0},{7,1},{4,2},{1,3},{6,4},{3,5},{0,6},{5,7},{10,8},{15,9},{12,... | collective-permute-start | bytes 417800 | tf_op jit(solution)/shard_map/ppermute | solution.py:241
  48.6 0.0 collective-permute-start.16
  48.6 0.0 collective-permute-done.14
  48.6 0.8 %collective-permute-start.18 = (bf16[272,256]{1,0:T(8,128)(2,1)S(1)}, bf16[272,256]{1,0:T(8,128)(2,1)S(1)}, u32[]{:S(2)}, u32[]{:S(2)}) collective-permute-start(bf16[272,256]{1,0:T(8,128)(2,1)S(1)} %fusion.5), channel_id=1, source_target_pairs={{0,2},{1,7},{2,4},{3,1},{4,6},{5,3},{6,0},{7,5},{8,10},{9,15},{10,... | collective-permute-start | bytes 417800 | tf_op jit(solution)/shard_map/ppermute | solution.py:241
  49.4 3.1 %collective-permute-done.15 = bf16[272,256]{1,0:T(8,128)(2,1)S(1)} collective-permute-done((bf16[272,256]{1,0:T(8,128)(2,1)S(1)}, bf16[272,256]{1,0:T(8,128)(2,1)S(1)}, u32[]{:S(2)}, u32[]{:S(2)}) %collective-permute-start.15) | collective-permute-done | bytes 139296 | tf_op jit(solution)/shard_map/ppermute | solution.py:241
  52.6 0.5 collective-permute-done.16
  53.1 0.1 fusion.2
  53.2 3.3 %collective-permute-start.17 = (bf16[272,256]{1,0:T(8,128)(2,1)S(1)}, bf16[272,256]{1,0:T(8,128)(2,1)S(1)}, u32[]{:S(2)}, u32[]{:S(2)}) collective-permute-start(bf16[272,256]{1,0:T(8,128)(2,1)S(1)} %fusion.2), channel_id=1, source_target_pairs={{2,0},{7,1},{4,2},{1,3},{6,4},{3,5},{0,6},{5,7},{10,8},{15,9},{12,... | collective-permute-start | bytes 417800 | tf_op jit(solution)/shard_map/ppermute | solution.py:241
  56.4 0.0 collective-permute-done.18
  56.4 2.6 %collective-permute-done.17 = bf16[272,256]{1,0:T(8,128)(2,1)S(1)} collective-permute-done((bf16[272,256]{1,0:T(8,128)(2,1)S(1)}, bf16[272,256]{1,0:T(8,128)(2,1)S(1)}, u32[]{:S(2)}, u32[]{:S(2)}) %collective-permute-start.17) | collective-permute-done | bytes 139296 | tf_op jit(solution)/shard_map/ppermute | solution.py:241
  59.0 0.1 fusion.4
  59.1 0.7 %fusion.11 = (f32[256,128]{1,0:T(8,128)}, f32[256,128]{1,0:T(8,128)}) fusion(f32[272,256]{1,0:T(8,128)S(1)} %fusion.4), kind=kLoop, calls=%fused_computation.25 | loop fusion | bytes 524288 | tf_op jit(solution)/shard_map/slice | solution.py:277
  59.8 0.6 subtract_bitcast_fusion
  (5 shorter events, 0.0 us)
Async XLA Ops:
  2.7 1.7 %collective-permute-start.2 = (bf16[528,128]{1,0:T(8,128)(2,1)S(1)}, bf16[528,128]{1,0:T(8,128)(2,1)S(1)}, u32[]{:S(2)}, u32[]{:S(2)}) collective-permute-start(bf16[528,128]{1,0:T(8,128)(2,1)S(1)} %get-tuple-element.23.own), channel_id=1, source_target_pairs={{0,1},{1,0},{2,3},{3,2},{4,5},{5,4},{6,7},{7,6},{8,9},{9,8},{10,11... | collective-permute-start | bytes 405512 | tf_op jit(solution)/shard_map/ppermute | solution.py:241
  2.8 12.8 %collective-permute-start = (bf16[528,128]{1,0:T(8,128)(2,1)S(1)}, bf16[528,128]{1,0:T(8,128)(2,1)S(1)}, u32[]{:S(2)}, u32[]{:S(2)}) collective-permute-start(bf16[528,128]{1,0:T(8,128)(2,1)S(1)} %get-tuple-element.23.own), channel_id=1, source_target_pairs={{0,2},{1,7},{2,4},{3,1},{4,6},{5,3},{6,0},{7,5},{8,10},{9,15},{10,... | collective-permute-start | bytes 405512 | tf_op jit(solution)/shard_map/ppermute | solution.py:241
  4.3 11.2 %collective-permute-start.5 = (f32[8,128]{1,0:T(8,128)S(1)}, f32[8,128]{1,0:T(8,128)S(1)}, u32[]{:S(2)}, u32[]{:S(2)}) collective-permute-start(f32[8,128]{1,0:T(8,128)S(1)} %get-tuple-element.25), channel_id=1, source_target_pairs={{0,192},{16,208},{32,224},{48,240},{64,128},{80,144},{96,160},{112... | collective-permute-start | bytes 12296 | tf_op jit(solution)/shard_map/ppermute | solution.py:246
  10.6 7.5 %collective-permute-start.4 = (f32[8,128]{1,0:T(8,128)S(1)}, f32[8,128]{1,0:T(8,128)S(1)}, u32[]{:S(2)}, u32[]{:S(2)}) collective-permute-start(f32[8,128]{1,0:T(8,128)S(1)} %get-tuple-element.25), channel_id=1, source_target_pairs={{0,128},{16,144},{32,160},{48,176},{64,192},{80,208},{96,224},{112... | collective-permute-start | bytes 12296 | tf_op jit(solution)/shard_map/ppermute | solution.py:246
  11.5 6.6 %collective-permute-start.3 = (f32[8,128]{1,0:T(8,128)S(1)}, f32[8,128]{1,0:T(8,128)S(1)}, u32[]{:S(2)}, u32[]{:S(2)}) collective-permute-start(f32[8,128]{1,0:T(8,128)S(1)} %get-tuple-element.25), channel_id=1, source_target_pairs={{0,64},{16,80},{32,96},{48,112},{64,0},{80,16},{96,32},{112,48},{1... | collective-permute-start | bytes 12296 | tf_op jit(solution)/shard_map/ppermute | solution.py:246
  13.0 13.9 %collective-permute-start.10 = (bf16[528,128]{1,0:T(8,128)(2,1)S(1)}, bf16[528,128]{1,0:T(8,128)(2,1)S(1)}, u32[]{:S(2)}, u32[]{:S(2)}) collective-permute-start(bf16[528,128]{1,0:T(8,128)(2,1)S(1)} %get-tuple-element.23.own), channel_id=1, source_target_pairs={{2,0},{7,1},{4,2},{1,3},{6,4},{3,5},{0,6},{5,7},{10,8},{15,9},{12,... | collective-permute-start | bytes 405512 | tf_op jit(solution)/shard_map/ppermute | solution.py:241
  15.5 7.8 %collective-permute-start.1 = (bf16[528,128]{1,0:T(8,128)(2,1)S(1)}, bf16[528,128]{1,0:T(8,128)(2,1)S(1)}, u32[]{:S(2)}, u32[]{:S(2)}) collective-permute-start(bf16[528,128]{1,0:T(8,128)(2,1)S(1)} %collective-permute-done.near), channel_id=1, source_target_pairs={{0,1},{1,0},{2,3},{3,2},{4,5},{5,4},{6,7},{7,6},{8,9},{9,8},{10,11... | collective-permute-start | bytes 405512 | tf_op jit(solution)/shard_map/ppermute | solution.py:241
  18.2 5.2 %collective-permute-start.6 = (f32[8,128]{1,0:T(8,128)S(1)}, f32[8,128]{1,0:T(8,128)S(1)}, u32[]{:S(2)}, u32[]{:S(2)}) collective-permute-start(f32[8,128]{1,0:T(8,128)S(1)} %add_add_fusion.1), channel_id=1, source_target_pairs={{0,8},{1,9},{2,10},{3,11},{4,12},{5,13},{6,14},{7,15},{8,0},{9,1},... | collective-permute-start | bytes 12296 | tf_op jit(solution)/shard_map/ppermute | solution.py:246
  23.4 5.0 %collective-permute-start.9 = (f32[8,128]{1,0:T(8,128)S(1)}, f32[8,128]{1,0:T(8,128)S(1)}, u32[]{:S(2)}, u32[]{:S(2)}) collective-permute-start(f32[8,128]{1,0:T(8,128)S(1)} %add.65), channel_id=1, source_target_pairs={{0,48},{16,32},{32,16},{48,0},{64,112},{80,96},{96,80},{112,64},{1... | collective-permute-start | bytes 12296 | tf_op jit(solution)/shard_map/ppermute | solution.py:246
  24.3 5.8 %collective-permute-start.8 = (f32[8,128]{1,0:T(8,128)S(1)}, f32[8,128]{1,0:T(8,128)S(1)}, u32[]{:S(2)}, u32[]{:S(2)}) collective-permute-start(f32[8,128]{1,0:T(8,128)S(1)} %add.65), channel_id=1, source_target_pairs={{0,32},{16,48},{32,0},{48,16},{64,96},{80,112},{96,64},{112,80},{1... | collective-permute-start | bytes 12296 | tf_op jit(solution)/shard_map/ppermute | solution.py:246
  25.3 4.8 %collective-permute-start.7 = (f32[8,128]{1,0:T(8,128)S(1)}, f32[8,128]{1,0:T(8,128)S(1)}, u32[]{:S(2)}, u32[]{:S(2)}) collective-permute-start(f32[8,128]{1,0:T(8,128)S(1)} %add.65), channel_id=1, source_target_pairs={{0,16},{16,0},{32,48},{48,32},{64,80},{80,64},{96,112},{112,96},{1... | collective-permute-start | bytes 12296 | tf_op jit(solution)/shard_map/ppermute | solution.py:246
  26.9 4.4 %collective-permute-start.13 = (bf16[528,128]{1,0:T(8,128)(2,1)S(1)}, bf16[528,128]{1,0:T(8,128)(2,1)S(1)}, u32[]{:S(2)}, u32[]{:S(2)}) collective-permute-start(bf16[528,128]{1,0:T(8,128)(2,1)S(1)} %collective-permute-done.near), channel_id=1, source_target_pairs={{0,3},{1,6},{2,5},{3,0},{4,7},{5,2},{6,1},{7,4},{8,11},{9,14},{10,... | collective-permute-start | bytes 405512 | tf_op jit(solution)/shard_map/ppermute | solution.py:241
  26.9 7.0 %collective-permute-start.11 = (bf16[528,128]{1,0:T(8,128)(2,1)S(1)}, bf16[528,128]{1,0:T(8,128)(2,1)S(1)}, u32[]{:S(2)}, u32[]{:S(2)}) collective-permute-start(bf16[528,128]{1,0:T(8,128)(2,1)S(1)} %collective-permute-done.near), channel_id=1, source_target_pairs={{0,2},{1,7},{2,4},{3,1},{4,6},{5,3},{6,0},{7,5},{8,10},{9,15},{10,... | collective-permute-start | bytes 405512 | tf_op jit(solution)/shard_map/ppermute | solution.py:241
  28.4 2.7 %collective-permute-start.12 = (bf16[528,128]{1,0:T(8,128)(2,1)S(1)}, bf16[528,128]{1,0:T(8,128)(2,1)S(1)}, u32[]{:S(2)}, u32[]{:S(2)}) collective-permute-start(bf16[528,128]{1,0:T(8,128)(2,1)S(1)} %collective-permute-done.10.far), channel_id=1, source_target_pairs={{0,1},{1,0},{2,3},{3,2},{4,5},{5,4},{6,7},{7,6},{8,9},{9,8},{10,11... | collective-permute-start | bytes 405512 | tf_op jit(solution)/shard_map/ppermute | solution.py:241
  46.1 2.5 %collective-permute-start.14 = (bf16[3,272,256]{2,1,0:T(8,128)(2,1)S(1)}, bf16[3,272,256]{2,1,0:T(8,128)(2,1)S(1)}, u32[]{:S(2)}, u32[]{:S(2)}) collective-permute-start(bf16[3,272,256]{2,1,0:T(8,128)(2,1)S(1)} %get-tuple-element.32), channel_id=1, source_target_pairs={{0,1},{1,0},{2,3},{3,2},{4,5},{5,4},{6,7},{7,6},{8,9},{9,8},{10,11... | collective-permute-start | bytes 1253384 | tf_op jit(solution)/shard_map/ppermute | solution.py:241
  46.1 6.5 %collective-permute-start.15 = (bf16[272,256]{1,0:T(8,128)(2,1)S(1)}, bf16[272,256]{1,0:T(8,128)(2,1)S(1)}, u32[]{:S(2)}, u32[]{:S(2)}) collective-permute-start(bf16[272,256]{1,0:T(8,128)(2,1)S(1)} %get-tuple-element.34), channel_id=1, source_target_pairs={{2,0},{7,1},{4,2},{1,3},{6,4},{3,5},{0,6},{5,7},{10,8},{15,9},{12,... | collective-permute-start | bytes 417800 | tf_op jit(solution)/shard_map/ppermute | solution.py:241
  48.6 4.5 %collective-permute-start.16 = (bf16[272,256]{1,0:T(8,128)(2,1)S(1)}, bf16[272,256]{1,0:T(8,128)(2,1)S(1)}, u32[]{:S(2)}, u32[]{:S(2)}) collective-permute-start(bf16[272,256]{1,0:T(8,128)(2,1)S(1)} %get-tuple-element.35), channel_id=1, source_target_pairs={{3,0},{6,1},{5,2},{0,3},{7,4},{2,5},{1,6},{4,7},{11,8},{14,9},{13,... | collective-permute-start | bytes 417800 | tf_op jit(solution)/shard_map/ppermute | solution.py:241
  48.6 7.8 %collective-permute-start.18 = (bf16[272,256]{1,0:T(8,128)(2,1)S(1)}, bf16[272,256]{1,0:T(8,128)(2,1)S(1)}, u32[]{:S(2)}, u32[]{:S(2)}) collective-permute-start(bf16[272,256]{1,0:T(8,128)(2,1)S(1)} %fusion.5), channel_id=1, source_target_pairs={{0,2},{1,7},{2,4},{3,1},{4,6},{5,3},{6,0},{7,5},{8,10},{9,15},{10,... | collective-permute-start | bytes 417800 | tf_op jit(solution)/shard_map/ppermute | solution.py:241
  53.2 5.9 %collective-permute-start.17 = (bf16[272,256]{1,0:T(8,128)(2,1)S(1)}, bf16[272,256]{1,0:T(8,128)(2,1)S(1)}, u32[]{:S(2)}, u32[]{:S(2)}) collective-permute-start(bf16[272,256]{1,0:T(8,128)(2,1)S(1)} %fusion.2), channel_id=1, source_target_pairs={{2,0},{7,1},{4,2},{1,3},{6,4},{3,5},{0,6},{5,7},{10,8},{15,9},{12,... | collective-permute-start | bytes 417800 | tf_op jit(solution)/shard_map/ppermute | solution.py:241

commit v10 on v9

--- a/solution.py
+++ b/solution.py
@@ -15,8 +15,6 @@
 CHIPS = 4
 PAIRS = 32
 PACKED = 2 * ROWS + 16
-EXTRA = 16
-LIMBS = tuple(2.0 ** (6 - 5 * place) for place in range(6))
 NEG = -1e30
 INV_ROOT = 1.0 / math.sqrt(HEAD_DIM)
 SCALE2 = INV_ROOT * math.log2(math.e)
@@ -30,16 +28,32 @@
     return jnp.dot(a, b, preferred_element_type=jnp.float32)
 
 
-def pack_kernel(
-    keys, values, logprob, docs, response, queries_hbm, grads_hbm,
-    packed, sums, queries, grads, arrived,
-):
+def fetch_kernel(queries_hbm, grads_hbm, queries, grads, arrived):
     fetches = [
         pltpu.make_async_copy(source, target, arrived.at[number])
         for number, (source, target) in enumerate(((queries_hbm, queries), (grads_hbm, grads)))
     ]
     for fetch in fetches:
         fetch.start()
+    for fetch in fetches:
+        fetch.wait()
+
+
+def fetch(queries, grads):
+    return pl.pallas_call(
+        fetch_kernel,
+        out_shape=(
+            pltpu.VMEM(queries.shape, jnp.bfloat16),
+            pltpu.VMEM(grads.shape, jnp.bfloat16),
+        ),
+        in_specs=[HBM] * 2,
+        out_specs=(VMEM,) * 2,
+        scratch_shapes=[pltpu.SemaphoreType.DMA((2,))],
+        cost_estimate=pl.CostEstimate(flops=0, bytes_accessed=2 * MIB, transcendentals=0),
+    )(*(pltpu.with_memory_space_constraint(x, pltpu.HBM) for x in (queries, grads)))
+
+
+def pack_kernel(keys, values, logprob, docs, response, packed, sums):
     pair = lax.axis_index("pb") * 2 + lax.axis_index("ka") // BLOCKS
     odd = (docs[...] & 1).astype(jnp.float32)
     even = 1.0 - odd
@@ -49,31 +63,25 @@
     table = jnp.zeros((8, HEAD_DIM), jnp.float32)
     for kind, term in enumerate((scored * even, scored * odd, live * even, live * odd)):
         table = jnp.where(lane == kind * PAIRS + pair, jnp.sum(term, keepdims=True), table)
-    sums[...] = table
+    sums[...] = jnp.broadcast_to(table[:1], sums.shape)
     packed[:ROWS, :] = keys[...]
     packed[ROWS : 2 * ROWS, :] = values[...]
     count = jnp.broadcast_to(jnp.sum(even, keepdims=True), (16, HEAD_DIM))
     packed[2 * ROWS :, :] = count.astype(jnp.bfloat16)
-    for fetch in fetches:
-        fetch.wait()
-
-
-def pack(keys, values, logprob, docs, response, queries, grads):
+
+
+def pack(keys, values, logprob, docs, response):
     wide = (ROWS // 128, 128)
-    far_off = (pltpu.with_memory_space_constraint(x, pltpu.HBM) for x in (queries, grads))
     return pl.pallas_call(
         pack_kernel,
         out_shape=(
             pltpu.VMEM((PACKED, HEAD_DIM), jnp.bfloat16),
-            pltpu.VMEM((8, HEAD_DIM), jnp.float32),
-            pltpu.VMEM(queries.shape, jnp.bfloat16),
-            pltpu.VMEM(grads.shape, jnp.bfloat16),
-        ),
-        in_specs=[VMEM] * 5 + [HBM] * 2,
-        out_specs=(VMEM,) * 4,
-        scratch_shapes=[pltpu.SemaphoreType.DMA((2,))],
-        cost_estimate=pl.CostEstimate(flops=10000, bytes_accessed=2 * MIB, transcendentals=0),
-    )(keys, values, logprob.reshape(wide), docs.reshape(wide), response.reshape(wide), *far_off)
+            jax.ShapeDtypeStruct((ROWS, HEAD_DIM), jnp.float32),
+        ),
+        in_specs=[VMEM] * 5,
+        out_specs=(VMEM,) * 2,
+        cost_estimate=pl.CostEstimate(flops=10000, bytes_accessed=MIB // 2, transcendentals=0),
+    )(keys, values, logprob.reshape(wide), docs.reshape(wide), response.reshape(wide))
 
 
 def spans():
@@ -81,7 +89,7 @@
 
 
 def attend_kernel(
-    queries, grads, table, own, near, far, opposite, own_s, near_s, far_s, opposite_s,
+    queries, grads, own, near, far, opposite, own_s, near_s, far_s, opposite_s,
     attention, grad_queries, own_part, near_part, far_part, opposite_part, swap_parts,
     opposite_s_part,
     keys, values, keys_t, values_t, bias, scores, probs, grad_scores, acc_k, acc_v,
@@ -108,17 +116,6 @@
         term = blocks[block][2 * ROWS :, :].astype(jnp.float32)
         count = term if count is None else count + term
     cut = count[:1, :1].astype(jnp.int32)
-    rest = jnp.abs(table[:1, :])
-    place_row = lax.broadcasted_iota(jnp.int32, (EXTRA, HEAD_DIM), 0)
-    limbs = jnp.zeros((EXTRA, HEAD_DIM), jnp.float32)
-    for number, scale in enumerate(LIMBS):
-        limb = jnp.floor(rest * (1.0 / scale))
-        rest = rest - limb * scale
-        limbs = jnp.where(place_row == number, limb, limbs)
-    limbs = limbs.astype(jnp.bfloat16)
-    for part in parts:
-        part[ROWS:, :HEAD_DIM] = limbs
-        part[ROWS:, HEAD_DIM:] = limbs
     row = first_row + lax.broadcasted_iota(jnp.int32, (ROWS, ROWS), 0)
     lane = lax.broadcasted_iota(jnp.int32, (ROWS, ROWS), 1)
     start = jnp.where(row >= cut, cut, 0)
@@ -182,14 +179,14 @@
                 acc_k[:, span] = part_k
                 acc_v[:, span] = part_v
             else:
-                parts[block][:ROWS, :HEAD_DIM] = (part_k * INV_ROOT).astype(jnp.bfloat16).T
-                parts[block][:ROWS, HEAD_DIM:] = part_v.astype(jnp.bfloat16).T
+                parts[block][:, :HEAD_DIM] = (part_k * INV_ROOT).astype(jnp.bfloat16).T
+                parts[block][:, HEAD_DIM:] = part_v.astype(jnp.bfloat16).T
         grad_queries[:, columns[head]] = dot(grad_scores[slot], keys[...]) * INV_ROOT
 
 
-def attend(queries, grads, table, blocks):
+def attend(queries, grads, blocks):
     width = HEADS * HEAD_DIM
-    part = jax.ShapeDtypeStruct((ROWS + EXTRA, 2 * HEAD_DIM), jnp.bfloat16)
+    part = jax.ShapeDtypeStruct((ROWS, 2 * HEAD_DIM), jnp.bfloat16)
     return pl.pallas_call(
         attend_kernel,
         out_shape=(
@@ -199,10 +196,10 @@
             part,
             part,
             part,
-            jax.ShapeDtypeStruct((3, ROWS + EXTRA, 2 * HEAD_DIM), jnp.bfloat16),
-            part,
-        ),
-        in_specs=[VMEM] * (3 + BLOCKS),
+            jax.ShapeDtypeStruct((3, ROWS, 2 * HEAD_DIM), jnp.bfloat16),
+            part,
+        ),
+        in_specs=[VMEM] * (2 + BLOCKS),
         out_specs=(VMEM,) * 8,
         scratch_shapes=[
             pltpu.VMEM((PAIR_SPAN, HEAD_DIM), jnp.bfloat16),
@@ -222,7 +219,7 @@
             bytes_accessed=4 * MIB,
             transcendentals=HEADS * ROWS * PAIR_SPAN,
         ),
-    )(queries, grads, table, *blocks)
+    )(queries, grads, *blocks)
 
 
 def at(half, chip, core):
@@ -245,25 +242,22 @@
         routes = [[(place, place ^ mask) for place in extent] for mask in masks]
         return sum((lax.ppermute(table, axis, route) for route in routes), table)
 
-    own, table, queries, grad_output = pack(
-        key_heads, value_heads, token_logprob, doc_ids, response, queries, grad_output
-    )
+    own, sums = pack(key_heads, value_heads, token_logprob, doc_ids, response)
+    queries, grad_output = fetch(queries, grad_output)
+    columns = [list(range(low, 16, 2)) for low in (0, 1)]
+    sums = lax.all_gather(sums, "pb", axis_index_groups=columns)
+    sums = lax.optimization_barrier(sums)
     near = send(own, ahead)
     far = send(own, back)
     own_s = send(own, swap)
-    own_s, table = lax.optimization_barrier((own_s, table))
-    table = exchange(table, "pb", (4, 8, 12))
-    table = exchange(table, "ka", (8,))
     opposite = send(near, ahead)
     opposite_s = send(near, cross)
     near_s = send(near, swap)
     far_s = send(far, swap)
-    near_s, table = lax.optimization_barrier((near_s, table))
-    table = exchange(table, "pb", (1, 2, 3))
 
     blocks = (own, near, far, opposite, own_s, near_s, far_s, opposite_s)
     attention, grad_queries, own_p, near_p, far_p, opposite_p, swap_p, opposite_s_p = attend(
-        queries, grad_output, table, blocks
+        queries, grad_output, blocks
     )
     passed = send(opposite_p, back)
     passed_s = send(opposite_s_p, cross_back)
@@ -273,12 +267,14 @@
     far_sum = far_p + swapped[2]
     near_part = send(near_sum, back)
     far_part = send(far_sum, ahead)
+    _, sums = lax.optimization_barrier((near_sum, sums))
+    table = exchange(jnp.sum(sums[:, :8, :], axis=0), "ka", (1,))
+    table = exchange(table, "ka", (2, 4, 6))
+    table = exchange(table, ("pb", "ka"), (8, 16, 24))
+    table = table[0].reshape(4, PAIRS)
+    margins = table[0] / table[2] - table[1] / table[3]
     total = own_p.astype(wide) + swapped[0] + near_part + far_part
-    grad_keys, grad_values = total[:ROWS, :HEAD_DIM], total[:ROWS, HEAD_DIM:]
-    sums = sum(total[ROWS + number, :HEAD_DIM] * scale for number, scale in enumerate(LIMBS))
-    sums = sums.reshape(4, PAIRS)
-    margins = sums[1] / sums[3] - sums[0] / sums[2]
-    return (attention, grad_queries, grad_keys, grad_values, margins)
+    return (attention, grad_queries, total[:, :HEAD_DIM], total[:, HEAD_DIM:], margins)
 
 
 def solution(mesh):

time: 61.5 us -> 78 us (1.27)
  between operations: 0.69 us -> 14.1 us
  waiting for transfers between devices: 15.4 us -> 25.7 us
  starting transfers between devices: 28.5 us -> 20.6 us
    all_gather x0 -> x1, waiting for transfers between devices: none -> 8.08 us  [per_device(): sums = lax.all_gather(sums, 'pb', axis_index_groups=columns)]
    ppermute x7, starting transfers between devices: 14.5 us -> 8.79 us  [exchange(): return sum((lax.ppermute(table, axis, route) for route in routes), table)]
    ppermute x7, waiting for transfers between devices: 5.44 us -> 7.7 us  [exchange(): return sum((lax.ppermute(table, axis, route) for route in routes), table)]
    ppermute x12, starting transfers between devices: 14 us -> 11.8 us  [send(): return lax.ppermute(block, 'ka', route)]
    pallas_call x0 -> x1, Pallas kernels: none -> 1.13 us  [fetch(): pl.pallas_call(fetch_kernel, out_shape=(pltpu.VMEM(queries.shape, jnp.bfl...]
  transfers between devices with their start and end apart: 19 -> 20, of which waited for: 8 -> 11; matrix products, arithmetic and copies ran while one was open for 0% -> 2% of each run, Pallas kernels for 0% -> 17%
where the time goes in v10:
time: 78 us; the launch traced here: 77.5 us
  waiting for transfers between devices  25.7 us (33%)
  starting transfers between devices  20.6 us (26%)
  Pallas kernels  14.9 us (19%)
  between operations  14.1 us (18%)
  other arithmetic  1.52 us (2%)
    pallas_call x1, Pallas kernels, attend(): pl.pallas_call(attend_kernel, out_shape=(jax.ShapeDtypeStruct((ROWS, widt...  12 us
    ppermute x12, starting transfers between devices, send(): return lax.ppermute(block, 'ka', route)  11.8 us
    ppermute x12, waiting for transfers between devices, send(): return lax.ppermute(block, 'ka', route)  9.91 us
    ppermute x7, starting transfers between devices, exchange(): return sum((lax.ppermute(table, axis, route) for route in routes), table)  8.79 us
    all_gather x1, waiting for transfers between devices, per_device(): sums = lax.all_gather(sums, 'pb', axis_index_groups=columns)  8.08 us
    ppermute x7, waiting for transfers between devices, exchange(): return sum((lax.ppermute(table, axis, route) for route in routes), table)  7.7 us
    pallas_call x1, Pallas kernels, pack(): pl.pallas_call(pack_kernel, out_shape=(pltpu.VMEM((PACKED, HEAD_DIM), jnp...  1.69 us
  transfers between devices with their start and end apart: 20, of which 11 were waited for; matrix products, arithmetic and copies ran while one was open for 2% of the time, Pallas kernels for 17%

profile of v10, /device:TPU:8, one launch (start us, length us, event | category | flops | bytes accessed | tf_op | source)
XLA Modules:
  0.0 77.5 jit_solution(7459946613974978006)
XLA Ops:
  7.2 0.0 all-gather.3.cloned.1.call-start
  7.2 1.7 %shard_map.111 = (bf16[528,128]{1,0:T(8,128)(2,1)S(1)}, f32[256,128]{1,0:T(8,128)}) custom-call(bf16[256,128]{1,0:T(8,128)(2,1)} %keys.1, bf16[256,128]{1,0:T(8,128)(2,1)} %values.1, f32[2,128]{1,0:T(2,128)} %bitcast.20, s32[2,128]{1,0:T(2,128)} %bitcast.21, s32[2,128]{1,0:T(2,128)} %bitcast.22), custom_call_target="tpu_custom_call" | custom-call | flops 10000 | bytes 524288 | tf_op jit(solution)/shard_map/pallas_call | solution.py:75
  8.9 0.0 all-gather.3.cloned.1.call-update
  8.9 1.6 %collective-permute-start = (bf16[528,128]{1,0:T(8,128)(2,1)S(1)}, bf16[528,128]{1,0:T(8,128)(2,1)S(1)}, u32[]{:S(2)}, u32[]{:S(2)}) collective-permute-start(bf16[528,128]{1,0:T(8,128)(2,1)S(1)} %get-tuple-element.20.own), channel_id=1, source_target_pairs={{0,2},{1,7},{2,4},{3,1},{4,6},{5,3},{6,0},{7,5},{8,10},{9,15},{10,... | collective-permute-start | bytes 405512 | tf_op jit(solution)/shard_map/ppermute | solution.py:238
  10.5 1.7 %collective-permute-start.1 = (bf16[528,128]{1,0:T(8,128)(2,1)S(1)}, bf16[528,128]{1,0:T(8,128)(2,1)S(1)}, u32[]{:S(2)}, u32[]{:S(2)}) collective-permute-start(bf16[528,128]{1,0:T(8,128)(2,1)S(1)} %get-tuple-element.20.own), channel_id=1, source_target_pairs={{2,0},{7,1},{4,2},{1,3},{6,4},{3,5},{0,6},{5,7},{10,8},{15,9},{12,... | collective-permute-start | bytes 405512 | tf_op jit(solution)/shard_map/ppermute | solution.py:238
  12.2 0.0 collective-permute-start.3
  12.2 3.0 %collective-permute-done.near = bf16[528,128]{1,0:T(8,128)(2,1)S(1)} collective-permute-done((bf16[528,128]{1,0:T(8,128)(2,1)S(1)}, bf16[528,128]{1,0:T(8,128)(2,1)S(1)}, u32[]{:S(2)}, u32[]{:S(2)}) %collective-permute-start) | collective-permute-done | bytes 135200 | tf_op jit(solution)/shard_map/ppermute | solution.py:238
  15.3 1.5 %collective-permute-start.2 = (bf16[528,128]{1,0:T(8,128)(2,1)S(1)}, bf16[528,128]{1,0:T(8,128)(2,1)S(1)}, u32[]{:S(2)}, u32[]{:S(2)}) collective-permute-start(bf16[528,128]{1,0:T(8,128)(2,1)S(1)} %collective-permute-done.near), channel_id=1, source_target_pairs={{0,2},{1,7},{2,4},{3,1},{4,6},{5,3},{6,0},{7,5},{8,10},{9,15},{10,... | collective-permute-start | bytes 405512 | tf_op jit(solution)/shard_map/ppermute | solution.py:238
  16.8 0.0 collective-permute-start.4
  16.8 0.9 %collective-permute-start.6 = (bf16[528,128]{1,0:T(8,128)(2,1)S(1)}, bf16[528,128]{1,0:T(8,128)(2,1)S(1)}, u32[]{:S(2)}, u32[]{:S(2)}) collective-permute-start(bf16[528,128]{1,0:T(8,128)(2,1)S(1)} %collective-permute-done.near), channel_id=1, source_target_pairs={{0,3},{1,6},{2,5},{3,0},{4,7},{5,2},{6,1},{7,4},{8,11},{9,14},{10,... | collective-permute-start | bytes 405512 | tf_op jit(solution)/shard_map/ppermute | solution.py:238
  17.7 0.0 collective-permute-done.1.far
  17.7 1.0 %collective-permute-start.5 = (bf16[528,128]{1,0:T(8,128)(2,1)S(1)}, bf16[528,128]{1,0:T(8,128)(2,1)S(1)}, u32[]{:S(2)}, u32[]{:S(2)}) collective-permute-start(bf16[528,128]{1,0:T(8,128)(2,1)S(1)} %collective-permute-done.1.far), channel_id=1, source_target_pairs={{0,1},{1,0},{2,3},{3,2},{4,5},{5,4},{6,7},{7,6},{8,9},{9,8},{10,11... | collective-permute-start | bytes 405512 | tf_op jit(solution)/shard_map/ppermute | solution.py:238
  18.6 1.1 %shard_map.110 = (bf16[256,768]{1,0:T(8,128)(2,1)S(1)}, bf16[256,768]{1,0:T(8,128)(2,1)S(1)}) custom-call(bf16[256,768]{1,0:T(8,128)(2,1)} %queries_hbm.1, bf16[256,768]{1,0:T(8,128)(2,1)} %grads_hbm.1), custom_call_target="tpu_custom_call" | custom-call | bytes 2097152 | tf_op jit(solution)/shard_map/pallas_call | solution.py:43
  19.8 0.0 collective-permute-done.3.own_s
  19.8 1.7 %collective-permute-done.2.opposite = bf16[528,128]{1,0:T(8,128)(2,1)S(1)} collective-permute-done((bf16[528,128]{1,0:T(8,128)(2,1)S(1)}, bf16[528,128]{1,0:T(8,128)(2,1)S(1)}, u32[]{:S(2)}, u32[]{:S(2)}) %collective-permute-start.2) | collective-permute-done | bytes 135200 | tf_op jit(solution)/shard_map/ppermute | solution.py:238
  21.5 0.0 collective-permute-done.4.near_s
  21.5 0.0 collective-permute-done.6.opposite_s
  21.5 0.0 collective-permute-done.5.far_s
  21.5 12.0 %shard_map.112 = (bf16[256,768]{1,0:T(8,128)(2,1)}, f32[256,768]{1,0:T(8,128)}, bf16[256,256]{1,0:T(8,128)(2,1)S(1)}, bf16[256,256]{1,0:T(8,128)(2,1)S(1)}, bf16...) custom-call(bf16[256,768]{1,0:T(8,128)(2,1)S(1)} %get-tuple-element., ...), custom_call_target="tpu_custom_call" | custom-call | flops 4831838208 | bytes 4194304 | tf_op jit(solution)/shard_map/pallas_call | solution.py:190
  33.6 1.5 %collective-permute-start.7 = (bf16[3,256,256]{2,1,0:T(8,128)(2,1)S(1)}, bf16[3,256,256]{2,1,0:T(8,128)(2,1)S(1)}, u32[]{:S(2)}, u32[]{:S(2)}) collective-permute-start(bf16[3,256,256]{2,1,0:T(8,128)(2,1)S(1)} %get-tuple-element.24), channel_id=1, source_target_pairs={{0,1},{1,0},{2,3},{3,2},{4,5},{5,4},{6,7},{7,6},{8,9},{9,8},{10,11... | collective-permute-start | bytes 1179656 | tf_op jit(solution)/shard_map/ppermute | solution.py:238
  35.0 1.2 %collective-permute-start.8 = (bf16[256,256]{1,0:T(8,128)(2,1)S(1)}, bf16[256,256]{1,0:T(8,128)(2,1)S(1)}, u32[]{:S(2)}, u32[]{:S(2)}) collective-permute-start(bf16[256,256]{1,0:T(8,128)(2,1)S(1)} %get-tuple-element.26), channel_id=1, source_target_pairs={{2,0},{7,1},{4,2},{1,3},{6,4},{3,5},{0,6},{5,7},{10,8},{15,9},{12,... | collective-permute-start | bytes 393224 | tf_op jit(solution)/shard_map/ppermute | solution.py:238
  36.2 0.0 collective-permute-start.9
  36.3 4.5 %collective-permute-done.8 = bf16[256,256]{1,0:T(8,128)(2,1)S(1)} collective-permute-done((bf16[256,256]{1,0:T(8,128)(2,1)S(1)}, bf16[256,256]{1,0:T(8,128)(2,1)S(1)}, u32[]{:S(2)}, u32[]{:S(2)}) %collective-permute-start.8) | collective-permute-done | bytes 131104 | tf_op jit(solution)/shard_map/ppermute | solution.py:238
  40.8 0.6 collective-permute-done.9
  41.4 0.0 collective-permute-done.7
  41.4 0.1 fusion.2
  41.5 2.4 %collective-permute-start.10 = (bf16[256,256]{1,0:T(8,128)(2,1)S(1)}, bf16[256,256]{1,0:T(8,128)(2,1)S(1)}, u32[]{:S(2)}, u32[]{:S(2)}) collective-permute-start(bf16[256,256]{1,0:T(8,128)(2,1)S(1)} %fusion.2), channel_id=1, source_target_pairs={{2,0},{7,1},{4,2},{1,3},{6,4},{3,5},{0,6},{5,7},{10,8},{15,9},{12,... | collective-permute-start | bytes 393224 | tf_op jit(solution)/shard_map/ppermute | solution.py:238
  43.8 0.1 collective-permute-start.11
  43.9 8.1 %all-gather.3.cloned.1.call-done = f32[2048,128]{1,0:T(8,128)} async-done(((f32[256,128]{1,0:T(8,128)}), f32[2048,128]{1,0:T(8,128)}) %all-gather.3.cloned.1.call-update) | async-done | bytes 1048592 | tf_op jit(solution)/shard_map/all_gather | solution.py:248
  52.0 0.8 slice_reduce_fusion
  52.8 0.0 collective-permute-start.12
  52.8 1.2 %collective-permute-done.12 = f32[8,128]{1,0:T(8,128)S(1)} collective-permute-done((f32[8,128]{1,0:T(8,128)S(1)}, f32[8,128]{1,0:T(8,128)S(1)}, u32[]{:S(2)}, u32[]{:S(2)}) %collective-permute-start.12) | collective-permute-done | bytes 4128 | tf_op jit(solution)/shard_map/ppermute | solution.py:243
  53.9 1.5 %collective-permute-start.13 = (f32[8,128]{1,0:T(8,128)S(1)}, f32[8,128]{1,0:T(8,128)S(1)}, u32[]{:S(2)}, u32[]{:S(2)}) collective-permute-start(f32[8,128]{1,0:T(8,128)S(1)} %add.49), channel_id=1, source_target_pairs={{0,2},{1,3},{2,0},{3,1},{4,6},{5,7},{6,4},{7,5},{8,10},{9,11},{10,... | collective-permute-start | bytes 12296 | tf_op jit(solution)/shard_map/ppermute | solution.py:243
  55.4 2.7 %collective-permute-start.14 = (f32[8,128]{1,0:T(8,128)S(1)}, f32[8,128]{1,0:T(8,128)S(1)}, u32[]{:S(2)}, u32[]{:S(2)}) collective-permute-start(f32[8,128]{1,0:T(8,128)S(1)} %add.49), channel_id=1, source_target_pairs={{0,4},{1,5},{2,6},{3,7},{4,0},{5,1},{6,2},{7,3},{8,12},{9,13},{10,... | collective-permute-start | bytes 12296 | tf_op jit(solution)/shard_map/ppermute | solution.py:243
  58.1 0.5 collective-permute-start.15
  58.6 0.0 collective-permute-done.10
  58.6 0.0 collective-permute-done.11
  58.6 0.1 fusion.4
  58.7 1.8 %collective-permute-done.14 = f32[8,128]{1,0:T(8,128)S(1)} collective-permute-done((f32[8,128]{1,0:T(8,128)S(1)}, f32[8,128]{1,0:T(8,128)S(1)}, u32[]{:S(2)}, u32[]{:S(2)}) %collective-permute-start.14) | collective-permute-done | bytes 4128 | tf_op jit(solution)/shard_map/ppermute | solution.py:243
  60.5 2.4 %collective-permute-done.15 = f32[8,128]{1,0:T(8,128)S(1)} collective-permute-done((f32[8,128]{1,0:T(8,128)S(1)}, f32[8,128]{1,0:T(8,128)S(1)}, u32[]{:S(2)}, u32[]{:S(2)}) %collective-permute-start.15) | collective-permute-done | bytes 4128 | tf_op jit(solution)/shard_map/ppermute | solution.py:243
  62.9 2.1 %collective-permute-start.16 = (f32[8,128]{1,0:T(8,128)S(1)}, f32[8,128]{1,0:T(8,128)S(1)}, u32[]{:S(2)}, u32[]{:S(2)}) collective-permute-start(f32[8,128]{1,0:T(8,128)S(1)} %add_add_fusion.1), channel_id=1, source_target_pairs={{0,8},{1,9},{2,10},{3,11},{4,12},{5,13},{6,14},{7,15},{8,0},{9,1},... | collective-permute-start | bytes 12296 | tf_op jit(solution)/shard_map/ppermute | solution.py:243
  65.0 1.4 %collective-permute-start.17 = (f32[8,128]{1,0:T(8,128)S(1)}, f32[8,128]{1,0:T(8,128)S(1)}, u32[]{:S(2)}, u32[]{:S(2)}) collective-permute-start(f32[8,128]{1,0:T(8,128)S(1)} %add_add_fusion.1), channel_id=1, source_target_pairs={{0,16},{1,17},{2,18},{3,19},{4,20},{5,21},{6,22},{7,23},{8,24},{9,... | collective-permute-start | bytes 12296 | tf_op jit(solution)/shard_map/ppermute | solution.py:243
  66.5 0.5 collective-permute-start.18
  67.0 0.7 fusion.6
  67.7 0.3 collective-permute-done.16
  68.0 0.6 collective-permute-done.17
  68.6 1.4 %collective-permute-done.18 = f32[8,128]{1,0:T(8,128)S(1)} collective-permute-done((f32[8,128]{1,0:T(8,128)S(1)}, f32[8,128]{1,0:T(8,128)S(1)}, u32[]{:S(2)}, u32[]{:S(2)}) %collective-permute-start.18) | collective-permute-done | bytes 4128 | tf_op jit(solution)/shard_map/ppermute | solution.py:243
  70.1 0.6 subtract_bitcast_fusion
  (5 shorter events, 0.0 us)
Async XLA Ops:
  7.2 44.8 %all-gather.3.cloned.1.call-start = ((), (), s32[]{:S(2)}) async-start(), calls=%async_computation | async-start | bytes 1179648 | tf_op jit(solution)/shard_map/all_gather | solution.py:248
  8.9 6.4 %collective-permute-start = (bf16[528,128]{1,0:T(8,128)(2,1)S(1)}, bf16[528,128]{1,0:T(8,128)(2,1)S(1)}, u32[]{:S(2)}, u32[]{:S(2)}) collective-permute-start(bf16[528,128]{1,0:T(8,128)(2,1)S(1)} %get-tuple-element.20.own), channel_id=1, source_target_pairs={{0,2},{1,7},{2,4},{3,1},{4,6},{5,3},{6,0},{7,5},{8,10},{9,15},{10,... | collective-permute-start | bytes 405512 | tf_op jit(solution)/shard_map/ppermute | solution.py:238
  10.5 7.2 %collective-permute-start.1 = (bf16[528,128]{1,0:T(8,128)(2,1)S(1)}, bf16[528,128]{1,0:T(8,128)(2,1)S(1)}, u32[]{:S(2)}, u32[]{:S(2)}) collective-permute-start(bf16[528,128]{1,0:T(8,128)(2,1)S(1)} %get-tuple-element.20.own), channel_id=1, source_target_pairs={{2,0},{7,1},{4,2},{1,3},{6,4},{3,5},{0,6},{5,7},{10,8},{15,9},{12,... | collective-permute-start | bytes 405512 | tf_op jit(solution)/shard_map/ppermute | solution.py:238
  12.2 7.5 %collective-permute-start.3 = (bf16[528,128]{1,0:T(8,128)(2,1)S(1)}, bf16[528,128]{1,0:T(8,128)(2,1)S(1)}, u32[]{:S(2)}, u32[]{:S(2)}) collective-permute-start(bf16[528,128]{1,0:T(8,128)(2,1)S(1)} %get-tuple-element.20.own), channel_id=1, source_target_pairs={{0,1},{1,0},{2,3},{3,2},{4,5},{5,4},{6,7},{7,6},{8,9},{9,8},{10,11... | collective-permute-start | bytes 405512 | tf_op jit(solution)/shard_map/ppermute | solution.py:238
  15.3 6.2 %collective-permute-start.2 = (bf16[528,128]{1,0:T(8,128)(2,1)S(1)}, bf16[528,128]{1,0:T(8,128)(2,1)S(1)}, u32[]{:S(2)}, u32[]{:S(2)}) collective-permute-start(bf16[528,128]{1,0:T(8,128)(2,1)S(1)} %collective-permute-done.near), channel_id=1, source_target_pairs={{0,2},{1,7},{2,4},{3,1},{4,6},{5,3},{6,0},{7,5},{8,10},{9,15},{10,... | collective-permute-start | bytes 405512 | tf_op jit(solution)/shard_map/ppermute | solution.py:238
  16.8 4.7 %collective-permute-start.4 = (bf16[528,128]{1,0:T(8,128)(2,1)S(1)}, bf16[528,128]{1,0:T(8,128)(2,1)S(1)}, u32[]{:S(2)}, u32[]{:S(2)}) collective-permute-start(bf16[528,128]{1,0:T(8,128)(2,1)S(1)} %collective-permute-done.near), channel_id=1, source_target_pairs={{0,1},{1,0},{2,3},{3,2},{4,5},{5,4},{6,7},{7,6},{8,9},{9,8},{10,11... | collective-permute-start | bytes 405512 | tf_op jit(solution)/shard_map/ppermute | solution.py:238
  16.8 4.7 %collective-permute-start.6 = (bf16[528,128]{1,0:T(8,128)(2,1)S(1)}, bf16[528,128]{1,0:T(8,128)(2,1)S(1)}, u32[]{:S(2)}, u32[]{:S(2)}) collective-permute-start(bf16[528,128]{1,0:T(8,128)(2,1)S(1)} %collective-permute-done.near), channel_id=1, source_target_pairs={{0,3},{1,6},{2,5},{3,0},{4,7},{5,2},{6,1},{7,4},{8,11},{9,14},{10,... | collective-permute-start | bytes 405512 | tf_op jit(solution)/shard_map/ppermute | solution.py:238
  17.7 3.8 %collective-permute-start.5 = (bf16[528,128]{1,0:T(8,128)(2,1)S(1)}, bf16[528,128]{1,0:T(8,128)(2,1)S(1)}, u32[]{:S(2)}, u32[]{:S(2)}) collective-permute-start(bf16[528,128]{1,0:T(8,128)(2,1)S(1)} %collective-permute-done.1.far), channel_id=1, source_target_pairs={{0,1},{1,0},{2,3},{3,2},{4,5},{5,4},{6,7},{7,6},{8,9},{9,8},{10,11... | collective-permute-start | bytes 405512 | tf_op jit(solution)/shard_map/ppermute | solution.py:238
  33.6 7.8 %collective-permute-start.7 = (bf16[3,256,256]{2,1,0:T(8,128)(2,1)S(1)}, bf16[3,256,256]{2,1,0:T(8,128)(2,1)S(1)}, u32[]{:S(2)}, u32[]{:S(2)}) collective-permute-start(bf16[3,256,256]{2,1,0:T(8,128)(2,1)S(1)} %get-tuple-element.24), channel_id=1, source_target_pairs={{0,1},{1,0},{2,3},{3,2},{4,5},{5,4},{6,7},{7,6},{8,9},{9,8},{10,11... | collective-permute-start | bytes 1179656 | tf_op jit(solution)/shard_map/ppermute | solution.py:238
  35.0 5.8 %collective-permute-start.8 = (bf16[256,256]{1,0:T(8,128)(2,1)S(1)}, bf16[256,256]{1,0:T(8,128)(2,1)S(1)}, u32[]{:S(2)}, u32[]{:S(2)}) collective-permute-start(bf16[256,256]{1,0:T(8,128)(2,1)S(1)} %get-tuple-element.26), channel_id=1, source_target_pairs={{2,0},{7,1},{4,2},{1,3},{6,4},{3,5},{0,6},{5,7},{10,8},{15,9},{12,... | collective-permute-start | bytes 393224 | tf_op jit(solution)/shard_map/ppermute | solution.py:238
  36.2 5.1 %collective-permute-start.9 = (bf16[256,256]{1,0:T(8,128)(2,1)S(1)}, bf16[256,256]{1,0:T(8,128)(2,1)S(1)}, u32[]{:S(2)}, u32[]{:S(2)}) collective-permute-start(bf16[256,256]{1,0:T(8,128)(2,1)S(1)} %get-tuple-element.27), channel_id=1, source_target_pairs={{3,0},{6,1},{5,2},{0,3},{7,4},{2,5},{1,6},{4,7},{11,8},{14,9},{13,... | collective-permute-start | bytes 393224 | tf_op jit(solution)/shard_map/ppermute | solution.py:238
  41.5 17.2 %collective-permute-start.10 = (bf16[256,256]{1,0:T(8,128)(2,1)S(1)}, bf16[256,256]{1,0:T(8,128)(2,1)S(1)}, u32[]{:S(2)}, u32[]{:S(2)}) collective-permute-start(bf16[256,256]{1,0:T(8,128)(2,1)S(1)} %fusion.2), channel_id=1, source_target_pairs={{2,0},{7,1},{4,2},{1,3},{6,4},{3,5},{0,6},{5,7},{10,8},{15,9},{12,... | collective-permute-start | bytes 393224 | tf_op jit(solution)/shard_map/ppermute | solution.py:238
  43.8 14.8 %collective-permute-start.11 = (bf16[256,256]{1,0:T(8,128)(2,1)S(1)}, bf16[256,256]{1,0:T(8,128)(2,1)S(1)}, u32[]{:S(2)}, u32[]{:S(2)}) collective-permute-start(bf16[256,256]{1,0:T(8,128)(2,1)S(1)} %fusion.5), channel_id=1, source_target_pairs={{0,2},{1,7},{2,4},{3,1},{4,6},{5,3},{6,0},{7,5},{8,10},{9,15},{10,... | collective-permute-start | bytes 393224 | tf_op jit(solution)/shard_map/ppermute | solution.py:238
  52.8 1.2 %collective-permute-start.12 = (f32[8,128]{1,0:T(8,128)S(1)}, f32[8,128]{1,0:T(8,128)S(1)}, u32[]{:S(2)}, u32[]{:S(2)}) collective-permute-start(f32[8,128]{1,0:T(8,128)S(1)} %slice_reduce_fusion), channel_id=1, source_target_pairs={{0,1},{1,0},{2,3},{3,2},{4,5},{5,4},{6,7},{7,6},{8,9},{9,8},{10,11... | collective-permute-start | bytes 12296 | tf_op jit(solution)/shard_map/ppermute | solution.py:243
  53.9 4.8 %collective-permute-start.13 = (f32[8,128]{1,0:T(8,128)S(1)}, f32[8,128]{1,0:T(8,128)S(1)}, u32[]{:S(2)}, u32[]{:S(2)}) collective-permute-start(f32[8,128]{1,0:T(8,128)S(1)} %add.49), channel_id=1, source_target_pairs={{0,2},{1,3},{2,0},{3,1},{4,6},{5,7},{6,4},{7,5},{8,10},{9,11},{10,... | collective-permute-start | bytes 12296 | tf_op jit(solution)/shard_map/ppermute | solution.py:243
  55.4 5.1 %collective-permute-start.14 = (f32[8,128]{1,0:T(8,128)S(1)}, f32[8,128]{1,0:T(8,128)S(1)}, u32[]{:S(2)}, u32[]{:S(2)}) collective-permute-start(f32[8,128]{1,0:T(8,128)S(1)} %add.49), channel_id=1, source_target_pairs={{0,4},{1,5},{2,6},{3,7},{4,0},{5,1},{6,2},{7,3},{8,12},{9,13},{10,... | collective-permute-start | bytes 12296 | tf_op jit(solution)/shard_map/ppermute | solution.py:243
  58.1 4.8 %collective-permute-start.15 = (f32[8,128]{1,0:T(8,128)S(1)}, f32[8,128]{1,0:T(8,128)S(1)}, u32[]{:S(2)}, u32[]{:S(2)}) collective-permute-start(f32[8,128]{1,0:T(8,128)S(1)} %add.49), channel_id=1, source_target_pairs={{0,6},{1,7},{2,4},{3,5},{4,2},{5,3},{6,0},{7,1},{8,14},{9,15},{10,... | collective-permute-start | bytes 12296 | tf_op jit(solution)/shard_map/ppermute | solution.py:243
  62.9 5.1 %collective-permute-start.16 = (f32[8,128]{1,0:T(8,128)S(1)}, f32[8,128]{1,0:T(8,128)S(1)}, u32[]{:S(2)}, u32[]{:S(2)}) collective-permute-start(f32[8,128]{1,0:T(8,128)S(1)} %add_add_fusion.1), channel_id=1, source_target_pairs={{0,8},{1,9},{2,10},{3,11},{4,12},{5,13},{6,14},{7,15},{8,0},{9,1},... | collective-permute-start | bytes 12296 | tf_op jit(solution)/shard_map/ppermute | solution.py:243
  65.0 3.6 %collective-permute-start.17 = (f32[8,128]{1,0:T(8,128)S(1)}, f32[8,128]{1,0:T(8,128)S(1)}, u32[]{:S(2)}, u32[]{:S(2)}) collective-permute-start(f32[8,128]{1,0:T(8,128)S(1)} %add_add_fusion.1), channel_id=1, source_target_pairs={{0,16},{1,17},{2,18},{3,19},{4,20},{5,21},{6,22},{7,23},{8,24},{9,... | collective-permute-start | bytes 12296 | tf_op jit(solution)/shard_map/ppermute | solution.py:243
  66.5 3.6 %collective-permute-start.18 = (f32[8,128]{1,0:T(8,128)S(1)}, f32[8,128]{1,0:T(8,128)S(1)}, u32[]{:S(2)}, u32[]{:S(2)}) collective-permute-start(f32[8,128]{1,0:T(8,128)S(1)} %add_add_fusion.1), channel_id=1, source_target_pairs={{0,24},{1,25},{2,26},{3,27},{4,28},{5,29},{6,30},{7,31},{8,16},{9,... | collective-permute-start | bytes 12296 | tf_op jit(solution)/shard_map/ppermute | solution.py:243
Sparse Core Ops, SparseCore 0:
  10.4 41.5 all-gather.2

commit v11 on v7

--- a/solution.py
+++ b/solution.py
@@ -28,6 +28,31 @@
     return jnp.dot(a, b, preferred_element_type=jnp.float32)
 
 
+def fetch_kernel(queries_hbm, grads_hbm, queries, grads, arrived):
+    fetches = [
+        pltpu.make_async_copy(source, target, arrived.at[number])
+        for number, (source, target) in enumerate(((queries_hbm, queries), (grads_hbm, grads)))
+    ]
+    for fetch in fetches:
+        fetch.start()
+    for fetch in fetches:
+        fetch.wait()
+
+
+def fetch(queries, grads):
+    return pl.pallas_call(
+        fetch_kernel,
+        out_shape=(
+            pltpu.VMEM(queries.shape, jnp.bfloat16),
+            pltpu.VMEM(grads.shape, jnp.bfloat16),
+        ),
+        in_specs=[HBM] * 2,
+        out_specs=(VMEM,) * 2,
+        scratch_shapes=[pltpu.SemaphoreType.DMA((2,))],
+        cost_estimate=pl.CostEstimate(flops=0, bytes_accessed=2 * MIB, transcendentals=0),
+    )(*(pltpu.with_memory_space_constraint(x, pltpu.HBM) for x in (queries, grads)))
+
+
 def split(value):
     high = value.astype(jnp.bfloat16).astype(jnp.float32)
     middle = (value - high).astype(jnp.bfloat16).astype(jnp.float32)
@@ -57,7 +82,7 @@
     wide = (ROWS // 128, 128)
     return pl.pallas_call(
         pack_kernel,
-        out_shape=jax.ShapeDtypeStruct((PACKED, HEAD_DIM), jnp.bfloat16),
+        out_shape=pltpu.VMEM((PACKED, HEAD_DIM), jnp.bfloat16),
         in_specs=[VMEM] * 5,
         out_specs=VMEM,
         cost_estimate=pl.CostEstimate(flops=10000, bytes_accessed=MIB // 2, transcendentals=0),
@@ -69,19 +94,11 @@
 
 
 def attend_kernel(
-    queries_hbm, grads_hbm, own_hbm, near, far, opposite, own_s, near_s, far_s, opposite_s,
+    queries, grads, own, near, far, opposite, own_s, near_s, far_s, opposite_s,
     attention, grad_queries, own_part, near_part, far_part, opposite_part, swap_parts,
     opposite_s_part, margin,
-    queries, grads, own, arrived, keys, values, keys_t, values_t, bias, scores, probs, grad_scores, acc_k, acc_v,
+    keys, values, keys_t, values_t, bias, scores, probs, grad_scores, acc_k, acc_v,
 ):
-    fetches = [
-        pltpu.make_async_copy(source, target, arrived.at[number])
-        for number, (source, target) in enumerate(
-            ((own_hbm, own), (queries_hbm, queries), (grads_hbm, grads))
-        )
-    ]
-    for fetch in fetches:
-        fetch.start()
     place = lax.axis_index("ka")
     core = lax.rem(place, 2)
     chip = lax.rem(place // 2, CHIPS)
@@ -94,9 +111,7 @@
         swap_parts.at[0], swap_parts.at[1], swap_parts.at[2], opposite_s_part,
     )
     totals = None
-    for block, span in spans()[::-1]:
-        if block == 0:
-            fetches[0].wait()
+    for block, span in spans():
         key = blocks[block][:ROWS, :]
         value = blocks[block][ROWS : 2 * ROWS, :]
         keys[span, :] = key
@@ -114,7 +129,7 @@
 
     pair = lax.axis_index("pb") * 2 + place // BLOCKS
     value = total_of(0, 3) / total_of(6, 7) - total_of(3, 6) / total_of(7, 8)
-    margin[...] = jnp.broadcast_to(jnp.where(wide == pair, value, 0.0)[None], margin.shape)
+    margin[...] = jnp.where(wide == pair, value, 0.0)
     cut = total_of(8, 9)[:1].astype(jnp.int32)
     row = first_row + lax.broadcasted_iota(jnp.int32, (ROWS, ROWS), 0)
     lane = lax.broadcasted_iota(jnp.int32, (ROWS, ROWS), 1)
@@ -141,14 +156,12 @@
     def max_of(top):
         return jnp.max(top, axis=1, keepdims=True) * SCALE2
 
-    fetches[1].wait()
     top = total = None
     for block, span in spans():
         top = score_step(0, span, top)
     row_max = max_of(top)
     for block, span in spans():
         total = prob_step(0, span, row_max, total)
-    fetches[2].wait()
     for head in range(HEADS):
         slot = head % 2
         query = queries[:, columns[head]]
@@ -187,7 +200,6 @@
 
 
 def attend(queries, grads, blocks):
-    far_off = (queries, grads, blocks[0])
     width = HEADS * HEAD_DIM
     part = jax.ShapeDtypeStruct((ROWS, 2 * HEAD_DIM), jnp.bfloat16)
     return pl.pallas_call(
@@ -201,15 +213,11 @@
             part,
             jax.ShapeDtypeStruct((3, ROWS, 2 * HEAD_DIM), jnp.bfloat16),
             part,
-            jax.ShapeDtypeStruct((8, 8, HEAD_DIM), jnp.float32),
+            jax.ShapeDtypeStruct((8, HEAD_DIM), jnp.float32),
         ),
-        in_specs=[HBM] * 3 + [VMEM] * 7,
+        in_specs=[VMEM] * (2 + BLOCKS),
         out_specs=(VMEM,) * 9,
         scratch_shapes=[
-            pltpu.VMEM((ROWS, width), jnp.bfloat16),
-            pltpu.VMEM((ROWS, width), jnp.bfloat16),
-            pltpu.VMEM((PACKED, HEAD_DIM), jnp.bfloat16),
-            pltpu.SemaphoreType.DMA((3,)),
             pltpu.VMEM((PAIR_SPAN, HEAD_DIM), jnp.bfloat16),
             pltpu.VMEM((PAIR_SPAN, HEAD_DIM), jnp.bfloat16),
             pltpu.VMEM((HEAD_DIM, PAIR_SPAN), jnp.bfloat16),
@@ -227,7 +235,7 @@
             bytes_accessed=4 * MIB,
             transcendentals=HEADS * ROWS * PAIR_SPAN,
         ),
-    )(*(pltpu.with_memory_space_constraint(x, pltpu.HBM) for x in far_off), *blocks[1:])
+    )(queries, grads, *blocks)
 
 
 def at(half, chip, core):
@@ -245,7 +253,12 @@
     def send(block, route):
         return lax.ppermute(block, "ka", route)
 
+    def exchange(table, axis, mask):
+        route = [(place, place ^ mask) for place in range(16)]
+        return table + lax.ppermute(table, axis, route)
+
     own = pack(key_heads, value_heads, token_logprob, doc_ids, response)
+    queries, grad_output = fetch(queries, grad_output)
     near = send(own, ahead)
     far = send(own, back)
     own_s = send(own, swap)
@@ -258,23 +271,26 @@
     attention, grad_queries, own_p, near_p, far_p, opposite_p, swap_p, opposite_s_p, margin = (
         attend(queries, grad_output, blocks)
     )
+    swapped = send(swap_p, swap)
     passed = send(opposite_p, back)
     passed_s = send(opposite_s_p, cross_back)
-    swapped = send(swap_p, swap)
+    margin = exchange(margin, "pb", 8)
     swapped, margin = lax.optimization_barrier((swapped, margin))
-    columns = [list(range(low, 16, 2)) for low in (0, 1)]
-    margin = jnp.sum(lax.all_to_all(margin, "pb", 0, 0, axis_index_groups=columns, tiled=True), axis=0)
+    margin = exchange(margin, "pb", 4)
     passed, margin = lax.optimization_barrier((passed, margin))
     wide = jnp.float32
     near_sum = (near_p.astype(wide) + swapped[1] + passed + passed_s).astype(jnp.bfloat16)
     far_sum = far_p + swapped[2]
     near_part = send(near_sum, back)
     far_part = send(far_sum, ahead)
+    margin = exchange(margin, "pb", 2)
     far_part, margin = lax.optimization_barrier((far_part, margin))
-    turns = [[(place, place ^ bits) for place in range(256)] for bits in (8, 16, 24)]
-    margin = sum((lax.ppermute(margin, ("pb", "ka"), turn) for turn in turns), margin)
+    margin = exchange(margin, "pb", 1)
+    margin = exchange(margin, "ka", 8)
     total = own_p.astype(wide) + swapped[0] + near_part + far_part
-    return (attention, grad_queries, total[:, :HEAD_DIM], total[:, HEAD_DIM:], margin[0, :PAIRS])
+    return (
+        attention, grad_queries, total[:, :HEAD_DIM], total[:, HEAD_DIM:], margin[0, :PAIRS]
+    )
 
 
 def solution(mesh):

time: 63.6 us -> 58 us (0.912)
  the two profiles are of different devices: /device:TPU:6 before, /device:TPU:8 now
where the time goes in v11:
time: 58 us; the launch traced here: 57.8 us
  waiting for transfers between devices  20.9 us (36%)
  starting transfers between devices  20.5 us (35%)
  Pallas kernels  14.3 us (25%)
  local copies, waits for them, and re-layouts  1.23 us (2%)
  between operations  0.69 us (1%)
    ppermute x5, starting transfers between devices, exchange(): return table + lax.ppermute(table, axis, route)  13 us
    pallas_call x1, Pallas kernels, attend(): pl.pallas_call(attend_kernel, out_shape=(jax.ShapeDtypeStruct((ROWS, widt...  12.1 us
    ppermute x5, waiting for transfers between devices, exchange(): return table + lax.ppermute(table, axis, route)  10.9 us
    ppermute x12, waiting for transfers between devices, send(): return lax.ppermute(block, 'ka', route)  10 us
    ppermute x12, starting transfers between devices, send(): return lax.ppermute(block, 'ka', route)  7.59 us
  transfers between devices with their start and end apart: 17, of which 10 were waited for; matrix products, arithmetic and copies ran while one was open for 2% of the time, Pallas kernels for 2%

profile of v11, /device:TPU:8, one launch (start us, length us, event | category | flops | bytes accessed | tf_op | source)
XLA Modules:
  0.0 57.8 jit_solution(8804830391118159911)
XLA Ops:
  0.6 1.0 %shard_map.111.own = bf16[528,128]{1,0:T(8,128)(2,1)S(1)} custom-call(bf16[256,128]{1,0:T(8,128)(2,1)} %keys.1, bf16[256,128]{1,0:T(8,128)(2,1)} %values.1, f32[2,128]{1,0:T(2,128)} %bitcast.13, s32[2,128]{1,0:T(2,128)} %bitcast.14, s32[2,128]{1,0:T(2,128)} %bitcast.15), custom_call_target="tpu_custom_call" | custom-call | flops 10000 | bytes 524288 | tf_op jit(solution)/shard_map/pallas_call | solution.py:83
  1.7 2.8 %collective-permute-start.1 = (bf16[528,128]{1,0:T(8,128)(2,1)S(1)}, bf16[528,128]{1,0:T(8,128)(2,1)S(1)}, u32[]{:S(2)}, u32[]{:S(2)}) collective-permute-start(bf16[528,128]{1,0:T(8,128)(2,1)S(1)} %shard_map.111.own), channel_id=1, source_target_pairs={{2,0},{7,1},{4,2},{1,3},{6,4},{3,5},{0,6},{5,7},{10,8},{15,9},{12,... | collective-permute-start | bytes 405512 | tf_op jit(solution)/shard_map/ppermute | solution.py:254
  4.5 0.0 collective-permute-start
  4.5 0.0 collective-permute-start.3
  4.5 3.6 %collective-permute-done.1.far = bf16[528,128]{1,0:T(8,128)(2,1)S(1)} collective-permute-done((bf16[528,128]{1,0:T(8,128)(2,1)S(1)}, bf16[528,128]{1,0:T(8,128)(2,1)S(1)}, u32[]{:S(2)}, u32[]{:S(2)}) %collective-permute-start.1) | collective-permute-done | bytes 135200 | tf_op jit(solution)/shard_map/ppermute | solution.py:254
  8.1 0.0 collective-permute-start.5
  8.1 2.6 %collective-permute-done.near = bf16[528,128]{1,0:T(8,128)(2,1)S(1)} collective-permute-done((bf16[528,128]{1,0:T(8,128)(2,1)S(1)}, bf16[528,128]{1,0:T(8,128)(2,1)S(1)}, u32[]{:S(2)}, u32[]{:S(2)}) %collective-permute-start) | collective-permute-done | bytes 135200 | tf_op jit(solution)/shard_map/ppermute | solution.py:254
  10.7 0.0 collective-permute-start.6
  10.7 0.6 %collective-permute-start.4 = (bf16[528,128]{1,0:T(8,128)(2,1)S(1)}, bf16[528,128]{1,0:T(8,128)(2,1)S(1)}, u32[]{:S(2)}, u32[]{:S(2)}) collective-permute-start(bf16[528,128]{1,0:T(8,128)(2,1)S(1)} %collective-permute-done.near), channel_id=1, source_target_pairs={{0,1},{1,0},{2,3},{3,2},{4,5},{5,4},{6,7},{7,6},{8,9},{9,8},{10,11... | collective-permute-start | bytes 405512 | tf_op jit(solution)/shard_map/ppermute | solution.py:254
  11.4 1.5 %collective-permute-start.2 = (bf16[528,128]{1,0:T(8,128)(2,1)S(1)}, bf16[528,128]{1,0:T(8,128)(2,1)S(1)}, u32[]{:S(2)}, u32[]{:S(2)}) collective-permute-start(bf16[528,128]{1,0:T(8,128)(2,1)S(1)} %collective-permute-done.near), channel_id=1, source_target_pairs={{0,2},{1,7},{2,4},{3,1},{4,6},{5,3},{6,0},{7,5},{8,10},{9,15},{10,... | collective-permute-start | bytes 405512 | tf_op jit(solution)/shard_map/ppermute | solution.py:254
  12.9 1.1 %shard_map.110 = (bf16[256,768]{1,0:T(8,128)(2,1)S(1)}, bf16[256,768]{1,0:T(8,128)(2,1)S(1)}) custom-call(bf16[256,768]{1,0:T(8,128)(2,1)} %queries_hbm.1, bf16[256,768]{1,0:T(8,128)(2,1)} %grads_hbm.1), custom_call_target="tpu_custom_call" | custom-call | bytes 2097152 | tf_op jit(solution)/shard_map/pallas_call | solution.py:43
  14.0 0.0 collective-permute-done.3.own_s
  14.0 0.0 collective-permute-done.5.far_s
  14.0 1.1 %collective-permute-done.6.opposite_s = bf16[528,128]{1,0:T(8,128)(2,1)S(1)} collective-permute-done((bf16[528,128]{1,0:T(8,128)(2,1)S(1)}, bf16[528,128]{1,0:T(8,128)(2,1)S(1)}, u32[]{:S(2)}, u32[]{:S(2)}) %collective-permute-start.6) | collective-permute-done | bytes 135200 | tf_op jit(solution)/shard_map/ppermute | solution.py:254
  15.2 0.0 collective-permute-done.4.near_s
  15.2 2.4 %collective-permute-done.2.opposite = bf16[528,128]{1,0:T(8,128)(2,1)S(1)} collective-permute-done((bf16[528,128]{1,0:T(8,128)(2,1)S(1)}, bf16[528,128]{1,0:T(8,128)(2,1)S(1)}, u32[]{:S(2)}, u32[]{:S(2)}) %collective-permute-start.2) | collective-permute-done | bytes 135200 | tf_op jit(solution)/shard_map/ppermute | solution.py:254
  17.6 12.1 %shard_map.112 = (bf16[256,768]{1,0:T(8,128)(2,1)}, f32[256,768]{1,0:T(8,128)}, bf16[256,256]{1,0:T(8,128)(2,1)S(1)}, bf16[256,256]{1,0:T(8,128)(2,1)S(1)}, bf16...) custom-call(bf16[256,768]{1,0:T(8,128)(2,1)S(1)} %get-tuple-element., ...), custom_call_target="tpu_custom_call" | custom-call | flops 4831838208 | bytes 4194304 | tf_op jit(solution)/shard_map/pallas_call | solution.py:205
  29.7 0.0 collective-permute-start.7
  29.7 7.2 %collective-permute-start.8 = (f32[8,128]{1,0:T(8,128)S(1)}, f32[8,128]{1,0:T(8,128)S(1)}, u32[]{:S(2)}, u32[]{:S(2)}) collective-permute-start(f32[8,128]{1,0:T(8,128)S(1)} %get-tuple-element.28), channel_id=1, source_target_pairs={{0,128},{16,144},{32,160},{48,176},{64,192},{80,208},{96,224},{112... | collective-permute-start | bytes 12296 | tf_op jit(solution)/shard_map/ppermute | solution.py:258
  36.9 0.6 collective-permute-start.9
  37.5 0.0 collective-permute-start.11
  37.5 1.0 %collective-permute-done.8 = f32[8,128]{1,0:T(8,128)S(1)} collective-permute-done((f32[8,128]{1,0:T(8,128)S(1)}, f32[8,128]{1,0:T(8,128)S(1)}, u32[]{:S(2)}, u32[]{:S(2)}) %collective-permute-start.8) | collective-permute-done | bytes 4128 | tf_op jit(solution)/shard_map/ppermute | solution.py:258
  38.5 0.0 collective-permute-done.7
  38.5 2.0 %collective-permute-start.10 = (f32[8,128]{1,0:T(8,128)S(1)}, f32[8,128]{1,0:T(8,128)S(1)}, u32[]{:S(2)}, u32[]{:S(2)}) collective-permute-start(f32[8,128]{1,0:T(8,128)S(1)} %add.36), channel_id=1, source_target_pairs={{0,64},{16,80},{32,96},{48,112},{64,0},{80,16},{96,32},{112,48},{1... | collective-permute-start | bytes 12296 | tf_op jit(solution)/shard_map/ppermute | solution.py:258
  40.5 0.4 collective-permute-start.13
  40.9 2.1 %collective-permute-done.10 = f32[8,128]{1,0:T(8,128)S(1)} collective-permute-done((f32[8,128]{1,0:T(8,128)S(1)}, f32[8,128]{1,0:T(8,128)S(1)}, u32[]{:S(2)}, u32[]{:S(2)}) %collective-permute-start.10) | collective-permute-done | bytes 4128 | tf_op jit(solution)/shard_map/ppermute | solution.py:258
  43.0 0.3 collective-permute-done.9
  43.3 0.0 collective-permute-done.11
  43.3 0.1 fusion.2
  43.3 1.6 %collective-permute-start.12 = (bf16[256,256]{1,0:T(8,128)(2,1)S(1)}, bf16[256,256]{1,0:T(8,128)(2,1)S(1)}, u32[]{:S(2)}, u32[]{:S(2)}) collective-permute-start(bf16[256,256]{1,0:T(8,128)(2,1)S(1)} %fusion.2), channel_id=1, source_target_pairs={{2,0},{7,1},{4,2},{1,3},{6,4},{3,5},{0,6},{5,7},{10,8},{15,9},{12,... | collective-permute-start | bytes 393224 | tf_op jit(solution)/shard_map/ppermute | solution.py:254
  45.0 1.0 %collective-permute-start.14 = (f32[8,128]{1,0:T(8,128)S(1)}, f32[8,128]{1,0:T(8,128)S(1)}, u32[]{:S(2)}, u32[]{:S(2)}) collective-permute-start(f32[8,128]{1,0:T(8,128)S(1)} %add.39), channel_id=1, source_target_pairs={{0,32},{16,48},{32,0},{48,16},{64,96},{80,112},{96,64},{112,80},{1... | collective-permute-start | bytes 12296 | tf_op jit(solution)/shard_map/ppermute | solution.py:258
  46.0 2.6 %collective-permute-done.14 = f32[8,128]{1,0:T(8,128)S(1)} collective-permute-done((f32[8,128]{1,0:T(8,128)S(1)}, f32[8,128]{1,0:T(8,128)S(1)}, u32[]{:S(2)}, u32[]{:S(2)}) %collective-permute-start.14) | collective-permute-done | bytes 4128 | tf_op jit(solution)/shard_map/ppermute | solution.py:258
  48.6 0.0 collective-permute-done.13
  48.6 0.4 collective-permute-start.15
  49.0 3.2 %collective-permute-done.15 = f32[8,128]{1,0:T(8,128)S(1)} collective-permute-done((f32[8,128]{1,0:T(8,128)S(1)}, f32[8,128]{1,0:T(8,128)S(1)}, u32[]{:S(2)}, u32[]{:S(2)}) %collective-permute-start.15) | collective-permute-done | bytes 4128 | tf_op jit(solution)/shard_map/ppermute | solution.py:258
  52.2 2.3 %collective-permute-start.16 = (f32[8,128]{1,0:T(8,128)S(1)}, f32[8,128]{1,0:T(8,128)S(1)}, u32[]{:S(2)}, u32[]{:S(2)}) collective-permute-start(f32[8,128]{1,0:T(8,128)S(1)} %add.46), channel_id=1, source_target_pairs={{0,8},{1,9},{2,10},{3,11},{4,12},{5,13},{6,14},{7,15},{8,0},{9,1},... | collective-permute-start | bytes 12296 | tf_op jit(solution)/shard_map/ppermute | solution.py:258
  54.5 0.0 collective-permute-done.12
  54.5 0.1 fusion.4
  54.6 0.7 %fusion.5 = (f32[256,128]{1,0:T(8,128)}, f32[256,128]{1,0:T(8,128)}) fusion(f32[256,256]{1,0:T(8,128)S(1)} %fusion.4), kind=kLoop, calls=%fused_computation.9 | loop fusion | bytes 524288 | tf_op jit(solution)/shard_map/slice | solution.py:292
  55.3 2.0 %collective-permute-done.16 = f32[8,128]{1,0:T(8,128)S(1)} collective-permute-done((f32[8,128]{1,0:T(8,128)S(1)}, f32[8,128]{1,0:T(8,128)S(1)}, u32[]{:S(2)}, u32[]{:S(2)}) %collective-permute-start.16) | collective-permute-done | bytes 4128 | tf_op jit(solution)/shard_map/ppermute | solution.py:258
  57.3 0.5 slice_bitcast_fusion
  (6 shorter events, 0.0 us)
Async XLA Ops:
  1.7 6.5 %collective-permute-start.1 = (bf16[528,128]{1,0:T(8,128)(2,1)S(1)}, bf16[528,128]{1,0:T(8,128)(2,1)S(1)}, u32[]{:S(2)}, u32[]{:S(2)}) collective-permute-start(bf16[528,128]{1,0:T(8,128)(2,1)S(1)} %shard_map.111.own), channel_id=1, source_target_pairs={{2,0},{7,1},{4,2},{1,3},{6,4},{3,5},{0,6},{5,7},{10,8},{15,9},{12,... | collective-permute-start | bytes 405512 | tf_op jit(solution)/shard_map/ppermute | solution.py:254
  4.5 6.2 %collective-permute-start = (bf16[528,128]{1,0:T(8,128)(2,1)S(1)}, bf16[528,128]{1,0:T(8,128)(2,1)S(1)}, u32[]{:S(2)}, u32[]{:S(2)}) collective-permute-start(bf16[528,128]{1,0:T(8,128)(2,1)S(1)} %shard_map.111.own), channel_id=1, source_target_pairs={{0,2},{1,7},{2,4},{3,1},{4,6},{5,3},{6,0},{7,5},{8,10},{9,15},{10,... | collective-permute-start | bytes 405512 | tf_op jit(solution)/shard_map/ppermute | solution.py:254
  4.5 9.5 %collective-permute-start.3 = (bf16[528,128]{1,0:T(8,128)(2,1)S(1)}, bf16[528,128]{1,0:T(8,128)(2,1)S(1)}, u32[]{:S(2)}, u32[]{:S(2)}) collective-permute-start(bf16[528,128]{1,0:T(8,128)(2,1)S(1)} %shard_map.111.own), channel_id=1, source_target_pairs={{0,1},{1,0},{2,3},{3,2},{4,5},{5,4},{6,7},{7,6},{8,9},{9,8},{10,11... | collective-permute-start | bytes 405512 | tf_op jit(solution)/shard_map/ppermute | solution.py:254
  8.1 5.9 %collective-permute-start.5 = (bf16[528,128]{1,0:T(8,128)(2,1)S(1)}, bf16[528,128]{1,0:T(8,128)(2,1)S(1)}, u32[]{:S(2)}, u32[]{:S(2)}) collective-permute-start(bf16[528,128]{1,0:T(8,128)(2,1)S(1)} %collective-permute-done.1.far), channel_id=1, source_target_pairs={{0,1},{1,0},{2,3},{3,2},{4,5},{5,4},{6,7},{7,6},{8,9},{9,8},{10,11... | collective-permute-start | bytes 405512 | tf_op jit(solution)/shard_map/ppermute | solution.py:254
  10.7 4.4 %collective-permute-start.6 = (bf16[528,128]{1,0:T(8,128)(2,1)S(1)}, bf16[528,128]{1,0:T(8,128)(2,1)S(1)}, u32[]{:S(2)}, u32[]{:S(2)}) collective-permute-start(bf16[528,128]{1,0:T(8,128)(2,1)S(1)} %collective-permute-done.near), channel_id=1, source_target_pairs={{0,3},{1,6},{2,5},{3,0},{4,7},{5,2},{6,1},{7,4},{8,11},{9,14},{10,... | collective-permute-start | bytes 405512 | tf_op jit(solution)/shard_map/ppermute | solution.py:254
  10.7 4.4 %collective-permute-start.4 = (bf16[528,128]{1,0:T(8,128)(2,1)S(1)}, bf16[528,128]{1,0:T(8,128)(2,1)S(1)}, u32[]{:S(2)}, u32[]{:S(2)}) collective-permute-start(bf16[528,128]{1,0:T(8,128)(2,1)S(1)} %collective-permute-done.near), channel_id=1, source_target_pairs={{0,1},{1,0},{2,3},{3,2},{4,5},{5,4},{6,7},{7,6},{8,9},{9,8},{10,11... | collective-permute-start | bytes 405512 | tf_op jit(solution)/shard_map/ppermute | solution.py:254
  11.4 6.2 %collective-permute-start.2 = (bf16[528,128]{1,0:T(8,128)(2,1)S(1)}, bf16[528,128]{1,0:T(8,128)(2,1)S(1)}, u32[]{:S(2)}, u32[]{:S(2)}) collective-permute-start(bf16[528,128]{1,0:T(8,128)(2,1)S(1)} %collective-permute-done.near), channel_id=1, source_target_pairs={{0,2},{1,7},{2,4},{3,1},{4,6},{5,3},{6,0},{7,5},{8,10},{9,15},{10,... | collective-permute-start | bytes 405512 | tf_op jit(solution)/shard_map/ppermute | solution.py:254
  29.7 8.8 %collective-permute-start.7 = (bf16[3,256,256]{2,1,0:T(8,128)(2,1)S(1)}, bf16[3,256,256]{2,1,0:T(8,128)(2,1)S(1)}, u32[]{:S(2)}, u32[]{:S(2)}) collective-permute-start(bf16[3,256,256]{2,1,0:T(8,128)(2,1)S(1)} %get-tuple-element.27), channel_id=1, source_target_pairs={{0,1},{1,0},{2,3},{3,2},{4,5},{5,4},{6,7},{7,6},{8,9},{9,8},{10,11... | collective-permute-start | bytes 1179656 | tf_op jit(solution)/shard_map/ppermute | solution.py:254
  29.7 8.8 %collective-permute-start.8 = (f32[8,128]{1,0:T(8,128)S(1)}, f32[8,128]{1,0:T(8,128)S(1)}, u32[]{:S(2)}, u32[]{:S(2)}) collective-permute-start(f32[8,128]{1,0:T(8,128)S(1)} %get-tuple-element.28), channel_id=1, source_target_pairs={{0,128},{16,144},{32,160},{48,176},{64,192},{80,208},{96,224},{112... | collective-permute-start | bytes 12296 | tf_op jit(solution)/shard_map/ppermute | solution.py:258
  36.9 6.4 %collective-permute-start.9 = (bf16[256,256]{1,0:T(8,128)(2,1)S(1)}, bf16[256,256]{1,0:T(8,128)(2,1)S(1)}, u32[]{:S(2)}, u32[]{:S(2)}) collective-permute-start(bf16[256,256]{1,0:T(8,128)(2,1)S(1)} %get-tuple-element.31), channel_id=1, source_target_pairs={{2,0},{7,1},{4,2},{1,3},{6,4},{3,5},{0,6},{5,7},{10,8},{15,9},{12,... | collective-permute-start | bytes 393224 | tf_op jit(solution)/shard_map/ppermute | solution.py:254
  37.5 5.8 %collective-permute-start.11 = (bf16[256,256]{1,0:T(8,128)(2,1)S(1)}, bf16[256,256]{1,0:T(8,128)(2,1)S(1)}, u32[]{:S(2)}, u32[]{:S(2)}) collective-permute-start(bf16[256,256]{1,0:T(8,128)(2,1)S(1)} %get-tuple-element.34), channel_id=1, source_target_pairs={{3,0},{6,1},{5,2},{0,3},{7,4},{2,5},{1,6},{4,7},{11,8},{14,9},{13,... | collective-permute-start | bytes 393224 | tf_op jit(solution)/shard_map/ppermute | solution.py:254
  38.5 4.5 %collective-permute-start.10 = (f32[8,128]{1,0:T(8,128)S(1)}, f32[8,128]{1,0:T(8,128)S(1)}, u32[]{:S(2)}, u32[]{:S(2)}) collective-permute-start(f32[8,128]{1,0:T(8,128)S(1)} %add.36), channel_id=1, source_target_pairs={{0,64},{16,80},{32,96},{48,112},{64,0},{80,16},{96,32},{112,48},{1... | collective-permute-start | bytes 12296 | tf_op jit(solution)/shard_map/ppermute | solution.py:258
  40.5 8.1 %collective-permute-start.13 = (bf16[256,256]{1,0:T(8,128)(2,1)S(1)}, bf16[256,256]{1,0:T(8,128)(2,1)S(1)}, u32[]{:S(2)}, u32[]{:S(2)}) collective-permute-start(bf16[256,256]{1,0:T(8,128)(2,1)S(1)} %bitcast_add_fusion), channel_id=1, source_target_pairs={{0,2},{1,7},{2,4},{3,1},{4,6},{5,3},{6,0},{7,5},{8,10},{9,15},{10,... | collective-permute-start | bytes 393224 | tf_op jit(solution)/shard_map/ppermute | solution.py:254
  43.3 11.1 %collective-permute-start.12 = (bf16[256,256]{1,0:T(8,128)(2,1)S(1)}, bf16[256,256]{1,0:T(8,128)(2,1)S(1)}, u32[]{:S(2)}, u32[]{:S(2)}) collective-permute-start(bf16[256,256]{1,0:T(8,128)(2,1)S(1)} %fusion.2), channel_id=1, source_target_pairs={{2,0},{7,1},{4,2},{1,3},{6,4},{3,5},{0,6},{5,7},{10,8},{15,9},{12,... | collective-permute-start | bytes 393224 | tf_op jit(solution)/shard_map/ppermute | solution.py:254
  45.0 3.6 %collective-permute-start.14 = (f32[8,128]{1,0:T(8,128)S(1)}, f32[8,128]{1,0:T(8,128)S(1)}, u32[]{:S(2)}, u32[]{:S(2)}) collective-permute-start(f32[8,128]{1,0:T(8,128)S(1)} %add.39), channel_id=1, source_target_pairs={{0,32},{16,48},{32,0},{48,16},{64,96},{80,112},{96,64},{112,80},{1... | collective-permute-start | bytes 12296 | tf_op jit(solution)/shard_map/ppermute | solution.py:258
  48.6 3.6 %collective-permute-start.15 = (f32[8,128]{1,0:T(8,128)S(1)}, f32[8,128]{1,0:T(8,128)S(1)}, u32[]{:S(2)}, u32[]{:S(2)}) collective-permute-start(f32[8,128]{1,0:T(8,128)S(1)} %add.44), channel_id=1, source_target_pairs={{0,16},{16,0},{32,48},{48,32},{64,80},{80,64},{96,112},{112,96},{1... | collective-permute-start | bytes 12296 | tf_op jit(solution)/shard_map/ppermute | solution.py:258
  52.2 5.1 %collective-permute-start.16 = (f32[8,128]{1,0:T(8,128)S(1)}, f32[8,128]{1,0:T(8,128)S(1)}, u32[]{:S(2)}, u32[]{:S(2)}) collective-permute-start(f32[8,128]{1,0:T(8,128)S(1)} %add.46), channel_id=1, source_target_pairs={{0,8},{1,9},{2,10},{3,11},{4,12},{5,13},{6,14},{7,15},{8,0},{9,1},... | collective-permute-start | bytes 12296 | tf_op jit(solution)/shard_map/ppermute | solution.py:258

commit v12 on v11

--- a/solution.py
+++ b/solution.py
@@ -89,6 +89,34 @@
     )(keys, values, logprob.reshape(wide), docs.reshape(wide), response.reshape(wide))
 
 
+def total_of(totals, low, high):
+    lane = lax.broadcasted_iota(jnp.int32, totals.shape, 1)
+    chosen = jnp.where((lane >= low) & (lane < high), totals, 0.0)
+    return jnp.sum(chosen, axis=1, keepdims=True)
+
+
+def margin_kernel(*refs):
+    totals = refs[0][2 * ROWS :, :].astype(jnp.float32)
+    for ref in refs[1:BLOCKS]:
+        totals += ref[2 * ROWS :, :].astype(jnp.float32)
+    totals = totals[:8, :]
+    pair = lax.axis_index("pb") * 2 + lax.axis_index("ka") // BLOCKS
+    first = total_of(totals, 0, 3) / total_of(totals, 6, 7)
+    second = total_of(totals, 3, 6) / total_of(totals, 7, 8)
+    lane = lax.broadcasted_iota(jnp.int32, (8, HEAD_DIM), 1)
+    refs[BLOCKS][...] = jnp.where(lane == pair, first - second, 0.0)
+
+
+def pair_margin(blocks):
+    return pl.pallas_call(
+        margin_kernel,
+        out_shape=pltpu.VMEM((8, HEAD_DIM), jnp.float32),
+        in_specs=[VMEM] * BLOCKS,
+        out_specs=VMEM,
+        cost_estimate=pl.CostEstimate(flops=10000, bytes_accessed=65536, transcendentals=0),
+    )(*blocks)
+
+
 def spans():
     return [(block, slice(block * ROWS, (block + 1) * ROWS)) for block in range(BLOCKS)]
 
@@ -96,7 +124,7 @@
 def attend_kernel(
     queries, grads, own, near, far, opposite, own_s, near_s, far_s, opposite_s,
     attention, grad_queries, own_part, near_part, far_part, opposite_part, swap_parts,
-    opposite_s_part, margin,
+    opposite_s_part,
     keys, values, keys_t, values_t, bias, scores, probs, grad_scores, acc_k, acc_v,
 ):
     place = lax.axis_index("ka")
@@ -121,16 +149,7 @@
         term = blocks[block][2 * ROWS :, :].astype(jnp.float32)
         totals = term if totals is None else totals + term
     totals = totals[:8, :]
-    wide = lax.broadcasted_iota(jnp.int32, (8, HEAD_DIM), 1)
-
-    def total_of(low, high):
-        chosen = jnp.where((wide >= low) & (wide < high), totals, 0.0)
-        return jnp.sum(chosen, axis=1, keepdims=True)
-
-    pair = lax.axis_index("pb") * 2 + place // BLOCKS
-    value = total_of(0, 3) / total_of(6, 7) - total_of(3, 6) / total_of(7, 8)
-    margin[...] = jnp.where(wide == pair, value, 0.0)
-    cut = total_of(8, 9)[:1].astype(jnp.int32)
+    cut = total_of(totals, 8, 9)[:1].astype(jnp.int32)
     row = first_row + lax.broadcasted_iota(jnp.int32, (ROWS, ROWS), 0)
     lane = lax.broadcasted_iota(jnp.int32, (ROWS, ROWS), 1)
     start = jnp.where(row >= cut, cut, 0)
@@ -213,10 +232,9 @@
             part,
             jax.ShapeDtypeStruct((3, ROWS, 2 * HEAD_DIM), jnp.bfloat16),
             part,
-            jax.ShapeDtypeStruct((8, HEAD_DIM), jnp.float32),
         ),
         in_specs=[VMEM] * (2 + BLOCKS),
-        out_specs=(VMEM,) * 9,
+        out_specs=(VMEM,) * 8,
         scratch_shapes=[
             pltpu.VMEM((PAIR_SPAN, HEAD_DIM), jnp.bfloat16),
             pltpu.VMEM((PAIR_SPAN, HEAD_DIM), jnp.bfloat16),
@@ -253,39 +271,44 @@
     def send(block, route):
         return lax.ppermute(block, "ka", route)
 
-    def exchange(table, axis, mask):
-        route = [(place, place ^ mask) for place in range(16)]
-        return table + lax.ppermute(table, axis, route)
+    def exchange(table, axis, *masks):
+        routes = [[(place, place ^ mask) for place in range(16)] for mask in masks]
+        return sum((lax.ppermute(table, axis, route) for route in routes), table)
 
     own = pack(key_heads, value_heads, token_logprob, doc_ids, response)
     queries, grad_output = fetch(queries, grad_output)
     near = send(own, ahead)
-    far = send(own, back)
     own_s = send(own, swap)
+    own_later, own_s = lax.optimization_barrier((own, own_s))
+    far = send(own_later, back)
     opposite = send(near, ahead)
     opposite_s = send(near, cross)
     near_s = send(near, swap)
     far_s = send(far, swap)
 
     blocks = (own, near, far, opposite, own_s, near_s, far_s, opposite_s)
-    attention, grad_queries, own_p, near_p, far_p, opposite_p, swap_p, opposite_s_p, margin = (
-        attend(queries, grad_output, blocks)
+    margin = pair_margin(blocks)
+    near, margin = lax.optimization_barrier((near, margin))
+    blocks = (own, near, far, opposite, own_s, near_s, far_s, opposite_s)
+    margin = exchange(margin, "pb", 4, 8, 12)
+    attention, grad_queries, own_p, near_p, far_p, opposite_p, swap_p, opposite_s_p = attend(
+        queries, grad_output, blocks
+    )
+    own_p, near_p, far_p, opposite_p, swap_p, opposite_s_p, margin = lax.optimization_barrier(
+        (own_p, near_p, far_p, opposite_p, swap_p, opposite_s_p, margin)
     )
     swapped = send(swap_p, swap)
     passed = send(opposite_p, back)
     passed_s = send(opposite_s_p, cross_back)
-    margin = exchange(margin, "pb", 8)
+    margin = exchange(margin, "pb", 2)
     swapped, margin = lax.optimization_barrier((swapped, margin))
-    margin = exchange(margin, "pb", 4)
-    passed, margin = lax.optimization_barrier((passed, margin))
+    margin = exchange(margin, "pb", 1)
+    passed, passed_s, margin = lax.optimization_barrier((passed, passed_s, margin))
     wide = jnp.float32
     near_sum = (near_p.astype(wide) + swapped[1] + passed + passed_s).astype(jnp.bfloat16)
     far_sum = far_p + swapped[2]
     near_part = send(near_sum, back)
     far_part = send(far_sum, ahead)
-    margin = exchange(margin, "pb", 2)
-    far_part, margin = lax.optimization_barrier((far_part, margin))
-    margin = exchange(margin, "pb", 1)
     margin = exchange(margin, "ka", 8)
     total = own_p.astype(wide) + swapped[0] + near_part + far_part
     return (

time: 58 us -> 62.3 us (1.074)
  the two profiles are of different devices: /device:TPU:8 before, /device:TPU:1 now
where the time goes in v12:
time: 62.3 us; the launch traced here: 62 us
  starting transfers between devices  26 us (42%)
  Pallas kernels  15.7 us (25%)
  waiting for transfers between devices  13.2 us (21%)
  local copies, waits for them, and re-layouts  6.19 us (10%)
  between operations  0.83 us (1%)
    ppermute x12, starting transfers between devices, send(): return lax.ppermute(block, 'ka', route)  15 us
    pallas_call x1, Pallas kernels, attend(): pl.pallas_call(attend_kernel, out_shape=(jax.ShapeDtypeStruct((ROWS, widt...  12.1 us
    ppermute x6, starting transfers between devices, exchange(): return sum((lax.ppermute(table, axis, route) for route in routes), table)  11 us
    ppermute x12, waiting for transfers between devices, send(): return lax.ppermute(block, 'ka', route)  10.3 us
    unnamed x32, local copies, waits for them, and re-layouts  4.96 us
    ppermute x6, waiting for transfers between devices, exchange(): return sum((lax.ppermute(table, axis, route) for route in routes), table)  2.86 us
    pallas_call x1, Pallas kernels, pair_margin(): pl.pallas_call(margin_kernel, out_shape=pltpu.VMEM((8, HEAD_DIM), jnp.flo...  1.38 us
  transfers between devices with their start and end apart: 18, of which 9 were waited for; matrix products, arithmetic and copies ran while one was open for 1% of the time, Pallas kernels for 21%

profile of v12, /device:TPU:1, one launch (start us, length us, event | category | flops | bytes accessed | tf_op | source)
XLA Modules:
  0.0 62.0 jit_solution(4595828846323764789)
XLA Ops:
  0.6 1.0 %shard_map.111.refs_0_.own = bf16[528,128]{1,0:T(8,128)(2,1)S(1)} custom-call(bf16[256,128]{1,0:T(8,128)(2,1)} %keys.1, bf16[256,128]{1,0:T(8,128)(2,1)} %values.1, f32[2,128]{1,0:T(2,128)} %bitcast.13, s32[2,128]{1,0:T(2,128)} %bitcast.14, s32[2,128]{1,0:T(2,128)} %bitcast.15), custom_call_target="tpu_custom_call" | custom-call | flops 10000 | bytes 524288 | tf_op jit(solution)/shard_map/pallas_call | solution.py:83
  1.7 0.0 copy-start
  1.7 3.3 %collective-permute-start.1 = (bf16[528,128]{1,0:T(8,128)(2,1)S(1)}, bf16[528,128]{1,0:T(8,128)(2,1)S(1)}, u32[]{:S(2)}, u32[]{:S(2)}) collective-permute-start(bf16[528,128]{1,0:T(8,128)(2,1)S(1)} %shard_map.111.refs_0_.own), channel_id=1, source_target_pairs={{0,1},{1,0},{2,3},{3,2},{4,5},{5,4},{6,7},{7,6},{8,9},{9,8},{10,11... | collective-permute-start | bytes 405512 | tf_op jit(solution)/shard_map/ppermute | solution.py:272
  5.0 0.7 %collective-permute-start = (bf16[528,128]{1,0:T(8,128)(2,1)S(1)}, bf16[528,128]{1,0:T(8,128)(2,1)S(1)}, u32[]{:S(2)}, u32[]{:S(2)}) collective-permute-start(bf16[528,128]{1,0:T(8,128)(2,1)S(1)} %shard_map.111.refs_0_.own), channel_id=1, source_target_pairs={{0,2},{1,7},{2,4},{3,1},{4,6},{5,3},{6,0},{7,5},{8,10},{9,15},{10,... | collective-permute-start | bytes 405512 | tf_op jit(solution)/shard_map/ppermute | solution.py:272
  5.8 0.2 collective-permute-done.1.refs_4_.own_s
  6.0 0.5 collective-permute-start.2
  6.5 2.4 %collective-permute-done.refs_1_.near = bf16[528,128]{1,0:T(8,128)(2,1)S(1)} collective-permute-done((bf16[528,128]{1,0:T(8,128)(2,1)S(1)}, bf16[528,128]{1,0:T(8,128)(2,1)S(1)}, u32[]{:S(2)}, u32[]{:S(2)}) %collective-permute-start) | collective-permute-done | bytes 135200 | tf_op jit(solution)/shard_map/ppermute | solution.py:272
  8.9 3.0 %collective-permute-start.6 = (bf16[528,128]{1,0:T(8,128)(2,1)S(1)}, bf16[528,128]{1,0:T(8,128)(2,1)S(1)}, u32[]{:S(2)}, u32[]{:S(2)}) collective-permute-start(bf16[528,128]{1,0:T(8,128)(2,1)S(1)} %collective-permute-done.refs_1_.near), channel_id=1, source_target_pairs={{0,3},{1,6},{2,5},{3,0},{4,7},{5,2},{6,1},{7,4},{8,11},{9,14},{10,... | collective-permute-start | bytes 405512 | tf_op jit(solution)/shard_map/ppermute | solution.py:272
  11.8 0.6 collective-permute-start.4
  12.4 0.0 collective-permute-start.3
  12.4 0.0 collective-permute-done.2.refs_2_.far
  12.4 2.1 %collective-permute-start.5 = (bf16[528,128]{1,0:T(8,128)(2,1)S(1)}, bf16[528,128]{1,0:T(8,128)(2,1)S(1)}, u32[]{:S(2)}, u32[]{:S(2)}) collective-permute-start(bf16[528,128]{1,0:T(8,128)(2,1)S(1)} %collective-permute-done.2.refs_2_.far), channel_id=1, source_target_pairs={{0,1},{1,0},{2,3},{3,2},{4,5},{5,4},{6,7},{7,6},{8,9},{9,8},{10,11... | collective-permute-start | bytes 405512 | tf_op jit(solution)/shard_map/ppermute | solution.py:272
  14.6 1.1 %shard_map.110 = (bf16[256,768]{1,0:T(8,128)(2,1)S(1)}, bf16[256,768]{1,0:T(8,128)(2,1)S(1)}) custom-call(bf16[256,768]{1,0:T(8,128)(2,1)} %queries_hbm.1, bf16[256,768]{1,0:T(8,128)(2,1)} %grads_hbm.1), custom_call_target="tpu_custom_call" | custom-call | bytes 2097152 | tf_op jit(solution)/shard_map/pallas_call | solution.py:43
  15.7 0.0 collective-permute-done.6.refs_7_.opposite_s
  15.8 0.0 copy-start.1
  15.8 0.0 copy-start.5
  15.8 0.0 collective-permute-done.4.refs_5_.near_s
  15.8 2.1 %collective-permute-done.3.refs_3_.opposite = bf16[528,128]{1,0:T(8,128)(2,1)S(1)} collective-permute-done((bf16[528,128]{1,0:T(8,128)(2,1)S(1)}, bf16[528,128]{1,0:T(8,128)(2,1)S(1)}, u32[]{:S(2)}, u32[]{:S(2)}) %collective-permute-start.3) | collective-permute-done | bytes 135200 | tf_op jit(solution)/shard_map/ppermute | solution.py:272
  17.9 0.6 %copy-done.12 = bf16[528,128]{1,0:T(8,128)(2,1)} copy-done((bf16[528,128]{1,0:T(8,128)(2,1)}, bf16[528,128]{1,0:T(8,128)(2,1)S(1)}, u32[]{:S(2)}) %copy-start.12) | copy-done | bytes 135192
  18.6 0.7 %copy-done.14 = bf16[528,128]{1,0:T(8,128)(2,1)} copy-done((bf16[528,128]{1,0:T(8,128)(2,1)}, bf16[528,128]{1,0:T(8,128)(2,1)S(1)}, u32[]{:S(2)}) %copy-start.14) | copy-done | bytes 135192
  19.2 1.4 %shard_map.112 = f32[8,128]{1,0:T(8,128)S(1)} custom-call(bf16[528,128]{1,0:T(8,128)(2,1)} %copy-done, bf16[528,128]{1,0:T(8,128)(2,1)} %copy-done.4, bf16[528,128]{1,0:T(8,128)(2,1)} %copy-done.6, bf16[528,128]{1,0:T(8,128)(2,1)} %copy-done.12, bf16[528,128]{1,0:T(8,128)(2,1)} %copy-done.2, bf16[528,128]{1,0:T(8,128)(2,1)} %copy-done.10, ...), custom_call_target="tpu_custom_call" | custom-call | flops 10000 | bytes 65536 | tf_op jit(solution)/shard_map/pallas_call | solution.py:111
  20.6 3.9 %collective-permute-start.9 = (f32[8,128]{1,0:T(8,128)S(1)}, f32[8,128]{1,0:T(8,128)S(1)}, u32[]{:S(2)}, u32[]{:S(2)}) collective-permute-start(f32[8,128]{1,0:T(8,128)S(1)} %shard_map.112), channel_id=1, source_target_pairs={{0,192},{16,208},{32,224},{48,240},{64,128},{80,144},{96,160},{112... | collective-permute-start | bytes 12296 | tf_op jit(solution)/shard_map/ppermute | solution.py:276
  24.5 1.0 %collective-permute-start.8 = (f32[8,128]{1,0:T(8,128)S(1)}, f32[8,128]{1,0:T(8,128)S(1)}, u32[]{:S(2)}, u32[]{:S(2)}) collective-permute-start(f32[8,128]{1,0:T(8,128)S(1)} %shard_map.112), channel_id=1, source_target_pairs={{0,128},{16,144},{32,160},{48,176},{64,192},{80,208},{96,224},{112... | collective-permute-start | bytes 12296 | tf_op jit(solution)/shard_map/ppermute | solution.py:276
  25.5 1.2 %collective-permute-start.7 = (f32[8,128]{1,0:T(8,128)S(1)}, f32[8,128]{1,0:T(8,128)S(1)}, u32[]{:S(2)}, u32[]{:S(2)}) collective-permute-start(f32[8,128]{1,0:T(8,128)S(1)} %shard_map.112), channel_id=1, source_target_pairs={{0,64},{16,80},{32,96},{48,112},{64,0},{80,16},{96,32},{112,48},{1... | collective-permute-start | bytes 12296 | tf_op jit(solution)/shard_map/ppermute | solution.py:276
  26.7 0.9 %copy-done.9 = bf16[528,128]{1,0:T(8,128)(2,1)S(1)} copy-done((bf16[528,128]{1,0:T(8,128)(2,1)S(1)}, bf16[528,128]{1,0:T(8,128)(2,1)}, u32[]{:S(2)}) %copy-start.9) | copy-done | bytes 135192
  27.6 0.9 %copy-done.11 = bf16[528,128]{1,0:T(8,128)(2,1)S(1)} copy-done((bf16[528,128]{1,0:T(8,128)(2,1)S(1)}, bf16[528,128]{1,0:T(8,128)(2,1)}, u32[]{:S(2)}) %copy-start.11) | copy-done | bytes 135192
  28.5 0.9 %copy-done.13 = bf16[528,128]{1,0:T(8,128)(2,1)S(1)} copy-done((bf16[528,128]{1,0:T(8,128)(2,1)S(1)}, bf16[528,128]{1,0:T(8,128)(2,1)}, u32[]{:S(2)}) %copy-start.13) | copy-done | bytes 135192
  29.4 0.9 %copy-done.15 = bf16[528,128]{1,0:T(8,128)(2,1)S(1)} copy-done((bf16[528,128]{1,0:T(8,128)(2,1)S(1)}, bf16[528,128]{1,0:T(8,128)(2,1)}, u32[]{:S(2)}) %copy-start.15) | copy-done | bytes 135192
  30.3 12.1 %shard_map.113 = (bf16[256,768]{1,0:T(8,128)(2,1)}, f32[256,768]{1,0:T(8,128)}, bf16[256,256]{1,0:T(8,128)(2,1)S(1)}, bf16[256,256]{1,0:T(8,128)(2,1)S(1)}, bf16...) custom-call(bf16[256,768]{1,0:T(8,128)(2,1)S(1)} %get-tuple-element., ...), custom_call_target="tpu_custom_call" | custom-call | flops 4831838208 | bytes 4194304 | tf_op jit(solution)/shard_map/pallas_call | solution.py:224
  42.5 0.0 collective-permute-done.8
  42.5 0.0 collective-permute-done.7
  42.5 3.5 %collective-permute-start.10 = (bf16[3,256,256]{2,1,0:T(8,128)(2,1)S(1)}, bf16[3,256,256]{2,1,0:T(8,128)(2,1)S(1)}, u32[]{:S(2)}, u32[]{:S(2)}) collective-permute-start(bf16[3,256,256]{2,1,0:T(8,128)(2,1)S(1)} %get-tuple-element.46), channel_id=1, source_target_pairs={{0,1},{1,0},{2,3},{3,2},{4,5},{5,4},{6,7},{7,6},{8,9},{9,8},{10,11... | collective-permute-start | bytes 1179656 | tf_op jit(solution)/shard_map/ppermute | solution.py:272
  46.0 0.7 %collective-permute-start.11 = (f32[8,128]{1,0:T(8,128)S(1)}, f32[8,128]{1,0:T(8,128)S(1)}, u32[]{:S(2)}, u32[]{:S(2)}) collective-permute-start(f32[8,128]{1,0:T(8,128)S(1)} %add_add_fusion), channel_id=1, source_target_pairs={{0,32},{16,48},{32,0},{48,16},{64,96},{80,112},{96,64},{112,80},{1... | collective-permute-start | bytes 12296 | tf_op jit(solution)/shard_map/ppermute | solution.py:276
  46.7 0.0 collective-permute-start.13
  46.8 1.7 %collective-permute-done.11 = f32[8,128]{1,0:T(8,128)S(1)} collective-permute-done((f32[8,128]{1,0:T(8,128)S(1)}, f32[8,128]{1,0:T(8,128)S(1)}, u32[]{:S(2)}, u32[]{:S(2)}) %collective-permute-start.11) | collective-permute-done | bytes 4128 | tf_op jit(solution)/shard_map/ppermute | solution.py:276
  48.5 1.3 %collective-permute-start.14 = (f32[8,128]{1,0:T(8,128)S(1)}, f32[8,128]{1,0:T(8,128)S(1)}, u32[]{:S(2)}, u32[]{:S(2)}) collective-permute-start(f32[8,128]{1,0:T(8,128)S(1)} %add.42), channel_id=1, source_target_pairs={{0,16},{16,0},{32,48},{48,32},{64,80},{80,64},{96,112},{112,96},{1... | collective-permute-start | bytes 12296 | tf_op jit(solution)/shard_map/ppermute | solution.py:276
  49.8 1.1 %collective-permute-start.16 = (bf16[256,256]{1,0:T(8,128)(2,1)S(1)}, bf16[256,256]{1,0:T(8,128)(2,1)S(1)}, u32[]{:S(2)}, u32[]{:S(2)}) collective-permute-start(bf16[256,256]{1,0:T(8,128)(2,1)S(1)} %bitcast_add_fusion), channel_id=1, source_target_pairs={{0,2},{1,7},{2,4},{3,1},{4,6},{5,3},{6,0},{7,5},{8,10},{9,15},{10,... | collective-permute-start | bytes 393224 | tf_op jit(solution)/shard_map/ppermute | solution.py:272
  50.9 0.3 collective-permute-done.14
  51.2 1.4 %collective-permute-done.12 = bf16[256,256]{1,0:T(8,128)(2,1)S(1)} collective-permute-done((bf16[256,256]{1,0:T(8,128)(2,1)S(1)}, bf16[256,256]{1,0:T(8,128)(2,1)S(1)}, u32[]{:S(2)}, u32[]{:S(2)}) %collective-permute-start.12) | collective-permute-done | bytes 131104 | tf_op jit(solution)/shard_map/ppermute | solution.py:272
  52.6 0.6 collective-permute-done.13
  53.2 2.9 %collective-permute-start.17 = (f32[8,128]{1,0:T(8,128)S(1)}, f32[8,128]{1,0:T(8,128)S(1)}, u32[]{:S(2)}, u32[]{:S(2)}) collective-permute-start(f32[8,128]{1,0:T(8,128)S(1)} %add.45), channel_id=1, source_target_pairs={{0,8},{1,9},{2,10},{3,11},{4,12},{5,13},{6,14},{7,15},{8,0},{9,1},... | collective-permute-start | bytes 12296 | tf_op jit(solution)/shard_map/ppermute | solution.py:276
  56.1 0.1 fusion.2
  56.2 0.1 collective-permute-start.15
  56.2 0.9 %collective-permute-done.17 = f32[8,128]{1,0:T(8,128)S(1)} collective-permute-done((f32[8,128]{1,0:T(8,128)S(1)}, f32[8,128]{1,0:T(8,128)S(1)}, u32[]{:S(2)}, u32[]{:S(2)}) %collective-permute-start.17) | collective-permute-done | bytes 4128 | tf_op jit(solution)/shard_map/ppermute | solution.py:276
  57.1 0.5 slice_bitcast_fusion
  57.6 3.6 %collective-permute-done.15 = bf16[256,256]{1,0:T(8,128)(2,1)S(1)} collective-permute-done((bf16[256,256]{1,0:T(8,128)(2,1)S(1)}, bf16[256,256]{1,0:T(8,128)(2,1)S(1)}, u32[]{:S(2)}, u32[]{:S(2)}) %collective-permute-start.15) | collective-permute-done | bytes 131104 | tf_op jit(solution)/shard_map/ppermute | solution.py:272
  61.3 0.1 fusion.4
  61.3 0.7 %fusion.5 = (f32[256,128]{1,0:T(8,128)}, f32[256,128]{1,0:T(8,128)}) fusion(f32[256,256]{1,0:T(8,128)S(1)} %fusion.4), kind=kLoop, calls=%fused_computation.10 | loop fusion | bytes 524288 | tf_op jit(solution)/shard_map/slice | solution.py:315
  (33 shorter events, 0.1 us)
Async XLA Ops:
  1.7 14.0 %copy-start = (bf16[528,128]{1,0:T(8,128)(2,1)}, bf16[528,128]{1,0:T(8,128)(2,1)S(1)}, u32[]{:S(2)}) copy-start(bf16[528,128]{1,0:T(8,128)(2,1)S(1)} %shard_map.111.refs_0_.own) | copy-start | bytes 405508
  1.7 4.3 %collective-permute-start.1 = (bf16[528,128]{1,0:T(8,128)(2,1)S(1)}, bf16[528,128]{1,0:T(8,128)(2,1)S(1)}, u32[]{:S(2)}, u32[]{:S(2)}) collective-permute-start(bf16[528,128]{1,0:T(8,128)(2,1)S(1)} %shard_map.111.refs_0_.own), channel_id=1, source_target_pairs={{0,1},{1,0},{2,3},{3,2},{4,5},{5,4},{6,7},{7,6},{8,9},{9,8},{10,11... | collective-permute-start | bytes 405512 | tf_op jit(solution)/shard_map/ppermute | solution.py:272
  5.0 3.9 %collective-permute-start = (bf16[528,128]{1,0:T(8,128)(2,1)S(1)}, bf16[528,128]{1,0:T(8,128)(2,1)S(1)}, u32[]{:S(2)}, u32[]{:S(2)}) collective-permute-start(bf16[528,128]{1,0:T(8,128)(2,1)S(1)} %shard_map.111.refs_0_.own), channel_id=1, source_target_pairs={{0,2},{1,7},{2,4},{3,1},{4,6},{5,3},{6,0},{7,5},{8,10},{9,15},{10,... | collective-permute-start | bytes 405512 | tf_op jit(solution)/shard_map/ppermute | solution.py:272
  6.0 9.7 %copy-start.2 = (bf16[528,128]{1,0:T(8,128)(2,1)}, bf16[528,128]{1,0:T(8,128)(2,1)S(1)}, u32[]{:S(2)}) copy-start(bf16[528,128]{1,0:T(8,128)(2,1)S(1)} %collective-permute-done.1.refs_4_.own_s) | copy-start | bytes 405508
  6.0 6.4 %collective-permute-start.2 = (bf16[528,128]{1,0:T(8,128)(2,1)S(1)}, bf16[528,128]{1,0:T(8,128)(2,1)S(1)}, u32[]{:S(2)}, u32[]{:S(2)}) collective-permute-start(bf16[528,128]{1,0:T(8,128)(2,1)S(1)} %shard_map.111.refs_0_.own), channel_id=1, source_target_pairs={{2,0},{7,1},{4,2},{1,3},{6,4},{3,5},{0,6},{5,7},{10,8},{15,9},{12,... | collective-permute-start | bytes 405512 | tf_op jit(solution)/shard_map/ppermute | solution.py:272
  8.9 6.8 %copy-start.4 = (bf16[528,128]{1,0:T(8,128)(2,1)}, bf16[528,128]{1,0:T(8,128)(2,1)S(1)}, u32[]{:S(2)}) copy-start(bf16[528,128]{1,0:T(8,128)(2,1)S(1)} %collective-permute-done.refs_1_.near) | copy-start | bytes 405508
  8.9 6.9 %collective-permute-start.6 = (bf16[528,128]{1,0:T(8,128)(2,1)S(1)}, bf16[528,128]{1,0:T(8,128)(2,1)S(1)}, u32[]{:S(2)}, u32[]{:S(2)}) collective-permute-start(bf16[528,128]{1,0:T(8,128)(2,1)S(1)} %collective-permute-done.refs_1_.near), channel_id=1, source_target_pairs={{0,3},{1,6},{2,5},{3,0},{4,7},{5,2},{6,1},{7,4},{8,11},{9,14},{10,... | collective-permute-start | bytes 405512 | tf_op jit(solution)/shard_map/ppermute | solution.py:272
  11.8 4.0 %collective-permute-start.4 = (bf16[528,128]{1,0:T(8,128)(2,1)S(1)}, bf16[528,128]{1,0:T(8,128)(2,1)S(1)}, u32[]{:S(2)}, u32[]{:S(2)}) collective-permute-start(bf16[528,128]{1,0:T(8,128)(2,1)S(1)} %collective-permute-done.refs_1_.near), channel_id=1, source_target_pairs={{0,1},{1,0},{2,3},{3,2},{4,5},{5,4},{6,7},{7,6},{8,9},{9,8},{10,11... | collective-permute-start | bytes 405512 | tf_op jit(solution)/shard_map/ppermute | solution.py:272
  12.4 5.5 %collective-permute-start.3 = (bf16[528,128]{1,0:T(8,128)(2,1)S(1)}, bf16[528,128]{1,0:T(8,128)(2,1)S(1)}, u32[]{:S(2)}, u32[]{:S(2)}) collective-permute-start(bf16[528,128]{1,0:T(8,128)(2,1)S(1)} %collective-permute-done.refs_1_.near), channel_id=1, source_target_pairs={{0,2},{1,7},{2,4},{3,1},{4,6},{5,3},{6,0},{7,5},{8,10},{9,15},{10,... | collective-permute-start | bytes 405512 | tf_op jit(solution)/shard_map/ppermute | solution.py:272
  12.4 3.3 %copy-start.6 = (bf16[528,128]{1,0:T(8,128)(2,1)}, bf16[528,128]{1,0:T(8,128)(2,1)S(1)}, u32[]{:S(2)}) copy-start(bf16[528,128]{1,0:T(8,128)(2,1)S(1)} %collective-permute-done.2.refs_2_.far) | copy-start | bytes 405508
  12.4 5.5 %collective-permute-start.5 = (bf16[528,128]{1,0:T(8,128)(2,1)S(1)}, bf16[528,128]{1,0:T(8,128)(2,1)S(1)}, u32[]{:S(2)}, u32[]{:S(2)}) collective-permute-start(bf16[528,128]{1,0:T(8,128)(2,1)S(1)} %collective-permute-done.2.refs_2_.far), channel_id=1, source_target_pairs={{0,1},{1,0},{2,3},{3,2},{4,5},{5,4},{6,7},{7,6},{8,9},{9,8},{10,11... | collective-permute-start | bytes 405512 | tf_op jit(solution)/shard_map/ppermute | solution.py:272
  15.8 2.2 %copy-start.8 = (bf16[528,128]{1,0:T(8,128)(2,1)}, bf16[528,128]{1,0:T(8,128)(2,1)S(1)}, u32[]{:S(2)}) copy-start(bf16[528,128]{1,0:T(8,128)(2,1)S(1)} %collective-permute-done.6.refs_7_.opposite_s) | copy-start | bytes 405508
  15.8 10.9 %copy-start.1 = (bf16[528,128]{1,0:T(8,128)(2,1)S(1)}, bf16[528,128]{1,0:T(8,128)(2,1)}, u32[]{:S(2)}) copy-start(bf16[528,128]{1,0:T(8,128)(2,1)} %copy-done) | copy-start | bytes 405508
  15.8 10.9 %copy-start.3 = (bf16[528,128]{1,0:T(8,128)(2,1)S(1)}, bf16[528,128]{1,0:T(8,128)(2,1)}, u32[]{:S(2)}) copy-start(bf16[528,128]{1,0:T(8,128)(2,1)} %copy-done.2) | copy-start | bytes 405508
  15.8 10.9 %copy-start.5 = (bf16[528,128]{1,0:T(8,128)(2,1)S(1)}, bf16[528,128]{1,0:T(8,128)(2,1)}, u32[]{:S(2)}) copy-start(bf16[528,128]{1,0:T(8,128)(2,1)} %copy-done.4) | copy-start | bytes 405508
  15.8 10.9 %copy-start.7 = (bf16[528,128]{1,0:T(8,128)(2,1)S(1)}, bf16[528,128]{1,0:T(8,128)(2,1)}, u32[]{:S(2)}) copy-start(bf16[528,128]{1,0:T(8,128)(2,1)} %copy-done.6) | copy-start | bytes 405508
  15.8 2.1 %copy-start.10 = (bf16[528,128]{1,0:T(8,128)(2,1)}, bf16[528,128]{1,0:T(8,128)(2,1)S(1)}, u32[]{:S(2)}) copy-start(bf16[528,128]{1,0:T(8,128)(2,1)S(1)} %collective-permute-done.4.refs_5_.near_s) | copy-start | bytes 405508
  17.9 0.7 %copy-start.12 = (bf16[528,128]{1,0:T(8,128)(2,1)}, bf16[528,128]{1,0:T(8,128)(2,1)S(1)}, u32[]{:S(2)}) copy-start(bf16[528,128]{1,0:T(8,128)(2,1)S(1)} %collective-permute-done.3.refs_3_.opposite) | copy-start | bytes 405508
  18.6 0.7 %copy-start.14 = (bf16[528,128]{1,0:T(8,128)(2,1)}, bf16[528,128]{1,0:T(8,128)(2,1)S(1)}, u32[]{:S(2)}) copy-start(bf16[528,128]{1,0:T(8,128)(2,1)S(1)} %collective-permute-done.5.refs_6_.far_s) | copy-start | bytes 405508
  20.6 21.9 %collective-permute-start.9 = (f32[8,128]{1,0:T(8,128)S(1)}, f32[8,128]{1,0:T(8,128)S(1)}, u32[]{:S(2)}, u32[]{:S(2)}) collective-permute-start(f32[8,128]{1,0:T(8,128)S(1)} %shard_map.112), channel_id=1, source_target_pairs={{0,192},{16,208},{32,224},{48,240},{64,128},{80,144},{96,160},{112... | collective-permute-start | bytes 12296 | tf_op jit(solution)/shard_map/ppermute | solution.py:276
  24.5 18.0 %collective-permute-start.8 = (f32[8,128]{1,0:T(8,128)S(1)}, f32[8,128]{1,0:T(8,128)S(1)}, u32[]{:S(2)}, u32[]{:S(2)}) collective-permute-start(f32[8,128]{1,0:T(8,128)S(1)} %shard_map.112), channel_id=1, source_target_pairs={{0,128},{16,144},{32,160},{48,176},{64,192},{80,208},{96,224},{112... | collective-permute-start | bytes 12296 | tf_op jit(solution)/shard_map/ppermute | solution.py:276
  25.5 17.0 %collective-permute-start.7 = (f32[8,128]{1,0:T(8,128)S(1)}, f32[8,128]{1,0:T(8,128)S(1)}, u32[]{:S(2)}, u32[]{:S(2)}) collective-permute-start(f32[8,128]{1,0:T(8,128)S(1)} %shard_map.112), channel_id=1, source_target_pairs={{0,64},{16,80},{32,96},{48,112},{64,0},{80,16},{96,32},{112,48},{1... | collective-permute-start | bytes 12296 | tf_op jit(solution)/shard_map/ppermute | solution.py:276
  26.7 0.9 %copy-start.9 = (bf16[528,128]{1,0:T(8,128)(2,1)S(1)}, bf16[528,128]{1,0:T(8,128)(2,1)}, u32[]{:S(2)}) copy-start(bf16[528,128]{1,0:T(8,128)(2,1)} %copy-done.8) | copy-start | bytes 405508
  27.6 0.9 %copy-start.11 = (bf16[528,128]{1,0:T(8,128)(2,1)S(1)}, bf16[528,128]{1,0:T(8,128)(2,1)}, u32[]{:S(2)}) copy-start(bf16[528,128]{1,0:T(8,128)(2,1)} %copy-done.10) | copy-start | bytes 405508
  28.5 0.9 %copy-start.13 = (bf16[528,128]{1,0:T(8,128)(2,1)S(1)}, bf16[528,128]{1,0:T(8,128)(2,1)}, u32[]{:S(2)}) copy-start(bf16[528,128]{1,0:T(8,128)(2,1)} %copy-done.12) | copy-start | bytes 405508
  29.4 0.9 %copy-start.15 = (bf16[528,128]{1,0:T(8,128)(2,1)S(1)}, bf16[528,128]{1,0:T(8,128)(2,1)}, u32[]{:S(2)}) copy-start(bf16[528,128]{1,0:T(8,128)(2,1)} %copy-done.14) | copy-start | bytes 405508
  42.5 6.0 %collective-permute-start.10 = (bf16[3,256,256]{2,1,0:T(8,128)(2,1)S(1)}, bf16[3,256,256]{2,1,0:T(8,128)(2,1)S(1)}, u32[]{:S(2)}, u32[]{:S(2)}) collective-permute-start(bf16[3,256,256]{2,1,0:T(8,128)(2,1)S(1)} %get-tuple-element.46), channel_id=1, source_target_pairs={{0,1},{1,0},{2,3},{3,2},{4,5},{5,4},{6,7},{7,6},{8,9},{9,8},{10,11... | collective-permute-start | bytes 1179656 | tf_op jit(solution)/shard_map/ppermute | solution.py:272
  46.0 2.5 %collective-permute-start.11 = (f32[8,128]{1,0:T(8,128)S(1)}, f32[8,128]{1,0:T(8,128)S(1)}, u32[]{:S(2)}, u32[]{:S(2)}) collective-permute-start(f32[8,128]{1,0:T(8,128)S(1)} %add_add_fusion), channel_id=1, source_target_pairs={{0,32},{16,48},{32,0},{48,16},{64,96},{80,112},{96,64},{112,80},{1... | collective-permute-start | bytes 12296 | tf_op jit(solution)/shard_map/ppermute | solution.py:276
  46.7 5.9 %collective-permute-start.12 = (bf16[256,256]{1,0:T(8,128)(2,1)S(1)}, bf16[256,256]{1,0:T(8,128)(2,1)S(1)}, u32[]{:S(2)}, u32[]{:S(2)}) collective-permute-start(bf16[256,256]{1,0:T(8,128)(2,1)S(1)} %get-tuple-element.50), channel_id=1, source_target_pairs={{2,0},{7,1},{4,2},{1,3},{6,4},{3,5},{0,6},{5,7},{10,8},{15,9},{12,... | collective-permute-start | bytes 393224 | tf_op jit(solution)/shard_map/ppermute | solution.py:272
  46.7 6.4 %collective-permute-start.13 = (bf16[256,256]{1,0:T(8,128)(2,1)S(1)}, bf16[256,256]{1,0:T(8,128)(2,1)S(1)}, u32[]{:S(2)}, u32[]{:S(2)}) collective-permute-start(bf16[256,256]{1,0:T(8,128)(2,1)S(1)} %get-tuple-element.51), channel_id=1, source_target_pairs={{3,0},{6,1},{5,2},{0,3},{7,4},{2,5},{1,6},{4,7},{11,8},{14,9},{13,... | collective-permute-start | bytes 393224 | tf_op jit(solution)/shard_map/ppermute | solution.py:272
  48.5 2.8 %collective-permute-start.14 = (f32[8,128]{1,0:T(8,128)S(1)}, f32[8,128]{1,0:T(8,128)S(1)}, u32[]{:S(2)}, u32[]{:S(2)}) collective-permute-start(f32[8,128]{1,0:T(8,128)S(1)} %add.42), channel_id=1, source_target_pairs={{0,16},{16,0},{32,48},{48,32},{64,80},{80,64},{96,112},{112,96},{1... | collective-permute-start | bytes 12296 | tf_op jit(solution)/shard_map/ppermute | solution.py:276
  49.8 7.9 %collective-permute-start.16 = (bf16[256,256]{1,0:T(8,128)(2,1)S(1)}, bf16[256,256]{1,0:T(8,128)(2,1)S(1)}, u32[]{:S(2)}, u32[]{:S(2)}) collective-permute-start(bf16[256,256]{1,0:T(8,128)(2,1)S(1)} %bitcast_add_fusion), channel_id=1, source_target_pairs={{0,2},{1,7},{2,4},{3,1},{4,6},{5,3},{6,0},{7,5},{8,10},{9,15},{10,... | collective-permute-start | bytes 393224 | tf_op jit(solution)/shard_map/ppermute | solution.py:272
  53.2 4.0 %collective-permute-start.17 = (f32[8,128]{1,0:T(8,128)S(1)}, f32[8,128]{1,0:T(8,128)S(1)}, u32[]{:S(2)}, u32[]{:S(2)}) collective-permute-start(f32[8,128]{1,0:T(8,128)S(1)} %add.45), channel_id=1, source_target_pairs={{0,8},{1,9},{2,10},{3,11},{4,12},{5,13},{6,14},{7,15},{8,0},{9,1},... | collective-permute-start | bytes 12296 | tf_op jit(solution)/shard_map/ppermute | solution.py:276
  56.2 5.1 %collective-permute-start.15 = (bf16[256,256]{1,0:T(8,128)(2,1)S(1)}, bf16[256,256]{1,0:T(8,128)(2,1)S(1)}, u32[]{:S(2)}, u32[]{:S(2)}) collective-permute-start(bf16[256,256]{1,0:T(8,128)(2,1)S(1)} %fusion.2), channel_id=1, source_target_pairs={{2,0},{7,1},{4,2},{1,3},{6,4},{3,5},{0,6},{5,7},{10,8},{15,9},{12,... | collective-permute-start | bytes 393224 | tf_op jit(solution)/shard_map/ppermute | solution.py:272

commit v13 on v12

--- a/solution.py
+++ b/solution.py
@@ -113,6 +113,7 @@
         out_shape=pltpu.VMEM((8, HEAD_DIM), jnp.float32),
         in_specs=[VMEM] * BLOCKS,
         out_specs=VMEM,
+        compiler_params=pltpu.CompilerParams(vmem_limit_bytes=MIB),
         cost_estimate=pl.CostEstimate(flops=10000, bytes_accessed=65536, transcendentals=0),
     )(*blocks)
 
@@ -272,7 +273,8 @@
         return lax.ppermute(block, "ka", route)
 
     def exchange(table, axis, *masks):
-        routes = [[(place, place ^ mask) for place in range(16)] for mask in masks]
+        extent = range(lax.axis_size(axis))
+        routes = [[(place, place ^ mask) for place in extent] for mask in masks]
         return sum((lax.ppermute(table, axis, route) for route in routes), table)
 
     own = pack(key_heads, value_heads, token_logprob, doc_ids, response)
@@ -290,7 +292,7 @@
     margin = pair_margin(blocks)
     near, margin = lax.optimization_barrier((near, margin))
     blocks = (own, near, far, opposite, own_s, near_s, far_s, opposite_s)
-    margin = exchange(margin, "pb", 4, 8, 12)
+    margin = exchange(margin, "pb", 8)
     attention, grad_queries, own_p, near_p, far_p, opposite_p, swap_p, opposite_s_p = attend(
         queries, grad_output, blocks
     )
@@ -300,15 +302,17 @@
     swapped = send(swap_p, swap)
     passed = send(opposite_p, back)
     passed_s = send(opposite_s_p, cross_back)
+    margin = exchange(margin, "pb", 4)
+    swapped, margin = lax.optimization_barrier((swapped, margin))
     margin = exchange(margin, "pb", 2)
-    swapped, margin = lax.optimization_barrier((swapped, margin))
-    margin = exchange(margin, "pb", 1)
     passed, passed_s, margin = lax.optimization_barrier((passed, passed_s, margin))
     wide = jnp.float32
     near_sum = (near_p.astype(wide) + swapped[1] + passed + passed_s).astype(jnp.bfloat16)
     far_sum = far_p + swapped[2]
     near_part = send(near_sum, back)
     far_part = send(far_sum, ahead)
+    margin = exchange(margin, "pb", 1)
+    far_part, margin = lax.optimization_barrier((far_part, margin))
     margin = exchange(margin, "ka", 8)
     total = own_p.astype(wide) + swapped[0] + near_part + far_part
     return (

time: 62.3 us -> 55.4 us (0.89)
  the two profiles are of different devices: /device:TPU:1 before, /device:TPU:8 now
where the time goes in v13:
time: 55.4 us; the launch traced here: 55.3 us
  starting transfers between devices  21.3 us (38%)
  waiting for transfers between devices  17.4 us (31%)
  Pallas kernels  14.4 us (26%)
  local copies, waits for them, and re-layouts  1.23 us (2%)
  between operations  0.72 us (1%)
    ppermute x5, starting transfers between devices, exchange(): return sum((lax.ppermute(table, axis, route) for route in routes), table)  12.9 us
    pallas_call x1, Pallas kernels, attend(): pl.pallas_call(attend_kernel, out_shape=(jax.ShapeDtypeStruct((ROWS, widt...  12.1 us
    ppermute x5, waiting for transfers between devices, exchange(): return sum((lax.ppermute(table, axis, route) for route in routes), table)  10.7 us
    ppermute x12, starting transfers between devices, send(): return lax.ppermute(block, 'ka', route)  8.41 us
    ppermute x12, waiting for transfers between devices, send(): return lax.ppermute(block, 'ka', route)  6.73 us
    pallas_call x1, Pallas kernels, fetch(): pl.pallas_call(fetch_kernel, out_shape=(pltpu.VMEM(queries.shape, jnp.bfl...  1.13 us
  transfers between devices with their start and end apart: 17, of which 6 were waited for; matrix products, arithmetic and copies ran while one was open for 2% of the time, Pallas kernels for 24%

profile of v13, /device:TPU:8, one launch (start us, length us, event | category | flops | bytes accessed | tf_op | source)
XLA Modules:
  0.0 55.3 jit_solution(18337834032200436752)
XLA Ops:
  0.6 1.0 %shard_map.111.refs_0_.own = bf16[528,128]{1,0:T(8,128)(2,1)S(1)} custom-call(bf16[256,128]{1,0:T(8,128)(2,1)} %keys.1, bf16[256,128]{1,0:T(8,128)(2,1)} %values.1, f32[2,128]{1,0:T(2,128)} %bitcast.13, s32[2,128]{1,0:T(2,128)} %bitcast.14, s32[2,128]{1,0:T(2,128)} %bitcast.15), custom_call_target="tpu_custom_call" | custom-call | flops 10000 | bytes 524288 | tf_op jit(solution)/shard_map/pallas_call | solution.py:83
  1.7 0.1 collective-permute-start.1
  1.8 1.6 %collective-permute-start = (bf16[528,128]{1,0:T(8,128)(2,1)S(1)}, bf16[528,128]{1,0:T(8,128)(2,1)S(1)}, u32[]{:S(2)}, u32[]{:S(2)}) collective-permute-start(bf16[528,128]{1,0:T(8,128)(2,1)S(1)} %shard_map.111.refs_0_.own), channel_id=1, source_target_pairs={{0,2},{1,7},{2,4},{3,1},{4,6},{5,3},{6,0},{7,5},{8,10},{9,15},{10,... | collective-permute-start | bytes 405512 | tf_op jit(solution)/shard_map/ppermute | solution.py:273
  3.3 0.0 collective-permute-done.1.refs_4_.own_s
  3.3 2.5 %collective-permute-start.2 = (bf16[528,128]{1,0:T(8,128)(2,1)S(1)}, bf16[528,128]{1,0:T(8,128)(2,1)S(1)}, u32[]{:S(2)}, u32[]{:S(2)}) collective-permute-start(bf16[528,128]{1,0:T(8,128)(2,1)S(1)} %shard_map.111.refs_0_.own), channel_id=1, source_target_pairs={{2,0},{7,1},{4,2},{1,3},{6,4},{3,5},{0,6},{5,7},{10,8},{15,9},{12,... | collective-permute-start | bytes 405512 | tf_op jit(solution)/shard_map/ppermute | solution.py:273
  5.9 2.2 %collective-permute-done.refs_1_.near = bf16[528,128]{1,0:T(8,128)(2,1)S(1)} collective-permute-done((bf16[528,128]{1,0:T(8,128)(2,1)S(1)}, bf16[528,128]{1,0:T(8,128)(2,1)S(1)}, u32[]{:S(2)}, u32[]{:S(2)}) %collective-permute-start) | collective-permute-done | bytes 135200 | tf_op jit(solution)/shard_map/ppermute | solution.py:273
  8.1 0.0 collective-permute-start.6
  8.1 2.7 %collective-permute-start.4 = (bf16[528,128]{1,0:T(8,128)(2,1)S(1)}, bf16[528,128]{1,0:T(8,128)(2,1)S(1)}, u32[]{:S(2)}, u32[]{:S(2)}) collective-permute-start(bf16[528,128]{1,0:T(8,128)(2,1)S(1)} %collective-permute-done.refs_1_.near), channel_id=1, source_target_pairs={{0,1},{1,0},{2,3},{3,2},{4,5},{5,4},{6,7},{7,6},{8,9},{9,8},{10,11... | collective-permute-start | bytes 405512 | tf_op jit(solution)/shard_map/ppermute | solution.py:273
  10.8 0.0 collective-permute-start.3
  10.8 0.0 collective-permute-done.2.refs_2_.far
  10.8 0.5 collective-permute-start.5
  11.4 1.1 %shard_map.110 = (bf16[256,768]{1,0:T(8,128)(2,1)S(1)}, bf16[256,768]{1,0:T(8,128)(2,1)S(1)}) custom-call(bf16[256,768]{1,0:T(8,128)(2,1)} %queries_hbm.1, bf16[256,768]{1,0:T(8,128)(2,1)} %grads_hbm.1), custom_call_target="tpu_custom_call" | custom-call | bytes 2097152 | tf_op jit(solution)/shard_map/pallas_call | solution.py:43
  12.5 0.0 collective-permute-done.6.refs_7_.opposite_s
  12.5 0.0 collective-permute-done.4.refs_5_.near_s
  12.5 4.5 %collective-permute-done.3.refs_3_.opposite = bf16[528,128]{1,0:T(8,128)(2,1)S(1)} collective-permute-done((bf16[528,128]{1,0:T(8,128)(2,1)S(1)}, bf16[528,128]{1,0:T(8,128)(2,1)S(1)}, u32[]{:S(2)}, u32[]{:S(2)}) %collective-permute-start.3) | collective-permute-done | bytes 135200 | tf_op jit(solution)/shard_map/ppermute | solution.py:273
  17.0 0.0 collective-permute-done.5.refs_6_.far_s
  17.0 0.1 shard_map.112
  17.1 7.4 %collective-permute-start.7 = (f32[8,128]{1,0:T(8,128)S(1)}, f32[8,128]{1,0:T(8,128)S(1)}, u32[]{:S(2)}, u32[]{:S(2)}) collective-permute-start(f32[8,128]{1,0:T(8,128)S(1)} %shard_map.112), channel_id=1, source_target_pairs={{0,128},{16,144},{32,160},{48,176},{64,192},{80,208},{96,224},{112... | collective-permute-start | bytes 12296 | tf_op jit(solution)/shard_map/ppermute | solution.py:278
  24.5 12.1 %shard_map.113 = (bf16[256,768]{1,0:T(8,128)(2,1)}, f32[256,768]{1,0:T(8,128)}, bf16[256,256]{1,0:T(8,128)(2,1)S(1)}, bf16[256,256]{1,0:T(8,128)(2,1)S(1)}, bf16...) custom-call(bf16[256,768]{1,0:T(8,128)(2,1)S(1)} %get-tuple-element., ...), custom_call_target="tpu_custom_call" | custom-call | flops 4831838208 | bytes 4194304 | tf_op jit(solution)/shard_map/pallas_call | solution.py:225
  36.7 0.0 collective-permute-done.7
  36.7 0.0 collective-permute-start.8
  36.7 1.8 %collective-permute-start.9 = (f32[8,128]{1,0:T(8,128)S(1)}, f32[8,128]{1,0:T(8,128)S(1)}, u32[]{:S(2)}, u32[]{:S(2)}) collective-permute-start(f32[8,128]{1,0:T(8,128)S(1)} %add.36), channel_id=1, source_target_pairs={{0,64},{16,80},{32,96},{48,112},{64,0},{80,16},{96,32},{112,48},{1... | collective-permute-start | bytes 12296 | tf_op jit(solution)/shard_map/ppermute | solution.py:278
  38.5 0.0 collective-permute-start.10
  38.5 0.0 collective-permute-start.11
  38.5 3.0 %collective-permute-done.9 = f32[8,128]{1,0:T(8,128)S(1)} collective-permute-done((f32[8,128]{1,0:T(8,128)S(1)}, f32[8,128]{1,0:T(8,128)S(1)}, u32[]{:S(2)}, u32[]{:S(2)}) %collective-permute-start.9) | collective-permute-done | bytes 4128 | tf_op jit(solution)/shard_map/ppermute | solution.py:278
  41.5 0.0 collective-permute-done.8
  41.5 1.0 %collective-permute-start.12 = (f32[8,128]{1,0:T(8,128)S(1)}, f32[8,128]{1,0:T(8,128)S(1)}, u32[]{:S(2)}, u32[]{:S(2)}) collective-permute-start(f32[8,128]{1,0:T(8,128)S(1)} %add.37), channel_id=1, source_target_pairs={{0,32},{16,48},{32,0},{48,16},{64,96},{80,112},{96,64},{112,80},{1... | collective-permute-start | bytes 12296 | tf_op jit(solution)/shard_map/ppermute | solution.py:278
  42.5 0.1 collective-permute-start.14
  42.6 2.5 %collective-permute-done.12 = f32[8,128]{1,0:T(8,128)S(1)} collective-permute-done((f32[8,128]{1,0:T(8,128)S(1)}, f32[8,128]{1,0:T(8,128)S(1)}, u32[]{:S(2)}, u32[]{:S(2)}) %collective-permute-start.12) | collective-permute-done | bytes 4128 | tf_op jit(solution)/shard_map/ppermute | solution.py:278
  45.1 0.0 collective-permute-done.10
  45.1 0.0 collective-permute-done.11
  45.1 0.1 fusion.2
  45.2 0.8 %collective-permute-start.13 = (bf16[256,256]{1,0:T(8,128)(2,1)S(1)}, bf16[256,256]{1,0:T(8,128)(2,1)S(1)}, u32[]{:S(2)}, u32[]{:S(2)}) collective-permute-start(bf16[256,256]{1,0:T(8,128)(2,1)S(1)} %fusion.2), channel_id=1, source_target_pairs={{2,0},{7,1},{4,2},{1,3},{6,4},{3,5},{0,6},{5,7},{10,8},{15,9},{12,... | collective-permute-start | bytes 393224 | tf_op jit(solution)/shard_map/ppermute | solution.py:273
  46.0 0.4 collective-permute-start.15
  46.5 3.2 %collective-permute-done.15 = f32[8,128]{1,0:T(8,128)S(1)} collective-permute-done((f32[8,128]{1,0:T(8,128)S(1)}, f32[8,128]{1,0:T(8,128)S(1)}, u32[]{:S(2)}, u32[]{:S(2)}) %collective-permute-start.15) | collective-permute-done | bytes 4128 | tf_op jit(solution)/shard_map/ppermute | solution.py:278
  49.6 0.0 collective-permute-done.14
  49.6 2.3 %collective-permute-start.16 = (f32[8,128]{1,0:T(8,128)S(1)}, f32[8,128]{1,0:T(8,128)S(1)}, u32[]{:S(2)}, u32[]{:S(2)}) collective-permute-start(f32[8,128]{1,0:T(8,128)S(1)} %add.45), channel_id=1, source_target_pairs={{0,8},{1,9},{2,10},{3,11},{4,12},{5,13},{6,14},{7,15},{8,0},{9,1},... | collective-permute-start | bytes 12296 | tf_op jit(solution)/shard_map/ppermute | solution.py:278
  51.9 0.0 collective-permute-done.13
  51.9 0.1 fusion.4
  52.0 0.7 %fusion.5 = (f32[256,128]{1,0:T(8,128)}, f32[256,128]{1,0:T(8,128)}) fusion(f32[256,256]{1,0:T(8,128)S(1)} %fusion.4), kind=kLoop, calls=%fused_computation.9 | loop fusion | bytes 524288 | tf_op jit(solution)/shard_map/slice | solution.py:319
  52.7 2.0 %collective-permute-done.16 = f32[8,128]{1,0:T(8,128)S(1)} collective-permute-done((f32[8,128]{1,0:T(8,128)S(1)}, f32[8,128]{1,0:T(8,128)S(1)}, u32[]{:S(2)}, u32[]{:S(2)}) %collective-permute-start.16) | collective-permute-done | bytes 4128 | tf_op jit(solution)/shard_map/ppermute | solution.py:278
  54.8 0.5 slice_bitcast_fusion
  (6 shorter events, 0.0 us)
Async XLA Ops:
  1.7 1.7 %collective-permute-start.1 = (bf16[528,128]{1,0:T(8,128)(2,1)S(1)}, bf16[528,128]{1,0:T(8,128)(2,1)S(1)}, u32[]{:S(2)}, u32[]{:S(2)}) collective-permute-start(bf16[528,128]{1,0:T(8,128)(2,1)S(1)} %shard_map.111.refs_0_.own), channel_id=1, source_target_pairs={{0,1},{1,0},{2,3},{3,2},{4,5},{5,4},{6,7},{7,6},{8,9},{9,8},{10,11... | collective-permute-start | bytes 405512 | tf_op jit(solution)/shard_map/ppermute | solution.py:273
  1.8 6.3 %collective-permute-start = (bf16[528,128]{1,0:T(8,128)(2,1)S(1)}, bf16[528,128]{1,0:T(8,128)(2,1)S(1)}, u32[]{:S(2)}, u32[]{:S(2)}) collective-permute-start(bf16[528,128]{1,0:T(8,128)(2,1)S(1)} %shard_map.111.refs_0_.own), channel_id=1, source_target_pairs={{0,2},{1,7},{2,4},{3,1},{4,6},{5,3},{6,0},{7,5},{8,10},{9,15},{10,... | collective-permute-start | bytes 405512 | tf_op jit(solution)/shard_map/ppermute | solution.py:273
  3.3 7.5 %collective-permute-start.2 = (bf16[528,128]{1,0:T(8,128)(2,1)S(1)}, bf16[528,128]{1,0:T(8,128)(2,1)S(1)}, u32[]{:S(2)}, u32[]{:S(2)}) collective-permute-start(bf16[528,128]{1,0:T(8,128)(2,1)S(1)} %shard_map.111.refs_0_.own), channel_id=1, source_target_pairs={{2,0},{7,1},{4,2},{1,3},{6,4},{3,5},{0,6},{5,7},{10,8},{15,9},{12,... | collective-permute-start | bytes 405512 | tf_op jit(solution)/shard_map/ppermute | solution.py:273
  8.1 4.4 %collective-permute-start.6 = (bf16[528,128]{1,0:T(8,128)(2,1)S(1)}, bf16[528,128]{1,0:T(8,128)(2,1)S(1)}, u32[]{:S(2)}, u32[]{:S(2)}) collective-permute-start(bf16[528,128]{1,0:T(8,128)(2,1)S(1)} %collective-permute-done.refs_1_.near), channel_id=1, source_target_pairs={{0,3},{1,6},{2,5},{3,0},{4,7},{5,2},{6,1},{7,4},{8,11},{9,14},{10,... | collective-permute-start | bytes 405512 | tf_op jit(solution)/shard_map/ppermute | solution.py:273
  8.1 4.5 %collective-permute-start.4 = (bf16[528,128]{1,0:T(8,128)(2,1)S(1)}, bf16[528,128]{1,0:T(8,128)(2,1)S(1)}, u32[]{:S(2)}, u32[]{:S(2)}) collective-permute-start(bf16[528,128]{1,0:T(8,128)(2,1)S(1)} %collective-permute-done.refs_1_.near), channel_id=1, source_target_pairs={{0,1},{1,0},{2,3},{3,2},{4,5},{5,4},{6,7},{7,6},{8,9},{9,8},{10,11... | collective-permute-start | bytes 405512 | tf_op jit(solution)/shard_map/ppermute | solution.py:273
  10.8 6.2 %collective-permute-start.3 = (bf16[528,128]{1,0:T(8,128)(2,1)S(1)}, bf16[528,128]{1,0:T(8,128)(2,1)S(1)}, u32[]{:S(2)}, u32[]{:S(2)}) collective-permute-start(bf16[528,128]{1,0:T(8,128)(2,1)S(1)} %collective-permute-done.refs_1_.near), channel_id=1, source_target_pairs={{0,2},{1,7},{2,4},{3,1},{4,6},{5,3},{6,0},{7,5},{8,10},{9,15},{10,... | collective-permute-start | bytes 405512 | tf_op jit(solution)/shard_map/ppermute | solution.py:273
  10.8 6.2 %collective-permute-start.5 = (bf16[528,128]{1,0:T(8,128)(2,1)S(1)}, bf16[528,128]{1,0:T(8,128)(2,1)S(1)}, u32[]{:S(2)}, u32[]{:S(2)}) collective-permute-start(bf16[528,128]{1,0:T(8,128)(2,1)S(1)} %collective-permute-done.2.refs_2_.far), channel_id=1, source_target_pairs={{0,1},{1,0},{2,3},{3,2},{4,5},{5,4},{6,7},{7,6},{8,9},{9,8},{10,11... | collective-permute-start | bytes 405512 | tf_op jit(solution)/shard_map/ppermute | solution.py:273
  17.1 19.5 %collective-permute-start.7 = (f32[8,128]{1,0:T(8,128)S(1)}, f32[8,128]{1,0:T(8,128)S(1)}, u32[]{:S(2)}, u32[]{:S(2)}) collective-permute-start(f32[8,128]{1,0:T(8,128)S(1)} %shard_map.112), channel_id=1, source_target_pairs={{0,128},{16,144},{32,160},{48,176},{64,192},{80,208},{96,224},{112... | collective-permute-start | bytes 12296 | tf_op jit(solution)/shard_map/ppermute | solution.py:278
  36.7 4.8 %collective-permute-start.8 = (bf16[3,256,256]{2,1,0:T(8,128)(2,1)S(1)}, bf16[3,256,256]{2,1,0:T(8,128)(2,1)S(1)}, u32[]{:S(2)}, u32[]{:S(2)}) collective-permute-start(bf16[3,256,256]{2,1,0:T(8,128)(2,1)S(1)} %get-tuple-element.48), channel_id=1, source_target_pairs={{0,1},{1,0},{2,3},{3,2},{4,5},{5,4},{6,7},{7,6},{8,9},{9,8},{10,11... | collective-permute-start | bytes 1179656 | tf_op jit(solution)/shard_map/ppermute | solution.py:273
  36.7 4.8 %collective-permute-start.9 = (f32[8,128]{1,0:T(8,128)S(1)}, f32[8,128]{1,0:T(8,128)S(1)}, u32[]{:S(2)}, u32[]{:S(2)}) collective-permute-start(f32[8,128]{1,0:T(8,128)S(1)} %add.36), channel_id=1, source_target_pairs={{0,64},{16,80},{32,96},{48,112},{64,0},{80,16},{96,32},{112,48},{1... | collective-permute-start | bytes 12296 | tf_op jit(solution)/shard_map/ppermute | solution.py:278
  38.5 6.7 %collective-permute-start.10 = (bf16[256,256]{1,0:T(8,128)(2,1)S(1)}, bf16[256,256]{1,0:T(8,128)(2,1)S(1)}, u32[]{:S(2)}, u32[]{:S(2)}) collective-permute-start(bf16[256,256]{1,0:T(8,128)(2,1)S(1)} %get-tuple-element.52), channel_id=1, source_target_pairs={{2,0},{7,1},{4,2},{1,3},{6,4},{3,5},{0,6},{5,7},{10,8},{15,9},{12,... | collective-permute-start | bytes 393224 | tf_op jit(solution)/shard_map/ppermute | solution.py:273
  38.5 6.7 %collective-permute-start.11 = (bf16[256,256]{1,0:T(8,128)(2,1)S(1)}, bf16[256,256]{1,0:T(8,128)(2,1)S(1)}, u32[]{:S(2)}, u32[]{:S(2)}) collective-permute-start(bf16[256,256]{1,0:T(8,128)(2,1)S(1)} %get-tuple-element.53), channel_id=1, source_target_pairs={{3,0},{6,1},{5,2},{0,3},{7,4},{2,5},{1,6},{4,7},{11,8},{14,9},{13,... | collective-permute-start | bytes 393224 | tf_op jit(solution)/shard_map/ppermute | solution.py:273
  41.5 3.6 %collective-permute-start.12 = (f32[8,128]{1,0:T(8,128)S(1)}, f32[8,128]{1,0:T(8,128)S(1)}, u32[]{:S(2)}, u32[]{:S(2)}) collective-permute-start(f32[8,128]{1,0:T(8,128)S(1)} %add.37), channel_id=1, source_target_pairs={{0,32},{16,48},{32,0},{48,16},{64,96},{80,112},{96,64},{112,80},{1... | collective-permute-start | bytes 12296 | tf_op jit(solution)/shard_map/ppermute | solution.py:278
  42.5 7.1 %collective-permute-start.14 = (bf16[256,256]{1,0:T(8,128)(2,1)S(1)}, bf16[256,256]{1,0:T(8,128)(2,1)S(1)}, u32[]{:S(2)}, u32[]{:S(2)}) collective-permute-start(bf16[256,256]{1,0:T(8,128)(2,1)S(1)} %bitcast_add_fusion), channel_id=1, source_target_pairs={{0,2},{1,7},{2,4},{3,1},{4,6},{5,3},{6,0},{7,5},{8,10},{9,15},{10,... | collective-permute-start | bytes 393224 | tf_op jit(solution)/shard_map/ppermute | solution.py:273
  45.2 6.7 %collective-permute-start.13 = (bf16[256,256]{1,0:T(8,128)(2,1)S(1)}, bf16[256,256]{1,0:T(8,128)(2,1)S(1)}, u32[]{:S(2)}, u32[]{:S(2)}) collective-permute-start(bf16[256,256]{1,0:T(8,128)(2,1)S(1)} %fusion.2), channel_id=1, source_target_pairs={{2,0},{7,1},{4,2},{1,3},{6,4},{3,5},{0,6},{5,7},{10,8},{15,9},{12,... | collective-permute-start | bytes 393224 | tf_op jit(solution)/shard_map/ppermute | solution.py:273
  46.0 3.6 %collective-permute-start.15 = (f32[8,128]{1,0:T(8,128)S(1)}, f32[8,128]{1,0:T(8,128)S(1)}, u32[]{:S(2)}, u32[]{:S(2)}) collective-permute-start(f32[8,128]{1,0:T(8,128)S(1)} %add.40), channel_id=1, source_target_pairs={{0,16},{16,0},{32,48},{48,32},{64,80},{80,64},{96,112},{112,96},{1... | collective-permute-start | bytes 12296 | tf_op jit(solution)/shard_map/ppermute | solution.py:278
  49.6 5.1 %collective-permute-start.16 = (f32[8,128]{1,0:T(8,128)S(1)}, f32[8,128]{1,0:T(8,128)S(1)}, u32[]{:S(2)}, u32[]{:S(2)}) collective-permute-start(f32[8,128]{1,0:T(8,128)S(1)} %add.45), channel_id=1, source_target_pairs={{0,8},{1,9},{2,10},{3,11},{4,12},{5,13},{6,14},{7,15},{8,0},{9,1},... | collective-permute-start | bytes 12296 | tf_op jit(solution)/shard_map/ppermute | solution.py:278

commit v14 on v13

--- a/solution.py
+++ b/solution.py
@@ -285,7 +285,8 @@
     far = send(own_later, back)
     opposite = send(near, ahead)
     opposite_s = send(near, cross)
-    near_s = send(near, swap)
+    near_later, far = lax.optimization_barrier((near, far))
+    near_s = send(near_later, swap)
     far_s = send(far, swap)
 
     blocks = (own, near, far, opposite, own_s, near_s, far_s, opposite_s)
@@ -311,9 +312,8 @@
     far_sum = far_p + swapped[2]
     near_part = send(near_sum, back)
     far_part = send(far_sum, ahead)
-    margin = exchange(margin, "pb", 1)
-    far_part, margin = lax.optimization_barrier((far_part, margin))
-    margin = exchange(margin, "ka", 8)
+    _, far_part, margin = lax.optimization_barrier((near_sum, far_part, margin))
+    margin = exchange(margin, ("pb", "ka"), 8, 16, 24)
     total = own_p.astype(wide) + swapped[0] + near_part + far_part
     return (
         attention, grad_queries, total[:, :HEAD_DIM], total[:, HEAD_DIM:], margin[0, :PAIRS]

time: 55.4 us -> 56.1 us (1.013)
  starting transfers between devices: 21.3 us -> 25.6 us
  waiting for transfers between devices: 17.4 us -> 13.9 us
    ppermute x12, starting transfers between devices: 8.41 us -> 11.9 us  [send(): return lax.ppermute(block, 'ka', route)]
    ppermute x5 -> x6, waiting for transfers between devices: 10.7 us -> 7.92 us  [exchange(): return sum((lax.ppermute(table, axis, route) for route in routes), table)]
    ppermute x12, waiting for transfers between devices: 6.73 us -> 5.97 us  [send(): return lax.ppermute(block, 'ka', route)]
    ppermute x5 -> x6, starting transfers between devices: 12.9 us -> 13.7 us  [exchange(): return sum((lax.ppermute(table, axis, route) for route in routes), table)]
  transfers between devices with their start and end apart: 17 -> 18, of which waited for: 6 -> 7; matrix products, arithmetic and copies ran while one was open for 2% -> 2% of each run, Pallas kernels for 24% -> 24%
where the time goes in v14:
time: 56.1 us; the launch traced here: 56 us
  starting transfers between devices  25.6 us (46%)
  Pallas kernels  14.4 us (26%)
  waiting for transfers between devices  13.9 us (25%)
  local copies, waits for them, and re-layouts  1.23 us (2%)
  between operations  0.71 us (1%)
    ppermute x6, starting transfers between devices, exchange(): return sum((lax.ppermute(table, axis, route) for route in routes), table)  13.7 us
    pallas_call x1, Pallas kernels, attend(): pl.pallas_call(attend_kernel, out_shape=(jax.ShapeDtypeStruct((ROWS, widt...  12.1 us
    ppermute x12, starting transfers between devices, send(): return lax.ppermute(block, 'ka', route)  11.9 us
    ppermute x6, waiting for transfers between devices, exchange(): return sum((lax.ppermute(table, axis, route) for route in routes), table)  7.92 us
    ppermute x12, waiting for transfers between devices, send(): return lax.ppermute(block, 'ka', route)  5.97 us
    pallas_call x1, Pallas kernels, fetch(): pl.pallas_call(fetch_kernel, out_shape=(pltpu.VMEM(queries.shape, jnp.bfl...  1.13 us
  transfers between devices with their start and end apart: 18, of which 7 were waited for; matrix products, arithmetic and copies ran while one was open for 2% of the time, Pallas kernels for 24%

profile of v14, /device:TPU:8, one launch (start us, length us, event | category | flops | bytes accessed | tf_op | source)
XLA Modules:
  0.0 56.0 jit_solution(9397659556494958739)
XLA Ops:
  0.6 1.0 %shard_map.111.refs_0_.own = bf16[528,128]{1,0:T(8,128)(2,1)S(1)} custom-call(bf16[256,128]{1,0:T(8,128)(2,1)} %keys.1, bf16[256,128]{1,0:T(8,128)(2,1)} %values.1, f32[2,128]{1,0:T(2,128)} %bitcast.13, s32[2,128]{1,0:T(2,128)} %bitcast.14, s32[2,128]{1,0:T(2,128)} %bitcast.15), custom_call_target="tpu_custom_call" | custom-call | flops 10000 | bytes 524288 | tf_op jit(solution)/shard_map/pallas_call | solution.py:83
  1.7 0.1 collective-permute-start.1
  1.8 1.6 %collective-permute-start = (bf16[528,128]{1,0:T(8,128)(2,1)S(1)}, bf16[528,128]{1,0:T(8,128)(2,1)S(1)}, u32[]{:S(2)}, u32[]{:S(2)}) collective-permute-start(bf16[528,128]{1,0:T(8,128)(2,1)S(1)} %shard_map.111.refs_0_.own), channel_id=1, source_target_pairs={{0,2},{1,7},{2,4},{3,1},{4,6},{5,3},{6,0},{7,5},{8,10},{9,15},{10,... | collective-permute-start | bytes 405512 | tf_op jit(solution)/shard_map/ppermute | solution.py:273
  3.3 0.0 collective-permute-done.1.refs_4_.own_s
  3.3 2.5 %collective-permute-start.2 = (bf16[528,128]{1,0:T(8,128)(2,1)S(1)}, bf16[528,128]{1,0:T(8,128)(2,1)S(1)}, u32[]{:S(2)}, u32[]{:S(2)}) collective-permute-start(bf16[528,128]{1,0:T(8,128)(2,1)S(1)} %shard_map.111.refs_0_.own), channel_id=1, source_target_pairs={{2,0},{7,1},{4,2},{1,3},{6,4},{3,5},{0,6},{5,7},{10,8},{15,9},{12,... | collective-permute-start | bytes 405512 | tf_op jit(solution)/shard_map/ppermute | solution.py:273
  5.9 2.2 %collective-permute-done.refs_1_.near = bf16[528,128]{1,0:T(8,128)(2,1)S(1)} collective-permute-done((bf16[528,128]{1,0:T(8,128)(2,1)S(1)}, bf16[528,128]{1,0:T(8,128)(2,1)S(1)}, u32[]{:S(2)}, u32[]{:S(2)}) %collective-permute-start) | collective-permute-done | bytes 135200 | tf_op jit(solution)/shard_map/ppermute | solution.py:273
  8.1 0.0 collective-permute-start.6
  8.1 1.0 %collective-permute-start.3 = (bf16[528,128]{1,0:T(8,128)(2,1)S(1)}, bf16[528,128]{1,0:T(8,128)(2,1)S(1)}, u32[]{:S(2)}, u32[]{:S(2)}) collective-permute-start(bf16[528,128]{1,0:T(8,128)(2,1)S(1)} %collective-permute-done.refs_1_.near), channel_id=1, source_target_pairs={{0,2},{1,7},{2,4},{3,1},{4,6},{5,3},{6,0},{7,5},{8,10},{9,15},{10,... | collective-permute-start | bytes 405512 | tf_op jit(solution)/shard_map/ppermute | solution.py:273
  9.1 0.0 collective-permute-done.2.refs_2_.far
  9.1 2.3 %collective-permute-start.4 = (bf16[528,128]{1,0:T(8,128)(2,1)S(1)}, bf16[528,128]{1,0:T(8,128)(2,1)S(1)}, u32[]{:S(2)}, u32[]{:S(2)}) collective-permute-start(bf16[528,128]{1,0:T(8,128)(2,1)S(1)} %collective-permute-done.refs_1_.near), channel_id=1, source_target_pairs={{0,1},{1,0},{2,3},{3,2},{4,5},{5,4},{6,7},{7,6},{8,9},{9,8},{10,11... | collective-permute-start | bytes 405512 | tf_op jit(solution)/shard_map/ppermute | solution.py:273
  11.4 0.0 collective-permute-start.5
  11.4 1.1 %shard_map.110 = (bf16[256,768]{1,0:T(8,128)(2,1)S(1)}, bf16[256,768]{1,0:T(8,128)(2,1)S(1)}) custom-call(bf16[256,768]{1,0:T(8,128)(2,1)} %queries_hbm.1, bf16[256,768]{1,0:T(8,128)(2,1)} %grads_hbm.1), custom_call_target="tpu_custom_call" | custom-call | bytes 2097152 | tf_op jit(solution)/shard_map/pallas_call | solution.py:43
  12.5 0.0 collective-permute-done.6.refs_7_.opposite_s
  12.5 2.6 %collective-permute-done.3.refs_3_.opposite = bf16[528,128]{1,0:T(8,128)(2,1)S(1)} collective-permute-done((bf16[528,128]{1,0:T(8,128)(2,1)S(1)}, bf16[528,128]{1,0:T(8,128)(2,1)S(1)}, u32[]{:S(2)}, u32[]{:S(2)}) %collective-permute-start.3) | collective-permute-done | bytes 135200 | tf_op jit(solution)/shard_map/ppermute | solution.py:273
  15.1 0.0 collective-permute-done.4.refs_5_.near_s
  15.1 0.0 collective-permute-done.5.refs_6_.far_s
  15.2 0.1 shard_map.112
  15.2 7.4 %collective-permute-start.7 = (f32[8,128]{1,0:T(8,128)S(1)}, f32[8,128]{1,0:T(8,128)S(1)}, u32[]{:S(2)}, u32[]{:S(2)}) collective-permute-start(f32[8,128]{1,0:T(8,128)S(1)} %shard_map.112), channel_id=1, source_target_pairs={{0,128},{16,144},{32,160},{48,176},{64,192},{80,208},{96,224},{112... | collective-permute-start | bytes 12296 | tf_op jit(solution)/shard_map/ppermute | solution.py:278
  22.6 12.1 %shard_map.113 = (bf16[256,768]{1,0:T(8,128)(2,1)}, f32[256,768]{1,0:T(8,128)}, bf16[256,256]{1,0:T(8,128)(2,1)S(1)}, bf16[256,256]{1,0:T(8,128)(2,1)S(1)}, bf16...) custom-call(bf16[256,768]{1,0:T(8,128)(2,1)S(1)} %get-tuple-element., ...), custom_call_target="tpu_custom_call" | custom-call | flops 4831838208 | bytes 4194304 | tf_op jit(solution)/shard_map/pallas_call | solution.py:225
  34.8 0.0 collective-permute-done.7
  34.8 0.0 collective-permute-start.8
  34.8 1.8 %collective-permute-start.9 = (f32[8,128]{1,0:T(8,128)S(1)}, f32[8,128]{1,0:T(8,128)S(1)}, u32[]{:S(2)}, u32[]{:S(2)}) collective-permute-start(f32[8,128]{1,0:T(8,128)S(1)} %add.39), channel_id=1, source_target_pairs={{0,64},{16,80},{32,96},{48,112},{64,0},{80,16},{96,32},{112,48},{1... | collective-permute-start | bytes 12296 | tf_op jit(solution)/shard_map/ppermute | solution.py:278
  36.6 1.9 %collective-permute-start.10 = (bf16[256,256]{1,0:T(8,128)(2,1)S(1)}, bf16[256,256]{1,0:T(8,128)(2,1)S(1)}, u32[]{:S(2)}, u32[]{:S(2)}) collective-permute-start(bf16[256,256]{1,0:T(8,128)(2,1)S(1)} %get-tuple-element.56), channel_id=1, source_target_pairs={{2,0},{7,1},{4,2},{1,3},{6,4},{3,5},{0,6},{5,7},{10,8},{15,9},{12,... | collective-permute-start | bytes 393224 | tf_op jit(solution)/shard_map/ppermute | solution.py:273
  38.4 0.0 collective-permute-start.11
  38.5 1.1 %collective-permute-done.9 = f32[8,128]{1,0:T(8,128)S(1)} collective-permute-done((f32[8,128]{1,0:T(8,128)S(1)}, f32[8,128]{1,0:T(8,128)S(1)}, u32[]{:S(2)}, u32[]{:S(2)}) %collective-permute-start.9) | collective-permute-done | bytes 4128 | tf_op jit(solution)/shard_map/ppermute | solution.py:278
  39.6 0.0 collective-permute-done.8
  39.6 1.0 %collective-permute-start.12 = (f32[8,128]{1,0:T(8,128)S(1)}, f32[8,128]{1,0:T(8,128)S(1)}, u32[]{:S(2)}, u32[]{:S(2)}) collective-permute-start(f32[8,128]{1,0:T(8,128)S(1)} %add.40), channel_id=1, source_target_pairs={{0,32},{16,48},{32,0},{48,16},{64,96},{80,112},{96,64},{112,80},{1... | collective-permute-start | bytes 12296 | tf_op jit(solution)/shard_map/ppermute | solution.py:278
  40.6 0.1 collective-permute-start.14
  40.7 2.5 %collective-permute-done.12 = f32[8,128]{1,0:T(8,128)S(1)} collective-permute-done((f32[8,128]{1,0:T(8,128)S(1)}, f32[8,128]{1,0:T(8,128)S(1)}, u32[]{:S(2)}, u32[]{:S(2)}) %collective-permute-start.12) | collective-permute-done | bytes 4128 | tf_op jit(solution)/shard_map/ppermute | solution.py:278
  43.2 0.0 collective-permute-done.10
  43.2 0.0 collective-permute-done.11
  43.2 0.1 fusion.2
  43.3 2.5 %collective-permute-start.13 = (bf16[256,256]{1,0:T(8,128)(2,1)S(1)}, bf16[256,256]{1,0:T(8,128)(2,1)S(1)}, u32[]{:S(2)}, u32[]{:S(2)}) collective-permute-start(bf16[256,256]{1,0:T(8,128)(2,1)S(1)} %fusion.2), channel_id=1, source_target_pairs={{2,0},{7,1},{4,2},{1,3},{6,4},{3,5},{0,6},{5,7},{10,8},{15,9},{12,... | collective-permute-start | bytes 393224 | tf_op jit(solution)/shard_map/ppermute | solution.py:273
  45.8 1.1 %collective-permute-done.14 = bf16[256,256]{1,0:T(8,128)(2,1)S(1)} collective-permute-done((bf16[256,256]{1,0:T(8,128)(2,1)S(1)}, bf16[256,256]{1,0:T(8,128)(2,1)S(1)}, u32[]{:S(2)}, u32[]{:S(2)}) %collective-permute-start.14) | collective-permute-done | bytes 131104 | tf_op jit(solution)/shard_map/ppermute | solution.py:273
  46.9 1.6 %collective-permute-start.17 = (f32[8,128]{1,0:T(8,128)S(1)}, f32[8,128]{1,0:T(8,128)S(1)}, u32[]{:S(2)}, u32[]{:S(2)}) collective-permute-start(f32[8,128]{1,0:T(8,128)S(1)} %add.43), channel_id=1, source_target_pairs={{0,24},{1,25},{2,26},{3,27},{4,28},{5,29},{6,30},{7,31},{8,16},{9,... | collective-permute-start | bytes 12296 | tf_op jit(solution)/shard_map/ppermute | solution.py:278
  48.5 1.9 %collective-permute-start.16 = (f32[8,128]{1,0:T(8,128)S(1)}, f32[8,128]{1,0:T(8,128)S(1)}, u32[]{:S(2)}, u32[]{:S(2)}) collective-permute-start(f32[8,128]{1,0:T(8,128)S(1)} %add.43), channel_id=1, source_target_pairs={{0,16},{1,17},{2,18},{3,19},{4,20},{5,21},{6,22},{7,23},{8,24},{9,... | collective-permute-start | bytes 12296 | tf_op jit(solution)/shard_map/ppermute | solution.py:278
  50.4 0.0 collective-permute-start.15
  50.4 0.0 collective-permute-done.13
  50.4 0.1 fusion.4
  50.5 0.7 %fusion.5 = (f32[256,128]{1,0:T(8,128)}, f32[256,128]{1,0:T(8,128)}) fusion(f32[256,256]{1,0:T(8,128)S(1)} %fusion.4), kind=kLoop, calls=%fused_computation.10 | loop fusion | bytes 524288 | tf_op jit(solution)/shard_map/slice | solution.py:319
  51.2 0.0 collective-permute-done.17
  51.2 0.9 %collective-permute-done.16 = f32[8,128]{1,0:T(8,128)S(1)} collective-permute-done((f32[8,128]{1,0:T(8,128)S(1)}, f32[8,128]{1,0:T(8,128)S(1)}, u32[]{:S(2)}, u32[]{:S(2)}) %collective-permute-start.16) | collective-permute-done | bytes 4128 | tf_op jit(solution)/shard_map/ppermute | solution.py:278
  52.1 3.4 %collective-permute-done.15 = f32[8,128]{1,0:T(8,128)S(1)} collective-permute-done((f32[8,128]{1,0:T(8,128)S(1)}, f32[8,128]{1,0:T(8,128)S(1)}, u32[]{:S(2)}, u32[]{:S(2)}) %collective-permute-start.15) | collective-permute-done | bytes 4128 | tf_op jit(solution)/shard_map/ppermute | solution.py:278
  55.5 0.5 slice_bitcast_fusion
  (5 shorter events, 0.0 us)
Async XLA Ops:
  1.7 1.7 %collective-permute-start.1 = (bf16[528,128]{1,0:T(8,128)(2,1)S(1)}, bf16[528,128]{1,0:T(8,128)(2,1)S(1)}, u32[]{:S(2)}, u32[]{:S(2)}) collective-permute-start(bf16[528,128]{1,0:T(8,128)(2,1)S(1)} %shard_map.111.refs_0_.own), channel_id=1, source_target_pairs={{0,1},{1,0},{2,3},{3,2},{4,5},{5,4},{6,7},{7,6},{8,9},{9,8},{10,11... | collective-permute-start | bytes 405512 | tf_op jit(solution)/shard_map/ppermute | solution.py:273
  1.8 6.3 %collective-permute-start = (bf16[528,128]{1,0:T(8,128)(2,1)S(1)}, bf16[528,128]{1,0:T(8,128)(2,1)S(1)}, u32[]{:S(2)}, u32[]{:S(2)}) collective-permute-start(bf16[528,128]{1,0:T(8,128)(2,1)S(1)} %shard_map.111.refs_0_.own), channel_id=1, source_target_pairs={{0,2},{1,7},{2,4},{3,1},{4,6},{5,3},{6,0},{7,5},{8,10},{9,15},{10,... | collective-permute-start | bytes 405512 | tf_op jit(solution)/shard_map/ppermute | solution.py:273
  3.3 5.8 %collective-permute-start.2 = (bf16[528,128]{1,0:T(8,128)(2,1)S(1)}, bf16[528,128]{1,0:T(8,128)(2,1)S(1)}, u32[]{:S(2)}, u32[]{:S(2)}) collective-permute-start(bf16[528,128]{1,0:T(8,128)(2,1)S(1)} %shard_map.111.refs_0_.own), channel_id=1, source_target_pairs={{2,0},{7,1},{4,2},{1,3},{6,4},{3,5},{0,6},{5,7},{10,8},{15,9},{12,... | collective-permute-start | bytes 405512 | tf_op jit(solution)/shard_map/ppermute | solution.py:273
  8.1 4.4 %collective-permute-start.6 = (bf16[528,128]{1,0:T(8,128)(2,1)S(1)}, bf16[528,128]{1,0:T(8,128)(2,1)S(1)}, u32[]{:S(2)}, u32[]{:S(2)}) collective-permute-start(bf16[528,128]{1,0:T(8,128)(2,1)S(1)} %collective-permute-done.refs_1_.near), channel_id=1, source_target_pairs={{0,3},{1,6},{2,5},{3,0},{4,7},{5,2},{6,1},{7,4},{8,11},{9,14},{10,... | collective-permute-start | bytes 405512 | tf_op jit(solution)/shard_map/ppermute | solution.py:273
  8.1 7.1 %collective-permute-start.3 = (bf16[528,128]{1,0:T(8,128)(2,1)S(1)}, bf16[528,128]{1,0:T(8,128)(2,1)S(1)}, u32[]{:S(2)}, u32[]{:S(2)}) collective-permute-start(bf16[528,128]{1,0:T(8,128)(2,1)S(1)} %collective-permute-done.refs_1_.near), channel_id=1, source_target_pairs={{0,2},{1,7},{2,4},{3,1},{4,6},{5,3},{6,0},{7,5},{8,10},{9,15},{10,... | collective-permute-start | bytes 405512 | tf_op jit(solution)/shard_map/ppermute | solution.py:273
  9.1 6.0 %collective-permute-start.4 = (bf16[528,128]{1,0:T(8,128)(2,1)S(1)}, bf16[528,128]{1,0:T(8,128)(2,1)S(1)}, u32[]{:S(2)}, u32[]{:S(2)}) collective-permute-start(bf16[528,128]{1,0:T(8,128)(2,1)S(1)} %collective-permute-done.refs_1_.near), channel_id=1, source_target_pairs={{0,1},{1,0},{2,3},{3,2},{4,5},{5,4},{6,7},{7,6},{8,9},{9,8},{10,11... | collective-permute-start | bytes 405512 | tf_op jit(solution)/shard_map/ppermute | solution.py:273
  11.4 3.8 %collective-permute-start.5 = (bf16[528,128]{1,0:T(8,128)(2,1)S(1)}, bf16[528,128]{1,0:T(8,128)(2,1)S(1)}, u32[]{:S(2)}, u32[]{:S(2)}) collective-permute-start(bf16[528,128]{1,0:T(8,128)(2,1)S(1)} %collective-permute-done.2.refs_2_.far), channel_id=1, source_target_pairs={{0,1},{1,0},{2,3},{3,2},{4,5},{5,4},{6,7},{7,6},{8,9},{9,8},{10,11... | collective-permute-start | bytes 405512 | tf_op jit(solution)/shard_map/ppermute | solution.py:273
  15.2 19.5 %collective-permute-start.7 = (f32[8,128]{1,0:T(8,128)S(1)}, f32[8,128]{1,0:T(8,128)S(1)}, u32[]{:S(2)}, u32[]{:S(2)}) collective-permute-start(f32[8,128]{1,0:T(8,128)S(1)} %shard_map.112), channel_id=1, source_target_pairs={{0,128},{16,144},{32,160},{48,176},{64,192},{80,208},{96,224},{112... | collective-permute-start | bytes 12296 | tf_op jit(solution)/shard_map/ppermute | solution.py:278
  34.8 4.8 %collective-permute-start.8 = (bf16[3,256,256]{2,1,0:T(8,128)(2,1)S(1)}, bf16[3,256,256]{2,1,0:T(8,128)(2,1)S(1)}, u32[]{:S(2)}, u32[]{:S(2)}) collective-permute-start(bf16[3,256,256]{2,1,0:T(8,128)(2,1)S(1)} %get-tuple-element.52), channel_id=1, source_target_pairs={{0,1},{1,0},{2,3},{3,2},{4,5},{5,4},{6,7},{7,6},{8,9},{9,8},{10,11... | collective-permute-start | bytes 1179656 | tf_op jit(solution)/shard_map/ppermute | solution.py:273
  34.8 4.8 %collective-permute-start.9 = (f32[8,128]{1,0:T(8,128)S(1)}, f32[8,128]{1,0:T(8,128)S(1)}, u32[]{:S(2)}, u32[]{:S(2)}) collective-permute-start(f32[8,128]{1,0:T(8,128)S(1)} %add.39), channel_id=1, source_target_pairs={{0,64},{16,80},{32,96},{48,112},{64,0},{80,16},{96,32},{112,48},{1... | collective-permute-start | bytes 12296 | tf_op jit(solution)/shard_map/ppermute | solution.py:278
  36.6 6.7 %collective-permute-start.10 = (bf16[256,256]{1,0:T(8,128)(2,1)S(1)}, bf16[256,256]{1,0:T(8,128)(2,1)S(1)}, u32[]{:S(2)}, u32[]{:S(2)}) collective-permute-start(bf16[256,256]{1,0:T(8,128)(2,1)S(1)} %get-tuple-element.56), channel_id=1, source_target_pairs={{2,0},{7,1},{4,2},{1,3},{6,4},{3,5},{0,6},{5,7},{10,8},{15,9},{12,... | collective-permute-start | bytes 393224 | tf_op jit(solution)/shard_map/ppermute | solution.py:273
  38.4 4.8 %collective-permute-start.11 = (bf16[256,256]{1,0:T(8,128)(2,1)S(1)}, bf16[256,256]{1,0:T(8,128)(2,1)S(1)}, u32[]{:S(2)}, u32[]{:S(2)}) collective-permute-start(bf16[256,256]{1,0:T(8,128)(2,1)S(1)} %get-tuple-element.57), channel_id=1, source_target_pairs={{3,0},{6,1},{5,2},{0,3},{7,4},{2,5},{1,6},{4,7},{11,8},{14,9},{13,... | collective-permute-start | bytes 393224 | tf_op jit(solution)/shard_map/ppermute | solution.py:273
  39.6 3.6 %collective-permute-start.12 = (f32[8,128]{1,0:T(8,128)S(1)}, f32[8,128]{1,0:T(8,128)S(1)}, u32[]{:S(2)}, u32[]{:S(2)}) collective-permute-start(f32[8,128]{1,0:T(8,128)S(1)} %add.40), channel_id=1, source_target_pairs={{0,32},{16,48},{32,0},{48,16},{64,96},{80,112},{96,64},{112,80},{1... | collective-permute-start | bytes 12296 | tf_op jit(solution)/shard_map/ppermute | solution.py:278
  40.6 6.3 %collective-permute-start.14 = (bf16[256,256]{1,0:T(8,128)(2,1)S(1)}, bf16[256,256]{1,0:T(8,128)(2,1)S(1)}, u32[]{:S(2)}, u32[]{:S(2)}) collective-permute-start(bf16[256,256]{1,0:T(8,128)(2,1)S(1)} %bitcast_add_fusion), channel_id=1, source_target_pairs={{0,2},{1,7},{2,4},{3,1},{4,6},{5,3},{6,0},{7,5},{8,10},{9,15},{10,... | collective-permute-start | bytes 393224 | tf_op jit(solution)/shard_map/ppermute | solution.py:273
  43.3 7.1 %collective-permute-start.13 = (bf16[256,256]{1,0:T(8,128)(2,1)S(1)}, bf16[256,256]{1,0:T(8,128)(2,1)S(1)}, u32[]{:S(2)}, u32[]{:S(2)}) collective-permute-start(bf16[256,256]{1,0:T(8,128)(2,1)S(1)} %fusion.2), channel_id=1, source_target_pairs={{2,0},{7,1},{4,2},{1,3},{6,4},{3,5},{0,6},{5,7},{10,8},{15,9},{12,... | collective-permute-start | bytes 393224 | tf_op jit(solution)/shard_map/ppermute | solution.py:273
  46.9 4.3 %collective-permute-start.17 = (f32[8,128]{1,0:T(8,128)S(1)}, f32[8,128]{1,0:T(8,128)S(1)}, u32[]{:S(2)}, u32[]{:S(2)}) collective-permute-start(f32[8,128]{1,0:T(8,128)S(1)} %add.43), channel_id=1, source_target_pairs={{0,24},{1,25},{2,26},{3,27},{4,28},{5,29},{6,30},{7,31},{8,16},{9,... | collective-permute-start | bytes 12296 | tf_op jit(solution)/shard_map/ppermute | solution.py:278
  48.5 3.6 %collective-permute-start.16 = (f32[8,128]{1,0:T(8,128)S(1)}, f32[8,128]{1,0:T(8,128)S(1)}, u32[]{:S(2)}, u32[]{:S(2)}) collective-permute-start(f32[8,128]{1,0:T(8,128)S(1)} %add.43), channel_id=1, source_target_pairs={{0,16},{1,17},{2,18},{3,19},{4,20},{5,21},{6,22},{7,23},{8,24},{9,... | collective-permute-start | bytes 12296 | tf_op jit(solution)/shard_map/ppermute | solution.py:278
  50.4 5.1 %collective-permute-start.15 = (f32[8,128]{1,0:T(8,128)S(1)}, f32[8,128]{1,0:T(8,128)S(1)}, u32[]{:S(2)}, u32[]{:S(2)}) collective-permute-start(f32[8,128]{1,0:T(8,128)S(1)} %add.43), channel_id=1, source_target_pairs={{0,8},{1,9},{2,10},{3,11},{4,12},{5,13},{6,14},{7,15},{8,0},{9,1},... | collective-permute-start | bytes 12296 | tf_op jit(solution)/shard_map/ppermute | solution.py:278
